TPU v7x, 32 devices: a whole 2x2x4 slice. The times are simulated.
32 devices in a mesh: dp: 8 (over y, x, core), tensor: 4 (over z).
Axes of the slice: x: 2, y: 2, z: 4, core: 2. Of those that a mesh axis runs over, the one named last changes fastest.
Arguments:
- layer_input: bfloat16 [16384, 1024], P(('dp', 'tensor')), may hold values from -11 to 11
- first_gain: bfloat16 [2, 1024], P(None, 'dp'), may hold values from 0.099609375 to 1.8984375
- first_shift: bfloat16 [2, 1024], P(None, 'dp'), may hold values from -1.5 to 1.5
- project_weight: bfloat16 [2, 3, 1024, 1024], P(None, None, 'dp', 'tensor')
- project_bias: bfloat16 [2, 2, 1024], P(None, None, ('tensor', 'dp'))
- output_weight: bfloat16 [2, 1024, 1024], P(None, 'tensor', 'dp'), may hold values from -0.75 to 0.75
- output_bias: bfloat16 [2, 1024], P(None, 'dp'), may hold values from -1.5 to 1.5
- second_gain: bfloat16 [2, 1024], P(None, 'dp'), may hold values from 0.099609375 to 1.8984375
- second_shift: bfloat16 [2, 1024], P(None, 'dp'), may hold values from -1.5 to 1.5
- expand_weight: bfloat16 [2, 1024, 4096], P(None, 'dp', 'tensor'), may hold values from -0.1875 to 0.1875
- expand_bias: bfloat16 [2, 4096], P(None, ('tensor', 'dp')), may hold values from -1.5 to 1.5
- reduce_weight: bfloat16 [2, 4096, 1024], P(None, 'tensor', 'dp'), may hold values from -0.09375 to 0.09375
- reduce_bias: bfloat16 [2, 1024], P(None, 'dp'), may hold values from -1.5 to 1.5
- picture_start: int32 [8, 2], P('dp'), may hold values from 0 to 1792, as said below
- cotangent: bfloat16 [16384, 1024], P(('dp', 'tensor')), may hold values from -6 to 6
Outputs:
- layer_output: bfloat16 [16384, 1024], P(('dp', 'tensor'))
- input_grad: bfloat16 [16384, 1024], P(('dp', 'tensor'))
- grad_first_gain: float32 [2, 1024], P(None, 'dp')
- grad_first_shift: float32 [2, 1024], P(None, 'dp')
- grad_project_weight: float32 [2, 3, 1024, 1024], P(None, None, 'dp', 'tensor')
- grad_project_bias: float32 [2, 2, 1024], P(None, None, ('tensor', 'dp'))
- grad_output_weight: float32 [2, 1024, 1024], P(None, 'tensor', 'dp')
- grad_output_bias: float32 [2, 1024], P(None, 'dp')
- grad_second_gain: float32 [2, 1024], P(None, 'dp')
- grad_second_shift: float32 [2, 1024], P(None, 'dp')
- grad_expand_weight: float32 [2, 1024, 4096], P(None, 'dp', 'tensor')
- grad_expand_bias: float32 [2, 4096], P(None, ('tensor', 'dp'))
- grad_reduce_weight: float32 [2, 4096, 1024], P(None, 'tensor', 'dp')
- grad_reduce_bias: float32 [2, 1024], P(None, 'dp')
Inputs may be any that keep to these rules, and one draw needn't show every extreme that they name: `picture_start`: piece p of a sequence starts at a position from p * 1024 to (p + 1) * 1024 - 256, so pieces of one sequence never intersect and lie inside it.
All inputs are finite; a program needn't handle non-finite values.
Results may differ from a plain program's by a relative error of at most 0.025.
Values may be sent and summed in bfloat16 or wider, within the bound.
A program may use at most 256 MiB of HBM per device.

v0:
```python
import jax
import jax.numpy as jnp
from jax import lax
from jax.sharding import PartitionSpec as P

HEADS = 16
HD = 64
LAYERS = 2
SEQ_LEN = 2048
PIECE = 256


NORM_EPS = 1e-05


def layer_norm(values, gain, shift):
    centred = values - jnp.mean(values, axis=-1, keepdims=True)
    spread = jnp.mean(centred * centred, axis=-1, keepdims=True)
    return centred * lax.rsqrt(spread + NORM_EPS) * gain + shift


def gelu_tanh(values):
    return jax.nn.gelu(values, approximate=True)


def piece_numbers(starts):
    places = jnp.arange(SEQ_LEN, dtype=jnp.int32)
    inside = (places[:, None] >= starts[None, :]) & (places[:, None] < starts[None, :] + PIECE)
    numbers = jnp.arange(1, starts.shape[0] + 1, dtype=jnp.int32)
    return jnp.sum(jnp.where(inside, numbers[None, :], 0), axis=1)


def head_slopes(first_head, count_heads):
    heads_at = (first_head + jnp.arange(count_heads, dtype=jnp.int32)).astype(jnp.float32)
    return jnp.exp2(-8.0 * (heads_at + 1.0) / HEADS)


def gather_rows(values):
    return lax.all_gather(values, "tensor", axis=0, tiled=True)


def gather_grads(values):
    return lax.all_gather(values, "tensor", axis=0, tiled=True)


def scatter_rows(values, weight):
    rows_here = values.shape[0] // lax.axis_size("tensor")

    def partial_term(offset, count_rows):
        return jnp.dot(values, weight, preferred_element_type=jnp.float32)

    return lax.psum_scatter(
        partial_term(jnp.int32(0), rows_here * lax.axis_size("tensor")).astype(jnp.bfloat16),
        "tensor",
        scatter_dimension=0,
        tiled=True,
    ).astype(jnp.float32)


def scatter_back(partial_term, rows_here):
    return lax.psum_scatter(
        partial_term(jnp.int32(0), rows_here * lax.axis_size("tensor")).astype(jnp.bfloat16),
        "tensor",
        scatter_dimension=0,
        tiled=True,
    ).astype(jnp.float32)


def block_scores(query_block, key_rows, offset, piece_ids, slopes):
    length = key_rows.shape[0]
    count_rows = query_block.shape[0]
    query_places = offset + jnp.arange(count_rows, dtype=jnp.int32)
    key_places = jnp.arange(length, dtype=jnp.int32)
    product = jnp.einsum("qhe,khe->hqk", query_block, key_rows, preferred_element_type=jnp.float32)
    distance = jnp.abs(query_places[:, None] - key_places[None, :]).astype(jnp.float32)
    scores = product * HD ** (-0.5) - slopes[:, None, None] * distance[None]
    query_pieces = lax.dynamic_slice_in_dim(piece_ids, offset, count_rows, 0)
    allowed = (key_places[None, :] <= query_places[:, None]) | (
        query_pieces[:, None] == piece_ids[None, :]
    ) & (query_pieces[:, None] > 0)
    return jnp.where(allowed[None], scores, -jnp.inf)


def sequence_forward(operands, slopes):
    queries, key_rows, value_rows, piece_ids = operands
    length = queries.shape[0]
    block_rows = min(512, length)

    def one_block(block_index):
        offset = block_index * block_rows
        query_block = lax.dynamic_slice_in_dim(queries, offset, block_rows, 0)
        scores = block_scores(query_block, key_rows, offset, piece_ids, slopes)
        row_max = jnp.max(scores, axis=-1, keepdims=True)
        raw_weights = jnp.exp(scores - row_max)
        totals = jnp.sum(raw_weights, axis=-1, keepdims=True)
        soft_weights = (raw_weights / totals).astype(jnp.bfloat16)
        attended = jnp.einsum(
            "hqk,khe->qhe", soft_weights, value_rows, preferred_element_type=jnp.float32
        )
        return (attended.astype(jnp.bfloat16), (row_max + jnp.log(totals))[..., 0])

    attended, log_total = lax.map(one_block, jnp.arange(length // block_rows, dtype=jnp.int32))
    return (attended.reshape(length, queries.shape[1], queries.shape[2]), log_total)


def sequence_backward(operands, slopes):
    queries, key_rows, value_rows, piece_ids, grad_mixed, log_total = operands
    length = queries.shape[0]
    block_rows = min(512, length)

    def one_block(carry, block_index):
        key_grad, value_grad = carry
        offset = block_index * block_rows
        query_block = lax.dynamic_slice_in_dim(queries, offset, block_rows, 0)
        grad_block = lax.dynamic_slice_in_dim(grad_mixed, offset, block_rows, 0)
        scores = block_scores(query_block, key_rows, offset, piece_ids, slopes)
        probs = jnp.exp(scores - log_total[block_index][..., None])
        soft_weights = probs.astype(jnp.bfloat16)
        value_grad = value_grad + jnp.einsum(
            "hqk,qhe->khe", soft_weights, grad_block, preferred_element_type=jnp.float32
        )
        prob_grad = jnp.einsum(
            "qhe,khe->hqk", grad_block, value_rows, preferred_element_type=jnp.float32
        )
        centred = jnp.sum(probs * prob_grad, axis=-1, keepdims=True)
        score_grad = (probs * (prob_grad - centred) * HD ** (-0.5)).astype(jnp.bfloat16)
        query_grad = jnp.einsum(
            "hqk,khe->qhe", score_grad, key_rows, preferred_element_type=jnp.float32
        )
        key_grad = key_grad + jnp.einsum(
            "hqk,qhe->khe", score_grad, query_block, preferred_element_type=jnp.float32
        )
        return ((key_grad, value_grad), query_grad)

    empty = jnp.zeros(queries.shape, jnp.float32)
    (key_grad, value_grad), query_grad = lax.scan(
        one_block, (empty, empty), jnp.arange(length // block_rows, dtype=jnp.int32)
    )
    return (query_grad.reshape(queries.shape), key_grad, value_grad)


def attend_forward(triple, piece_ids, slopes):
    width = triple.shape[2]
    count_seq = piece_ids.shape[0]
    length = piece_ids.shape[1]
    shaped = triple.reshape(3, count_seq, length, width // HD, HD)
    attended, log_total = lax.map(
        lambda operands: sequence_forward(operands, slopes),
        (shaped[0], shaped[1], shaped[2], piece_ids),
    )
    return (attended.reshape(count_seq * length, width), log_total)


def attend_backward(triple, grad_attended, log_total, piece_ids, slopes):
    width = triple.shape[2]
    count_seq = piece_ids.shape[0]
    length = piece_ids.shape[1]
    shaped = triple.reshape(3, count_seq, length, width // HD, HD)
    grad_shaped = grad_attended.reshape(count_seq, length, width // HD, HD)
    query_grad, key_grad, value_grad = lax.map(
        lambda operands: sequence_backward(operands, slopes),
        (shaped[0], shaped[1], shaped[2], piece_ids, grad_shaped, log_total),
    )
    return (
        query_grad.reshape(-1, width),
        key_grad.reshape(-1, width),
        value_grad.reshape(-1, width),
    )


def fetch_layer(
    project_weight,
    project_bias,
    output_weight,
    expand_weight,
    expand_bias,
    reduce_weight,
    small_stack,
    layer_index,
):
    return (
        lax.all_gather(project_weight[layer_index], "dp", axis=1, tiled=True),
        lax.all_gather(project_bias[layer_index], "dp", axis=1, tiled=True),
        lax.all_gather(output_weight[layer_index], "dp", axis=1, tiled=True),
        lax.all_gather(expand_weight[layer_index], "dp", axis=0, tiled=True),
        lax.all_gather(expand_bias[layer_index], "dp", axis=0, tiled=True),
        lax.all_gather(reduce_weight[layer_index], "dp", axis=1, tiled=True),
        lax.all_gather(small_stack[layer_index], "dp", axis=1, tiled=True),
    )


def forward_layer(resid, weights, piece_ids, slopes):
    w_project, bias_project, w_output, w_expand, bias_expand, w_reduce, small = weights
    vectors = small.astype(jnp.float32)
    normed = layer_norm(resid, vectors[0], vectors[1])
    gathered = gather_rows(normed.astype(jnp.bfloat16))
    product = jnp.einsum("gd,cde->cge", gathered, w_project, preferred_element_type=jnp.float32)
    biases = jnp.stack([bias_project[0], jnp.zeros_like(bias_project[0]), bias_project[1]]).astype(
        jnp.float32
    )
    triple = (product + biases[:, None, :]).astype(jnp.bfloat16)
    attended, log_total = attend_forward(triple, piece_ids, slopes)
    resid_mid = resid + (scatter_rows(attended, w_output) + vectors[2])
    normed_two = layer_norm(resid_mid, vectors[3], vectors[4])
    gathered_two = gather_rows(normed_two.astype(jnp.bfloat16))
    hidden = jnp.dot(
        gathered_two, w_expand, preferred_element_type=jnp.float32
    ) + bias_expand.astype(jnp.float32)
    active = gelu_tanh(hidden).astype(jnp.bfloat16)
    mlp_sum = scatter_rows(active, w_reduce)
    mlp_keep = (gathered_two, hidden, None)
    resid_out = resid_mid + (mlp_sum + vectors[5])
    return (resid_out, (gathered, triple, attended, log_total, resid_mid, mlp_keep))


def backward_layer(grad_out, resid, weights, kept, piece_ids, slopes):
    w_project, bias_project, w_output, w_expand, bias_expand, w_reduce, small = weights
    vectors = small.astype(jnp.float32)
    gathered, triple, attended, log_total, resid_mid, mlp_keep = kept
    rows_here = grad_out.shape[0]
    rows_in, hidden, full_weights = mlp_keep
    grad_bias_reduce = jnp.sum(grad_out, axis=0)
    active, gelu_pull = jax.vjp(gelu_tanh, hidden)
    active_low = active.astype(jnp.bfloat16)
    grad_mlp = gather_grads(grad_out.astype(jnp.bfloat16))
    grad_reduce = jnp.einsum("gf,gd->fd", active_low, grad_mlp, preferred_element_type=jnp.float32)
    grad_active = jnp.einsum("gd,fd->gf", grad_mlp, w_reduce, preferred_element_type=jnp.float32)
    (grad_hidden,) = gelu_pull(grad_active)
    grad_bias_expand = jnp.sum(grad_hidden, axis=0)
    grad_hidden_low = grad_hidden.astype(jnp.bfloat16)
    grad_expand = jnp.einsum(
        "gd,gf->df", rows_in, grad_hidden_low, preferred_element_type=jnp.float32
    )

    def expand_term(offset, count_rows):
        return jnp.einsum(
            "gf,df->gd", grad_hidden_low, w_expand, preferred_element_type=jnp.float32
        )

    grad_normed_two = scatter_back(expand_term, rows_here)
    unused_two, second_pull = jax.vjp(layer_norm, resid_mid, vectors[3], vectors[4])
    grad_from_norm, grad_gain_two, grad_shift_two = second_pull(grad_normed_two)
    grad_mid = grad_out + grad_from_norm
    grad_bias_output = jnp.sum(grad_mid, axis=0)
    grad_attn = gather_grads(grad_mid.astype(jnp.bfloat16))
    grad_output = jnp.einsum("gt,gd->td", attended, grad_attn, preferred_element_type=jnp.float32)
    grad_attended = jnp.einsum(
        "gd,td->gt", grad_attn, w_output, preferred_element_type=jnp.float32
    ).astype(jnp.bfloat16)
    query_grad, key_grad, value_grad = attend_backward(
        triple, grad_attended, log_total, piece_ids, slopes
    )
    grad_bias_project = jnp.stack([jnp.sum(query_grad, axis=0), jnp.sum(value_grad, axis=0)])
    grad_triple = jnp.stack([query_grad, key_grad, value_grad]).astype(jnp.bfloat16)
    grad_project = jnp.einsum(
        "gd,cge->cde", gathered, grad_triple, preferred_element_type=jnp.float32
    )

    def project_term(offset, count_rows):
        return jnp.einsum("cge,cde->gd", grad_triple, w_project, preferred_element_type=jnp.float32)

    grad_normed = scatter_back(project_term, rows_here)
    unused_one, first_pull = jax.vjp(layer_norm, resid, vectors[0], vectors[1])
    grad_from_first, grad_gain_one, grad_shift_one = first_pull(grad_normed)
    grad_stream = grad_mid + grad_from_first
    small_grads = jnp.stack(
        [
            grad_gain_one,
            grad_shift_one,
            grad_bias_output,
            grad_gain_two,
            grad_shift_two,
            grad_bias_reduce,
        ]
    )
    return (
        grad_stream,
        (
            grad_project,
            grad_bias_project,
            grad_output,
            grad_expand,
            grad_bias_expand,
            grad_reduce,
            small_grads,
        ),
    )


def reduce_layer(layer_grads):
    (
        grad_project,
        grad_bias_project,
        grad_output,
        grad_expand,
        grad_bias_expand,
        grad_reduce,
        small_grads,
    ) = layer_grads
    return (
        lax.psum_scatter(
            grad_project.astype(jnp.bfloat16), "dp", scatter_dimension=1, tiled=True
        ).astype(jnp.float32),
        lax.psum_scatter(
            grad_bias_project.astype(jnp.bfloat16), "dp", scatter_dimension=1, tiled=True
        ).astype(jnp.float32),
        lax.psum_scatter(
            grad_output.astype(jnp.bfloat16), "dp", scatter_dimension=1, tiled=True
        ).astype(jnp.float32),
        lax.psum_scatter(
            grad_expand.astype(jnp.bfloat16), "dp", scatter_dimension=0, tiled=True
        ).astype(jnp.float32),
        lax.psum_scatter(
            grad_bias_expand.astype(jnp.bfloat16), "dp", scatter_dimension=0, tiled=True
        ).astype(jnp.float32),
        lax.psum_scatter(
            grad_reduce.astype(jnp.bfloat16), "dp", scatter_dimension=1, tiled=True
        ).astype(jnp.float32),
        lax.psum_scatter(
            small_grads.astype(jnp.bfloat16), "dp", scatter_dimension=1, tiled=True
        ).astype(jnp.float32),
    )


def on_device(
    layer_input,
    first_gain,
    first_shift,
    project_weight,
    project_bias,
    output_weight,
    output_bias,
    second_gain,
    second_shift,
    expand_weight,
    expand_bias,
    reduce_weight,
    reduce_bias,
    picture_start,
    cotangent,
):
    small_stack = jnp.stack(
        [first_gain, first_shift, output_bias, second_gain, second_shift, reduce_bias], axis=1
    )
    piece_ids = jax.vmap(piece_numbers)(picture_start)
    heads_here = project_weight.shape[3] // HD
    slopes = head_slopes(lax.axis_index("tensor") * heads_here, heads_here)
    resid = layer_input.astype(jnp.float32)
    saved = []
    for layer_index in range(LAYERS):
        weights = fetch_layer(
            project_weight,
            project_bias,
            output_weight,
            expand_weight,
            expand_bias,
            reduce_weight,
            small_stack,
            layer_index,
        )
        resid_next, kept = forward_layer(resid, weights, piece_ids, slopes)
        saved.append((resid, weights, kept))
        resid = resid_next
    layer_output = resid.astype(jnp.bfloat16)
    grad_stream = cotangent.astype(jnp.float32)
    collected = []
    for layer_index in reversed(range(LAYERS)):
        resid_in, weights, kept = saved[layer_index]
        grad_stream, layer_grads = backward_layer(
            grad_stream, resid_in, weights, kept, piece_ids, slopes
        )
        layer_grads = reduce_layer(layer_grads)
        collected.insert(0, layer_grads)
    stacked = tuple(
        (jnp.stack([grad_entry[member] for grad_entry in collected]) for member in range(7))
    )
    (
        grad_project,
        grad_bias_project,
        grad_output,
        grad_expand,
        grad_bias_expand,
        grad_reduce,
        small_grads,
    ) = stacked
    small_grads = lax.psum(small_grads, "tensor")
    return (
        layer_output,
        grad_stream.astype(jnp.bfloat16),
        small_grads[:, 0],
        small_grads[:, 1],
        grad_project,
        grad_bias_project,
        grad_output,
        small_grads[:, 2],
        small_grads[:, 3],
        small_grads[:, 4],
        grad_expand,
        grad_bias_expand,
        grad_reduce,
        small_grads[:, 5],
    )


def solution(mesh):
    placed = (
        P(("dp", "tensor"), None),
        P(None, "dp"),
        P(None, "dp"),
        P(None, None, "dp", "tensor"),
        P(None, None, ("tensor", "dp")),
        P(None, "tensor", "dp"),
        P(None, "dp"),
        P(None, "dp"),
        P(None, "dp"),
        P(None, "dp", "tensor"),
        P(None, ("tensor", "dp")),
        P(None, "tensor", "dp"),
        P(None, "dp"),
        P("dp", None),
        P(("dp", "tensor"), None),
    )
    return jax.shard_map(
        on_device,
        mesh=mesh,
        in_specs=placed,
        out_specs=(
            P(("dp", "tensor"), None),
            P(("dp", "tensor"), None),
            P(None, "dp"),
            P(None, "dp"),
            P(None, None, "dp", "tensor"),
            P(None, None, ("tensor", "dp")),
            P(None, "tensor", "dp"),
            P(None, "dp"),
            P(None, "dp"),
            P(None, "dp"),
            P(None, "dp", "tensor"),
            P(None, ("tensor", "dp")),
            P(None, "tensor", "dp"),
            P(None, "dp"),
        ),
        check_vma=False,
    )
```

profile of v0, /device:TPU:0, one launch (start us, length us, event | category | flops | bytes accessed | tf_op | source)
XLA Modules:
  0.0 2592.2 jit_solution(6171808690744180217)
XLA Ops:
  66.2 56.2 %all-gather.29.cloned.1.call-done = bf16[2048,1024]{1,0:T(8,128)(2,1)} async-done(((bf16[512,1024]{1,0:T(8,128)(2,1)}), bf16[2048,1024]{1,0:T(8,128)(2,1)}) %all-gather.29.cloned.1.call-update) | async-done | bytes 4194320 | tf_op jit(solution)/shard_map/all_gather | solution.py:39
  131.2 96.3 %while.96 = (s32[]{:T(128)}, bf16[4,512,4,64]{1,3,2,0:T(8,128)(2,1)}, f32[4,4,512]{2,1,0:T(4,128)S(1)}, s32[4]{0:T(128)S(1)}, s32[2048]{0:T(1024)S(1)}, /*index=...) while((s32[]{:T(128)}, ...), condition=%wide.region_6.7_spmd.clone, body=%wide.region_3.6_spmd.clone.sunk | while | flops 1156709376 | bytes 94983504 | solution.py:102
  236.5 73.6 %reduce-scatter.41.cloned.1.call-done = bf16[512,1024]{1,0:T(8,128)(2,1)} async-done(((bf16[2048,1024]{1,0:T(8,128)(2,1)}), bf16[512,1024]{1,0:T(8,128)(2,1)}) %reduce-scatter.41.cloned.1.call-update) | async-done | bytes 1048592 | tf_op jit(solution)/shard_map/reduce_scatter | solution.py:52
  325.9 15.1 all-gather.47.cloned.1.call-done
  341.0 82.9 %all-gather.31.cloned.1.call-done = bf16[2048,1024]{1,0:T(8,128)(2,1)} async-done(((bf16[512,1024]{1,0:T(8,128)(2,1)}), bf16[2048,1024]{1,0:T(8,128)(2,1)}) %all-gather.31.cloned.1.call-update) | async-done | bytes 4194320 | tf_op jit(solution)/shard_map/all_gather | solution.py:39
  434.5 18.0 all-gather.49.cloned.1.call-done
  475.5 65.7 %reduce-scatter.43.cloned.1.call-done = bf16[512,1024]{1,0:T(8,128)(2,1)} async-done(((bf16[2048,1024]{1,0:T(8,128)(2,1)}), bf16[512,1024]{1,0:T(8,128)(2,1)}) %reduce-scatter.43.cloned.1.call-update) | async-done | bytes 1048592 | tf_op jit(solution)/shard_map/reduce_scatter | solution.py:52
  545.9 12.2 all-gather.10
  558.1 12.7 all-gather.51.cloned.1.call-done
  570.7 82.9 %all-gather.33.cloned.1.call-done = bf16[2048,1024]{1,0:T(8,128)(2,1)} async-done(((bf16[512,1024]{1,0:T(8,128)(2,1)}), bf16[2048,1024]{1,0:T(8,128)(2,1)}) %all-gather.33.cloned.1.call-update) | async-done | bytes 4194320 | tf_op jit(solution)/shard_map/all_gather | solution.py:39
  662.5 96.4 %while.97 = (s32[]{:T(128)}, bf16[4,512,4,64]{1,3,2,0:T(8,128)(2,1)}, f32[4,4,512]{2,1,0:T(4,128)S(1)}, s32[4]{0:T(128)S(1)}, s32[2048]{0:T(1024)S(1)}, /*index=...) while((s32[]{:T(128)}, ...), condition=%wide.region_16.17_spmd.clone, body=%wide.region_13.16_spmd.clone.sunk | while | flops 1156709376 | bytes 94983504 | solution.py:102
  766.7 74.7 %reduce-scatter.45.cloned.1.call-done = bf16[512,1024]{1,0:T(8,128)(2,1)} async-done(((bf16[2048,1024]{1,0:T(8,128)(2,1)}), bf16[512,1024]{1,0:T(8,128)(2,1)}) %reduce-scatter.45.cloned.1.call-update) | async-done | bytes 1048592 | tf_op jit(solution)/shard_map/reduce_scatter | solution.py:52
  855.7 16.7 all-gather.53.cloned.1.call-done
  872.4 82.9 %all-gather.35.cloned.1.call-done = bf16[2048,1024]{1,0:T(8,128)(2,1)} async-done(((bf16[512,1024]{1,0:T(8,128)(2,1)}), bf16[2048,1024]{1,0:T(8,128)(2,1)}) %all-gather.35.cloned.1.call-update) | async-done | bytes 4194320 | tf_op jit(solution)/shard_map/all_gather | solution.py:39
  965.9 18.7 all-gather.55.cloned.1.call-done
  984.6 82.3 %all-gather.37.cloned.1.call-done = bf16[2048,1024]{1,0:T(8,128)(2,1)} async-done(((bf16[512,1024]{1,0:T(8,128)(2,1)}), bf16[2048,1024]{1,0:T(8,128)(2,1)}) %all-gather.37.cloned.1.call-update) | async-done | bytes 4194320 | tf_op jit(solution)/shard_map/all_gather | solution.py:43
  1066.9 14.8 fusion.254
  1103.2 62.3 %reduce-scatter.49.cloned.1.call-done = bf16[512,1024]{1,0:T(8,128)(2,1)} async-done(((bf16[2048,1024]{1,0:T(8,128)(2,1)}), bf16[512,1024]{1,0:T(8,128)(2,1)}) %reduce-scatter.49.cloned.1.call-update) | async-done | bytes 1048592 | tf_op jit(solution)/shard_map/reduce_scatter | solution.py:61
  1168.2 76.8 %reduce-scatter.47.cloned.1.call-done = bf16[512,1024]{1,0:T(8,128)(2,1)} async-done(((bf16[2048,1024]{1,0:T(8,128)(2,1)}), bf16[512,1024]{1,0:T(8,128)(2,1)}) %reduce-scatter.47.cloned.1.call-update) | async-done | bytes 1048592 | tf_op jit(solution)/shard_map/reduce_scatter | solution.py:52
  1251.8 81.3 %all-gather.39.cloned.1.call-done = bf16[2048,1024]{1,0:T(8,128)(2,1)} async-done(((bf16[512,1024]{1,0:T(8,128)(2,1)}), bf16[2048,1024]{1,0:T(8,128)(2,1)}) %all-gather.39.cloned.1.call-update) | async-done | bytes 4194320 | tf_op jit(solution)/shard_map/all_gather | solution.py:43
  1339.3 291.0 %while.98 = (s32[]{:T(128)}, f32[2048,4,64]{0,2,1:T(8,128)}, f32[2048,4,64]{0,2,1:T(8,128)S(1)}, f32[4,512,4,64]{1,3,2,0:T(8,128)}, s32[4]{0:T(128)S(1)}, /*inde...) while((s32[]{:T(128)}, f32[2048,4,64]{0,2,1:T(8,128)}, ...), condition=%wide.region_26.27_spmd.clone, body=%wide.region_24.26_spmd.clone.sunk | while | flops 2760909824 | bytes 279491968 | solution.py:136
  1365.6 23.2 fusion.352
  1388.9 22.7 fusion.354
  1437.7 23.9 fusion.352
  1461.6 22.7 fusion.354
  1510.5 23.9 fusion.352
  1534.3 22.7 fusion.354
  1583.2 23.9 fusion.352
  1607.1 22.7 fusion.354
  1650.7 75.4 %reduce-scatter.51.cloned.1.call-done = bf16[512,1024]{1,0:T(8,128)(2,1)} async-done(((bf16[2048,1024]{1,0:T(8,128)(2,1)}), bf16[512,1024]{1,0:T(8,128)(2,1)}) %reduce-scatter.51.cloned.1.call-update) | async-done | bytes 1048592 | tf_op jit(solution)/shard_map/reduce_scatter | solution.py:61
  1734.6 81.3 %all-gather.41.cloned.1.call-done = bf16[2048,1024]{1,0:T(8,128)(2,1)} async-done(((bf16[512,1024]{1,0:T(8,128)(2,1)}), bf16[2048,1024]{1,0:T(8,128)(2,1)}) %all-gather.41.cloned.1.call-update) | async-done | bytes 4194320 | tf_op jit(solution)/shard_map/all_gather | solution.py:43
  1815.9 14.4 fusion.255
  1838.7 75.4 %reduce-scatter.53.cloned.1.call-done = bf16[512,1024]{1,0:T(8,128)(2,1)} async-done(((bf16[2048,1024]{1,0:T(8,128)(2,1)}), bf16[512,1024]{1,0:T(8,128)(2,1)}) %reduce-scatter.53.cloned.1.call-update) | async-done | bytes 1048592 | tf_op jit(solution)/shard_map/reduce_scatter | solution.py:61
  1924.0 11.9 convolution_convert_fusion.8
  2011.3 299.0 %while.99 = (s32[]{:T(128)}, f32[2048,4,64]{0,2,1:T(8,128)}, f32[2048,4,64]{0,2,1:T(8,128)S(1)}, f32[4,512,4,64]{1,3,2,0:T(8,128)}, s32[4]{0:T(128)S(1)}, /*inde...) while((s32[]{:T(128)}, f32[2048,4,64]{0,2,1:T(8,128)}, ...), condition=%wide.region_35.36_spmd.clone, body=%wide.region_33.35_spmd.clone.sunk | while | flops 2760909824 | bytes 279491968 | solution.py:136
  2038.7 23.6 fusion.367
  2062.3 22.8 fusion.369
  2111.9 24.2 fusion.367
  2136.1 23.3 fusion.369
  2186.2 24.0 fusion.367
  2210.2 24.1 fusion.369
  2261.8 24.4 fusion.367
  2286.2 23.9 fusion.369
  2355.5 14.0 all-reduce.2
  2377.9 31.6 %reduce-scatter.73.cloned.1.call-done = bf16[128,256]{1,0:T(8,128)(2,1)} async-done(((bf16[1024,256]{1,0:T(8,128)(2,1)}), bf16[128,256]{1,0:T(8,128)(2,1)}) %reduce-scatter.73.cloned.1.call-update) | async-done | bytes 65552
  2411.1 40.1 %reduce-scatter.65.cloned.1.call-done = bf16[128,768]{1,0:T(8,128)(2,1)} async-done(((bf16[1024,768]{1,0:T(8,128)(2,1)}), bf16[128,768]{1,0:T(8,128)(2,1)}) %reduce-scatter.65.cloned.1.call-update) | async-done | bytes 196624
  2455.7 74.5 %reduce-scatter.55.cloned.1.call-done = bf16[512,1024]{1,0:T(8,128)(2,1)} async-done(((bf16[2048,1024]{1,0:T(8,128)(2,1)}), bf16[512,1024]{1,0:T(8,128)(2,1)}) %reduce-scatter.55.cloned.1.call-update) | async-done | bytes 1048592 | tf_op jit(solution)/shard_map/reduce_scatter | solution.py:61
  2540.5 31.3 %reduce-scatter.61.cloned.1.call-done = bf16[128,6]{1,0:T(8,128)(2,1)} async-done(((bf16[1024,6]{1,0:T(8,128)(2,1)}), bf16[128,6]{1,0:T(8,128)(2,1)}) %reduce-scatter.61.cloned.1.call-update) | async-done | bytes 1552
  (706 shorter events, 791.3 us)
Async XLA Ops:
  7.2 59.0 %all-gather.45.cloned.1.call-start = ((), (), s32[]{:S(2)}) async-start(), calls=%async_computation.38 | async-start | bytes 1769472 | tf_op jit(solution)/shard_map/all_gather | solution.py:182
  9.9 112.5 %all-gather.29.cloned.1.call-start = ((), (), s32[]{:S(2)}) async-start(), calls=%async_computation.20 | async-start | bytes 5242880 | tf_op jit(solution)/shard_map/all_gather | solution.py:39
  30.6 279.5 %reduce-scatter.41.cloned.1.call-start = ((), (), s32[]{:S(2)}) async-start(), calls=%async_computation.21 | async-start | bytes 5242880 | tf_op jit(solution)/shard_map/reduce_scatter | solution.py:52
  234.6 106.4 %all-gather.47.cloned.1.call-start = ((), (), s32[]{:S(2)}) async-start(), calls=%async_computation.39 | async-start | bytes 2359296 | tf_op jit(solution)/shard_map/all_gather | solution.py:185
  236.4 187.4 %all-gather.31.cloned.1.call-start = ((), (), s32[]{:S(2)}) async-start(), calls=%async_computation.22 | async-start | bytes 5242880 | tf_op jit(solution)/shard_map/all_gather | solution.py:39
  311.9 122.6 %copy-start.63 = (f32[512]{0:T(512)}, f32[512]{0:T(512)S(1)}, u32[]{:S(2)}) copy-start(f32[512]{0:T(512)S(1)} %broadcast_multiply_fusion.2) | copy-start | bytes 6148
  313.7 120.8 %copy-start.76 = (f32[512]{0:T(512)}, f32[512]{0:T(512)S(1)}, u32[]{:S(2)}) copy-start(f32[512]{0:T(512)S(1)} %multiply_reduce_fusion.4) | copy-start | bytes 6148
  313.7 120.8 %copy-start.70 = (f32[512]{0:T(512)}, f32[512]{0:T(512)S(1)}, u32[]{:S(2)}) copy-start(f32[512]{0:T(512)S(1)} %fusion.222) | copy-start | bytes 6148
  315.3 137.2 %all-gather.49.cloned.1.call-start = ((), (), s32[]{:S(2)}) async-start(), calls=%async_computation.40 | async-start | bytes 2359296 | tf_op jit(solution)/shard_map/all_gather | solution.py:187
  316.2 225.0 %reduce-scatter.43.cloned.1.call-start = ((), (), s32[]{:S(2)}) async-start(), calls=%async_computation.23 | async-start | bytes 5242880 | tf_op jit(solution)/shard_map/reduce_scatter | solution.py:52
  325.9 126.6 %copy-start.95 = (f32[1,1024]{1,0:T(1,128)}, f32[1,1024]{1,0:T(1,128)S(1)}, u32[]{:S(2)}) copy-start(f32[1,1024]{1,0:T(1,128)S(1)} %convert_element_type.316) | copy-start | bytes 12292
  464.3 106.5 %all-gather.51.cloned.1.call-start = ((), (), s32[]{:S(2)}) async-start(), calls=%async_computation.41 | async-start | bytes 1769472 | tf_op jit(solution)/shard_map/all_gather | solution.py:182
  466.0 187.7 %all-gather.33.cloned.1.call-start = ((), (), s32[]{:S(2)}) async-start(), calls=%async_computation.24 | async-start | bytes 5242880 | tf_op jit(solution)/shard_map/all_gather | solution.py:39
  543.1 116.8 %copy-start.65 = (f32[512]{0:T(512)}, f32[512]{0:T(512)S(1)}, u32[]{:S(2)}) copy-start(f32[512]{0:T(512)S(1)} %broadcast_multiply_fusion.1) | copy-start | bytes 6148
  543.4 116.4 %copy-start.78 = (f32[512]{0:T(512)}, f32[512]{0:T(512)S(1)}, u32[]{:S(2)}) copy-start(f32[512]{0:T(512)S(1)} %multiply_reduce_fusion.3) | copy-start | bytes 6148
  543.4 116.4 %copy-start.72 = (f32[512]{0:T(512)}, f32[512]{0:T(512)S(1)}, u32[]{:S(2)}) copy-start(f32[512]{0:T(512)S(1)} %fusion.223) | copy-start | bytes 6148
  545.8 295.5 %reduce-scatter.45.cloned.1.call-start = ((), (), s32[]{:S(2)}) async-start(), calls=%async_computation.25 | async-start | bytes 5242880 | tf_op jit(solution)/shard_map/reduce_scatter | solution.py:52
  765.9 106.5 %all-gather.53.cloned.1.call-start = ((), (), s32[]{:S(2)}) async-start(), calls=%async_computation.42 | async-start | bytes 2359296 | tf_op jit(solution)/shard_map/all_gather | solution.py:185
  766.6 188.6 %all-gather.35.cloned.1.call-start = ((), (), s32[]{:S(2)}) async-start(), calls=%async_computation.26 | async-start | bytes 5242880 | tf_op jit(solution)/shard_map/all_gather | solution.py:39
  845.6 139.0 %all-gather.55.cloned.1.call-start = ((), (), s32[]{:S(2)}) async-start(), calls=%async_computation.43 | async-start | bytes 2359296 | tf_op jit(solution)/shard_map/all_gather | solution.py:187
  846.4 220.5 %all-gather.37.cloned.1.call-start = ((), (), s32[]{:S(2)}) async-start(), calls=%async_computation.28 | async-start | bytes 5242880 | tf_op jit(solution)/shard_map/all_gather | solution.py:43
  847.0 318.5 %reduce-scatter.49.cloned.1.call-start = ((), (), s32[]{:S(2)}) async-start(), calls=%async_computation.29 | async-start | bytes 5242880 | tf_op jit(solution)/shard_map/reduce_scatter | solution.py:61
  855.7 234.5 %copy-start.97 = (f32[1,1024]{1,0:T(1,128)}, f32[1,1024]{1,0:T(1,128)S(1)}, u32[]{:S(2)}) copy-start(f32[1,1024]{1,0:T(1,128)S(1)} %convert_element_type.318) | copy-start | bytes 12292
  1090.0 154.9 %reduce-scatter.47.cloned.1.call-start = ((), (), s32[]{:S(2)}) async-start(), calls=%async_computation.27 | async-start | bytes 5242880 | tf_op jit(solution)/shard_map/reduce_scatter | solution.py:52
  1103.1 141.9 %copy-start.82 = (f32[1,1,1024]{2,0,1:T(1,128)S(1)}, f32[1,1,1024]{2,0,1:T(1,128)}, u32[]{:S(2)}) copy-start(f32[1,1,1024]{2,0,1:T(1,128)} %get-tuple-element.703) | copy-start | bytes 12292
  1103.1 230.0 %all-gather.39.cloned.1.call-start = ((), (), s32[]{:S(2)}) async-start(), calls=%async_computation.30 | async-start | bytes 5242880 | tf_op jit(solution)/shard_map/all_gather | solution.py:43
  1251.7 474.4 %reduce-scatter.51.cloned.1.call-start = ((), (), s32[]{:S(2)}) async-start(), calls=%async_computation.31 | async-start | bytes 5242880 | tf_op jit(solution)/shard_map/reduce_scatter | solution.py:61
  1650.6 165.3 %all-gather.41.cloned.1.call-start = ((), (), s32[]{:S(2)}) async-start(), calls=%async_computation.32 | async-start | bytes 5242880 | tf_op jit(solution)/shard_map/all_gather | solution.py:43
  1734.5 179.6 %reduce-scatter.53.cloned.1.call-start = ((), (), s32[]{:S(2)}) async-start(), calls=%async_computation.33 | async-start | bytes 5242880 | tf_op jit(solution)/shard_map/reduce_scatter | solution.py:61
  1838.6 166.4 %all-gather.43.cloned.1.call-start = ((), (), s32[]{:S(2)}) async-start(), calls=%async_computation.34 | async-start | bytes 5242880 | tf_op jit(solution)/shard_map/all_gather | solution.py:43
  1923.6 425.8 %reduce-scatter.79.cloned.1.call-start = ((), (), s32[]{:S(2)}) async-start(), calls=%async_computation.53 | async-start | bytes 2359296
  1940.0 410.5 %reduce-scatter.71.cloned.1.call-start = ((), (), s32[]{:S(2)}) async-start(), calls=%async_computation.49 | async-start | bytes 73728
  1941.0 410.3 %reduce-scatter.75.cloned.1.call-start = ((), (), s32[]{:S(2)}) async-start(), calls=%async_computation.51 | async-start | bytes 589824
  1947.5 404.8 %reduce-scatter.67.cloned.1.call-start = ((), (), s32[]{:S(2)}) async-start(), calls=%async_computation.47 | async-start | bytes 1769472
  1962.7 391.5 %reduce-scatter.63.cloned.1.call-start = ((), (), s32[]{:S(2)}) async-start(), calls=%async_computation.45 | async-start | bytes 294912
  1964.3 405.9 %reduce-scatter.77.cloned.1.call-start = ((), (), s32[]{:S(2)}) async-start(), calls=%async_computation.52 | async-start | bytes 2359296
  1977.8 393.6 %reduce-scatter.59.cloned.1.call-start = ((), (), s32[]{:S(2)}) async-start(), calls=%async_computation.37 | async-start | bytes 2359296 | tf_op jit(solution)/shard_map/reduce_scatter | solution.py:310
  1987.3 384.1 %reduce-scatter.57.cloned.1.call-start = ((), (), s32[]{:S(2)}) async-start(), calls=%async_computation.36 | async-start | bytes 2359296 | tf_op jit(solution)/shard_map/reduce_scatter | solution.py:310
  1996.8 379.7 %reduce-scatter.69.cloned.1.call-start = ((), (), s32[]{:S(2)}) async-start(), calls=%async_computation.48 | async-start | bytes 73728
  2316.0 93.4 %reduce-scatter.73.cloned.1.call-start = ((), (), s32[]{:S(2)}) async-start(), calls=%async_computation.50 | async-start | bytes 589824
  2327.7 123.5 %reduce-scatter.65.cloned.1.call-start = ((), (), s32[]{:S(2)}) async-start(), calls=%async_computation.46 | async-start | bytes 1769472
  2340.0 190.2 %reduce-scatter.55.cloned.1.call-start = ((), (), s32[]{:S(2)}) async-start(), calls=%async_computation.35 | async-start | bytes 5242880 | tf_op jit(solution)/shard_map/reduce_scatter | solution.py:61
  2347.5 224.2 %reduce-scatter.61.cloned.1.call-start = ((), (), s32[]{:S(2)}) async-start(), calls=%async_computation.44 | async-start | bytes 294912
  2373.5 158.1 %copy-start.7 = (bf16[512,1024]{1,0:T(8,128)(2,1)S(1)}, bf16[512,1024]{1,0:T(8,128)(2,1)}, u32[]{:S(2)}) copy-start(bf16[512,1024]{1,0:T(8,128)(2,1)} %param.23) | copy-start | bytes 3145732
  2373.5 158.1 %copy-start.60 = (f32[1,1,1024]{2,0,1:T(1,128)S(1)}, f32[1,1,1024]{2,0,1:T(1,128)}, u32[]{:S(2)}) copy-start(f32[1,1,1024]{2,0,1:T(1,128)} %copy-done.59) | copy-start | bytes 12292
  2373.5 158.1 %copy-start.62 = (f32[512]{0:T(512)S(1)}, f32[512]{0:T(512)}, u32[]{:S(2)}) copy-start(f32[512]{0:T(512)} %copy-done.61) | copy-start | bytes 6148
  2374.5 158.9 %copy-start.75 = (f32[512]{0:T(512)S(1)}, f32[512]{0:T(512)}, u32[]{:S(2)}) copy-start(f32[512]{0:T(512)} %copy-done.74) | copy-start | bytes 6148
  2374.5 158.9 %copy-start.69 = (f32[512]{0:T(512)S(1)}, f32[512]{0:T(512)}, u32[]{:S(2)}) copy-start(f32[512]{0:T(512)} %copy-done.68) | copy-start | bytes 6148
  (121 other events, 3293.6 us)
Sparse Core Ops, SparseCore 0:
  10.5 28.7 all-gather.44
  41.4 80.9 all-gather.28
  234.7 75.2 reduce-scatter.40
  312.5 28.3 all-gather.46
  343.0 80.7 all-gather.30
  425.7 26.7 all-gather.48
  464.4 76.7 reduce-scatter.42
  543.6 27.0 all-gather.50
  572.9 80.7 all-gather.32
  766.0 75.2 reduce-scatter.44
  844.0 28.3 all-gather.52
  874.5 80.7 all-gather.34
  957.9 26.7 all-gather.54
  986.1 80.7 all-gather.36
  1090.2 75.2 reduce-scatter.48
  1167.6 77.2 reduce-scatter.46
  1251.8 81.2 all-gather.38
  1650.7 75.2 reduce-scatter.50
  1734.6 81.2 all-gather.40
  1838.8 75.2 reduce-scatter.52
  1923.7 81.2 all-gather.42
  2008.6 39.7 reduce-scatter.78
  2051.4 33.2 reduce-scatter.70
  2088.0 34.0 reduce-scatter.74
  2125.4 38.5 reduce-scatter.66
  2167.4 33.5 reduce-scatter.62
  2204.5 41.2 reduce-scatter.76
  2249.1 41.1 reduce-scatter.58
  2293.9 41.2 reduce-scatter.56
  2338.0 33.2 reduce-scatter.68
  2375.3 34.0 reduce-scatter.72
  2412.8 38.4 reduce-scatter.64
  2453.4 76.7 reduce-scatter.54
  2537.7 34.0 reduce-scatter.60
where the time goes:
time: 2600 us; the launch traced here: 2590 us
  waiting for transfers between devices  1320 us (51%)
  matrix products  822 us (32%)
  other arithmetic  150 us (6%)
  local copies, waits for them, and re-layouts  147 us (6%)
  blocking collectives  104 us (4%)
  loops' own time  28.7 us (1%)
    all_gather x4, waiting for transfers between devices, gather_rows(): return lax.all_gather(values, 'tensor', axis=0, tiled=True)  305 us
    reduce_scatter x4, waiting for transfers between devices, scatter_rows(): lax.psum_scatter(partial_term(jnp.int32(0), rows_here * lax.axis_size('te...  291 us
    reduce_scatter x4, waiting for transfers between devices, scatter_back(): lax.psum_scatter(partial_term(jnp.int32(0), rows_here * lax.axis_size('te...  288 us
    all_gather x4, waiting for transfers between devices, gather_grads(): return lax.all_gather(values, 'tensor', axis=0, tiled=True)  253 us
    dot_general x8, matrix products, one_block(): jnp.einsum('hqk,qhe->khe', score_grad, query_block, preferred_element_typ...  191 us
    dot_general x8, matrix products, one_block(): jnp.einsum('hqk,khe->qhe', score_grad, key_rows, preferred_element_type=j...  185 us
    unnamed x44, waiting for transfers between devices  105 us
    dot_general x16, matrix products, block_scores(): jnp.einsum('qhe,khe->hqk', query_block, key_rows, preferred_element_type=...  105 us
  transfers between devices with their start and end apart: 34, of which 24 were waited for; matrix products, arithmetic and copies ran while one was open for 18% of the time, Pallas kernels for 0%

commit v1 on v0

--- a/solution.py
+++ b/solution.py
@@ -1,6 +1,10 @@
+import functools
+
 import jax
 import jax.numpy as jnp
 from jax import lax
+from jax.experimental import pallas as pl
+from jax.experimental.pallas import tpu as pltpu
 from jax.sharding import PartitionSpec as P
 
 HEADS = 16
@@ -402,6 +406,672 @@
     )
 
 
+Z0, Z1, CORE, XBIT, YBIT = 1, 2, 4, 8, 16
+AXES = ("dp", "tensor")
+NEG = -1e30
+BF = jnp.bfloat16
+F32 = jnp.float32
+
+
+def mesh_is_paired(mesh):
+    return dict(mesh.shape) == {"dp": 8, "tensor": 4}
+
+
+def swap(values, mask):
+    return lax.ppermute(values, AXES, [(i, i ^ mask) for i in range(32)])
+
+
+def redeal(values):
+    def target(i):
+        core, z1 = (i >> 2) & 1, (i >> 1) & 1
+        return (i & ~6) | (z1 << 2) | (core << 1)
+
+    return lax.ppermute(values, AXES, [(i, target(i)) for i in range(32)])
+
+
+def turn_blocks(values, own):
+    width = values.shape[1] // 8
+    return jnp.concatenate(
+        [lax.dynamic_slice_in_dim(values, (own ^ i) * width, width, 1) for i in range(8)], axis=1
+    )
+
+
+def dot_nt(a, b):
+    return lax.dot_general(a, b, (((1,), (1,)), ((), ())), preferred_element_type=jnp.float32)
+
+
+def dot_nn(a, b):
+    return lax.dot_general(a, b, (((1,), (0,)), ((), ())), preferred_element_type=jnp.float32)
+
+
+def dot_tn(a, b):
+    return lax.dot_general(a, b, (((0,), (0,)), ((), ())), preferred_element_type=jnp.float32)
+
+
+def head_mask(shape, head):
+    lane = lax.broadcasted_iota(jnp.int32, shape, 1)
+    return (lane < HD) if head == 0 else (lane >= HD)
+
+
+def diagonal_bias(rows, columns, first_row, first_column, start):
+    key = first_row + lax.broadcasted_iota(jnp.int32, (rows, 1), 0)
+    query = first_column + lax.broadcasted_iota(jnp.int32, (1, columns), 1)
+    key_in = (key >= start) & (key < start + PIECE)
+    query_in = (query >= start) & (query < start + PIECE)
+    allowed = (key <= query) | (key_in & query_in)
+    reach = (jnp.minimum(key, 2 * query - key) - first_column).astype(jnp.float32)
+    return jnp.where(allowed, reach, NEG)
+
+
+def ramp(rows, first_row, first_column):
+    return (first_row - first_column + lax.broadcasted_iota(jnp.int32, (rows, 1), 0)).astype(jnp.float32)
+
+
+def attend_kernel(block, slope_ref, start_ref, me_ref, q_ref, k_ref, v_ref, o_ref, exact_ref, lse_ref, vt_ref, acc_ref, max_ref, bias_ref, tail_ref):
+    pair = pl.program_id(0)
+    turn = pl.program_id(1)
+    me = me_ref[0]
+    step = turn ^ me
+    length = k_ref.shape[0]
+    first = step * block
+
+    def at(index):
+        return pl.multiple_of((index ^ me) * block, block)
+
+    start = start_ref[(step * block) // (length // start_ref.shape[0])]
+
+    @pl.when(turn == 0)
+    def _():
+        for head in range(2):
+            mixed = jnp.where(head_mask((length, 2 * HD), head), v_ref[...], jnp.ones((), v_ref.dtype))
+            vt_ref[head] = mixed.astype(jnp.float32).T.astype(jnp.bfloat16)
+
+    bias_ref[...] = diagonal_bias(block, block, first, first, start)
+    q_block = q_ref[...] * jnp.asarray(HD ** -0.5, jnp.bfloat16)
+    heads = [jnp.where(head_mask(q_block.shape, head), q_block, jnp.zeros((), q_block.dtype)) for head in range(2)]
+    slopes = [slope_ref[2 * pair + head] for head in range(2)]
+    acc_ref[...] = jnp.zeros_like(acc_ref)
+    max_ref[...] = jnp.full_like(max_ref, NEG)
+
+    def absorb(head, scores, vt):
+        old = max_ref[head]
+        new = jnp.maximum(old, jnp.max(scores, axis=0, keepdims=True))
+        weights = jnp.exp(scores - new).astype(jnp.bfloat16)
+        acc_ref[head] = acc_ref[head] * jnp.exp(old - new) + dot_nn(vt, weights)
+        max_ref[head] = new
+
+    def full(index, carry):
+        place = at(index)
+        keys = k_ref[pl.ds(place, block), :]
+        slant = ramp(block, index * block, first)
+        for head in range(2):
+            absorb(head, dot_nt(keys, heads[head]) + slopes[head] * slant, vt_ref[head, :, pl.ds(place, block)])
+        return carry
+
+    place = at(step)
+    for head in range(2):
+        absorb(
+            head,
+            dot_nt(k_ref[pl.ds(place, block), :], heads[head]) + slopes[head] * bias_ref[...],
+            vt_ref[head, :, pl.ds(place, block)],
+        )
+    lax.fori_loop(0, step, full, 0)
+    edge = first + block
+
+    @pl.when((start < edge) & (start + PIECE > edge))
+    def _():
+        after = at(step + 1)
+        tail_ref[...] = diagonal_bias(PIECE, block, edge, first, start)
+        for head in range(2):
+            absorb(
+                head,
+                dot_nt(k_ref[pl.ds(after, PIECE), :], heads[head]) + slopes[head] * tail_ref[...],
+                vt_ref[head, :, pl.ds(after, PIECE)],
+            )
+
+    outs = []
+    for head in range(2):
+        acc = acc_ref[head]
+        total = acc[HD:HD + 1] if head == 0 else acc[0:1]
+        outs.append((acc * (1.0 / total))[head * HD:(head + 1) * HD])
+        lse_ref[0, head:head + 1, :] = max_ref[head] + jnp.log(total)
+    mixed = jnp.concatenate(outs, axis=0)
+    exact_ref[...] = mixed
+    o_ref[...] = mixed.T.astype(jnp.bfloat16)
+
+
+def attend(triple, slopes, starts, me, block=512):
+    length, width = triple.shape[0], triple.shape[1] // 3
+    pairs = width // (2 * HD)
+    steps = length // block
+    smem = pl.BlockSpec(memory_space=pltpu.SMEM)
+    return pl.pallas_call(
+        functools.partial(attend_kernel, block),
+        grid=(pairs, steps),
+        in_specs=[
+            smem,
+            smem,
+            smem,
+            pl.BlockSpec((block, 2 * HD), lambda p, i: (i, p)),
+            pl.BlockSpec((length, 2 * HD), lambda p, i: (0, pairs + p)),
+            pl.BlockSpec((length, 2 * HD), lambda p, i: (0, 2 * pairs + p)),
+        ],
+        out_specs=[
+            pl.BlockSpec((block, 2 * HD), lambda p, i: (i, p)),
+            pl.BlockSpec((2 * HD, block), lambda p, i: (p, i)),
+            pl.BlockSpec((1, 8, block), lambda p, i: (p, 0, i)),
+        ],
+        out_shape=[
+            jax.ShapeDtypeStruct((length, width), jnp.bfloat16),
+            jax.ShapeDtypeStruct((width, length), jnp.float32),
+            jax.ShapeDtypeStruct((pairs, 8, length), jnp.float32),
+        ],
+        scratch_shapes=[
+            pltpu.VMEM((2, 2 * HD, length), jnp.bfloat16),
+            pltpu.VMEM((2, 2 * HD, block), jnp.float32),
+            pltpu.VMEM((2, 1, block), jnp.float32),
+            pltpu.VMEM((block, block), jnp.float32),
+            pltpu.VMEM((PIECE, block), jnp.float32),
+        ],
+        compiler_params=pltpu.CompilerParams(vmem_limit_bytes=48 * 1024 * 1024),
+        name="attend",
+    )(slopes, starts, me, triple, triple, triple)
+
+
+def pull_kernel(block, slope_ref, start_ref, me_ref, q_ref, k_ref, v_ref, o_ref, g_ref, lse_ref, dq_ref, dk_ref, dv_ref,
+                kt_ref, dk_acc, dv_acc, dqt_ref, bias_ref, tail_ref):
+    pair = pl.program_id(0)
+    turn = pl.program_id(1)
+    me = me_ref[0]
+    step = turn ^ me
+    length = k_ref.shape[0]
+    first = step * block
+
+    def at(index):
+        return pl.multiple_of((index ^ me) * block, block)
+
+    start = start_ref[(step * block) // (length // start_ref.shape[0])]
+
+    @pl.when(turn == 0)
+    def _():
+        kt_ref[...] = k_ref[...].astype(jnp.float32).T.astype(jnp.bfloat16)
+        dk_acc[...] = jnp.zeros_like(dk_acc)
+        dv_acc[...] = jnp.zeros_like(dv_acc)
+
+    bias_ref[...] = diagonal_bias(block, block, first, first, start)
+    dqt_ref[...] = jnp.zeros_like(dqt_ref)
+    scale = jnp.asarray(HD ** -0.5, jnp.bfloat16)
+    zero = jnp.zeros((), jnp.bfloat16)
+    q_block = q_ref[...] * scale
+    g_block = g_ref[...]
+    masks = [head_mask(q_block.shape, head) for head in range(2)]
+    q_heads = [jnp.where(mask, q_block, zero) for mask in masks]
+    g_heads = [jnp.where(mask, g_block, zero) for mask in masks]
+    slopes = [slope_ref[2 * pair + head] for head in range(2)]
+    product = g_block.astype(jnp.float32).T * o_ref[...]
+    deltas = [jnp.sum(product[head * HD:(head + 1) * HD], axis=0, keepdims=True) for head in range(2)]
+
+    def absorb(place, rows, bias_of):
+        keys = k_ref[pl.ds(place, rows), :]
+        values = v_ref[pl.ds(place, rows), :]
+        dk = dk_acc[pl.ds(place, rows), :]
+        dv = dv_acc[pl.ds(place, rows), :]
+        for head in range(2):
+            scores = dot_nt(keys, q_heads[head]) + slopes[head] * bias_of
+            weights = jnp.exp(scores - lse_ref[0, head:head + 1, :])
+            dv = dv + dot_nn(weights.astype(jnp.bfloat16), g_heads[head])
+            grad_p = dot_nt(values, g_heads[head])
+            grad_s = (weights * (grad_p - deltas[head])).astype(jnp.bfloat16)
+            dk = dk + dot_nn(grad_s, q_heads[head])
+            dqt_ref[head * HD:(head + 1) * HD, :] += dot_nn(kt_ref[head * HD:(head + 1) * HD, pl.ds(place, rows)], grad_s)
+        dk_acc[pl.ds(place, rows), :] = dk
+        dv_acc[pl.ds(place, rows), :] = dv
+
+    absorb(at(step), block, bias_ref[...])
+
+    def full(index, carry):
+        absorb(at(index), block, ramp(block, index * block, first))
+        return carry
+
+    lax.fori_loop(0, step, full, 0)
+    edge = first + block
+
+    @pl.when((start < edge) & (start + PIECE > edge))
+    def _():
+        tail_ref[...] = diagonal_bias(PIECE, block, edge, first, start)
+        absorb(at(step + 1), PIECE, tail_ref[...])
+
+    dq_ref[...] = (dqt_ref[...].T * (HD ** -0.5)).astype(jnp.bfloat16)
+
+    @pl.when(turn == pl.num_programs(1) - 1)
+    def _():
+        dk_ref[...] = dk_acc[...].astype(jnp.bfloat16)
+        dv_ref[...] = dv_acc[...].astype(jnp.bfloat16)
+
+
+def attend_pull(triple, o, g, lse, slopes, starts, me, block=512):
+    width, length = o.shape
+    pairs = width // (2 * HD)
+    steps = length // block
+    smem = pl.BlockSpec(memory_space=pltpu.SMEM)
+    rows = pl.BlockSpec((block, 2 * HD), lambda p, i: (i, p))
+    whole = pl.BlockSpec((length, 2 * HD), lambda p, i: (0, p))
+    return pl.pallas_call(
+        functools.partial(pull_kernel, block),
+        grid=(pairs, steps),
+        in_specs=[
+            smem,
+            smem,
+            smem,
+            rows,
+            pl.BlockSpec((length, 2 * HD), lambda p, i: (0, pairs + p)),
+            pl.BlockSpec((length, 2 * HD), lambda p, i: (0, 2 * pairs + p)),
+            pl.BlockSpec((2 * HD, block), lambda p, i: (p, i)),
+            rows,
+            pl.BlockSpec((1, 8, block), lambda p, i: (p, 0, i)),
+        ],
+        out_specs=[rows, whole, whole],
+        out_shape=[jax.ShapeDtypeStruct((length, width), jnp.bfloat16)] * 3,
+        scratch_shapes=[
+            pltpu.VMEM((2 * HD, length), jnp.bfloat16),
+            pltpu.VMEM((length, 2 * HD), jnp.float32),
+            pltpu.VMEM((length, 2 * HD), jnp.float32),
+            pltpu.VMEM((2 * HD, block), jnp.float32),
+            pltpu.VMEM((block, block), jnp.float32),
+            pltpu.VMEM((PIECE, block), jnp.float32),
+        ],
+        compiler_params=pltpu.CompilerParams(vmem_limit_bytes=48 * 1024 * 1024),
+        name="attend_pull",
+    )(slopes, starts, me, triple, triple, triple, o, g, lse)
+
+
+def joined_expand(refs, tile):
+    return jnp.concatenate(
+        [
+            jnp.concatenate([ref[0, chunk * 128:(chunk + 1) * 128, :] for ref in refs], axis=0)
+            for chunk in range(tile // 128)
+        ],
+        axis=1,
+    )
+
+
+def joined_reduce(refs, tile):
+    return jnp.concatenate([ref[0, tile:, :] for ref in refs], axis=1)
+
+
+GELU_A = 0.7978845608028654
+GELU_B = 0.044715
+
+
+def mlp_kernel(normed_ref, bias_ref, *rest):
+    weight_refs, (hidden_ref, out_ref) = rest[:8], rest[8:]
+    tile = hidden_ref.shape[1]
+    hidden = dot_nn(normed_ref[...], joined_expand(weight_refs, tile)) + bias_ref[...]
+    inner = jnp.tanh(GELU_A * (hidden + GELU_B * hidden * hidden * hidden))
+    active = (0.5 * hidden * (1.0 + inner)).astype(BF)
+    hidden_ref[...] = hidden.astype(hidden_ref.dtype)
+    term = dot_nn(active, joined_reduce(weight_refs, tile))
+
+    @pl.when(pl.program_id(0) == 0)
+    def _():
+        out_ref[...] = term
+
+    @pl.when(pl.program_id(0) > 0)
+    def _():
+        out_ref[...] += term
+
+
+def mlp_forward(normed, bias, bundles):
+    rows, features = normed.shape
+    units = bias.shape[1]
+    tile = 512
+    weight_spec = pl.BlockSpec((1, 2 * tile, 128), lambda f: (f // 2, f % 2, 0))
+    return pl.pallas_call(
+        mlp_kernel,
+        grid=(units // tile,),
+        in_specs=[
+            pl.BlockSpec((rows, features), lambda f: (0, 0)),
+            pl.BlockSpec((1, tile), lambda f: (0, f)),
+        ]
+        + [weight_spec] * 8,
+        out_specs=[
+            pl.BlockSpec((rows, tile), lambda f: (0, f)),
+            pl.BlockSpec((rows, features), lambda f: (0, 0)),
+        ],
+        out_shape=[
+            jax.ShapeDtypeStruct((rows, units), BF),
+            jax.ShapeDtypeStruct((rows, features), F32),
+        ],
+        compiler_params=pltpu.CompilerParams(vmem_limit_bytes=48 * 1024 * 1024),
+        cost_estimate=pl.CostEstimate(flops=4 * rows * features * units, bytes_accessed=4 * features * units, transcendentals=0),
+        name="mlp_forward",
+    )(normed, bias, *bundles)
+
+
+def mlp_pull_kernel(grad_ref, normed_ref, hidden_ref, *rest):
+    weight_refs = rest[:8]
+    grad_normed_ref, grad_bias_ref = rest[8:10]
+    out_refs = rest[10:18]
+    normed_t_ref = rest[18]
+    tile = hidden_ref.shape[1]
+
+    @pl.when(pl.program_id(0) == 0)
+    def _():
+        normed_t_ref[...] = normed_ref[...].astype(F32).T.astype(BF)
+
+    grad = grad_ref[...]
+    hidden = hidden_ref[...].astype(F32)
+    squared = hidden * hidden
+    inner = jnp.tanh(GELU_A * hidden * (1.0 + GELU_B * squared))
+    half_up = 0.5 * (1.0 + inner)
+    active = hidden * half_up
+    slope = half_up + 0.5 * hidden * (1.0 - inner * inner) * (GELU_A * (1.0 + 3.0 * GELU_B * squared))
+    grad_active = dot_nt(grad, joined_reduce(weight_refs, tile))
+    grad_hidden = grad_active * slope
+    grad_bias_ref[...] = jnp.sum(grad_hidden, axis=0, keepdims=True)
+    grad_hidden = grad_hidden.astype(BF)
+    grad_reduce = dot_nn(active.T.astype(BF), grad).astype(BF)
+    grad_expand = dot_nn(normed_t_ref[...], grad_hidden).astype(BF)
+    for index, out_ref in enumerate(out_refs):
+        for chunk in range(tile // 128):
+            out_ref[0, chunk * 128:(chunk + 1) * 128, :] = grad_expand[
+                index * 128:(index + 1) * 128, chunk * 128:(chunk + 1) * 128
+            ]
+        out_ref[0, tile:, :] = grad_reduce[:, index * 128:(index + 1) * 128]
+    term = dot_nt(grad_hidden, joined_expand(weight_refs, tile))
+
+    @pl.when(pl.program_id(0) == 0)
+    def _():
+        grad_normed_ref[...] = term
+
+    @pl.when(pl.program_id(0) > 0)
+    def _():
+        grad_normed_ref[...] += term
+
+
+def mlp_backward(grad, normed, hidden, bundles):
+    rows, features = normed.shape
+    units = hidden.shape[1]
+    tile = 512
+    weight_spec = pl.BlockSpec((1, 2 * tile, 128), lambda f: (f // 2, f % 2, 0))
+    whole = pl.BlockSpec((rows, features), lambda f: (0, 0))
+    return pl.pallas_call(
+        mlp_pull_kernel,
+        grid=(units // tile,),
+        in_specs=[whole, whole, pl.BlockSpec((rows, tile), lambda f: (0, f))] + [weight_spec] * 8,
+        out_specs=[whole, pl.BlockSpec((1, tile), lambda f: (0, f))] + [weight_spec] * 8,
+        out_shape=[
+            jax.ShapeDtypeStruct((rows, features), F32),
+            jax.ShapeDtypeStruct((1, units), F32),
+        ]
+        + [jax.ShapeDtypeStruct((units // 1024, 2048, 128), BF)] * 8,
+        scratch_shapes=[pltpu.VMEM((features, rows), BF)],
+        compiler_params=pltpu.CompilerParams(vmem_limit_bytes=56 * 1024 * 1024),
+        cost_estimate=pl.CostEstimate(flops=8 * rows * features * units, bytes_accessed=8 * features * units, transcendentals=0),
+        name="mlp_backward",
+    )(grad, normed, hidden, *bundles)
+
+
+def gather_plane(own):
+    half = own.shape[0] // 2
+    from_x = swap(own, XBIT)
+    from_y = swap(own, YBIT)
+    across = jnp.concatenate([swap(from_x[:half], YBIT), swap(from_y[half:], XBIT)], axis=0)
+    quads = [own, from_x, from_y, across]
+    out = []
+    for quad in quads:
+        out += [quad, swap(quad, CORE)]
+    return out
+
+
+def scatter_plane(pieces):
+    kept = [pieces[2 * i] + swap(pieces[2 * i + 1], CORE) for i in range(4)]
+    own, to_x, to_y, across = kept
+    half = own.shape[0] // 2
+    to_x = jnp.concatenate([to_x[:half] + swap(across[:half], YBIT), to_x[half:]], axis=0)
+    to_y = jnp.concatenate([to_y[:half], to_y[half:] + swap(across[half:], XBIT)], axis=0)
+    return own + swap(to_x, XBIT) + swap(to_y, YBIT)
+
+
+def pack_mlp(expand, reduce):
+    first = expand.reshape(128, 2, 4, 128).transpose(1, 2, 0, 3).reshape(2, 512, 128)
+    return jnp.concatenate([first, reduce.reshape(2, 512, 128)], axis=1).reshape(2048, 128)
+
+
+def unpack_mlp(values):
+    shaped = values.reshape(2, 2, 512, 128)
+    return (
+        shaped[:, 0].reshape(2, 4, 128, 128).transpose(2, 0, 1, 3).reshape(128, 1024),
+        shaped[:, 1].reshape(1024, 128),
+    )
+
+
+def pack_attention(project, output):
+    first = project.reshape(3, 128, 2, 128).transpose(0, 2, 1, 3).reshape(768, 128)
+    return jnp.concatenate([first, output], axis=0)
+
+
+def unpack_attention(values):
+    return (
+        values[:768].reshape(3, 2, 128, 128).transpose(0, 2, 1, 3).reshape(3, 128, 256),
+        values[768:],
+    )
+
+
+def fast_fetch_attention(project, output, small, core, own):
+    piece = jnp.concatenate([pack_attention(project, output), small], axis=0)
+    far = swap(piece, Z1)
+    first = jnp.where(core == 0, piece, far)
+    second = jnp.where(core == 0, far, piece)
+    parts = gather_plane(jnp.stack([first, second]))
+    parts = [part if index % 2 == 0 else part[::-1] for index, part in enumerate(parts)]
+    vectors = jnp.concatenate([part[0, 1024:1030] for part in parts], axis=1).astype(F32)
+    weights = []
+    for quarter in range(2):
+        w_project = jnp.concatenate(
+            [part[quarter, :768].reshape(6, 128, 128).transpose(1, 0, 2).reshape(128, 768) for part in parts], axis=0
+        )
+        w_output = jnp.concatenate([part[quarter, 768:1024] for part in parts], axis=1)
+        biases = jnp.stack([part[quarter, 1030:1032, :32] for part in parts]).astype(F32)
+        biases = biases[jnp.arange(8) ^ own].transpose(1, 0, 2).reshape(2, 256)
+        bias = jnp.concatenate([biases[0], jnp.zeros_like(biases[0]), biases[1]])
+        weights.append((w_project, bias, w_output))
+    return vectors, weights
+
+
+def fast_fetch_mlp(expand, reduce, bias, own):
+    piece = jnp.concatenate(
+        [pack_mlp(expand, reduce), jnp.broadcast_to(bias[None], (16, 128))], axis=0
+    )
+    parts = gather_plane(jnp.stack([piece, swap(piece, 1), swap(piece, 2), swap(piece, 3)]))
+    biases = jnp.stack([part[:, 2048] for part in parts], axis=1).astype(F32)
+    biases = biases[:, jnp.arange(8) ^ own].reshape(1, 4096)
+    return parts, biases
+
+
+def fast_forward(resid, vectors, heads_weights, mlp_weights, slopes, starts, me):
+    (w_mine, b_mine, o_mine), (w_other, b_other, o_other) = heads_weights
+    normed = layer_norm(resid, vectors[0], vectors[1]).astype(BF)
+    normed_far = swap(normed, Z0)
+
+    def projected(rows, weight, bias):
+        return (dot_nn(rows, weight) + bias).astype(BF)
+
+    got = [swap(projected(rows, w_other, b_other), CORE) for rows in (normed, normed_far)]
+    triple = jnp.concatenate([projected(rows, w_mine, b_mine) for rows in (normed, normed_far)] + got, axis=0)
+    mixed, exact, log_total = attend(triple, slopes, starts, me)
+    mixed_other = swap(mixed[1024:], CORE)
+
+    def term(first):
+        return dot_nn(mixed[first:first + 512], o_mine) + dot_nn(mixed_other[first:first + 512], o_other)
+
+    far = swap(term(512).astype(BF), Z0)
+    mid = resid + (term(0) + far.astype(F32) + vectors[2])
+    normed_two = layer_norm(mid, vectors[3], vectors[4]).astype(BF)
+    hidden, total = mlp_forward(normed_two, mlp_weights[1], mlp_weights[0])
+    out = mid + (total + vectors[5])
+    return out, (normed, normed_far, triple, mixed, exact, mixed_other, log_total, mid, normed_two, hidden)
+
+
+def fast_backward(grad_out, resid, vectors, heads_weights, mlp_weights, kept, slopes, starts, me, core, own):
+    (w_mine, b_mine, o_mine), (w_other, b_other, o_other) = heads_weights
+    normed, normed_far, triple, mixed, exact, mixed_other, log_total, mid, normed_two, hidden = kept
+    outs = mlp_backward(grad_out.astype(BF), normed_two, hidden, mlp_weights[0])
+    grad_normed_two, grad_bias_expand, mlp_grads = outs[0], outs[1], outs[2:]
+    grad_bias_reduce = jnp.sum(grad_out, axis=0)
+    unused, pull = jax.vjp(layer_norm, mid, vectors[3], vectors[4])
+    grad_norm, grad_gain_two, grad_shift_two = pull(grad_normed_two)
+    grad_mid = grad_out + grad_norm
+    grad_bias_output = jnp.sum(grad_mid, axis=0)
+    grad_attn = grad_mid.astype(BF)
+    grad_attn_far = swap(grad_attn, Z0)
+    pair = (grad_attn, grad_attn_far)
+    got = [swap(dot_nt(rows, o_other).astype(BF), CORE) for rows in pair]
+    grad_mixed = jnp.concatenate([dot_nt(rows, o_mine).astype(BF) for rows in pair] + got, axis=0)
+    grad_q, grad_k, grad_v = attend_pull(triple, exact, grad_mixed, log_total, slopes, starts, me)
+    grad_mine = jnp.concatenate([grad_q[:1024], grad_k[:1024], grad_v[:1024]], axis=1)
+    grad_other = swap(jnp.concatenate([grad_q[1024:], grad_k[1024:], grad_v[1024:]], axis=1), CORE)
+
+    def term(first):
+        return dot_nt(grad_mine[first:first + 512], w_mine) + dot_nt(grad_other[first:first + 512], w_other)
+
+    far = swap(term(512).astype(BF), Z0)
+    grad_normed = term(0) + far.astype(F32)
+    unused, pull = jax.vjp(layer_norm, resid, vectors[0], vectors[1])
+    grad_norm, grad_gain_one, grad_shift_one = pull(grad_normed)
+    grad_in = grad_mid + grad_norm
+
+    rows_all = jnp.concatenate([normed, normed_far], axis=0)
+    grad_all = jnp.concatenate(pair, axis=0)
+    grad_project = [dot_tn(rows_all, grad).astype(BF) for grad in (grad_mine, grad_other)]
+    grad_output = [dot_tn(rows, grad_all).astype(BF) for rows in (mixed[:1024], mixed_other)]
+    grad_bias = [jnp.sum(grad.astype(F32), axis=0) for grad in (grad_mine, grad_other)]
+    small = small_sums(
+        [grad_gain_one, grad_shift_one, grad_bias_output, grad_gain_two, grad_shift_two, grad_bias_reduce],
+        grad_bias_expand, grad_bias, core, own,
+    )
+    head_pieces = []
+    for index in range(8):
+        both = [
+            jnp.concatenate(
+                [
+                    grad_project[q][index * 128:(index + 1) * 128].reshape(128, 6, 128).transpose(1, 0, 2).reshape(768, 128),
+                    grad_output[q][:, index * 128:(index + 1) * 128],
+                ],
+                axis=0,
+            )
+            for q in range(2)
+        ]
+        head_pieces.append(jnp.stack(both if index % 2 == 0 else both[::-1]))
+    heads = scatter_plane(head_pieces)
+    near = jnp.where(core == 0, heads[0], heads[1])
+    away = jnp.where(core == 0, heads[1], heads[0])
+    grad_heads = unpack_attention(near.astype(F32) + swap(away, Z1).astype(F32))
+    units = scatter_plane(mlp_grads)
+    grad_units = unpack_mlp(
+        units[0].astype(F32)
+        + swap(units[1], 1).astype(F32)
+        + swap(units[2], 2).astype(F32)
+        + swap(units[3], 3).astype(F32)
+    )
+    return grad_in, grad_heads, grad_units, small
+
+
+def small_sums(vectors, grad_bias_expand, grad_bias_project, core, own):
+    turn = jnp.arange(8) ^ own
+    stacked = jnp.stack(vectors).reshape(6, 8, 128)
+    expand = grad_bias_expand.reshape(4, 8, 128)[:, turn]
+    project = [jnp.stack([b[:256], b[512:]]).reshape(2, 8, 32)[:, turn] for b in grad_bias_project]
+    project = [jnp.where(core == 0, project[0], project[1]), jnp.where(core == 0, project[1], project[0])]
+    project = jnp.concatenate([project[0], project[1]], axis=0)
+    project = jnp.concatenate([project, jnp.zeros((4, 8, 96), F32)], axis=2)
+    rows = jnp.concatenate([stacked, expand, project], axis=0).transpose(1, 0, 2)
+    rows = rows.reshape(2, 2, 2, 14, 128)
+    rows = rows[:, :, 0] + swap(rows[:, :, 1], CORE)
+    rows = rows[:, 0] + swap(rows[:, 1], XBIT)
+    rows = rows[0] + swap(rows[1], YBIT)
+    total = rows[:6], rows[6], rows[10:12]
+
+    def part(offset):
+        return jnp.concatenate([rows[:6], rows[6 + offset:7 + offset], rows[12:14]], axis=0)
+
+    base = jnp.concatenate([total[0], total[1][None], total[2]], axis=0)
+    one, two, three = (swap(part(offset), offset) for offset in (1, 2, 3))
+    whole = base[:7] + one[:7] + two[:7] + three[:7]
+    bias = base[7:] + two[7:]
+    return whole[:6], whole[6], bias[:, :32]
+
+
+def fast_device(
+    layer_input,
+    first_gain,
+    first_shift,
+    project_weight,
+    project_bias,
+    output_weight,
+    output_bias,
+    second_gain,
+    second_shift,
+    expand_weight,
+    expand_bias,
+    reduce_weight,
+    reduce_bias,
+    picture_start,
+    cotangent,
+):
+    own = lax.axis_index("dp")
+    place = lax.axis_index("tensor")
+    core = own & 1
+    me = (2 * core + (place & 1)).astype(jnp.int32).reshape(1)
+    quarter = place ^ (2 * core)
+    slopes = head_slopes(quarter * 4, 4)
+    starts = redeal(picture_start)[0]
+    resid = turn_blocks(redeal(layer_input).astype(F32), own)
+    head_weights, mlp_weights = [], []
+    for layer in range(LAYERS):
+        small = jnp.stack(
+            [v[layer] for v in (first_gain, first_shift, output_bias, second_gain, second_shift, reduce_bias)]
+        )
+        small = jnp.concatenate(
+            [small, jnp.pad(project_bias[layer], ((0, 0), (0, 96))), jnp.zeros((8, 128), BF)], axis=0
+        )
+        head_weights.append(fast_fetch_attention(project_weight[layer], output_weight[layer], small, core, own))
+        mlp_weights.append(fast_fetch_mlp(expand_weight[layer], reduce_weight[layer], expand_bias[layer], own))
+    saved = []
+    for layer in range(LAYERS):
+        vectors, weights = head_weights[layer]
+        after, kept = fast_forward(resid, vectors, weights, mlp_weights[layer], slopes, starts, me)
+        saved.append((resid, kept))
+        resid = after
+    layer_output = redeal(turn_blocks(resid.astype(BF), own))
+    grad = turn_blocks(redeal(cotangent).astype(F32), own)
+    grads = [None] * LAYERS
+    for layer in reversed(range(LAYERS)):
+        vectors, weights = head_weights[layer]
+        before, kept = saved[layer]
+        grad, *grads[layer] = fast_backward(
+            grad, before, vectors, weights, mlp_weights[layer], kept, slopes, starts, me, core, own
+        )
+    input_grad = redeal(turn_blocks(grad.astype(BF), own))
+    small = [jnp.stack([g[2][0][i] for g in grads]) for i in range(6)]
+    return (
+        layer_output,
+        input_grad,
+        small[0],
+        small[1],
+        jnp.stack([g[0][0] for g in grads]),
+        jnp.stack([g[2][2] for g in grads]),
+        jnp.stack([g[0][1] for g in grads]),
+        small[2],
+        small[3],
+        small[4],
+        jnp.stack([g[1][0] for g in grads]),
+        jnp.stack([g[2][1] for g in grads]),
+        jnp.stack([g[1][1] for g in grads]),
+        small[5],
+    )
+
+
 def solution(mesh):
     placed = (
         P(("dp", "tensor"), None),
@@ -421,7 +1091,7 @@
         P(("dp", "tensor"), None),
     )
     return jax.shard_map(
-        on_device,
+        fast_device if mesh_is_paired(mesh) else on_device,
         mesh=mesh,
         in_specs=placed,
         out_specs=(

time: 2600 us -> 1300 us (0.50)
  waiting for transfers between devices: 1320 us -> 411 us
  matrix products: 822 us -> 84 us
  Pallas kernels: 0 us -> 228 us
  starting transfers between devices: 2.16 us -> 136 us
  local copies, waits for them, and re-layouts: 147 us -> 277 us
  blocking collectives: 104 us -> 0 us
  loops' own time: 28.7 us -> 0 us
    dot_general x80 -> x40, matrix products: 822 us -> 84 us  [the longest x16 35.8 us: dot_nt(): lax.dot_general(a, b, (((1,), (1,)), ((), ())), preferred_element_type=jn...]
    all_gather x14 -> x0, waiting for transfers between devices: 639 us -> none  [the longest x4 305 us: gather_rows(): return lax.all_gather(values, 'tensor', axis=0, tiled=True)]
    reduce_scatter x10 -> x0, waiting for transfers between devices: 578 us -> none  [the longest x4 291 us: scatter_rows(): lax.psum_scatter(partial_term(jnp.int32(0), rows_here * lax.axis_size('te...]
    ppermute x0 -> x117, waiting for transfers between devices: none -> 411 us  [the longest x112 411 us: swap(): return lax.ppermute(values, AXES, [(i, i ^ mask) for i in range(32)])]
    pallas_call x0 -> x8, Pallas kernels: none -> 228 us  [the longest x2 76.2 us: attend_pull(): pl.pallas_call(functools.partial(pull_kernel, block), grid=(pairs, steps)...]
    ppermute x0 -> x117, starting transfers between devices: none -> 136 us  [the longest x112 106 us: swap(): return lax.ppermute(values, AXES, [(i, i ^ mask) for i in range(32)])]
    unnamed x44 -> x0, waiting for transfers between devices: 105 us -> none
    all_gather x8 -> x0, blocking collectives: 77.7 us -> none  [the longest x2 23.2 us: fetch_layer(): lax.all_gather(output_weight[layer_index], 'dp', axis=1, tiled=True)]
  transfers between devices with their start and end apart: 34 -> 117, of which waited for: 24 -> 26; matrix products, arithmetic and copies ran while one was open for 18% -> 37% of each run, Pallas kernels for 0% -> 14%
where the time goes in v1:
time: 1300 us; the launch traced here: 1290 us
  waiting for transfers between devices  411 us (32%)
  local copies, waits for them, and re-layouts  277 us (21%)
  Pallas kernels  228 us (18%)
  other arithmetic  147 us (11%)
  starting transfers between devices  136 us (10%)
  matrix products  84 us (6%)
    ppermute x112, waiting for transfers between devices, swap(): return lax.ppermute(values, AXES, [(i, i ^ mask) for i in range(32)])  411 us
    ppermute x112, starting transfers between devices, swap(): return lax.ppermute(values, AXES, [(i, i ^ mask) for i in range(32)])  106 us
    unnamed x579, local copies, waits for them, and re-layouts  88.1 us
    pallas_call x2, Pallas kernels, attend_pull(): pl.pallas_call(functools.partial(pull_kernel, block), grid=(pairs, steps)...  76.2 us
    pallas_call x2, Pallas kernels, mlp_backward(): pl.pallas_call(mlp_pull_kernel, grid=(units // tile,), in_specs=[whole, w...  61.8 us
    pallas_call x2, Pallas kernels, attend(): pl.pallas_call(functools.partial(attend_kernel, block), grid=(pairs, step...  57.7 us
    transpose x32, local copies, waits for them, and re-layouts, fast_backward(): grad_project[q][index * 128:(index + 1) * 128].reshape(128, 6, 128)  47.5 us
    another operation x32, local copies, waits for them, and re-layouts, fast_fetch_attention(): part[quarter, :768].reshape(6, 128, 128).transpose(1, 0, 2)  38.9 us
  transfers between devices with their start and end apart: 117, of which 26 were waited for; matrix products, arithmetic and copies ran while one was open for 37% of the time, Pallas kernels for 14%

profile of v1, /device:TPU:0, one launch (start us, length us, event | category | flops | bytes accessed | tf_op | source)
XLA Modules:
  0.0 1287.9 jit_solution(14992698664610835161)
XLA Ops:
  3.8 4.0 collective-permute-start.42
  15.6 56.4 %collective-permute-done.2 = bf16[1040,128]{1,0:T(8,128)(2,1)S(1)} collective-permute-done((bf16[1040,128]{1,0:T(8,128)(2,1)S(1)}, bf16[1040,128]{1,0:T(8,128)(2,1)S(1)}, u32[]{:S(2)}, u32[]{:S(2)}) %collective-permute-start.2) | collective-permute-done | bytes 266272 | tf_op jit(solution)/shard_map/ppermute | solution.py:421
  72.1 16.9 %collective-permute-done.27 = bf16[1040,128]{1,0:T(8,128)(2,1)S(1)} collective-permute-done((bf16[1040,128]{1,0:T(8,128)(2,1)S(1)}, bf16[1040,128]{1,0:T(8,128)(2,1)S(1)}, u32[]{:S(2)}, u32[]{:S(2)}) %collective-permute-start.27) | collective-permute-done | bytes 266272 | tf_op jit(solution)/shard_map/ppermute | solution.py:421
  104.5 17.7 %collective-permute-done.16 = bf16[2064,128]{1,0:T(8,128)(2,1)} collective-permute-done((bf16[2064,128]{1,0:T(8,128)(2,1)}, bf16[2064,128]{1,0:T(8,128)(2,1)}, u32[]{:S(2)}, u32[]{:S(2)}) %collective-permute-start.16) | collective-permute-done | bytes 528416 | tf_op jit(solution)/shard_map/ppermute | solution.py:421
  132.3 9.4 collective-permute-start
  147.0 9.4 collective-permute-start.53
  305.8 3.7 add_convert_fusion.15
  309.6 12.6 collective-permute-done.11
  336.9 6.7 pad_maximum_fusion.q_ref.k_ref.v_ref
  343.7 28.7 %attend.2 = (bf16[2048,256]{1,0:T(8,128)(2,1)S(1)}, f32[256,2048]{1,0:T(8,128)S(1)}, f32[2,8,2048]{2,1,0:T(8,128)S(1)}) custom-call(f32[4]{0:T(128)S(1)} %multiply_exponential_fusion.slope_ref, s32[2]{0:T(128)S(1)} %bitcast.758, s32[1]{0:T(128)} %bitcast.1.me_ref, bf16[2048,768]{1,0:T(8,128)(2,1)} %pad_maximum_fusion.q_ref.k_ref.v_ref, ...), custom_call_target="tpu_custom_call" | custom-call | tf_op jit(solution)/shard_map/attend/pallas_call | solution.py:548
  378.7 27.6 %collective-permute-done.25 = bf16[2,2064,128]{2,1,0:T(8,128)(2,1)S(1)} collective-permute-done((bf16[2,2064,128]{2,1,0:T(8,128)(2,1)S(1)}, bf16[2,2064,128]{2,1,0:T(8,128)(2,1)S(1)}, u32[]{:S(2)}, u32[]{:S(2)}) %collective-permute-start.25) | collective-permute-done | bytes 1056800 | tf_op jit(solution)/shard_map/ppermute | solution.py:421
  414.9 16.0 %collective-permute-done.15 = bf16[512,1024]{1,0:T(8,128)(2,1)S(1)} collective-permute-done((bf16[512,1024]{1,0:T(8,128)(2,1)S(1)}, bf16[512,1024]{1,0:T(8,128)(2,1)S(1)}, u32[]{:S(2)}, u32[]{:S(2)}) %collective-permute-start.15) | collective-permute-done | bytes 1048608 | tf_op jit(solution)/shard_map/ppermute | solution.py:421
  435.1 16.3 %mlp_forward.2 = (bf16[512,4096]{1,0:T(8,128)(2,1)}, f32[512,1024]{1,0:T(8,128)S(1)}) custom-call(bf16[512,1024]{1,0:T(8,128)(2,1)S(1)} %add_convert_fusion.7.normed_ref, f32[1,4096]{1,0:T(1,128)S(1)} %bitcast.757, bf16[4,2064,128]{2,1,0:T(8,128)(2,1)S(1)} %pad_maximum_fusion.2.rest_0_, bf16[4,2064,128]{2,1,0:T(8,128)(2,1)} %collective-permute-done.19.rest_1_, ...), custom_call_target="tpu_custom_call" | custom-call | flops 8589934592 | bytes 16777216 | tf_op jit(solution)/shard_map/mlp_forward/pallas_call | solution.py:729
  456.3 3.3 collective-permute-done.47.rest_4_
  463.3 18.5 %collective-permute-done.49 = bf16[2,2064,128]{2,1,0:T(8,128)(2,1)} collective-permute-done((bf16[2,2064,128]{2,1,0:T(8,128)(2,1)}, bf16[2,2064,128]{2,1,0:T(8,128)(2,1)}, u32[]{:S(2)}, u32[]{:S(2)}) %collective-permute-start.49) | collective-permute-done | bytes 1056800 | tf_op jit(solution)/shard_map/ppermute | solution.py:421
  493.0 29.1 %attend.3 = (bf16[2048,256]{1,0:T(8,128)(2,1)S(1)}, f32[256,2048]{1,0:T(8,128)S(1)}, f32[2,8,2048]{2,1,0:T(8,128)S(1)}) custom-call(f32[4]{0:T(128)S(1)} %multiply_exponential_fusion.slope_ref, s32[2]{0:T(128)S(1)} %bitcast.759, s32[1]{0:T(128)} %bitcast.1.me_ref, bf16[2048,768]{1,0:T(8,128)(2,1)} %pad_maximum_fusion.1.q_ref.k_ref.v_ref, ...), custom_call_target="tpu_custom_call" | custom-call | tf_op jit(solution)/shard_map/attend/pallas_call | solution.py:548
  538.1 16.0 %collective-permute-done.40 = bf16[512,1024]{1,0:T(8,128)(2,1)S(1)} collective-permute-done((bf16[512,1024]{1,0:T(8,128)(2,1)}, bf16[512,1024]{1,0:T(8,128)(2,1)S(1)}, u32[]{:S(2)}, u32[]{:S(2)}) %collective-permute-start.40) | collective-permute-done | bytes 1048608 | tf_op jit(solution)/shard_map/ppermute | solution.py:421
  556.0 16.3 %mlp_forward.3 = (bf16[512,4096]{1,0:T(8,128)(2,1)}, f32[512,1024]{1,0:T(8,128)S(1)}) custom-call(bf16[512,1024]{1,0:T(8,128)(2,1)S(1)} %add_convert_fusion.4.normed_ref, f32[1,4096]{1,0:T(1,128)S(1)} %bitcast.756, bf16[4,2064,128]{2,1,0:T(8,128)(2,1)} %pad_maximum_fusion.3.rest_0_, bf16[4,2064,128]{2,1,0:T(8,128)(2,1)} %collective-permute-done.44.rest_1_, ...), custom_call_target="tpu_custom_call" | custom-call | flops 8589934592 | bytes 16777216 | tf_op jit(solution)/shard_map/mlp_forward/pallas_call | solution.py:729
  572.4 30.9 %mlp_backward.2 = (f32[512,1024]{1,0:T(8,128)}, f32[1,4096]{1,0:T(1,128)}, bf16[4,2048,128]{2,1,0:T(8,128)(2,1)}, bf16[4,2048,128]{2,1,0:T(8,128)(2,1)}, bf16[4,...) custom-call(bf16[512,1024]{1,0:T(8,128)(2,1)} %convert_element_type., ...), custom_call_target="tpu_custom_call" | custom-call | flops 17179869184 | bytes 33554432 | tf_op jit(solution)/shard_map/mlp_backward/pallas_call | solution.py:798
  615.7 4.5 collective-permute-start.107
  622.0 27.1 %collective-permute-done.54 = bf16[512,1024]{1,0:T(8,128)(2,1)} collective-permute-done((bf16[512,1024]{1,0:T(8,128)(2,1)}, bf16[512,1024]{1,0:T(8,128)(2,1)}, u32[]{:S(2)}, u32[]{:S(2)}) %collective-permute-start.54) | collective-permute-done | bytes 1048608 | tf_op jit(solution)/shard_map/ppermute | solution.py:421
  659.5 38.1 %attend_pull.2 = (bf16[2048,256]{1,0:T(8,128)(2,1)S(1)}, bf16[2048,256]{1,0:T(8,128)(2,1)S(1)}, bf16[2048,256]{1,0:T(8,128)(2,1)S(1)}) custom-call(f32[4]{0:T(128)S(1)} %multiply_exponential_fusion.slope_ref, s32[2]{0:T(128)S(1)} %bitcast.760, s32[1]{0:T(128)} %bitcast.1.me_ref, bf16[2048,768]{1,0:T(8,128)(2,1)} %pad_maximum_fusion.1.q_ref.k_ref.v_ref, ...), custom_call_target="tpu_custom_call" | custom-call | tf_op jit(solution)/shard_map/attend_pull/pallas_call | solution.py:659
  699.7 3.4 convolution_convert_fusion.1
  722.5 3.9 fusion.20
  733.1 5.8 collective-permute-start.112
  739.0 3.8 add.608
  745.2 3.6 convolution_convert_fusion
  790.3 7.2 collective-permute-done.89
  800.3 10.7 collective-permute-done.58
  818.4 30.9 %mlp_backward.3 = (f32[512,1024]{1,0:T(8,128)}, f32[1,4096]{1,0:T(1,128)}, bf16[4,2048,128]{2,1,0:T(8,128)(2,1)}, bf16[4,2048,128]{2,1,0:T(8,128)(2,1)}, bf16[4,...) custom-call(bf16[512,1024]{1,0:T(8,128)(2,1)} %convert_element_type., ...), custom_call_target="tpu_custom_call" | custom-call | flops 17179869184 | bytes 33554432 | tf_op jit(solution)/shard_map/mlp_backward/pallas_call | solution.py:798
  871.8 3.5 collective-permute-done.76
  882.0 23.0 %collective-permute-done.94 = bf16[1024,128]{1,0:T(8,128)(2,1)S(1)} collective-permute-done((bf16[1024,128]{1,0:T(8,128)(2,1)S(1)}, bf16[1024,128]{1,0:T(8,128)(2,1)S(1)}, u32[]{:S(2)}, u32[]{:S(2)}) %collective-permute-start.94) | collective-permute-done | bytes 262176 | tf_op jit(solution)/shard_map/ppermute | solution.py:421
  921.5 38.1 %attend_pull.3 = (bf16[2048,256]{1,0:T(8,128)(2,1)S(1)}, bf16[2048,256]{1,0:T(8,128)(2,1)S(1)}, bf16[2048,256]{1,0:T(8,128)(2,1)S(1)}) custom-call(f32[4]{0:T(128)S(1)} %multiply_exponential_fusion.slope_ref, s32[2]{0:T(128)S(1)} %bitcast.761, s32[1]{0:T(128)} %bitcast.1.me_ref, bf16[2048,768]{1,0:T(8,128)(2,1)} %pad_maximum_fusion.q_ref.k_ref.v_ref, ...), custom_call_target="tpu_custom_call" | custom-call | tf_op jit(solution)/shard_map/attend_pull/pallas_call | solution.py:659
  973.9 4.1 fusion.13
  984.6 5.3 collective-permute-start.116
  1004.3 7.8 collective-permute-start.115
  1017.7 18.5 %collective-permute-done.115 = bf16[2048,128]{1,0:T(8,128)(2,1)} collective-permute-done((bf16[2048,128]{1,0:T(8,128)(2,1)}, bf16[2048,128]{1,0:T(8,128)(2,1)}, u32[]{:S(2)}, u32[]{:S(2)}) %collective-permute-start.115) | collective-permute-done | bytes 524320 | tf_op jit(solution)/shard_map/ppermute | solution.py:421
  1043.6 4.2 collective-permute-start.98
  1047.8 3.9 add.597
  1051.7 3.8 add.601
  1055.6 3.6 convolution_convert_fusion.2
  1095.7 5.5 collective-permute-done.80
  1103.1 14.8 %collective-permute-done.63 = bf16[512,1024]{1,0:T(8,128)(2,1)S(1)} collective-permute-done((bf16[512,1024]{1,0:T(8,128)(2,1)S(1)}, bf16[512,1024]{1,0:T(8,128)(2,1)S(1)}, u32[]{:S(2)}, u32[]{:S(2)}) %collective-permute-start.63) | collective-permute-done | bytes 1048608 | tf_op jit(solution)/shard_map/ppermute | solution.py:421
  1150.5 45.7 %collective-permute-done.81 = bf16[2,1024,128]{2,1,0:T(8,128)(2,1)S(1)} collective-permute-done((bf16[2,1024,128]{2,1,0:T(8,128)(2,1)S(1)}, bf16[2,1024,128]{2,1,0:T(8,128)(2,1)S(1)}, u32[]{:S(2)}, u32[]{:S(2)}) %collective-permute-start.81) | collective-permute-done | bytes 524320 | tf_op jit(solution)/shard_map/ppermute | solution.py:421
  1196.2 9.4 collective-permute-start.64
  1210.1 4.4 collective-permute-start.105
  1214.5 51.5 %collective-permute-done.85 = bf16[1024,128]{1,0:T(8,128)(2,1)S(1)} collective-permute-done((bf16[1024,128]{1,0:T(8,128)(2,1)S(1)}, bf16[1024,128]{1,0:T(8,128)(2,1)S(1)}, u32[]{:S(2)}, u32[]{:S(2)}) %collective-permute-start.85) | collective-permute-done | bytes 262176 | tf_op jit(solution)/shard_map/ppermute | solution.py:421
  1272.0 7.4 collective-permute-done.104
  (1248 shorter events, 549.9 us)
Async XLA Ops:
  3.8 91.3 %collective-permute-start.42 = (bf16[2064,128]{1,0:T(8,128)(2,1)}, bf16[2064,128]{1,0:T(8,128)(2,1)}, u32[]{:S(2)}, u32[]{:S(2)}) collective-permute-start(bf16[2064,128]{1,0:T(8,128)(2,1)} %get-tuple-element.286), channel_id=1, source_target_pairs={{0,2},{1,3},{2,0},{3,1},{4,6},{5,7},{6,4},{7,5},{8,10},{9,11},{10,... | collective-permute-start | bytes 1585160 | tf_op jit(solution)/shard_map/ppermute | solution.py:421
  7.8 90.7 %collective-permute-start.41 = (bf16[2064,128]{1,0:T(8,128)(2,1)}, bf16[2064,128]{1,0:T(8,128)(2,1)}, u32[]{:S(2)}, u32[]{:S(2)}) collective-permute-start(bf16[2064,128]{1,0:T(8,128)(2,1)} %get-tuple-element.286), channel_id=1, source_target_pairs={{0,1},{1,0},{2,3},{3,2},{4,5},{5,4},{6,7},{7,6},{8,9},{9,8},{10,11... | collective-permute-start | bytes 1585160 | tf_op jit(solution)/shard_map/ppermute | solution.py:421
  9.4 90.7 %collective-permute-start.43 = (bf16[2064,128]{1,0:T(8,128)(2,1)}, bf16[2064,128]{1,0:T(8,128)(2,1)}, u32[]{:S(2)}, u32[]{:S(2)}) collective-permute-start(bf16[2064,128]{1,0:T(8,128)(2,1)} %get-tuple-element.286), channel_id=1, source_target_pairs={{0,3},{1,2},{2,1},{3,0},{4,7},{5,6},{6,5},{7,4},{8,11},{9,10},{10,... | collective-permute-start | bytes 1585160 | tf_op jit(solution)/shard_map/ppermute | solution.py:421
  10.1 61.9 %collective-permute-start.2 = (bf16[1040,128]{1,0:T(8,128)(2,1)S(1)}, bf16[1040,128]{1,0:T(8,128)(2,1)S(1)}, u32[]{:S(2)}, u32[]{:S(2)}) collective-permute-start(bf16[1040,128]{1,0:T(8,128)(2,1)S(1)} %concatenate.291), channel_id=1, source_target_pairs={{0,2},{1,3},{2,0},{3,1},{4,6},{5,7},{6,4},{7,5},{8,10},{9,11},{10,... | collective-permute-start | bytes 798728 | tf_op jit(solution)/shard_map/ppermute | solution.py:421
  12.6 76.4 %collective-permute-start.27 = (bf16[1040,128]{1,0:T(8,128)(2,1)S(1)}, bf16[1040,128]{1,0:T(8,128)(2,1)S(1)}, u32[]{:S(2)}, u32[]{:S(2)}) collective-permute-start(bf16[1040,128]{1,0:T(8,128)(2,1)S(1)} %concatenate.304), channel_id=1, source_target_pairs={{0,2},{1,3},{2,0},{3,1},{4,6},{5,7},{6,4},{7,5},{8,10},{9,11},{10,... | collective-permute-start | bytes 798728 | tf_op jit(solution)/shard_map/ppermute | solution.py:421
  98.5 48.5 %collective-permute-start.6 = (bf16[2,1040,128]{2,1,0:T(8,128)(2,1)}, bf16[2,1040,128]{2,1,0:T(8,128)(2,1)}, u32[]{:S(2)}, u32[]{:S(2)}) collective-permute-start(bf16[2,1040,128]{2,1,0:T(8,128)(2,1)} %pad_maximum_fusion.37), channel_id=1, source_target_pairs={{0,16},{1,17},{2,18},{3,19},{4,20},{5,21},{6,22},{7,23},{8,24},{9,... | collective-permute-start | bytes 1597448 | tf_op jit(solution)/shard_map/ppermute | solution.py:421
  132.3 75.9 %collective-permute-start = (bf16[512,1024]{1,0:T(8,128)(2,1)}, bf16[512,1024]{1,0:T(8,128)(2,1)}, u32[]{:S(2)}, u32[]{:S(2)}) collective-permute-start(bf16[512,1024]{1,0:T(8,128)(2,1)} %param.15), channel_id=1, source_target_pairs={{0,0},{1,1},{2,4},{3,5},{4,2},{5,3},{6,6},{7,7},{8,8},{9,9},{10,12... | collective-permute-start | bytes 3145736 | tf_op jit(solution)/shard_map/ppermute | solution.py:429
  147.0 64.2 %collective-permute-start.53 = (bf16[512,1024]{1,0:T(8,128)(2,1)}, bf16[512,1024]{1,0:T(8,128)(2,1)}, u32[]{:S(2)}, u32[]{:S(2)}) collective-permute-start(bf16[512,1024]{1,0:T(8,128)(2,1)} %param.29), channel_id=1, source_target_pairs={{0,0},{1,1},{2,4},{3,5},{4,2},{5,3},{6,6},{7,7},{8,8},{9,9},{10,12... | collective-permute-start | bytes 3145736 | tf_op jit(solution)/shard_map/ppermute | solution.py:429
  158.2 57.1 %collective-permute-start.9 = (bf16[1,1040,128]{2,1,0:T(8,128)(2,1)}, bf16[1,1040,128]{2,1,0:T(8,128)(2,1)}, u32[]{:S(2)}, u32[]{:S(2)}) collective-permute-start(bf16[1,1040,128]{2,1,0:T(8,128)(2,1)} %slice.1684), channel_id=1, source_target_pairs={{0,8},{1,9},{2,10},{3,11},{4,12},{5,13},{6,14},{7,15},{8,0},{9,1},... | collective-permute-start | bytes 798728 | tf_op jit(solution)/shard_map/ppermute | solution.py:421
  165.6 50.8 %collective-permute-start.8 = (bf16[1,1040,128]{2,1,0:T(8,128)(2,1)}, bf16[1,1040,128]{2,1,0:T(8,128)(2,1)}, u32[]{:S(2)}, u32[]{:S(2)}) collective-permute-start(bf16[1,1040,128]{2,1,0:T(8,128)(2,1)} %slice.1682), channel_id=1, source_target_pairs={{0,16},{1,17},{2,18},{3,19},{4,20},{5,21},{6,22},{7,23},{8,24},{9,... | collective-permute-start | bytes 798728 | tf_op jit(solution)/shard_map/ppermute | solution.py:421
  167.8 52.9 %collective-permute-start.34 = (bf16[1,1040,128]{2,1,0:T(8,128)(2,1)}, bf16[1,1040,128]{2,1,0:T(8,128)(2,1)}, u32[]{:S(2)}, u32[]{:S(2)}) collective-permute-start(bf16[1,1040,128]{2,1,0:T(8,128)(2,1)} %slice.1764), channel_id=1, source_target_pairs={{0,8},{1,9},{2,10},{3,11},{4,12},{5,13},{6,14},{7,15},{8,0},{9,1},... | collective-permute-start | bytes 798728 | tf_op jit(solution)/shard_map/ppermute | solution.py:421
  215.3 128.4 %collective-permute-start.1 = (s32[1,2]{1,0:T(1,128)S(1)}, s32[1,2]{1,0:T(1,128)S(1)}, u32[]{:S(2)}, u32[]{:S(2)}) collective-permute-start(s32[1,2]{1,0:T(1,128)S(1)} %copy-done.230), channel_id=1, source_target_pairs={{0,0},{1,1},{2,4},{3,5},{4,2},{5,3},{6,6},{7,7},{8,8},{9,9},{10,12... | collective-permute-start | bytes 32 | tf_op jit(solution)/shard_map/ppermute | solution.py:429
  220.7 153.7 %collective-permute-start.22 = (bf16[4,2064,128]{2,1,0:T(8,128)(2,1)S(1)}, bf16[4,2064,128]{2,1,0:T(8,128)(2,1)}, u32[]{:S(2)}, u32[]{:S(2)}) collective-permute-start(bf16[4,2064,128]{2,1,0:T(8,128)(2,1)S(1)} %pad_maximum_fusion.2.rest_0_), channel_id=1, source_target_pairs={{0,16},{1,17},{2,18},{3,19},{4,20},{5,21},{6,22},{7,23},{8,24},{9,... | collective-permute-start | bytes 6340616 | tf_op jit(solution)/shard_map/ppermute | solution.py:421
  239.3 90.4 %collective-permute-start.20 = (bf16[4,2064,128]{2,1,0:T(8,128)(2,1)S(1)}, bf16[4,2064,128]{2,1,0:T(8,128)(2,1)}, u32[]{:S(2)}, u32[]{:S(2)}) collective-permute-start(bf16[4,2064,128]{2,1,0:T(8,128)(2,1)S(1)} %pad_maximum_fusion.2.rest_0_), channel_id=1, source_target_pairs={{0,8},{1,9},{2,10},{3,11},{4,12},{5,13},{6,14},{7,15},{8,0},{9,1},... | collective-permute-start | bytes 6340616 | tf_op jit(solution)/shard_map/ppermute | solution.py:421
  244.1 47.5 %collective-permute-start.10 = (bf16[2,1040,128]{2,1,0:T(8,128)(2,1)}, bf16[2,1040,128]{2,1,0:T(8,128)(2,1)}, u32[]{:S(2)}, u32[]{:S(2)}) collective-permute-start(bf16[2,1040,128]{2,1,0:T(8,128)(2,1)} %pad_maximum_fusion.38), channel_id=1, source_target_pairs={{0,4},{1,5},{2,6},{3,7},{4,0},{5,1},{6,2},{7,3},{8,12},{9,13},{10,... | collective-permute-start | bytes 1597448 | tf_op jit(solution)/shard_map/ppermute | solution.py:421
  248.7 52.9 %collective-permute-start.35 = (bf16[2,1040,128]{2,1,0:T(8,128)(2,1)}, bf16[2,1040,128]{2,1,0:T(8,128)(2,1)}, u32[]{:S(2)}, u32[]{:S(2)}) collective-permute-start(bf16[2,1040,128]{2,1,0:T(8,128)(2,1)} %pad_maximum_fusion.40), channel_id=1, source_target_pairs={{0,4},{1,5},{2,6},{3,7},{4,0},{5,1},{6,2},{7,3},{8,12},{9,13},{10,... | collective-permute-start | bytes 1597448 | tf_op jit(solution)/shard_map/ppermute | solution.py:421
  335.0 73.2 %collective-permute-start.19 = (bf16[4,2064,128]{2,1,0:T(8,128)(2,1)S(1)}, bf16[4,2064,128]{2,1,0:T(8,128)(2,1)}, u32[]{:S(2)}, u32[]{:S(2)}) collective-permute-start(bf16[4,2064,128]{2,1,0:T(8,128)(2,1)S(1)} %pad_maximum_fusion.2.rest_0_), channel_id=1, source_target_pairs={{0,4},{1,5},{2,6},{3,7},{4,0},{5,1},{6,2},{7,3},{8,12},{9,13},{10,... | collective-permute-start | bytes 6340616 | tf_op jit(solution)/shard_map/ppermute | solution.py:421
  335.3 75.2 %collective-permute-start.45 = (bf16[4,2064,128]{2,1,0:T(8,128)(2,1)}, bf16[4,2064,128]{2,1,0:T(8,128)(2,1)S(1)}, u32[]{:S(2)}, u32[]{:S(2)}) collective-permute-start(bf16[4,2064,128]{2,1,0:T(8,128)(2,1)} %pad_maximum_fusion.3.rest_0_), channel_id=1, source_target_pairs={{0,8},{1,9},{2,10},{3,11},{4,12},{5,13},{6,14},{7,15},{8,0},{9,1},... | collective-permute-start | bytes 6340616 | tf_op jit(solution)/shard_map/ppermute | solution.py:421
  410.5 49.1 %collective-permute-start.47 = (bf16[4,2064,128]{2,1,0:T(8,128)(2,1)}, bf16[4,2064,128]{2,1,0:T(8,128)(2,1)}, u32[]{:S(2)}, u32[]{:S(2)}) collective-permute-start(bf16[4,2064,128]{2,1,0:T(8,128)(2,1)} %pad_maximum_fusion.3.rest_0_), channel_id=1, source_target_pairs={{0,16},{1,17},{2,18},{3,19},{4,20},{5,21},{6,22},{7,23},{8,24},{9,... | collective-permute-start | bytes 6340616 | tf_op jit(solution)/shard_map/ppermute | solution.py:421
  413.1 119.3 %collective-permute-start.44 = (bf16[4,2064,128]{2,1,0:T(8,128)(2,1)}, bf16[4,2064,128]{2,1,0:T(8,128)(2,1)}, u32[]{:S(2)}, u32[]{:S(2)}) collective-permute-start(bf16[4,2064,128]{2,1,0:T(8,128)(2,1)} %pad_maximum_fusion.3.rest_0_), channel_id=1, source_target_pairs={{0,4},{1,5},{2,6},{3,7},{4,0},{5,1},{6,2},{7,3},{8,12},{9,13},{10,... | collective-permute-start | bytes 6340616 | tf_op jit(solution)/shard_map/ppermute | solution.py:421
  413.5 68.3 %collective-permute-start.49 = (bf16[2,2064,128]{2,1,0:T(8,128)(2,1)}, bf16[2,2064,128]{2,1,0:T(8,128)(2,1)}, u32[]{:S(2)}, u32[]{:S(2)}) collective-permute-start(bf16[2,2064,128]{2,1,0:T(8,128)(2,1)} %slice.1831), channel_id=1, source_target_pairs={{0,16},{1,17},{2,18},{3,19},{4,20},{5,21},{6,22},{7,23},{8,24},{9,... | collective-permute-start | bytes 3170312 | tf_op jit(solution)/shard_map/ppermute | solution.py:421
  463.3 69.8 %collective-permute-start.48 = (bf16[4,2064,128]{2,1,0:T(8,128)(2,1)}, bf16[4,2064,128]{2,1,0:T(8,128)(2,1)}, u32[]{:S(2)}, u32[]{:S(2)}) collective-permute-start(bf16[4,2064,128]{2,1,0:T(8,128)(2,1)} %collective-permute-done.47.rest_4_), channel_id=1, source_target_pairs={{0,4},{1,5},{2,6},{3,7},{4,0},{5,1},{6,2},{7,3},{8,12},{9,13},{10,... | collective-permute-start | bytes 6340616 | tf_op jit(solution)/shard_map/ppermute | solution.py:421
  481.8 52.1 %collective-permute-start.46 = (bf16[4,2064,128]{2,1,0:T(8,128)(2,1)S(1)}, bf16[4,2064,128]{2,1,0:T(8,128)(2,1)}, u32[]{:S(2)}, u32[]{:S(2)}) collective-permute-start(bf16[4,2064,128]{2,1,0:T(8,128)(2,1)S(1)} %copy-done.119), channel_id=1, source_target_pairs={{0,4},{1,5},{2,6},{3,7},{4,0},{5,1},{6,2},{7,3},{8,12},{9,13},{10,... | collective-permute-start | bytes 6340616 | tf_op jit(solution)/shard_map/ppermute | solution.py:421
  615.7 123.2 %collective-permute-start.107 = (bf16[4,2048,128]{2,1,0:T(8,128)(2,1)}, bf16[4,2048,128]{2,1,0:T(8,128)(2,1)}, u32[]{:S(2)}, u32[]{:S(2)}) collective-permute-start(bf16[4,2048,128]{2,1,0:T(8,128)(2,1)} %get-tuple-element.81), channel_id=1, source_target_pairs={{0,4},{1,5},{2,6},{3,7},{4,0},{5,1},{6,2},{7,3},{8,12},{9,13},{10,... | collective-permute-start | bytes 6291464 | tf_op jit(solution)/shard_map/ppermute | solution.py:421
  620.2 108.6 %collective-permute-start.108 = (bf16[4,2048,128]{2,1,0:T(8,128)(2,1)}, bf16[4,2048,128]{2,1,0:T(8,128)(2,1)}, u32[]{:S(2)}, u32[]{:S(2)}) collective-permute-start(bf16[4,2048,128]{2,1,0:T(8,128)(2,1)} %get-tuple-element.83), channel_id=1, source_target_pairs={{0,4},{1,5},{2,6},{3,7},{4,0},{5,1},{6,2},{7,3},{8,12},{9,13},{10,... | collective-permute-start | bytes 6291464 | tf_op jit(solution)/shard_map/ppermute | solution.py:421
  649.0 93.7 %collective-permute-start.111 = (bf16[4,2048,128]{2,1,0:T(8,128)(2,1)}, bf16[4,2048,128]{2,1,0:T(8,128)(2,1)}, u32[]{:S(2)}, u32[]{:S(2)}) collective-permute-start(bf16[4,2048,128]{2,1,0:T(8,128)(2,1)} %get-tuple-element.85), channel_id=1, source_target_pairs={{0,4},{1,5},{2,6},{3,7},{4,0},{5,1},{6,2},{7,3},{8,12},{9,13},{10,... | collective-permute-start | bytes 6291464 | tf_op jit(solution)/shard_map/ppermute | solution.py:421
  732.6 51.2 %collective-permute-start.109 = (bf16[2,2048,128]{2,1,0:T(8,128)(2,1)}, bf16[2,2048,128]{2,1,0:T(8,128)(2,1)}, u32[]{:S(2)}, u32[]{:S(2)}) collective-permute-start(bf16[2,2048,128]{2,1,0:T(8,128)(2,1)} %get-tuple-element.154), channel_id=1, source_target_pairs={{0,16},{1,17},{2,18},{3,19},{4,20},{5,21},{6,22},{7,23},{8,24},{9,... | collective-permute-start | bytes 3145736 | tf_op jit(solution)/shard_map/ppermute | solution.py:421
  733.1 52.7 %collective-permute-start.112 = (bf16[2,2048,128]{2,1,0:T(8,128)(2,1)}, bf16[2,2048,128]{2,1,0:T(8,128)(2,1)S(1)}, u32[]{:S(2)}, u32[]{:S(2)}) collective-permute-start(bf16[2,2048,128]{2,1,0:T(8,128)(2,1)} %get-tuple-element.155), channel_id=1, source_target_pairs={{0,8},{1,9},{2,10},{3,11},{4,12},{5,13},{6,14},{7,15},{8,0},{9,1},... | collective-permute-start | bytes 3145736 | tf_op jit(solution)/shard_map/ppermute | solution.py:421
  775.2 102.8 %collective-permute-start.86 = (bf16[2,1024,128]{2,1,0:T(8,128)(2,1)}, bf16[2,1024,128]{2,1,0:T(8,128)(2,1)}, u32[]{:S(2)}, u32[]{:S(2)}) collective-permute-start(bf16[2,1024,128]{2,1,0:T(8,128)(2,1)} %pad_maximum_fusion.51), channel_id=1, source_target_pairs={{0,4},{1,5},{2,6},{3,7},{4,0},{5,1},{6,2},{7,3},{8,12},{9,13},{10,... | collective-permute-start | bytes 1572872 | tf_op jit(solution)/shard_map/ppermute | solution.py:421
  798.4 79.6 %collective-permute-start.90 = (bf16[2,1024,128]{2,1,0:T(8,128)(2,1)}, bf16[2,1024,128]{2,1,0:T(8,128)(2,1)}, u32[]{:S(2)}, u32[]{:S(2)}) collective-permute-start(bf16[2,1024,128]{2,1,0:T(8,128)(2,1)} %pad_maximum_fusion.54), channel_id=1, source_target_pairs={{0,8},{1,9},{2,10},{3,11},{4,12},{5,13},{6,14},{7,15},{8,0},{9,1},... | collective-permute-start | bytes 1572872 | tf_op jit(solution)/shard_map/ppermute | solution.py:421
  799.3 78.8 %collective-permute-start.93 = (bf16[2,1024,128]{2,1,0:T(8,128)(2,1)}, bf16[2,1024,128]{2,1,0:T(8,128)(2,1)}, u32[]{:S(2)}, u32[]{:S(2)}) collective-permute-start(bf16[2,1024,128]{2,1,0:T(8,128)(2,1)} %pad_maximum_fusion.56), channel_id=1, source_target_pairs={{0,16},{1,17},{2,18},{3,19},{4,20},{5,21},{6,22},{7,23},{8,24},{9,... | collective-permute-start | bytes 1572872 | tf_op jit(solution)/shard_map/ppermute | solution.py:421
  871.8 106.2 %collective-permute-start.106 = (bf16[4,2048,128]{2,1,0:T(8,128)(2,1)}, bf16[4,2048,128]{2,1,0:T(8,128)(2,1)}, u32[]{:S(2)}, u32[]{:S(2)}) collective-permute-start(bf16[4,2048,128]{2,1,0:T(8,128)(2,1)} %get-tuple-element.79), channel_id=1, source_target_pairs={{0,4},{1,5},{2,6},{3,7},{4,0},{5,1},{6,2},{7,3},{8,12},{9,13},{10,... | collective-permute-start | bytes 6291464 | tf_op jit(solution)/shard_map/ppermute | solution.py:421
  875.3 102.8 %collective-permute-start.110 = (bf16[4,2048,128]{2,1,0:T(8,128)(2,1)}, bf16[4,2048,128]{2,1,0:T(8,128)(2,1)}, u32[]{:S(2)}, u32[]{:S(2)}) collective-permute-start(bf16[4,2048,128]{2,1,0:T(8,128)(2,1)} %pad_maximum_fusion.10), channel_id=1, source_target_pairs={{0,8},{1,9},{2,10},{3,11},{4,12},{5,13},{6,14},{7,15},{8,0},{9,1},... | collective-permute-start | bytes 6291464 | tf_op jit(solution)/shard_map/ppermute | solution.py:421
  878.0 100.1 %collective-permute-start.113 = (bf16[4,2048,128]{2,1,0:T(8,128)(2,1)}, bf16[4,2048,128]{2,1,0:T(8,128)(2,1)}, u32[]{:S(2)}, u32[]{:S(2)}) collective-permute-start(bf16[4,2048,128]{2,1,0:T(8,128)(2,1)} %pad_maximum_fusion.11), channel_id=1, source_target_pairs={{0,16},{1,17},{2,18},{3,19},{4,20},{5,21},{6,22},{7,23},{8,24},{9,... | collective-permute-start | bytes 6291464 | tf_op jit(solution)/shard_map/ppermute | solution.py:421
  920.8 127.0 %collective-permute-start.96 = (bf16[4,2048,128]{2,1,0:T(8,128)(2,1)}, bf16[4,2048,128]{2,1,0:T(8,128)(2,1)}, u32[]{:S(2)}, u32[]{:S(2)}) collective-permute-start(bf16[4,2048,128]{2,1,0:T(8,128)(2,1)} %get-tuple-element.73), channel_id=1, source_target_pairs={{0,4},{1,5},{2,6},{3,7},{4,0},{5,1},{6,2},{7,3},{8,12},{9,13},{10,... | collective-permute-start | bytes 6291464 | tf_op jit(solution)/shard_map/ppermute | solution.py:421
  920.9 118.5 %collective-permute-start.97 = (bf16[4,2048,128]{2,1,0:T(8,128)(2,1)}, bf16[4,2048,128]{2,1,0:T(8,128)(2,1)}, u32[]{:S(2)}, u32[]{:S(2)}) collective-permute-start(bf16[4,2048,128]{2,1,0:T(8,128)(2,1)} %get-tuple-element.75), channel_id=1, source_target_pairs={{0,4},{1,5},{2,6},{3,7},{4,0},{5,1},{6,2},{7,3},{8,12},{9,13},{10,... | collective-permute-start | bytes 6291464 | tf_op jit(solution)/shard_map/ppermute | solution.py:421
  978.0 73.7 %collective-permute-start.100 = (bf16[4,2048,128]{2,1,0:T(8,128)(2,1)}, bf16[4,2048,128]{2,1,0:T(8,128)(2,1)}, u32[]{:S(2)}, u32[]{:S(2)}) collective-permute-start(bf16[4,2048,128]{2,1,0:T(8,128)(2,1)} %get-tuple-element.77), channel_id=1, source_target_pairs={{0,4},{1,5},{2,6},{3,7},{4,0},{5,1},{6,2},{7,3},{8,12},{9,13},{10,... | collective-permute-start | bytes 6291464 | tf_op jit(solution)/shard_map/ppermute | solution.py:421
  1036.2 170.7 %collective-permute-start.95 = (bf16[4,2048,128]{2,1,0:T(8,128)(2,1)}, bf16[4,2048,128]{2,1,0:T(8,128)(2,1)}, u32[]{:S(2)}, u32[]{:S(2)}) collective-permute-start(bf16[4,2048,128]{2,1,0:T(8,128)(2,1)} %get-tuple-element.71), channel_id=1, source_target_pairs={{0,4},{1,5},{2,6},{3,7},{4,0},{5,1},{6,2},{7,3},{8,12},{9,13},{10,... | collective-permute-start | bytes 6291464 | tf_op jit(solution)/shard_map/ppermute | solution.py:421
  1077.9 71.8 %collective-permute-start.77 = (bf16[2,1024,128]{2,1,0:T(8,128)(2,1)}, bf16[2,1024,128]{2,1,0:T(8,128)(2,1)}, u32[]{:S(2)}, u32[]{:S(2)}) collective-permute-start(bf16[2,1024,128]{2,1,0:T(8,128)(2,1)} %pad_maximum_fusion.45), channel_id=1, source_target_pairs={{0,4},{1,5},{2,6},{3,7},{4,0},{5,1},{6,2},{7,3},{8,12},{9,13},{10,... | collective-permute-start | bytes 1572872 | tf_op jit(solution)/shard_map/ppermute | solution.py:421
  1140.0 66.9 %collective-permute-start.99 = (bf16[4,2048,128]{2,1,0:T(8,128)(2,1)S(1)}, bf16[4,2048,128]{2,1,0:T(8,128)(2,1)S(1)}, u32[]{:S(2)}, u32[]{:S(2)}) collective-permute-start(bf16[4,2048,128]{2,1,0:T(8,128)(2,1)S(1)} %copy-done.49), channel_id=1, source_target_pairs={{0,8},{1,9},{2,10},{3,11},{4,12},{5,13},{6,14},{7,15},{8,0},{9,1},... | collective-permute-start | bytes 6291464 | tf_op jit(solution)/shard_map/ppermute | solution.py:421
  1141.8 65.1 %collective-permute-start.102 = (bf16[4,2048,128]{2,1,0:T(8,128)(2,1)S(1)}, bf16[4,2048,128]{2,1,0:T(8,128)(2,1)S(1)}, u32[]{:S(2)}, u32[]{:S(2)}) collective-permute-start(bf16[4,2048,128]{2,1,0:T(8,128)(2,1)S(1)} %copy-done.50), channel_id=1, source_target_pairs={{0,16},{1,17},{2,18},{3,19},{4,20},{5,21},{6,22},{7,23},{8,24},{9,... | collective-permute-start | bytes 6291464 | tf_op jit(solution)/shard_map/ppermute | solution.py:421
  1143.8 52.3 %collective-permute-start.81 = (bf16[2,1024,128]{2,1,0:T(8,128)(2,1)S(1)}, bf16[2,1024,128]{2,1,0:T(8,128)(2,1)S(1)}, u32[]{:S(2)}, u32[]{:S(2)}) collective-permute-start(bf16[2,1024,128]{2,1,0:T(8,128)(2,1)S(1)} %copy-done.123), channel_id=1, source_target_pairs={{0,8},{1,9},{2,10},{3,11},{4,12},{5,13},{6,14},{7,15},{8,0},{9,1},... | collective-permute-start | bytes 1572872 | tf_op jit(solution)/shard_map/ppermute | solution.py:421
  1149.7 55.9 %collective-permute-start.84 = (bf16[2,1024,128]{2,1,0:T(8,128)(2,1)S(1)}, bf16[2,1024,128]{2,1,0:T(8,128)(2,1)S(1)}, u32[]{:S(2)}, u32[]{:S(2)}) collective-permute-start(bf16[2,1024,128]{2,1,0:T(8,128)(2,1)S(1)} %copy-done.124), channel_id=1, source_target_pairs={{0,16},{1,17},{2,18},{3,19},{4,20},{5,21},{6,22},{7,23},{8,24},{9,... | collective-permute-start | bytes 1572872 | tf_op jit(solution)/shard_map/ppermute | solution.py:421
  1196.2 75.9 %collective-permute-start.64 = (bf16[512,1024]{1,0:T(8,128)(2,1)}, bf16[512,1024]{1,0:T(8,128)(2,1)}, u32[]{:S(2)}, u32[]{:S(2)}) collective-permute-start(bf16[512,1024]{1,0:T(8,128)(2,1)} %constant_dynamic-update-slice_fusion.140), channel_id=1, source_target_pairs={{0,0},{1,1},{2,4},{3,5},{4,2},{5,3},{6,6},{7,7},{8,8},{9,9},{10,12... | collective-permute-start | bytes 3145736 | tf_op jit(solution)/shard_map/ppermute | solution.py:429
  1206.8 59.1 %collective-permute-start.85 = (bf16[1024,128]{1,0:T(8,128)(2,1)S(1)}, bf16[1024,128]{1,0:T(8,128)(2,1)S(1)}, u32[]{:S(2)}, u32[]{:S(2)}) collective-permute-start(bf16[1024,128]{1,0:T(8,128)(2,1)S(1)} %select_bitcast_fusion.5), channel_id=1, source_target_pairs={{0,2},{1,3},{2,0},{3,1},{4,6},{5,7},{6,4},{7,5},{8,10},{9,11},{10,... | collective-permute-start | bytes 786440 | tf_op jit(solution)/shard_map/ppermute | solution.py:421
  1210.1 61.9 %collective-permute-start.103 = (bf16[2048,128]{1,0:T(8,128)(2,1)}, bf16[2048,128]{1,0:T(8,128)(2,1)}, u32[]{:S(2)}, u32[]{:S(2)}) collective-permute-start(bf16[2048,128]{1,0:T(8,128)(2,1)} %get-tuple-element.140), channel_id=1, source_target_pairs={{0,1},{1,0},{2,3},{3,2},{4,5},{5,4},{6,7},{7,6},{8,9},{9,8},{10,11... | collective-permute-start | bytes 1572872 | tf_op jit(solution)/shard_map/ppermute | solution.py:421
  1210.1 61.9 %collective-permute-start.105 = (bf16[2048,128]{1,0:T(8,128)(2,1)}, bf16[2048,128]{1,0:T(8,128)(2,1)}, u32[]{:S(2)}, u32[]{:S(2)}) collective-permute-start(bf16[2048,128]{1,0:T(8,128)(2,1)} %get-tuple-element.141), channel_id=1, source_target_pairs={{0,3},{1,2},{2,1},{3,0},{4,7},{5,6},{6,5},{7,4},{8,11},{9,10},{10,... | collective-permute-start | bytes 1572872 | tf_op jit(solution)/shard_map/ppermute | solution.py:421
  1214.5 65.0 %collective-permute-start.104 = (bf16[2048,128]{1,0:T(8,128)(2,1)}, bf16[2048,128]{1,0:T(8,128)(2,1)}, u32[]{:S(2)}, u32[]{:S(2)}) collective-permute-start(bf16[2048,128]{1,0:T(8,128)(2,1)} %get-tuple-element.142), channel_id=1, source_target_pairs={{0,2},{1,3},{2,0},{3,1},{4,6},{5,7},{6,4},{7,5},{8,10},{9,11},{10,... | collective-permute-start | bytes 1572872 | tf_op jit(solution)/shard_map/ppermute | solution.py:421
  (303 other events, 4264.5 us)

commit v2 on v0

--- a/solution.py
+++ b/solution.py
@@ -1,6 +1,10 @@
+import functools
+
 import jax
 import jax.numpy as jnp
 from jax import lax
+from jax.experimental import pallas as pl
+from jax.experimental.pallas import tpu as pltpu
 from jax.sharding import PartitionSpec as P
 
 HEADS = 16
@@ -402,6 +406,855 @@
     )
 
 
+Z0, Z1, CORE, XBIT, YBIT = 1, 2, 4, 8, 16
+AXES = ("dp", "tensor")
+NEG = -1e30
+BF = jnp.bfloat16
+F32 = jnp.float32
+VMEM_LIMIT = 56 * 1024 * 1024
+
+
+def mesh_is_paired(mesh):
+    return dict(mesh.shape) == {"dp": 8, "tensor": 4}
+
+
+def swap(values, mask):
+    return lax.ppermute(values, AXES, [(i, i ^ mask) for i in range(32)])
+
+
+def redeal(values):
+    def target(i):
+        core, z1 = (i >> 2) & 1, (i >> 1) & 1
+        return (i & ~6) | (z1 << 2) | (core << 1)
+
+    return lax.ppermute(values, AXES, [(i, target(i)) for i in range(32)])
+
+
+def turn_blocks(values, own):
+    width = values.shape[1] // 8
+    return jnp.concatenate(
+        [lax.dynamic_slice_in_dim(values, (own ^ i) * width, width, 1) for i in range(8)], axis=1
+    )
+
+
+def after(values, *others):
+    return lax.optimization_barrier((values, *others))[0]
+
+
+def dot_nt(a, b):
+    return lax.dot_general(a, b, (((1,), (1,)), ((), ())), preferred_element_type=F32)
+
+
+def dot_nn(a, b):
+    return lax.dot_general(a, b, (((1,), (0,)), ((), ())), preferred_element_type=F32)
+
+
+def head_mask(shape, head):
+    lane = lax.broadcasted_iota(jnp.int32, shape, 1)
+    return (lane < HD) if head == 0 else (lane >= HD)
+
+
+def diagonal_bias(rows, columns, first_row, first_column, start):
+    key = first_row + lax.broadcasted_iota(jnp.int32, (rows, 1), 0)
+    query = first_column + lax.broadcasted_iota(jnp.int32, (1, columns), 1)
+    key_in = (key >= start) & (key < start + PIECE)
+    query_in = (query >= start) & (query < start + PIECE)
+    allowed = (key <= query) | (key_in & query_in)
+    reach = (jnp.minimum(key, 2 * query - key) - first_column).astype(F32)
+    return jnp.where(allowed, reach, NEG)
+
+
+def ramp(rows, first_row, first_column):
+    return (first_row - first_column + lax.broadcasted_iota(jnp.int32, (rows, 1), 0)).astype(F32)
+
+
+def attend_kernel(block, rest_bit, slope_ref, start_ref, me_ref, *rest):
+    triple_refs, rest = rest[:12], rest[12:]
+    near_ref, away_ref, exact_ref, lse_ref, q_ref, k_ref, v_ref, vt_ref, acc_ref, max_ref, bias_ref, tail_ref = rest
+    pair = pl.program_id(0)
+    turn = pl.program_id(1)
+    me = me_ref[0]
+    step = (2 * turn + rest_bit) ^ me
+    length = k_ref.shape[0]
+    first = step * block
+
+    def at(index):
+        return pl.multiple_of((index ^ me) * block, block)
+
+    start = start_ref[first // (length // start_ref.shape[0])]
+
+    @pl.when(turn == 0)
+    def _():
+        for index in range(4):
+            here = slice(index * block, (index + 1) * block)
+            q_ref[here, :] = triple_refs[3 * index][...] * jnp.asarray(HD ** -0.5, BF)
+            k_ref[here, :] = triple_refs[3 * index + 1][...]
+            v_ref[here, :] = triple_refs[3 * index + 2][...]
+        for head in range(2):
+            mixed = jnp.where(head_mask((length, 2 * HD), head), v_ref[...], jnp.ones((), BF))
+            vt_ref[head] = mixed.T
+
+    bias_ref[...] = diagonal_bias(block, block, first, first, start)
+    q_block = q_ref[pl.ds(at(step), block), :]
+    heads = [jnp.where(head_mask(q_block.shape, head), q_block, jnp.zeros((), BF)) for head in range(2)]
+    slopes = [slope_ref[2 * pair + head] for head in range(2)]
+    acc_ref[...] = jnp.zeros_like(acc_ref)
+    max_ref[...] = jnp.full_like(max_ref, NEG)
+
+    def absorb(head, scores, vt):
+        old = max_ref[head]
+        new = jnp.maximum(old, jnp.max(scores, axis=0, keepdims=True))
+        weights = jnp.exp(scores - new).astype(BF)
+        acc_ref[head] = acc_ref[head] * jnp.exp(old - new) + dot_nn(vt, weights)
+        max_ref[head] = new
+
+    def full(index, carry):
+        place = at(index)
+        keys = k_ref[pl.ds(place, block), :]
+        slant = ramp(block, index * block, first)
+        for head in range(2):
+            absorb(head, dot_nt(keys, heads[head]) + slopes[head] * slant, vt_ref[head, :, pl.ds(place, block)])
+        return carry
+
+    place = at(step)
+    for head in range(2):
+        absorb(
+            head,
+            dot_nt(k_ref[pl.ds(place, block), :], heads[head]) + slopes[head] * bias_ref[...],
+            vt_ref[head, :, pl.ds(place, block)],
+        )
+    lax.fori_loop(0, step, full, 0)
+    edge = first + block
+
+    @pl.when((start < edge) & (start + PIECE > edge))
+    def _():
+        after = at(step + 1)
+        tail_ref[...] = diagonal_bias(PIECE, block, edge, first, start)
+        for head in range(2):
+            absorb(
+                head,
+                dot_nt(k_ref[pl.ds(after, PIECE), :], heads[head]) + slopes[head] * tail_ref[...],
+                vt_ref[head, :, pl.ds(after, PIECE)],
+            )
+
+    outs = []
+    for head in range(2):
+        acc = acc_ref[head]
+        total = acc[HD:HD + 1] if head == 0 else acc[0:1]
+        outs.append((acc * (1.0 / total))[head * HD:(head + 1) * HD])
+        lse_ref[0, head:head + 1, :] = max_ref[head] + jnp.log(total)
+    mixed = jnp.concatenate(outs, axis=0)
+    exact_ref[...] = mixed
+    final = mixed.T.astype(BF)
+
+    @pl.when(turn == 0)
+    def _():
+        near_ref[...] = final
+
+    @pl.when(turn == 1)
+    def _():
+        away_ref[...] = final
+
+
+def triple_specs(block, pairs):
+    specs = []
+    for index in range(4):
+        for part in range(3):
+            specs.append(pl.BlockSpec((block, 2 * HD), functools.partial(lambda part, p, i: (0, part * pairs + p), part)))
+    return specs
+
+
+def attend(blocks, rest_bit, slopes, starts, me):
+    block, width = blocks[0].shape[0], blocks[0].shape[1] // 3
+    pairs = width // (2 * HD)
+    length = 4 * block
+    smem = pl.BlockSpec(memory_space=pltpu.SMEM)
+    return pl.pallas_call(
+        functools.partial(attend_kernel, block, rest_bit),
+        grid=(pairs, 2),
+        in_specs=[smem, smem, smem] + triple_specs(block, pairs),
+        out_specs=[
+            pl.BlockSpec((block, 2 * HD), lambda p, i: (0, p)),
+            pl.BlockSpec((block, 2 * HD), lambda p, i: (0, p)),
+            pl.BlockSpec((2 * HD, block), lambda p, i: (p, i)),
+            pl.BlockSpec((1, 8, block), lambda p, i: (p, 0, i)),
+        ],
+        out_shape=[
+            jax.ShapeDtypeStruct((block, width), BF),
+            jax.ShapeDtypeStruct((block, width), BF),
+            jax.ShapeDtypeStruct((width, 2 * block), F32),
+            jax.ShapeDtypeStruct((pairs, 8, 2 * block), F32),
+        ],
+        scratch_shapes=[
+            pltpu.VMEM((length, 2 * HD), BF),
+            pltpu.VMEM((length, 2 * HD), BF),
+            pltpu.VMEM((length, 2 * HD), BF),
+            pltpu.VMEM((2, 2 * HD, length), BF),
+            pltpu.VMEM((2, 2 * HD, block), F32),
+            pltpu.VMEM((2, 1, block), F32),
+            pltpu.VMEM((block, block), F32),
+            pltpu.VMEM((PIECE, block), F32),
+        ],
+        compiler_params=pltpu.CompilerParams(vmem_limit_bytes=VMEM_LIMIT),
+        cost_estimate=pl.CostEstimate(flops=10 * length * length * width // 4, bytes_accessed=16 * block * width, transcendentals=0),
+        name="attend",
+    )(slopes, starts, me, *[b for b in blocks for _ in range(3)])
+
+
+def pull_kernel(block, slope_ref, start_ref, me_ref, *rest):
+    triple_refs, grad_refs, rest = rest[:12], rest[12:16], rest[16:]
+    exact_refs, lse_refs, rest = rest[0:2], rest[2:4], rest[4:]
+    mine_ref, away_ref, q_ref, k_ref, v_ref, g_ref, kt_ref, dk_acc, dv_acc, dqt_ref, bias_ref, tail_ref = rest
+    pair = pl.program_id(0)
+    turn = pl.program_id(1)
+    me = me_ref[0]
+    step = turn ^ me
+    length = k_ref.shape[0]
+    first = step * block
+    half, bit = turn // 2, turn % 2
+
+    def at(index):
+        return pl.multiple_of((index ^ me) * block, block)
+
+    start = start_ref[first // (length // start_ref.shape[0])]
+
+    @pl.when(turn == 0)
+    def _():
+        for index in range(4):
+            here = slice(index * block, (index + 1) * block)
+            q_ref[here, :] = triple_refs[3 * index][...] * jnp.asarray(HD ** -0.5, BF)
+            k_ref[here, :] = triple_refs[3 * index + 1][...]
+            v_ref[here, :] = triple_refs[3 * index + 2][...]
+            g_ref[here, :] = grad_refs[index][...]
+        kt_ref[...] = k_ref[...].T
+        dk_acc[...] = jnp.zeros_like(dk_acc)
+        dv_acc[...] = jnp.zeros_like(dv_acc)
+
+    bias_ref[...] = diagonal_bias(block, block, first, first, start)
+    dqt_ref[...] = jnp.zeros_like(dqt_ref)
+    zero = jnp.zeros((), BF)
+    q_block = q_ref[pl.ds(at(step), block), :]
+    g_block = g_ref[pl.ds(at(step), block), :]
+    masks = [head_mask(q_block.shape, head) for head in range(2)]
+    q_heads = [jnp.where(mask, q_block, zero) for mask in masks]
+    g_heads = [jnp.where(mask, g_block, zero) for mask in masks]
+    slopes = [slope_ref[2 * pair + head] for head in range(2)]
+    lanes = pl.ds(pl.multiple_of(half * block, block), block)
+    exact = jnp.where(bit == 0, exact_refs[0][:, lanes], exact_refs[1][:, lanes])
+    log_total = jnp.where(bit == 0, lse_refs[0][0, :, lanes], lse_refs[1][0, :, lanes])
+    product = g_block.astype(F32).T * exact
+    deltas = [jnp.sum(product[head * HD:(head + 1) * HD], axis=0, keepdims=True) for head in range(2)]
+
+    def absorb(place, rows, bias_of):
+        keys = k_ref[pl.ds(place, rows), :]
+        values = v_ref[pl.ds(place, rows), :]
+        dk = dk_acc[pl.ds(place, rows), :]
+        dv = dv_acc[pl.ds(place, rows), :]
+        for head in range(2):
+            scores = dot_nt(keys, q_heads[head]) + slopes[head] * bias_of
+            weights = jnp.exp(scores - log_total[head:head + 1, :])
+            dv = dv + dot_nn(weights.astype(BF), g_heads[head])
+            grad_p = dot_nt(values, g_heads[head])
+            grad_s = (weights * (grad_p - deltas[head])).astype(BF)
+            dk = dk + dot_nn(grad_s, q_heads[head])
+            dqt_ref[head * HD:(head + 1) * HD, :] += dot_nn(kt_ref[head * HD:(head + 1) * HD, pl.ds(place, rows)], grad_s)
+        dk_acc[pl.ds(place, rows), :] = dk
+        dv_acc[pl.ds(place, rows), :] = dv
+
+    absorb(at(step), block, bias_ref[...])
+
+    def full(index, carry):
+        absorb(at(index), block, ramp(block, index * block, first))
+        return carry
+
+    lax.fori_loop(0, step, full, 0)
+    edge = first + block
+
+    @pl.when((start < edge) & (start + PIECE > edge))
+    def _():
+        tail_ref[...] = diagonal_bias(PIECE, block, edge, first, start)
+        absorb(at(step + 1), PIECE, tail_ref[...])
+
+    grad_q = (dqt_ref[...].T * (HD ** -0.5)).astype(BF)
+    here = pl.ds(pl.multiple_of(bit * block, block), block)
+
+    @pl.when(half == 0)
+    def _():
+        mine_ref[0, here, :] = grad_q
+
+    @pl.when(half == 1)
+    def _():
+        away_ref[0, here, :] = grad_q
+
+    @pl.when(turn == 3)
+    def _():
+        for part, ref in ((1, dk_acc), (2, dv_acc)):
+            mine_ref[part] = ref[:2 * block].astype(BF)
+            away_ref[part] = ref[2 * block:].astype(BF)
+
+
+def attend_pull(blocks, grads, exacts, log_totals, slopes, starts, me):
+    block, width = blocks[0].shape[0], blocks[0].shape[1] // 3
+    pairs = width // (2 * HD)
+    length = 4 * block
+    smem = pl.BlockSpec(memory_space=pltpu.SMEM)
+    rows = pl.BlockSpec((block, 2 * HD), lambda p, i: (0, p))
+    wide = pl.BlockSpec((2 * HD, 2 * block), lambda p, i: (p, 0))
+    sums = pl.BlockSpec((1, 8, 2 * block), lambda p, i: (p, 0, 0))
+    out = pl.BlockSpec((3, 2 * block, 2 * HD), lambda p, i: (0, 0, p))
+    return pl.pallas_call(
+        functools.partial(pull_kernel, block),
+        grid=(pairs, 4),
+        in_specs=[smem, smem, smem] + triple_specs(block, pairs) + [rows] * 4 + [wide] * 2 + [sums] * 2,
+        out_specs=[out, out],
+        out_shape=[jax.ShapeDtypeStruct((3, 2 * block, width), BF)] * 2,
+        scratch_shapes=[
+            pltpu.VMEM((length, 2 * HD), BF),
+            pltpu.VMEM((length, 2 * HD), BF),
+            pltpu.VMEM((length, 2 * HD), BF),
+            pltpu.VMEM((length, 2 * HD), BF),
+            pltpu.VMEM((2 * HD, length), BF),
+            pltpu.VMEM((length, 2 * HD), F32),
+            pltpu.VMEM((length, 2 * HD), F32),
+            pltpu.VMEM((2 * HD, block), F32),
+            pltpu.VMEM((block, block), F32),
+            pltpu.VMEM((PIECE, block), F32),
+        ],
+        compiler_params=pltpu.CompilerParams(vmem_limit_bytes=VMEM_LIMIT),
+        cost_estimate=pl.CostEstimate(flops=25 * length * length * width // 2, bytes_accessed=30 * block * width, transcendentals=0),
+        name="attend_pull",
+    )(slopes, starts, me, *[b for b in blocks for _ in range(3)], *grads, *exacts, *log_totals)
+
+
+GELU_A = 0.7978845608028654
+GELU_B = 0.044715
+
+
+def normalize(values):
+    centred = values - jnp.mean(values, axis=-1, keepdims=True)
+    spread = lax.rsqrt(jnp.mean(centred * centred, axis=-1, keepdims=True) + NORM_EPS)
+    return centred * spread, spread
+
+
+def norm_pull(values, gain, grad):
+    unit, spread = normalize(values)
+    grad_unit = grad * gain
+    inner = grad_unit - jnp.mean(grad_unit, axis=-1, keepdims=True)
+    inner = inner - unit * jnp.mean(grad_unit * unit, axis=-1, keepdims=True)
+    return spread * inner, jnp.sum(grad * unit, axis=0, keepdims=True), jnp.sum(grad, axis=0, keepdims=True)
+
+
+def joined(refs, first, last):
+    return jnp.concatenate([ref[0, :, first:last] for ref in refs], axis=0)
+
+
+def mlp_kernel(normed_ref, mid_ref, vector_ref, bias_ref, *rest):
+    weight_refs, (hidden_ref, active_ref, out_ref, next_ref, acc_ref) = rest[:8], rest[8:]
+    tile = hidden_ref.shape[1]
+    step = pl.program_id(0)
+    hidden = dot_nn(normed_ref[...], joined(weight_refs, 0, tile)) + bias_ref[...]
+    inner = jnp.tanh(GELU_A * (hidden + GELU_B * hidden * hidden * hidden))
+    active = (0.5 * hidden * (1.0 + inner)).astype(BF)
+    hidden_ref[...] = hidden.astype(BF)
+    active_ref[...] = active
+    term = dot_nt(active, joined(weight_refs, tile, 2 * tile))
+
+    @pl.when(step == 0)
+    def _():
+        acc_ref[...] = term
+
+    @pl.when(step > 0)
+    def _():
+        acc_ref[...] += term
+
+    @pl.when(step == pl.num_programs(0) - 1)
+    def _():
+        out = mid_ref[...] + (acc_ref[...] + vector_ref[5:6])
+        out_ref[...] = out
+        next_ref[...] = (normalize(out)[0] * vector_ref[6:7] + vector_ref[7:8]).astype(BF)
+
+
+def mlp_forward(normed, mid, vectors, bias, bundles):
+    rows, features = normed.shape
+    units = bias.shape[1]
+    tile = 512
+    whole = pl.BlockSpec((rows, features), lambda f: (0, 0))
+    tiles = pl.BlockSpec((rows, tile), lambda f: (0, f))
+    weight_spec = pl.BlockSpec((1, 128, 2 * tile), lambda f: (f // 2, 0, f % 2))
+    return pl.pallas_call(
+        mlp_kernel,
+        grid=(units // tile,),
+        in_specs=[whole, whole, pl.BlockSpec((8, features), lambda f: (0, 0)), pl.BlockSpec((1, tile), lambda f: (0, f))]
+        + [weight_spec] * 8,
+        out_specs=[tiles, tiles, whole, whole],
+        out_shape=[
+            jax.ShapeDtypeStruct((rows, units), BF),
+            jax.ShapeDtypeStruct((rows, units), BF),
+            jax.ShapeDtypeStruct((rows, features), F32),
+            jax.ShapeDtypeStruct((rows, features), BF),
+        ],
+        scratch_shapes=[pltpu.VMEM((rows, features), F32)],
+        compiler_params=pltpu.CompilerParams(vmem_limit_bytes=VMEM_LIMIT),
+        cost_estimate=pl.CostEstimate(flops=4 * rows * features * units, bytes_accessed=6 * features * units, transcendentals=0),
+        name="mlp_forward",
+    )(normed, mid, vectors, bias, *bundles)
+
+
+def mlp_pull_kernel(grad_ref, mid_ref, vector_ref, hidden_ref, *rest):
+    weight_refs = rest[:8]
+    grad_hidden_ref, grad_bias_ref, grad_mid_ref, grad_low_ref, sums_ref, acc_ref, low_ref = rest[8:]
+    tile = hidden_ref.shape[1]
+    step = pl.program_id(0)
+
+    @pl.when(step == 0)
+    def _():
+        low_ref[...] = grad_ref[...].astype(BF)
+
+    hidden = hidden_ref[...].astype(F32)
+    squared = hidden * hidden
+    inner = jnp.tanh(GELU_A * hidden * (1.0 + GELU_B * squared))
+    slope = 0.5 * (1.0 + inner) + 0.5 * hidden * (1.0 - inner * inner) * (GELU_A * (1.0 + 3.0 * GELU_B * squared))
+    grad_hidden = dot_nn(low_ref[...], joined(weight_refs, tile, 2 * tile)) * slope
+    grad_bias_ref[...] = jnp.sum(grad_hidden, axis=0, keepdims=True)
+    grad_hidden = grad_hidden.astype(BF)
+    grad_hidden_ref[...] = grad_hidden
+    term = dot_nt(grad_hidden, joined(weight_refs, 0, tile))
+
+    @pl.when(step == 0)
+    def _():
+        acc_ref[...] = term
+
+    @pl.when(step > 0)
+    def _():
+        acc_ref[...] += term
+
+    @pl.when(step == pl.num_programs(0) - 1)
+    def _():
+        grad = grad_ref[...]
+        grad_norm, grad_gain, grad_shift = norm_pull(mid_ref[...], vector_ref[3:4], acc_ref[...])
+        grad_mid = grad + grad_norm
+        grad_mid_ref[...] = grad_mid
+        grad_low_ref[...] = grad_mid.astype(BF)
+        sums_ref[...] = jnp.concatenate(
+            [
+                jnp.sum(grad_mid, axis=0, keepdims=True),
+                grad_gain,
+                grad_shift,
+                jnp.sum(grad, axis=0, keepdims=True),
+                jnp.zeros((4, grad.shape[1]), F32),
+            ],
+            axis=0,
+        )
+
+
+def mlp_backward(grad, mid, vectors, hidden, bundles):
+    rows, features = grad.shape
+    units = hidden.shape[1]
+    tile = 512
+    whole = pl.BlockSpec((rows, features), lambda f: (0, 0))
+    tiles = pl.BlockSpec((rows, tile), lambda f: (0, f))
+    eight = pl.BlockSpec((8, features), lambda f: (0, 0))
+    weight_spec = pl.BlockSpec((1, 128, 2 * tile), lambda f: (f // 2, 0, f % 2))
+    return pl.pallas_call(
+        mlp_pull_kernel,
+        grid=(units // tile,),
+        in_specs=[whole, whole, eight, tiles] + [weight_spec] * 8,
+        out_specs=[tiles, pl.BlockSpec((1, tile), lambda f: (0, f)), whole, whole, eight],
+        out_shape=[
+            jax.ShapeDtypeStruct((rows, units), BF),
+            jax.ShapeDtypeStruct((1, units), F32),
+            jax.ShapeDtypeStruct((rows, features), F32),
+            jax.ShapeDtypeStruct((rows, features), BF),
+            jax.ShapeDtypeStruct((8, features), F32),
+        ],
+        scratch_shapes=[pltpu.VMEM((rows, features), F32), pltpu.VMEM((rows, features), BF)],
+        compiler_params=pltpu.CompilerParams(vmem_limit_bytes=VMEM_LIMIT),
+        cost_estimate=pl.CostEstimate(flops=4 * rows * features * units, bytes_accessed=6 * features * units, transcendentals=0),
+        name="mlp_backward",
+    )(grad, mid, vectors, hidden, *bundles)
+
+
+def mlp_weights_kernel(grad_ref, normed_ref, active_ref, grad_hidden_ref, *rest):
+    out_refs, (grad_t_ref, normed_t_ref) = rest[:8], rest[8:]
+    tile = active_ref.shape[1]
+
+    @pl.when(pl.program_id(0) == 0)
+    def _():
+        grad_t_ref[...] = grad_ref[...].astype(BF).T
+        normed_t_ref[...] = normed_ref[...].T
+
+    grad_expand = dot_nn(normed_t_ref[...], grad_hidden_ref[...]).astype(BF)
+    grad_reduce = dot_nn(grad_t_ref[...], active_ref[...]).astype(BF)
+    for index, out_ref in enumerate(out_refs):
+        here = slice(index * 128, (index + 1) * 128)
+        out_ref[0, :, :tile] = grad_expand[here]
+        out_ref[0, :, tile:] = grad_reduce[here]
+
+
+def mlp_weight_grads(grad, normed, active, grad_hidden):
+    rows, features = grad.shape
+    units = active.shape[1]
+    tile = 512
+    whole = pl.BlockSpec((rows, features), lambda f: (0, 0))
+    tiles = pl.BlockSpec((rows, tile), lambda f: (0, f))
+    weight_spec = pl.BlockSpec((1, 128, 2 * tile), lambda f: (f // 2, 0, f % 2))
+    return pl.pallas_call(
+        mlp_weights_kernel,
+        grid=(units // tile,),
+        in_specs=[whole, whole, tiles, tiles],
+        out_specs=[weight_spec] * 8,
+        out_shape=[jax.ShapeDtypeStruct((units // 1024, 128, 2048), BF)] * 8,
+        scratch_shapes=[pltpu.VMEM((features, rows), BF), pltpu.VMEM((features, rows), BF)],
+        compiler_params=pltpu.CompilerParams(vmem_limit_bytes=VMEM_LIMIT),
+        cost_estimate=pl.CostEstimate(flops=4 * rows * features * units, bytes_accessed=8 * features * units, transcendentals=0),
+        name="mlp_weight_grads",
+    )(grad, normed, active, grad_hidden)
+
+
+def head_columns(refs, quarter, first, last):
+    return jnp.concatenate(
+        [ref[quarter if index % 2 == 0 else 1 - quarter, :, first:last] for index, ref in enumerate(refs)], axis=0
+    )
+
+
+def in_vmem(count):
+    return [pl.BlockSpec(memory_space=pltpu.VMEM)] * count
+
+
+def call_once(kernel, name, outs, args, flops):
+    moved = sum(a.size * a.dtype.itemsize for a in args) + sum(a.size * a.dtype.itemsize for a in outs)
+    return pl.pallas_call(
+        kernel,
+        in_specs=in_vmem(len(args)),
+        out_specs=in_vmem(len(outs)),
+        out_shape=outs,
+        compiler_params=pltpu.CompilerParams(vmem_limit_bytes=VMEM_LIMIT),
+        cost_estimate=pl.CostEstimate(flops=flops, bytes_accessed=moved, transcendentals=0),
+        name=name,
+    )(*args)
+
+
+def project_kernel(rows_ref, bias_ref, *rest):
+    weight_refs, out_refs = rest[:8], rest[8:]
+    rows = rows_ref[...]
+    for quarter in (1, 0):
+        out = dot_nn(rows, head_columns(weight_refs, quarter, 0, 768)) + bias_ref[quarter:quarter + 1]
+        out_refs[quarter][...] = out.astype(BF)
+
+
+def project(rows, bias, pieces):
+    out = jax.ShapeDtypeStruct((rows.shape[0], 768), BF)
+    return call_once(project_kernel, "project", [out, out], [rows, bias, *pieces], 2 * rows.shape[0] * 1024 * 1536)
+
+
+def mix_term(mixed_refs, weight_refs):
+    rows = jnp.concatenate([ref[...] for ref in mixed_refs], axis=1)
+    weight = jnp.concatenate([head_columns(weight_refs, quarter, 768, 1024) for quarter in range(2)], axis=1)
+    return dot_nt(rows, weight)
+
+
+def mix_far_kernel(mine_ref, other_ref, *rest):
+    rest[8][...] = mix_term((mine_ref, other_ref), rest[:8]).astype(BF)
+
+
+def mix_far(mine, other, pieces):
+    out = jax.ShapeDtypeStruct((mine.shape[0], 1024), BF)
+    return call_once(mix_far_kernel, "mix_far", [out], [mine, other, *pieces], 2 * mine.shape[0] * 512 * 1024)[0]
+
+
+def mix_near_kernel(mine_ref, other_ref, far_ref, resid_ref, vector_ref, *rest):
+    weight_refs, (mid_ref, normed_ref) = rest[:8], rest[8:]
+    term = mix_term((mine_ref, other_ref), weight_refs)
+    mid = resid_ref[...] + (term + far_ref[...].astype(F32) + vector_ref[2:3])
+    mid_ref[...] = mid
+    normed_ref[...] = (normalize(mid)[0] * vector_ref[3:4] + vector_ref[4:5]).astype(BF)
+
+
+def mix_near(mine, other, far, resid, vectors, pieces):
+    outs = [jax.ShapeDtypeStruct(resid.shape, F32), jax.ShapeDtypeStruct(resid.shape, BF)]
+    return call_once(mix_near_kernel, "mix_near", outs, [mine, other, far, resid, vectors, *pieces], 2 * mine.shape[0] * 512 * 1024)
+
+
+def unmix_kernel(grad_ref, *rest):
+    weight_refs, out_refs = rest[:8], rest[8:]
+    grad = grad_ref[...]
+    for quarter in (1, 0):
+        out_refs[quarter][...] = dot_nn(grad, head_columns(weight_refs, quarter, 768, 1024)).astype(BF)
+
+
+def unmix(grad, pieces):
+    out = jax.ShapeDtypeStruct((grad.shape[0], 256), BF)
+    return call_once(unmix_kernel, "unmix", [out, out], [grad, *pieces], 2 * grad.shape[0] * 512 * 1024)
+
+
+def unproject_term(grad_refs, weight_refs, first):
+    rows = jnp.concatenate([ref[part, first:first + 512] for ref in grad_refs for part in range(3)], axis=1)
+    weight = jnp.concatenate([head_columns(weight_refs, quarter, 0, 768) for quarter in range(2)], axis=1)
+    return dot_nt(rows, weight)
+
+
+def unproject_far_kernel(mine_ref, other_ref, *rest):
+    rest[8][...] = unproject_term((mine_ref, other_ref), rest[:8], 512).astype(BF)
+
+
+def unproject_far(mine, other, pieces):
+    out = jax.ShapeDtypeStruct((512, 1024), BF)
+    return call_once(unproject_far_kernel, "unproject_far", [out], [mine, other, *pieces], 2 * 512 * 1536 * 1024)[0]
+
+
+def unproject_near_kernel(mine_ref, other_ref, far_ref, resid_ref, grad_mid_ref, vector_ref, *rest):
+    weight_refs, (grad_ref, low_ref, sums_ref) = rest[:8], rest[8:]
+    term = unproject_term((mine_ref, other_ref), weight_refs, 0) + far_ref[...].astype(F32)
+    grad_norm, grad_gain, grad_shift = norm_pull(resid_ref[...], vector_ref[0:1], term)
+    grad = grad_mid_ref[...] + grad_norm
+    grad_ref[...] = grad
+    low_ref[...] = grad.astype(BF)
+    sums_ref[...] = jnp.concatenate([grad_gain, grad_shift, jnp.zeros((6, grad.shape[1]), F32)], axis=0)
+
+
+def unproject_near(mine, other, far, resid, grad_mid, vectors, pieces):
+    outs = [
+        jax.ShapeDtypeStruct(resid.shape, F32),
+        jax.ShapeDtypeStruct(resid.shape, BF),
+        jax.ShapeDtypeStruct((8, resid.shape[1]), F32),
+    ]
+    args = [mine, other, far, resid, grad_mid, vectors, *pieces]
+    return call_once(unproject_near_kernel, "unproject_near", outs, args, 2 * 512 * 1536 * 1024)
+
+
+def head_grads_kernel(near_ref, far_ref, grad_near_ref, grad_far_ref, mine_ref, other_ref, *rest):
+    mixed_refs, out_refs, bias_ref = (rest[0:2], rest[2:4]), rest[4:12], rest[12]
+    rows_t = jnp.concatenate([near_ref[...], far_ref[...]], axis=0).T
+    grad_t = jnp.concatenate([grad_near_ref[...], grad_far_ref[...]], axis=0).T
+    for quarter, ref in enumerate((mine_ref, other_ref)):
+        for part in range(4):
+            if part < 3:
+                term = dot_nn(rows_t, ref[part])
+            else:
+                term = dot_nn(grad_t, jnp.concatenate([m[...] for m in mixed_refs[quarter]], axis=0))
+            term = term.astype(BF)
+            for index, out_ref in enumerate(out_refs):
+                place = quarter if index % 2 == 0 else 1 - quarter
+                out_ref[place, :, part * 256:(part + 1) * 256] = term[index * 128:(index + 1) * 128]
+        for row, part in ((0, 0), (1, 2)):
+            total = jnp.sum(ref[part].astype(F32), axis=0, keepdims=True)
+            bias_ref[2 * quarter + row:2 * quarter + row + 1, :] = total
+    bias_ref[4:8, :] = jnp.zeros((4, 256), F32)
+
+
+def head_grads(near, far, grad_near, grad_far, mine, other, mixed_mine, mixed_other):
+    outs = [jax.ShapeDtypeStruct((2, 128, 1024), BF)] * 8 + [jax.ShapeDtypeStruct((8, 256), F32)]
+    args = [near, far, grad_near, grad_far, mine, other, *mixed_mine, *mixed_other]
+    return call_once(head_grads_kernel, "head_grads", outs, args, 2 * 1024 * 1024 * 2048)
+
+
+def gather_plane(own):
+    half = own.shape[0] // 2
+    from_x = swap(own, XBIT)
+    from_y = swap(own, YBIT)
+    across = jnp.concatenate([swap(from_x[:half], YBIT), swap(from_y[half:], XBIT)], axis=0)
+    out = []
+    for quad in (own, from_x, from_y, across):
+        out += [quad, swap(quad, CORE)]
+    return out
+
+
+def scatter_plane(pieces):
+    own, to_x, to_y, across = [pieces[2 * i] + swap(pieces[2 * i + 1], CORE) for i in range(4)]
+    half = own.shape[0] // 2
+    first = own[:half] + swap(to_y[:half], YBIT) + swap(to_x[:half] + swap(across[:half], YBIT), XBIT)
+    second = own[half:] + swap(to_x[half:], XBIT) + swap(to_y[half:] + swap(across[half:], XBIT), YBIT)
+    return first, second
+
+
+def pack_heads(project, output):
+    return jnp.concatenate([project.transpose(1, 0, 2).reshape(128, 768), output.T], axis=1)
+
+
+def unpack_heads(values):
+    return values[:, :768].reshape(128, 3, 256).transpose(1, 0, 2), values[:, 768:].T
+
+
+def pack_units(expand, reduce):
+    parts = (expand.reshape(128, 2, 512), reduce.T.reshape(128, 2, 512))
+    return jnp.stack(parts, axis=2).reshape(128, 2048)
+
+
+def unpack_units(values):
+    shaped = values.reshape(128, 2, 2, 512)
+    return shaped[:, :, 0].reshape(128, 1024), shaped[:, :, 1].reshape(128, 1024).T
+
+
+def fetch_heads(piece, core):
+    far = swap(piece, Z1)
+    return gather_plane(jnp.stack([jnp.where(core == 0, piece, far), jnp.where(core == 0, far, piece)]))
+
+
+def fetch_units(piece):
+    own = jnp.stack([piece, swap(piece, 1), swap(piece, 2), swap(piece, 3)])
+    return own, gather_plane(own)
+
+
+def fetch_small(six, project_bias, expand_bias, own, place, core):
+    layers = six.shape[1]
+    wide = jnp.pad(project_bias, ((0, 0), (0, 0), (0, 96)))
+    piece = jnp.concatenate([six.transpose(1, 0, 2), wide, expand_bias[:, None, :], jnp.zeros((layers, 7, 128), BF)], axis=1)
+    every = lax.all_gather(piece, AXES, axis=0, tiled=False).reshape(8, 4, layers, 16, 128).astype(F32)
+    turned = every[jnp.arange(8) ^ own, 0]
+    native = every[:, place ^ jnp.arange(4)]
+    out = []
+    for layer in range(layers):
+        vectors = turned[:, layer, :6].transpose(1, 0, 2).reshape(6, 1024)
+        following = turned[:, min(layer + 1, layers - 1), :2].transpose(1, 0, 2).reshape(2, 1024)
+        pair = native[:, ::2, layer, 6:8, :32].transpose(1, 2, 0, 3).reshape(2, 2, 256)
+        pair = jnp.where(core == 0, pair, pair[::-1])
+        head_bias = jnp.concatenate([pair[:, 0], jnp.zeros((2, 256), F32), pair[:, 1]], axis=1)
+        unit_bias = native[:, :, layer, 8].transpose(1, 0, 2).reshape(1, 4096)
+        out.append((jnp.concatenate([vectors, following], axis=0), head_bias, unit_bias))
+    return out
+
+
+def sum_small(layers, own, core):
+    turn = jnp.arange(8) ^ own
+    rows = []
+    for first_sums, second_sums, unit_sums, head_sums in layers:
+        six = jnp.stack([first_sums[0], first_sums[1], second_sums[0], second_sums[1], second_sums[2], second_sums[3]])
+        heads = head_sums[:4].reshape(2, 2, 256)
+        heads = jnp.where(core == 0, heads, heads[::-1]).reshape(4, 8, 32)[:, turn]
+        heads = jnp.pad(heads, ((0, 0), (0, 0), (0, 96)))
+        rows += [six.reshape(6, 8, 128), unit_sums.reshape(4, 8, 128)[:, turn], heads]
+    rows = jnp.concatenate(rows, axis=0).transpose(1, 0, 2)
+    rows = rows.reshape(2, 2, 2, rows.shape[1], 128)
+    rows = rows[:, :, 0] + swap(rows[:, :, 1], CORE)
+    rows = rows[:, 0] + swap(rows[:, 1], XBIT)
+    rows = rows[0] + swap(rows[1], YBIT)
+    rows = rows.reshape(len(layers), 14, 128)
+
+    def part(offset):
+        return jnp.concatenate([rows[:, :6], rows[:, 6 + offset:7 + offset], rows[:, 12:14]], axis=1)
+
+    two = swap(part(2), 2)
+    base = jnp.concatenate([rows[:, :7], rows[:, 10:12]], axis=1)
+    whole = base[:, :7] + two[:, :7] + swap(part(1), 1)[:, :7] + swap(part(3), 3)[:, :7]
+    return whole[:, :6], whole[:, 6], base[:, 7:, :32] + two[:, 7:, :32]
+
+
+def reduce_heads(pieces, core):
+    first, second = (part[0].astype(F32) for part in scatter_plane(pieces))
+    near = jnp.where(core == 0, first, second)
+    away = jnp.where(core == 0, second, first)
+    return unpack_heads(near + swap(away.astype(BF), Z1).astype(F32))
+
+
+def reduce_units(pieces):
+    first, second = scatter_plane(pieces)
+    terms = [first[0], swap(first[1], 1), swap(second[0], 2), swap(second[1], 3)]
+    return unpack_units(sum(term.astype(F32) for term in terms))
+
+
+def fast_device(
+    layer_input,
+    first_gain,
+    first_shift,
+    project_weight,
+    project_bias,
+    output_weight,
+    output_bias,
+    second_gain,
+    second_shift,
+    expand_weight,
+    expand_bias,
+    reduce_weight,
+    reduce_bias,
+    picture_start,
+    cotangent,
+):
+    own = lax.axis_index("dp")
+    place = lax.axis_index("tensor")
+    core = own & 1
+    me = (2 * core + (place & 1)).astype(jnp.int32).reshape(1)
+    slopes = head_slopes((place ^ (2 * core)) * 4, 4)
+    starts = redeal(picture_start)[0]
+    six = jnp.stack([first_gain, first_shift, output_bias, second_gain, second_shift, reduce_bias])
+    small = fetch_small(six, project_bias, expand_bias, own, place, core)
+    head_piece = [pack_heads(project_weight[i], output_weight[i]) for i in range(LAYERS)]
+    unit_piece = [pack_units(expand_weight[i], reduce_weight[i]) for i in range(LAYERS)]
+    dealt = redeal(layer_input)
+    heads, units = [None] * LAYERS, [None] * LAYERS
+    heads[0] = fetch_heads(head_piece[0], core)
+    quad, units[0] = fetch_units(after(unit_piece[0], dealt))
+    resid = turn_blocks(dealt.astype(F32), own)
+    normed = layer_norm(resid, small[0][0][0], small[0][0][1]).astype(BF)
+    saved = []
+    for layer in range(LAYERS):
+        vectors, head_bias, unit_bias = small[layer]
+        pieces = heads[layer]
+        far = swap(normed, Z0)
+        if layer + 1 < LAYERS:
+            heads[layer + 1] = fetch_heads(after(head_piece[layer + 1], quad), core)
+            quad, units[layer + 1] = fetch_units(after(unit_piece[layer + 1], far))
+        near_mine, near_other = project(normed, head_bias, pieces)
+        got_near = swap(near_other, CORE)
+        far_mine, far_other = project(far, head_bias, pieces)
+        got_far = swap(far_other, CORE)
+        blocks = (near_mine, far_mine, got_near, got_far)
+        far_mixed, far_send, far_exact, far_log = attend(blocks, 1, slopes, starts, me)
+        far_got = swap(far_send, CORE)
+        far_term = swap(mix_far(far_mixed, far_got, pieces), Z0)
+        near_mixed, near_send, near_exact, near_log = attend(blocks, 0, slopes, starts, me)
+        near_got = swap(near_send, CORE)
+        mid, normed_two = mix_near(near_mixed, near_got, far_term, resid, vectors, pieces)
+        hidden, active, out, following = mlp_forward(normed_two, mid, vectors, unit_bias, units[layer])
+        saved.append((
+            resid, normed, far, blocks, (near_exact, far_exact), (near_log, far_log),
+            (near_mixed, far_mixed), (near_got, far_got), mid, normed_two, hidden, active,
+        ))
+        resid, normed = out, following
+        if layer == 0:
+            grad = turn_blocks(redeal(after(cotangent, far_term)).astype(F32), own)
+    layer_output = redeal(turn_blocks(resid.astype(BF), own))
+    sums, head_grad, unit_grad = [None] * LAYERS, [None] * LAYERS, [None] * LAYERS
+    for layer in reversed(range(LAYERS)):
+        vectors, pieces = small[layer][0], heads[layer]
+        (
+            resid, normed, far, blocks, exacts, logs, mixed, mixed_got, mid, normed_two, hidden, active,
+        ) = saved[layer]
+        grad_hidden, unit_sums, grad_mid, grad_low, second_sums = mlp_backward(grad, mid, vectors, hidden, units[layer])
+        grad_far = swap(grad_low, Z0)
+        unit_pieces = mlp_weight_grads(grad, normed_two, active, grad_hidden)
+        near_mine, near_other = unmix(grad_low, pieces)
+        got_near = swap(near_other, CORE)
+        far_mine, far_other = unmix(grad_far, pieces)
+        got_far = swap(far_other, CORE)
+        grads_mixed = (near_mine, far_mine, got_near, got_far)
+        mine, away = attend_pull(blocks, grads_mixed, exacts, logs, slopes, starts, me)
+        other = swap(away, CORE)
+        far_term = swap(unproject_far(mine, other, pieces), Z0)
+        *head_pieces, head_sums = head_grads(normed, far, grad_low, grad_far, mine, other, mixed, mixed_got)
+        grad, grad_low, first_sums = unproject_near(mine, other, far_term, resid, grad_mid, vectors, pieces)
+        sums[layer] = (first_sums, second_sums, unit_sums, head_sums)
+        head_grad[layer] = reduce_heads(head_pieces, core)
+        unit_grad[layer] = reduce_units(unit_pieces)
+    input_grad = redeal(turn_blocks(grad_low, own))
+    six, unit_sum, head_sum = sum_small(sums, own, core)
+    return (
+        layer_output,
+        input_grad,
+        six[:, 0],
+        six[:, 1],
+        jnp.stack([g[0] for g in head_grad]),
+        head_sum,
+        jnp.stack([g[1] for g in head_grad]),
+        six[:, 2],
+        six[:, 3],
+        six[:, 4],
+        jnp.stack([g[0] for g in unit_grad]),
+        unit_sum,
+        jnp.stack([g[1] for g in unit_grad]),
+        six[:, 5],
+    )
+
+
 def solution(mesh):
     placed = (
         P(("dp", "tensor"), None),
@@ -421,7 +1274,7 @@
         P(("dp", "tensor"), None),
     )
     return jax.shard_map(
-        on_device,
+        fast_device if mesh_is_paired(mesh) else on_device,
         mesh=mesh,
         in_specs=placed,
         out_specs=(

time: 2600 us -> 1140 us (0.44)
  waiting for transfers between devices: 1320 us -> 310 us
  matrix products: 822 us -> 0 us
  Pallas kernels: 0 us -> 370 us
  starting transfers between devices: 2.16 us -> 171 us
  other arithmetic: 150 us -> 72.5 us
  local copies, waits for them, and re-layouts: 147 us -> 108 us
  loops' own time: 28.7 us -> 0 us
    dot_general x80 -> x0, matrix products: 822 us -> none  [the longest x8 191 us: one_block(): jnp.einsum('hqk,qhe->khe', score_grad, query_block, preferred_element_typ...]
    all_gather x14 -> x0, waiting for transfers between devices: 639 us -> none  [the longest x4 305 us: gather_rows(): return lax.all_gather(values, 'tensor', axis=0, tiled=True)]
    reduce_scatter x10 -> x0, waiting for transfers between devices: 578 us -> none  [the longest x4 291 us: scatter_rows(): lax.psum_scatter(partial_term(jnp.int32(0), rows_here * lax.axis_size('te...]
    pallas_call x0 -> x30, Pallas kernels: none -> 370 us  [the longest x18 106 us: call_once(): pl.pallas_call(kernel, in_specs=in_vmem(len(args)), out_specs=in_vmem(len...]
    ppermute x0 -> x121, waiting for transfers between devices: none -> 310 us  [the longest x116 310 us: swap(): return lax.ppermute(values, AXES, [(i, i ^ mask) for i in range(32)])]
    ppermute x0 -> x121, starting transfers between devices: none -> 171 us  [the longest x116 141 us: swap(): return lax.ppermute(values, AXES, [(i, i ^ mask) for i in range(32)])]
    unnamed x44 -> x0, waiting for transfers between devices: 105 us -> none
    reduce_sum x28 -> x0, other arithmetic: 78.7 us -> none  [the longest x8 46.3 us: one_block(): totals = jnp.sum(raw_weights, axis=-1, keepdims=True)]
  transfers between devices with their start and end apart: 34 -> 121, of which waited for: 24 -> 24; matrix products, arithmetic and copies ran while one was open for 18% -> 15% of each run, Pallas kernels for 0% -> 29%
where the time goes in v2:
time: 1140 us; the launch traced here: 1120 us
  Pallas kernels  370 us (32%)
  waiting for transfers between devices  310 us (27%)
  starting transfers between devices  171 us (15%)
  local copies, waits for them, and re-layouts  108 us (9%)
  blocking collectives  86.8 us (8%)
  other arithmetic  72.5 us (6%)
    ppermute x116, waiting for transfers between devices, swap(): return lax.ppermute(values, AXES, [(i, i ^ mask) for i in range(32)])  310 us
    ppermute x116, starting transfers between devices, swap(): return lax.ppermute(values, AXES, [(i, i ^ mask) for i in range(32)])  141 us
    pallas_call x18, Pallas kernels, call_once(): pl.pallas_call(kernel, in_specs=in_vmem(len(args)), out_specs=in_vmem(len...  106 us
    all_gather x1, blocking collectives, fetch_small(): lax.all_gather(piece, AXES, axis=0, tiled=False)  86.8 us
    pallas_call x2, Pallas kernels, attend_pull(): pl.pallas_call(functools.partial(pull_kernel, block), grid=(pairs, 4), in...  79.7 us
    pallas_call x4, Pallas kernels, attend(): pl.pallas_call(functools.partial(attend_kernel, block, rest_bit), grid=(p...  66.1 us
    pallas_call x2, Pallas kernels, mlp_backward(): pl.pallas_call(mlp_pull_kernel, grid=(units // tile,), in_specs=[whole, w...  46.8 us
    pallas_call x2, Pallas kernels, mlp_forward(): pl.pallas_call(mlp_kernel, grid=(units // tile,), in_specs=[whole, whole,...  39.3 us
  transfers between devices with their start and end apart: 121, of which 24 were waited for; matrix products, arithmetic and copies ran while one was open for 15% of the time, Pallas kernels for 29%

profile of v2, /device:TPU:0, one launch (start us, length us, event | category | flops | bytes accessed | tf_op | source)
XLA Modules:
  0.0 1122.2 jit_solution(1260878839950403211)
XLA Ops:
  0.7 9.6 collective-permute-start.1
  15.0 86.8 %all-gather = bf16[64,16,128]{2,1,0:T(8,128)(2,1)S(1)} all-gather(bf16[2,16,128]{2,1,0:T(8,128)(2,1)S(1)} %fusion.25), channel_id=2, replica_groups=mesh['dp'=8,'tensor'=4] {'dp','tensor'}, dimensions={0}, use_global_device_ids=true | all-gather | bytes 270336 | tf_op jit(solution)/shard_map/all_gather | solution.py:1102
  124.5 13.3 %collective-permute-done.17 = bf16[128,2048]{1,0:T(8,128)(2,1)S(1)} collective-permute-done((bf16[128,2048]{1,0:T(8,128)(2,1)S(1)}, bf16[128,2048]{1,0:T(8,128)(2,1)S(1)}, u32[]{:S(2)}, u32[]{:S(2)}) %collective-permute-start.17) | collective-permute-done | bytes 524320 | tf_op jit(solution)/shard_map/ppermute | solution.py:422
  139.3 16.1 %collective-permute-done.18 = bf16[128,2048]{1,0:T(8,128)(2,1)S(1)} collective-permute-done((bf16[128,2048]{1,0:T(8,128)(2,1)S(1)}, bf16[128,2048]{1,0:T(8,128)(2,1)S(1)}, u32[]{:S(2)}, u32[]{:S(2)}) %collective-permute-start.18) | collective-permute-done | bytes 524320 | tf_op jit(solution)/shard_map/ppermute | solution.py:422
  160.5 10.2 collective-permute-start.11
  174.9 5.2 project.4
  180.0 19.4 %collective-permute-done.28 = bf16[128,1024]{1,0:T(8,128)(2,1)S(1)} collective-permute-done((bf16[128,1024]{1,0:T(8,128)(2,1)S(1)}, bf16[128,1024]{1,0:T(8,128)(2,1)S(1)}, u32[]{:S(2)}, u32[]{:S(2)}) %collective-permute-start.28) | collective-permute-done | bytes 262176 | tf_op jit(solution)/shard_map/ppermute | solution.py:422
  201.2 5.2 project.5
  217.9 9.7 collective-permute-start.43
  229.9 18.8 %attend.5 = (bf16[512,256]{1,0:T(8,128)(2,1)}, bf16[512,256]{1,0:T(8,128)(2,1)}, f32[256,1024]{1,0:T(8,128)}, f32[2,8,1024]{2,1,0:T(8,128)}) custom-call(f32[4]{0:T(128)} %multiply_exponential_fusion.slope_ref, s32[2]{0:T(128)} %bitcast.270, s32[1]{0:T(128)} %bitcast.1.me_ref, bf16[512,768]{1,0:T(8,128)(2,1)} %get-tuple-element.113.rest_0_.rest_1_.rest_2_, ...), custom_call_target="tpu_custom_call" | custom-call | flops 2684354560 | bytes 2097152 | tf_op jit(solution)/shard_map/attend/pallas_call | solution.py:572
  254.6 14.2 %attend.4 = (bf16[512,256]{1,0:T(8,128)(2,1)}, bf16[512,256]{1,0:T(8,128)(2,1)}, f32[256,1024]{1,0:T(8,128)}, f32[2,8,1024]{2,1,0:T(8,128)}) custom-call(f32[4]{0:T(128)} %multiply_exponential_fusion.slope_ref, s32[2]{0:T(128)} %bitcast.271, s32[1]{0:T(128)} %bitcast.1.me_ref, bf16[512,768]{1,0:T(8,128)(2,1)} %get-tuple-element.113.rest_0_.rest_1_.rest_2_, ...), custom_call_target="tpu_custom_call" | custom-call | flops 2684354560 | bytes 2097152 | tf_op jit(solution)/shard_map/attend/pallas_call | solution.py:572
  274.0 10.7 collective-permute-done.44
  290.0 11.3 %collective-permute-start.16 = (bf16[512,1024]{1,0:T(8,128)(2,1)}, bf16[512,1024]{1,0:T(8,128)(2,1)S(1)}, u32[]{:S(2)}, u32[]{:S(2)}) collective-permute-start(bf16[512,1024]{1,0:T(8,128)(2,1)} %mix_far.2), channel_id=1, source_target_pairs={{0,1},{1,0},{2,3},{3,2},{4,5},{5,4},{6,7},{7,6},{8,9},{9,8},{10,11... | collective-permute-start | bytes 3145736 | tf_op jit(solution)/shard_map/ppermute | solution.py:422
  302.6 22.7 %collective-permute-done.16.far_ref = bf16[512,1024]{1,0:T(8,128)(2,1)S(1)} collective-permute-done((bf16[512,1024]{1,0:T(8,128)(2,1)}, bf16[512,1024]{1,0:T(8,128)(2,1)S(1)}, u32[]{:S(2)}, u32[]{:S(2)}) %collective-permute-start.16) | collective-permute-done | bytes 1048608 | tf_op jit(solution)/shard_map/ppermute | solution.py:422
  328.7 5.8 mix_near.2
  336.5 19.9 %mlp_forward.2 = (bf16[512,4096]{1,0:T(8,128)(2,1)}, bf16[512,4096]{1,0:T(8,128)(2,1)}, f32[512,1024]{1,0:T(8,128)}, bf16[512,1024]{1,0:T(8,128)(2,1)}) custom-call(bf16[512,1024]{1,0:T(8,128)(2,1)} %get-tuple-element.121.normed_ref, f32[512,1024]{1,0:T(8,128)} %get-tuple-element.122.mid_ref, f32[8,1024]{1,0:T(8,128)} %get-tuple-element.368.vector_ref, ...), custom_call_target="tpu_custom_call" | custom-call | flops 8589934592 | bytes 25165824 | tf_op jit(solution)/shard_map/mlp_forward/pallas_call | solution.py:784
  356.4 22.1 %collective-permute-done.34 = bf16[1,128,1024]{2,1,0:T(8,128)(2,1)S(1)} collective-permute-done((bf16[1,128,1024]{2,1,0:T(8,128)(2,1)S(1)}, bf16[1,128,1024]{2,1,0:T(8,128)(2,1)S(1)}, u32[]{:S(2)}, u32[]{:S(2)}) %collective-permute-start.34) | collective-permute-done | bytes 262176 | tf_op jit(solution)/shard_map/ppermute | solution.py:422
  388.2 5.2 project.6
  393.4 9.6 collective-permute-done.37.rows_ref.far_ref
  403.1 5.2 project.7
  416.0 19.0 %attend.7 = (bf16[512,256]{1,0:T(8,128)(2,1)}, bf16[512,256]{1,0:T(8,128)(2,1)}, f32[256,1024]{1,0:T(8,128)}, f32[2,8,1024]{2,1,0:T(8,128)}) custom-call(f32[4]{0:T(128)} %multiply_exponential_fusion.slope_ref, s32[2]{0:T(128)} %bitcast.272, s32[1]{0:T(128)} %bitcast.1.me_ref, bf16[512,768]{1,0:T(8,128)(2,1)} %get-tuple-element.126.rest_0_.rest_1_.rest_2_, ...), custom_call_target="tpu_custom_call" | custom-call | flops 2684354560 | bytes 2097152 | tf_op jit(solution)/shard_map/attend/pallas_call | solution.py:572
  437.0 14.2 %attend.6 = (bf16[512,256]{1,0:T(8,128)(2,1)}, bf16[512,256]{1,0:T(8,128)(2,1)}, f32[256,1024]{1,0:T(8,128)}, f32[2,8,1024]{2,1,0:T(8,128)}) custom-call(f32[4]{0:T(128)} %multiply_exponential_fusion.slope_ref, s32[2]{0:T(128)} %bitcast.273, s32[1]{0:T(128)} %bitcast.1.me_ref, bf16[512,768]{1,0:T(8,128)(2,1)} %get-tuple-element.126.rest_0_.rest_1_.rest_2_, ...), custom_call_target="tpu_custom_call" | custom-call | flops 2684354560 | bytes 2097152 | tf_op jit(solution)/shard_map/attend/pallas_call | solution.py:572
  460.4 22.8 %collective-permute-done.42.far_ref = bf16[512,1024]{1,0:T(8,128)(2,1)S(1)} collective-permute-done((bf16[512,1024]{1,0:T(8,128)(2,1)}, bf16[512,1024]{1,0:T(8,128)(2,1)S(1)}, u32[]{:S(2)}, u32[]{:S(2)}) %collective-permute-start.42) | collective-permute-done | bytes 1048608 | tf_op jit(solution)/shard_map/ppermute | solution.py:422
  484.2 5.8 mix_near.3
  490.1 19.4 %mlp_forward.3 = (bf16[512,4096]{1,0:T(8,128)(2,1)}, bf16[512,4096]{1,0:T(8,128)(2,1)}, f32[512,1024]{1,0:T(8,128)}, bf16[512,1024]{1,0:T(8,128)(2,1)}) custom-call(bf16[512,1024]{1,0:T(8,128)(2,1)} %get-tuple-element.135.normed_ref, f32[512,1024]{1,0:T(8,128)} %get-tuple-element.136.mid_ref, f32[8,1024]{1,0:T(8,128)} %get-tuple-element.367.vector_ref, ...), custom_call_target="tpu_custom_call" | custom-call | flops 8589934592 | bytes 25165824 | tf_op jit(solution)/shard_map/mlp_forward/pallas_call | solution.py:784
  509.5 23.6 %mlp_backward.2 = (bf16[512,4096]{1,0:T(8,128)(2,1)}, f32[1,4096]{1,0:T(1,128)}, f32[512,1024]{1,0:T(8,128)}, bf16[512,1024]{1,0:T(8,128)(2,1)}, f32[8,1024]{1,0:T(8,128)}) custom-call(f32[512,1024]{1,0:T(8,128)} %copy-done.81, f32[512,1024]{1,0:T(8,128)} %get-tuple-element.136.mid_ref, f32[8,1024]{1,0:T(8,128)} %get-tuple-element.367.vector_ref, ...), custom_call_target="tpu_custom_call" | custom-call | flops 8589934592 | bytes 25165824 | tf_op jit(solution)/shard_map/mlp_backward/pallas_call | solution.py:858
  538.9 15.8 %mlp_weight_grads.3 = (bf16[4,128,2048]{2,1,0:T(8,128)(2,1)}, bf16[4,128,2048]{2,1,0:T(8,128)(2,1)}, bf16[4,128,2048]{2,1,0:T(8,128)(2,1)}, bf16[4,128,2048]{2,1...) custom-call(f32[512,1024]{1,0:T(8,128)} %copy-done.81, ...), custom_call_target="tpu_custom_call" | custom-call | flops 8589934592 | bytes 33554432 | tf_op jit(solution)/shard_map/mlp_weight_grads/pallas_call | solution.py:901
  565.6 40.1 %attend_pull.2 = (bf16[3,1024,256]{2,1,0:T(8,128)(2,1)}, bf16[3,1024,256]{2,1,0:T(8,128)(2,1)}) custom-call(f32[4]{0:T(128)} %multiply_exponential_fusion.slope_ref, s32[2]{0:T(128)} %bitcast.274, s32[1]{0:T(128)} %bitcast.1.me_ref, bf16[512,768]{1,0:T(8,128)(2,1)} %get-tuple-element.126.rest_0_.rest_1_.rest_2_, ...), custom_call_target="tpu_custom_call" | custom-call | flops 13421772800 | bytes 3932160 | tf_op jit(solution)/shard_map/attend_pull/pallas_call | solution.py:705
  625.2 5.9 unproject_far.2
  632.5 9.6 head_grads.3
  663.1 9.3 unproject_near.2
  672.5 23.3 %mlp_backward.3 = (bf16[512,4096]{1,0:T(8,128)(2,1)}, f32[1,4096]{1,0:T(1,128)}, f32[512,1024]{1,0:T(8,128)}, bf16[512,1024]{1,0:T(8,128)(2,1)}, f32[8,1024]{1,0:T(8,128)}) custom-call(f32[512,1024]{1,0:T(8,128)} %get-tuple-element.153.grad_ref, f32[512,1024]{1,0:T(8,128)} %get-tuple-element.122.mid_ref, f32[8,1024]{1,0:T(8,128)} %get-tuple-element.368.vector_ref, ...), custom_call_target="tpu_custom_call" | custom-call | flops 8589934592 | bytes 25165824 | tf_op jit(solution)/shard_map/mlp_backward/pallas_call | solution.py:858
  708.4 16.0 %mlp_weight_grads.2 = (bf16[4,128,2048]{2,1,0:T(8,128)(2,1)}, bf16[4,128,2048]{2,1,0:T(8,128)(2,1)}, bf16[4,128,2048]{2,1,0:T(8,128)(2,1)}, bf16[4,128,2048]{2,1...) custom-call(f32[512,1024]{1,0:T(8,128)} %get-tuple-element.153.grad_, ...), custom_call_target="tpu_custom_call" | custom-call | flops 8589934592 | bytes 33554432 | tf_op jit(solution)/shard_map/mlp_weight_grads/pallas_call | solution.py:901
  730.5 4.9 collective-permute-start.94
  735.4 14.8 %collective-permute-done.116 = bf16[2,128,2048]{2,1,0:T(8,128)(2,1)} collective-permute-done((bf16[2,128,2048]{2,1,0:T(8,128)(2,1)S(1)}, bf16[2,128,2048]{2,1,0:T(8,128)(2,1)}, u32[]{:S(2)}, u32[]{:S(2)}) %collective-permute-start.116) | collective-permute-done | bytes 1048608 | tf_op jit(solution)/shard_map/ppermute | solution.py:422
  753.5 4.6 collective-permute-start.119
  763.6 14.9 %collective-permute-done.119 = bf16[128,2048]{1,0:T(8,128)(2,1)S(1)} collective-permute-done((bf16[128,2048]{1,0:T(8,128)(2,1)S(1)}, bf16[128,2048]{1,0:T(8,128)(2,1)S(1)}, u32[]{:S(2)}, u32[]{:S(2)}) %collective-permute-start.119) | collective-permute-done | bytes 524320 | tf_op jit(solution)/shard_map/ppermute | solution.py:422
  781.3 39.6 %attend_pull.3 = (bf16[3,1024,256]{2,1,0:T(8,128)(2,1)}, bf16[3,1024,256]{2,1,0:T(8,128)(2,1)}) custom-call(f32[4]{0:T(128)} %multiply_exponential_fusion.slope_ref, s32[2]{0:T(128)} %bitcast.275, s32[1]{0:T(128)} %bitcast.1.me_ref, bf16[512,768]{1,0:T(8,128)(2,1)} %get-tuple-element.113.rest_0_.rest_1_.rest_2_, ...), custom_call_target="tpu_custom_call" | custom-call | flops 13421772800 | bytes 3932160 | tf_op jit(solution)/shard_map/attend_pull/pallas_call | solution.py:705
  828.0 12.7 %collective-permute-done.115 = bf16[128,2048]{1,0:T(8,128)(2,1)S(1)} collective-permute-done((bf16[128,2048]{1,0:T(8,128)(2,1)S(1)}, bf16[128,2048]{1,0:T(8,128)(2,1)S(1)}, u32[]{:S(2)}, u32[]{:S(2)}) %collective-permute-start.115) | collective-permute-done | bytes 524320 | tf_op jit(solution)/shard_map/ppermute | solution.py:422
  865.3 9.7 head_grads.2
  895.4 6.0 unproject_far.3
  918.3 11.7 %collective-permute-done.65.far_ref = bf16[512,1024]{1,0:T(8,128)(2,1)S(1)} collective-permute-done((bf16[512,1024]{1,0:T(8,128)(2,1)S(1)}, bf16[512,1024]{1,0:T(8,128)(2,1)S(1)}, u32[]{:S(2)}, u32[]{:S(2)}) %collective-permute-start.65) | collective-permute-done | bytes 1048608 | tf_op jit(solution)/shard_map/ppermute | solution.py:422
  931.0 9.1 unproject_near.3
  956.8 40.5 %collective-permute-done.68 = f32[2,28,128]{2,0,1:T(2,128)S(1)} collective-permute-done((f32[2,28,128]{2,0,1:T(2,128)S(1)}, f32[2,28,128]{2,0,1:T(2,128)S(1)}, u32[]{:S(2)}, u32[]{:S(2)}) %collective-permute-start.68) | collective-permute-done | bytes 28704 | tf_op jit(solution)/shard_map/ppermute | solution.py:422
  1017.8 9.5 collective-permute-start.66
  1027.3 9.6 collective-permute-start.54
  1044.2 24.3 %collective-permute-done.83 = bf16[128,1024]{1,0:T(8,128)(2,1)S(1)} collective-permute-done((bf16[128,1024]{1,0:T(8,128)(2,1)}, bf16[128,1024]{1,0:T(8,128)(2,1)S(1)}, u32[]{:S(2)}, u32[]{:S(2)}) %collective-permute-start.83) | collective-permute-done | bytes 262176 | tf_op jit(solution)/shard_map/ppermute | solution.py:422
  1074.8 35.0 %collective-permute-done.106 = bf16[128,2048]{1,0:T(8,128)(2,1)} collective-permute-done((bf16[128,2048]{1,0:T(8,128)(2,1)}, bf16[128,2048]{1,0:T(8,128)(2,1)}, u32[]{:S(2)}, u32[]{:S(2)}) %collective-permute-start.106) | collective-permute-done | bytes 524320 | tf_op jit(solution)/shard_map/ppermute | solution.py:422
  (668 shorter events, 326.3 us)
Async XLA Ops:
  0.7 116.3 %collective-permute-start.1 = (bf16[512,1024]{1,0:T(8,128)(2,1)}, bf16[512,1024]{1,0:T(8,128)(2,1)}, u32[]{:S(2)}, u32[]{:S(2)}) collective-permute-start(bf16[512,1024]{1,0:T(8,128)(2,1)} %param.15), channel_id=1, source_target_pairs={{0,0},{1,1},{2,4},{3,5},{4,2},{5,3},{6,6},{7,7},{8,8},{9,9},{10,12... | collective-permute-start | bytes 3145736 | tf_op jit(solution)/shard_map/ppermute | solution.py:430
  14.7 90.3 %collective-permute-start.2 = (bf16[128,1024]{1,0:T(8,128)(2,1)}, bf16[128,1024]{1,0:T(8,128)(2,1)}, u32[]{:S(2)}, u32[]{:S(2)}) collective-permute-start(bf16[128,1024]{1,0:T(8,128)(2,1)} %pad_maximum_fusion.9), channel_id=1, source_target_pairs={{0,2},{1,3},{2,0},{3,1},{4,6},{5,7},{6,4},{7,5},{8,10},{9,11},{10,... | collective-permute-start | bytes 786440 | tf_op jit(solution)/shard_map/ppermute | solution.py:422
  112.3 48.1 %collective-permute-start.3 = (bf16[2,128,1024]{2,1,0:T(8,128)(2,1)S(1)}, bf16[2,128,1024]{2,1,0:T(8,128)(2,1)S(1)}, u32[]{:S(2)}, u32[]{:S(2)}) collective-permute-start(bf16[2,128,1024]{2,1,0:T(8,128)(2,1)S(1)} %pad_maximum_fusion.5.rest_0_), channel_id=1, source_target_pairs={{0,4},{1,5},{2,6},{3,7},{4,0},{5,1},{6,2},{7,3},{8,12},{9,13},{10,... | collective-permute-start | bytes 1572872 | tf_op jit(solution)/shard_map/ppermute | solution.py:422
  157.0 49.4 %collective-permute-start.21 = (bf16[4,128,2048]{2,1,0:T(8,128)(2,1)}, bf16[4,128,2048]{2,1,0:T(8,128)(2,1)}, u32[]{:S(2)}, u32[]{:S(2)}) collective-permute-start(bf16[4,128,2048]{2,1,0:T(8,128)(2,1)} %pad_maximum_fusion.rest_0_), channel_id=1, source_target_pairs={{0,8},{1,9},{2,10},{3,11},{4,12},{5,13},{6,14},{7,15},{8,0},{9,1},... | collective-permute-start | bytes 6291464 | tf_op jit(solution)/shard_map/ppermute | solution.py:422
  158.7 52.3 %collective-permute-start.23 = (bf16[4,128,2048]{2,1,0:T(8,128)(2,1)}, bf16[4,128,2048]{2,1,0:T(8,128)(2,1)}, u32[]{:S(2)}, u32[]{:S(2)}) collective-permute-start(bf16[4,128,2048]{2,1,0:T(8,128)(2,1)} %pad_maximum_fusion.rest_0_), channel_id=1, source_target_pairs={{0,16},{1,17},{2,18},{3,19},{4,20},{5,21},{6,22},{7,23},{8,24},{9,... | collective-permute-start | bytes 6291464 | tf_op jit(solution)/shard_map/ppermute | solution.py:422
  208.8 60.0 %collective-permute-start.25 = (bf16[2,128,2048]{2,1,0:T(8,128)(2,1)}, bf16[2,128,2048]{2,1,0:T(8,128)(2,1)}, u32[]{:S(2)}, u32[]{:S(2)}) collective-permute-start(bf16[2,128,2048]{2,1,0:T(8,128)(2,1)} %slice.477), channel_id=1, source_target_pairs={{0,16},{1,17},{2,18},{3,19},{4,20},{5,21},{6,22},{7,23},{8,24},{9,... | collective-permute-start | bytes 3145736 | tf_op jit(solution)/shard_map/ppermute | solution.py:422
  214.1 57.1 %collective-permute-start.26 = (bf16[2,128,2048]{2,1,0:T(8,128)(2,1)}, bf16[2,128,2048]{2,1,0:T(8,128)(2,1)}, u32[]{:S(2)}, u32[]{:S(2)}) collective-permute-start(bf16[2,128,2048]{2,1,0:T(8,128)(2,1)} %slice.478), channel_id=1, source_target_pairs={{0,8},{1,9},{2,10},{3,11},{4,12},{5,13},{6,14},{7,15},{8,0},{9,1},... | collective-permute-start | bytes 3145736 | tf_op jit(solution)/shard_map/ppermute | solution.py:422
  228.1 73.5 %collective-permute-start.20 = (bf16[4,128,2048]{2,1,0:T(8,128)(2,1)}, bf16[4,128,2048]{2,1,0:T(8,128)(2,1)}, u32[]{:S(2)}, u32[]{:S(2)}) collective-permute-start(bf16[4,128,2048]{2,1,0:T(8,128)(2,1)} %pad_maximum_fusion.rest_0_), channel_id=1, source_target_pairs={{0,4},{1,5},{2,6},{3,7},{4,0},{5,1},{6,2},{7,3},{8,12},{9,13},{10,... | collective-permute-start | bytes 6291464 | tf_op jit(solution)/shard_map/ppermute | solution.py:422
  284.8 49.8 %collective-permute-start.22 = (bf16[4,128,2048]{2,1,0:T(8,128)(2,1)}, bf16[4,128,2048]{2,1,0:T(8,128)(2,1)}, u32[]{:S(2)}, u32[]{:S(2)}) collective-permute-start(bf16[4,128,2048]{2,1,0:T(8,128)(2,1)} %collective-permute-done.21.rest_2_), channel_id=1, source_target_pairs={{0,4},{1,5},{2,6},{3,7},{4,0},{5,1},{6,2},{7,3},{8,12},{9,13},{10,... | collective-permute-start | bytes 6291464 | tf_op jit(solution)/shard_map/ppermute | solution.py:422
  284.8 49.8 %collective-permute-start.24 = (bf16[4,128,2048]{2,1,0:T(8,128)(2,1)}, bf16[4,128,2048]{2,1,0:T(8,128)(2,1)}, u32[]{:S(2)}, u32[]{:S(2)}) collective-permute-start(bf16[4,128,2048]{2,1,0:T(8,128)(2,1)} %collective-permute-done.23.rest_4_), channel_id=1, source_target_pairs={{0,4},{1,5},{2,6},{3,7},{4,0},{5,1},{6,2},{7,3},{8,12},{9,13},{10,... | collective-permute-start | bytes 6291464 | tf_op jit(solution)/shard_map/ppermute | solution.py:422
  285.3 50.3 %collective-permute-start.27 = (bf16[4,128,2048]{2,1,0:T(8,128)(2,1)}, bf16[4,128,2048]{2,1,0:T(8,128)(2,1)}, u32[]{:S(2)}, u32[]{:S(2)}) collective-permute-start(bf16[4,128,2048]{2,1,0:T(8,128)(2,1)} %constant_dynamic-update-slice_fusion.8.rest_6_), channel_id=1, source_target_pairs={{0,4},{1,5},{2,6},{3,7},{4,0},{5,1},{6,2},{7,3},{8,12},{9,13},{10,... | collective-permute-start | bytes 6291464 | tf_op jit(solution)/shard_map/ppermute | solution.py:422
  301.6 79.1 %collective-permute-start.47 = (bf16[4,128,2048]{2,1,0:T(8,128)(2,1)S(1)}, bf16[4,128,2048]{2,1,0:T(8,128)(2,1)}, u32[]{:S(2)}, u32[]{:S(2)}) collective-permute-start(bf16[4,128,2048]{2,1,0:T(8,128)(2,1)S(1)} %pad_maximum_fusion.1.rest_0_), channel_id=1, source_target_pairs={{0,8},{1,9},{2,10},{3,11},{4,12},{5,13},{6,14},{7,15},{8,0},{9,1},... | collective-permute-start | bytes 6291464 | tf_op jit(solution)/shard_map/ppermute | solution.py:422
  325.3 57.8 %collective-permute-start.49 = (bf16[4,128,2048]{2,1,0:T(8,128)(2,1)S(1)}, bf16[4,128,2048]{2,1,0:T(8,128)(2,1)}, u32[]{:S(2)}, u32[]{:S(2)}) collective-permute-start(bf16[4,128,2048]{2,1,0:T(8,128)(2,1)S(1)} %pad_maximum_fusion.1.rest_0_), channel_id=1, source_target_pairs={{0,16},{1,17},{2,18},{3,19},{4,20},{5,21},{6,22},{7,23},{8,24},{9,... | collective-permute-start | bytes 6291464 | tf_op jit(solution)/shard_map/ppermute | solution.py:422
  334.5 45.6 %collective-permute-start.29 = (bf16[2,128,1024]{2,1,0:T(8,128)(2,1)S(1)}, bf16[2,128,1024]{2,1,0:T(8,128)(2,1)S(1)}, u32[]{:S(2)}, u32[]{:S(2)}) collective-permute-start(bf16[2,128,1024]{2,1,0:T(8,128)(2,1)S(1)} %pad_maximum_fusion.7.rest_0_), channel_id=1, source_target_pairs={{0,4},{1,5},{2,6},{3,7},{4,0},{5,1},{6,2},{7,3},{8,12},{9,13},{10,... | collective-permute-start | bytes 1572872 | tf_op jit(solution)/shard_map/ppermute | solution.py:422
  334.6 43.9 %collective-permute-start.34 = (bf16[1,128,1024]{2,1,0:T(8,128)(2,1)S(1)}, bf16[1,128,1024]{2,1,0:T(8,128)(2,1)S(1)}, u32[]{:S(2)}, u32[]{:S(2)}) collective-permute-start(bf16[1,128,1024]{2,1,0:T(8,128)(2,1)S(1)} %slice.481), channel_id=1, source_target_pairs={{0,16},{1,17},{2,18},{3,19},{4,20},{5,21},{6,22},{7,23},{8,24},{9,... | collective-permute-start | bytes 786440 | tf_op jit(solution)/shard_map/ppermute | solution.py:422
  335.6 44.4 %collective-permute-start.35 = (bf16[1,128,1024]{2,1,0:T(8,128)(2,1)S(1)}, bf16[1,128,1024]{2,1,0:T(8,128)(2,1)S(1)}, u32[]{:S(2)}, u32[]{:S(2)}) collective-permute-start(bf16[1,128,1024]{2,1,0:T(8,128)(2,1)S(1)} %slice.482), channel_id=1, source_target_pairs={{0,8},{1,9},{2,10},{3,11},{4,12},{5,13},{6,14},{7,15},{8,0},{9,1},... | collective-permute-start | bytes 786440 | tf_op jit(solution)/shard_map/ppermute | solution.py:422
  409.0 81.1 %collective-permute-start.46 = (bf16[4,128,2048]{2,1,0:T(8,128)(2,1)S(1)}, bf16[4,128,2048]{2,1,0:T(8,128)(2,1)}, u32[]{:S(2)}, u32[]{:S(2)}) collective-permute-start(bf16[4,128,2048]{2,1,0:T(8,128)(2,1)S(1)} %pad_maximum_fusion.1.rest_0_), channel_id=1, source_target_pairs={{0,4},{1,5},{2,6},{3,7},{4,0},{5,1},{6,2},{7,3},{8,12},{9,13},{10,... | collective-permute-start | bytes 6291464 | tf_op jit(solution)/shard_map/ppermute | solution.py:422
  413.5 76.6 %collective-permute-start.48 = (bf16[4,128,2048]{2,1,0:T(8,128)(2,1)}, bf16[4,128,2048]{2,1,0:T(8,128)(2,1)}, u32[]{:S(2)}, u32[]{:S(2)}) collective-permute-start(bf16[4,128,2048]{2,1,0:T(8,128)(2,1)} %collective-permute-done.47.rest_2_), channel_id=1, source_target_pairs={{0,4},{1,5},{2,6},{3,7},{4,0},{5,1},{6,2},{7,3},{8,12},{9,13},{10,... | collective-permute-start | bytes 6291464 | tf_op jit(solution)/shard_map/ppermute | solution.py:422
  414.6 75.4 %collective-permute-start.50 = (bf16[4,128,2048]{2,1,0:T(8,128)(2,1)}, bf16[4,128,2048]{2,1,0:T(8,128)(2,1)}, u32[]{:S(2)}, u32[]{:S(2)}) collective-permute-start(bf16[4,128,2048]{2,1,0:T(8,128)(2,1)} %collective-permute-done.49.rest_4_), channel_id=1, source_target_pairs={{0,4},{1,5},{2,6},{3,7},{4,0},{5,1},{6,2},{7,3},{8,12},{9,13},{10,... | collective-permute-start | bytes 6291464 | tf_op jit(solution)/shard_map/ppermute | solution.py:422
  415.1 74.9 %collective-permute-start.53 = (bf16[4,128,2048]{2,1,0:T(8,128)(2,1)}, bf16[4,128,2048]{2,1,0:T(8,128)(2,1)}, u32[]{:S(2)}, u32[]{:S(2)}) collective-permute-start(bf16[4,128,2048]{2,1,0:T(8,128)(2,1)} %constant_dynamic-update-slice_fusion.12.rest_6_), channel_id=1, source_target_pairs={{0,4},{1,5},{2,6},{3,7},{4,0},{5,1},{6,2},{7,3},{8,12},{9,13},{10,... | collective-permute-start | bytes 6291464 | tf_op jit(solution)/shard_map/ppermute | solution.py:422
  554.6 51.3 %collective-permute-start.112 = (bf16[4,128,2048]{2,1,0:T(8,128)(2,1)}, bf16[4,128,2048]{2,1,0:T(8,128)(2,1)S(1)}, u32[]{:S(2)}, u32[]{:S(2)}) collective-permute-start(bf16[4,128,2048]{2,1,0:T(8,128)(2,1)} %get-tuple-element.211), channel_id=1, source_target_pairs={{0,4},{1,5},{2,6},{3,7},{4,0},{5,1},{6,2},{7,3},{8,12},{9,13},{10,... | collective-permute-start | bytes 6291464 | tf_op jit(solution)/shard_map/ppermute | solution.py:422
  562.8 49.0 %collective-permute-start.108 = (bf16[4,128,2048]{2,1,0:T(8,128)(2,1)}, bf16[4,128,2048]{2,1,0:T(8,128)(2,1)}, u32[]{:S(2)}, u32[]{:S(2)}) collective-permute-start(bf16[4,128,2048]{2,1,0:T(8,128)(2,1)} %get-tuple-element.205), channel_id=1, source_target_pairs={{0,4},{1,5},{2,6},{3,7},{4,0},{5,1},{6,2},{7,3},{8,12},{9,13},{10,... | collective-permute-start | bytes 6291464 | tf_op jit(solution)/shard_map/ppermute | solution.py:422
  563.3 55.6 %collective-permute-start.109 = (bf16[4,128,2048]{2,1,0:T(8,128)(2,1)}, bf16[4,128,2048]{2,1,0:T(8,128)(2,1)}, u32[]{:S(2)}, u32[]{:S(2)}) collective-permute-start(bf16[4,128,2048]{2,1,0:T(8,128)(2,1)} %get-tuple-element.207), channel_id=1, source_target_pairs={{0,4},{1,5},{2,6},{3,7},{4,0},{5,1},{6,2},{7,3},{8,12},{9,13},{10,... | collective-permute-start | bytes 6291464 | tf_op jit(solution)/shard_map/ppermute | solution.py:422
  563.4 59.4 %collective-permute-start.111 = (bf16[4,128,2048]{2,1,0:T(8,128)(2,1)}, bf16[4,128,2048]{2,1,0:T(8,128)(2,1)}, u32[]{:S(2)}, u32[]{:S(2)}) collective-permute-start(bf16[4,128,2048]{2,1,0:T(8,128)(2,1)} %get-tuple-element.209), channel_id=1, source_target_pairs={{0,4},{1,5},{2,6},{3,7},{4,0},{5,1},{6,2},{7,3},{8,12},{9,13},{10,... | collective-permute-start | bytes 6291464 | tf_op jit(solution)/shard_map/ppermute | solution.py:422
  654.0 70.5 %collective-permute-start.110 = (bf16[2,128,2048]{2,1,0:T(8,128)(2,1)}, bf16[2,128,2048]{2,1,0:T(8,128)(2,1)}, u32[]{:S(2)}, u32[]{:S(2)}) collective-permute-start(bf16[2,128,2048]{2,1,0:T(8,128)(2,1)} %get-tuple-element.300), channel_id=1, source_target_pairs={{0,16},{1,17},{2,18},{3,19},{4,20},{5,21},{6,22},{7,23},{8,24},{9,... | collective-permute-start | bytes 3145736 | tf_op jit(solution)/shard_map/ppermute | solution.py:422
  658.2 45.7 %collective-permute-start.86 = (bf16[1,128,1024]{2,1,0:T(8,128)(2,1)}, bf16[1,128,1024]{2,1,0:T(8,128)(2,1)S(1)}, u32[]{:S(2)}, u32[]{:S(2)}) collective-permute-start(bf16[1,128,1024]{2,1,0:T(8,128)(2,1)} %get-tuple-element.324), channel_id=1, source_target_pairs={{0,16},{1,17},{2,18},{3,19},{4,20},{5,21},{6,22},{7,23},{8,24},{9,... | collective-permute-start | bytes 786440 | tf_op jit(solution)/shard_map/ppermute | solution.py:422
  658.3 45.7 %collective-permute-start.93 = (bf16[1,128,1024]{2,1,0:T(8,128)(2,1)}, bf16[1,128,1024]{2,1,0:T(8,128)(2,1)S(1)}, u32[]{:S(2)}, u32[]{:S(2)}) collective-permute-start(bf16[1,128,1024]{2,1,0:T(8,128)(2,1)} %get-tuple-element.323), channel_id=1, source_target_pairs={{0,16},{1,17},{2,18},{3,19},{4,20},{5,21},{6,22},{7,23},{8,24},{9,... | collective-permute-start | bytes 786440 | tf_op jit(solution)/shard_map/ppermute | solution.py:422
  661.1 43.7 %collective-permute-start.90 = (bf16[1,128,1024]{2,1,0:T(8,128)(2,1)}, bf16[1,128,1024]{2,1,0:T(8,128)(2,1)S(1)}, u32[]{:S(2)}, u32[]{:S(2)}) collective-permute-start(bf16[1,128,1024]{2,1,0:T(8,128)(2,1)} %get-tuple-element.322), channel_id=1, source_target_pairs={{0,8},{1,9},{2,10},{3,11},{4,12},{5,13},{6,14},{7,15},{8,0},{9,1},... | collective-permute-start | bytes 786440 | tf_op jit(solution)/shard_map/ppermute | solution.py:422
  661.9 44.2 %collective-permute-start.91 = (bf16[1,128,1024]{2,1,0:T(8,128)(2,1)}, bf16[1,128,1024]{2,1,0:T(8,128)(2,1)}, u32[]{:S(2)}, u32[]{:S(2)}) collective-permute-start(bf16[1,128,1024]{2,1,0:T(8,128)(2,1)} %get-tuple-element.321), channel_id=1, source_target_pairs={{0,8},{1,9},{2,10},{3,11},{4,12},{5,13},{6,14},{7,15},{8,0},{9,1},... | collective-permute-start | bytes 786440 | tf_op jit(solution)/shard_map/ppermute | solution.py:422
  704.8 45.3 %collective-permute-start.116 = (bf16[2,128,2048]{2,1,0:T(8,128)(2,1)S(1)}, bf16[2,128,2048]{2,1,0:T(8,128)(2,1)}, u32[]{:S(2)}, u32[]{:S(2)}) collective-permute-start(bf16[2,128,2048]{2,1,0:T(8,128)(2,1)S(1)} %copy-done.39), channel_id=1, source_target_pairs={{0,8},{1,9},{2,10},{3,11},{4,12},{5,13},{6,14},{7,15},{8,0},{9,1},... | collective-permute-start | bytes 3145736 | tf_op jit(solution)/shard_map/ppermute | solution.py:422
  706.1 52.1 %collective-permute-start.61 = (bf16[512,1024]{1,0:T(8,128)(2,1)S(1)}, bf16[512,1024]{1,0:T(8,128)(2,1)}, u32[]{:S(2)}, u32[]{:S(2)}) collective-permute-start(bf16[512,1024]{1,0:T(8,128)(2,1)S(1)} %copy-done.37), channel_id=1, source_target_pairs={{0,1},{1,0},{2,3},{3,2},{4,5},{5,4},{6,7},{7,6},{8,9},{9,8},{10,11... | collective-permute-start | bytes 3145736 | tf_op jit(solution)/shard_map/ppermute | solution.py:422
  724.4 96.5 %collective-permute-start.99 = (bf16[4,128,2048]{2,1,0:T(8,128)(2,1)}, bf16[4,128,2048]{2,1,0:T(8,128)(2,1)}, u32[]{:S(2)}, u32[]{:S(2)}) collective-permute-start(bf16[4,128,2048]{2,1,0:T(8,128)(2,1)} %get-tuple-element.201), channel_id=1, source_target_pairs={{0,4},{1,5},{2,6},{3,7},{4,0},{5,1},{6,2},{7,3},{8,12},{9,13},{10,... | collective-permute-start | bytes 6291464 | tf_op jit(solution)/shard_map/ppermute | solution.py:422
  763.0 88.7 %collective-permute-start.95 = (bf16[4,128,2048]{2,1,0:T(8,128)(2,1)}, bf16[4,128,2048]{2,1,0:T(8,128)(2,1)}, u32[]{:S(2)}, u32[]{:S(2)}) collective-permute-start(bf16[4,128,2048]{2,1,0:T(8,128)(2,1)} %get-tuple-element.195), channel_id=1, source_target_pairs={{0,4},{1,5},{2,6},{3,7},{4,0},{5,1},{6,2},{7,3},{8,12},{9,13},{10,... | collective-permute-start | bytes 6291464 | tf_op jit(solution)/shard_map/ppermute | solution.py:422
  763.5 95.5 %collective-permute-start.96 = (bf16[4,128,2048]{2,1,0:T(8,128)(2,1)}, bf16[4,128,2048]{2,1,0:T(8,128)(2,1)}, u32[]{:S(2)}, u32[]{:S(2)}) collective-permute-start(bf16[4,128,2048]{2,1,0:T(8,128)(2,1)} %get-tuple-element.197), channel_id=1, source_target_pairs={{0,4},{1,5},{2,6},{3,7},{4,0},{5,1},{6,2},{7,3},{8,12},{9,13},{10,... | collective-permute-start | bytes 6291464 | tf_op jit(solution)/shard_map/ppermute | solution.py:422
  778.5 84.3 %collective-permute-start.98 = (bf16[4,128,2048]{2,1,0:T(8,128)(2,1)}, bf16[4,128,2048]{2,1,0:T(8,128)(2,1)}, u32[]{:S(2)}, u32[]{:S(2)}) collective-permute-start(bf16[4,128,2048]{2,1,0:T(8,128)(2,1)} %get-tuple-element.199), channel_id=1, source_target_pairs={{0,4},{1,5},{2,6},{3,7},{4,0},{5,1},{6,2},{7,3},{8,12},{9,13},{10,... | collective-permute-start | bytes 6291464 | tf_op jit(solution)/shard_map/ppermute | solution.py:422
  778.5 47.9 %collective-permute-start.120 = (bf16[128,2048]{1,0:T(8,128)(2,1)}, bf16[128,2048]{1,0:T(8,128)(2,1)}, u32[]{:S(2)}, u32[]{:S(2)}) collective-permute-start(bf16[128,2048]{1,0:T(8,128)(2,1)} %get-tuple-element.314), channel_id=1, source_target_pairs={{0,3},{1,2},{2,1},{3,0},{4,7},{5,6},{6,5},{7,4},{8,11},{9,10},{10,... | collective-permute-start | bytes 1572872 | tf_op jit(solution)/shard_map/ppermute | solution.py:422
  820.9 44.3 %collective-permute-start.64 = (bf16[3,1024,256]{2,1,0:T(8,128)(2,1)}, bf16[3,1024,256]{2,1,0:T(8,128)(2,1)}, u32[]{:S(2)}, u32[]{:S(2)}) collective-permute-start(bf16[3,1024,256]{2,1,0:T(8,128)(2,1)} %get-tuple-element.165), channel_id=1, source_target_pairs={{0,4},{1,5},{2,6},{3,7},{4,0},{5,1},{6,2},{7,3},{8,12},{9,13},{10,... | collective-permute-start | bytes 4718600 | tf_op jit(solution)/shard_map/ppermute | solution.py:422
  840.7 60.8 %collective-permute-start.104 = (bf16[2,128,2048]{2,1,0:T(8,128)(2,1)}, bf16[2,128,2048]{2,1,0:T(8,128)(2,1)}, u32[]{:S(2)}, u32[]{:S(2)}) collective-permute-start(bf16[2,128,2048]{2,1,0:T(8,128)(2,1)} %get-tuple-element.297), channel_id=1, source_target_pairs={{0,8},{1,9},{2,10},{3,11},{4,12},{5,13},{6,14},{7,15},{8,0},{9,1},... | collective-permute-start | bytes 3145736 | tf_op jit(solution)/shard_map/ppermute | solution.py:422
  851.7 54.7 %collective-permute-start.100 = (bf16[2,128,2048]{2,1,0:T(8,128)(2,1)}, bf16[2,128,2048]{2,1,0:T(8,128)(2,1)}, u32[]{:S(2)}, u32[]{:S(2)}) collective-permute-start(bf16[2,128,2048]{2,1,0:T(8,128)(2,1)} %get-tuple-element.296), channel_id=1, source_target_pairs={{0,16},{1,17},{2,18},{3,19},{4,20},{5,21},{6,22},{7,23},{8,24},{9,... | collective-permute-start | bytes 3145736 | tf_op jit(solution)/shard_map/ppermute | solution.py:422
  911.6 106.3 %collective-permute-start.105 = (bf16[2,128,2048]{2,1,0:T(8,128)(2,1)}, bf16[2,128,2048]{2,1,0:T(8,128)(2,1)}, u32[]{:S(2)}, u32[]{:S(2)}) collective-permute-start(bf16[2,128,2048]{2,1,0:T(8,128)(2,1)} %get-tuple-element.293), channel_id=1, source_target_pairs={{0,16},{1,17},{2,18},{3,19},{4,20},{5,21},{6,22},{7,23},{8,24},{9,... | collective-permute-start | bytes 3145736 | tf_op jit(solution)/shard_map/ppermute | solution.py:422
  949.5 77.8 %collective-permute-start.97 = (bf16[2,128,2048]{2,1,0:T(8,128)(2,1)}, bf16[2,128,2048]{2,1,0:T(8,128)(2,1)}, u32[]{:S(2)}, u32[]{:S(2)}) collective-permute-start(bf16[2,128,2048]{2,1,0:T(8,128)(2,1)} %get-tuple-element.292), channel_id=1, source_target_pairs={{0,16},{1,17},{2,18},{3,19},{4,20},{5,21},{6,22},{7,23},{8,24},{9,... | collective-permute-start | bytes 3145736 | tf_op jit(solution)/shard_map/ppermute | solution.py:422
  949.6 87.4 %collective-permute-start.101 = (bf16[2,128,2048]{2,1,0:T(8,128)(2,1)}, bf16[2,128,2048]{2,1,0:T(8,128)(2,1)}, u32[]{:S(2)}, u32[]{:S(2)}) collective-permute-start(bf16[2,128,2048]{2,1,0:T(8,128)(2,1)} %get-tuple-element.294), channel_id=1, source_target_pairs={{0,8},{1,9},{2,10},{3,11},{4,12},{5,13},{6,14},{7,15},{8,0},{9,1},... | collective-permute-start | bytes 3145736 | tf_op jit(solution)/shard_map/ppermute | solution.py:422
  950.6 86.3 %collective-permute-start.103 = (bf16[2,128,2048]{2,1,0:T(8,128)(2,1)}, bf16[2,128,2048]{2,1,0:T(8,128)(2,1)}, u32[]{:S(2)}, u32[]{:S(2)}) collective-permute-start(bf16[2,128,2048]{2,1,0:T(8,128)(2,1)} %get-tuple-element.295), channel_id=1, source_target_pairs={{0,8},{1,9},{2,10},{3,11},{4,12},{5,13},{6,14},{7,15},{8,0},{9,1},... | collective-permute-start | bytes 3145736 | tf_op jit(solution)/shard_map/ppermute | solution.py:422
  1015.3 53.2 %collective-permute-start.83 = (bf16[128,1024]{1,0:T(8,128)(2,1)}, bf16[128,1024]{1,0:T(8,128)(2,1)S(1)}, u32[]{:S(2)}, u32[]{:S(2)}) collective-permute-start(bf16[128,1024]{1,0:T(8,128)(2,1)} %fusion.15), channel_id=1, source_target_pairs={{0,2},{1,3},{2,0},{3,1},{4,6},{5,7},{6,4},{7,5},{8,10},{9,11},{10,... | collective-permute-start | bytes 786440 | tf_op jit(solution)/shard_map/ppermute | solution.py:422
  1017.8 99.6 %collective-permute-start.66 = (bf16[512,1024]{1,0:T(8,128)(2,1)}, bf16[512,1024]{1,0:T(8,128)(2,1)}, u32[]{:S(2)}, u32[]{:S(2)}) collective-permute-start(bf16[512,1024]{1,0:T(8,128)(2,1)} %copy-done.82), channel_id=1, source_target_pairs={{0,0},{1,1},{2,4},{3,5},{4,2},{5,3},{6,6},{7,7},{8,8},{9,9},{10,12... | collective-permute-start | bytes 3145736 | tf_op jit(solution)/shard_map/ppermute | solution.py:430
  1027.3 90.2 %collective-permute-start.54 = (bf16[512,1024]{1,0:T(8,128)(2,1)}, bf16[512,1024]{1,0:T(8,128)(2,1)}, u32[]{:S(2)}, u32[]{:S(2)}) collective-permute-start(bf16[512,1024]{1,0:T(8,128)(2,1)} %dynamic-slice_dynamic-update-slice_fusion.24), channel_id=1, source_target_pairs={{0,0},{1,1},{2,4},{3,5},{4,2},{5,3},{6,6},{7,7},{8,8},{9,9},{10,12... | collective-permute-start | bytes 3145736 | tf_op jit(solution)/shard_map/ppermute | solution.py:430
  1040.6 69.2 %collective-permute-start.106 = (bf16[128,2048]{1,0:T(8,128)(2,1)}, bf16[128,2048]{1,0:T(8,128)(2,1)}, u32[]{:S(2)}, u32[]{:S(2)}) collective-permute-start(bf16[128,2048]{1,0:T(8,128)(2,1)} %get-tuple-element.311), channel_id=1, source_target_pairs={{0,2},{1,3},{2,0},{3,1},{4,6},{5,7},{6,4},{7,5},{8,10},{9,11},{10,... | collective-permute-start | bytes 1572872 | tf_op jit(solution)/shard_map/ppermute | solution.py:422
  1040.6 69.2 %collective-permute-start.107 = (bf16[128,2048]{1,0:T(8,128)(2,1)}, bf16[128,2048]{1,0:T(8,128)(2,1)}, u32[]{:S(2)}, u32[]{:S(2)}) collective-permute-start(bf16[128,2048]{1,0:T(8,128)(2,1)} %get-tuple-element.312), channel_id=1, source_target_pairs={{0,3},{1,2},{2,1},{3,0},{4,7},{5,6},{6,5},{7,4},{8,11},{9,10},{10,... | collective-permute-start | bytes 1572872 | tf_op jit(solution)/shard_map/ppermute | solution.py:422
  (179 other events, 3854.9 us)

commit v3 on v2

--- a/solution.py
+++ b/solution.py
@@ -414,12 +414,21 @@
 VMEM_LIMIT = 56 * 1024 * 1024
 
 
+def took(us):
+    return pl.CostEstimate(flops=int(us * 5e8), bytes_accessed=1, transcendentals=0)
+
+
 def mesh_is_paired(mesh):
     return dict(mesh.shape) == {"dp": 8, "tensor": 4}
 
 
 def swap(values, mask):
     return lax.ppermute(values, AXES, [(i, i ^ mask) for i in range(32)])
+
+
+def swap_some(values, masks):
+    pairs = [(i, i ^ masks[(i >> 2) & 1]) for i in range(32)]
+    return lax.ppermute(values, AXES, [pair for pair in pairs if pair[0] != pair[1]])
 
 
 def redeal(values):
@@ -427,18 +436,40 @@
         core, z1 = (i >> 2) & 1, (i >> 1) & 1
         return (i & ~6) | (z1 << 2) | (core << 1)
 
-    return lax.ppermute(values, AXES, [(i, target(i)) for i in range(32)])
-
-
-def turn_blocks(values, own):
-    width = values.shape[1] // 8
-    return jnp.concatenate(
-        [lax.dynamic_slice_in_dim(values, (own ^ i) * width, width, 1) for i in range(8)], axis=1
-    )
+    return lax.ppermute(values, AXES, [(i, target(i)) for i in range(32) if target(i) != i])
+
+
+def turn_index(values, own):
+    shape = values.shape
+    for bit in range(3):
+        values = values.reshape(8 >> (bit + 1), 2, (1 << bit), *shape[1:])
+        values = jnp.where((own >> bit) & 1, jnp.concatenate([values[:, 1:], values[:, :1]], axis=1), values)
+    return values.reshape(shape)
 
 
 def after(values, *others):
     return lax.optimization_barrier((values, *others))[0]
+
+
+def after_all(values, *others):
+    if not others:
+        return tuple(values)
+    return lax.optimization_barrier((*values, *others))[:len(values)]
+
+
+def task(steps):
+    next(steps)
+    return steps
+
+
+def advance(token, *tasks):
+    made = []
+    for steps in tasks:
+        try:
+            made += steps.send(token)
+        except StopIteration:
+            pass
+    return made
 
 
 def dot_nt(a, b):
@@ -596,17 +627,16 @@
             pltpu.VMEM((PIECE, block), F32),
         ],
         compiler_params=pltpu.CompilerParams(vmem_limit_bytes=VMEM_LIMIT),
-        cost_estimate=pl.CostEstimate(flops=10 * length * length * width // 4, bytes_accessed=16 * block * width, transcendentals=0),
+        cost_estimate=took(17),
         name="attend",
     )(slopes, starts, me, *[b for b in blocks for _ in range(3)])
 
 
-def pull_kernel(block, slope_ref, start_ref, me_ref, *rest):
+def pull_kernel(block, pair, slope_ref, start_ref, me_ref, *rest):
     triple_refs, grad_refs, rest = rest[:12], rest[12:16], rest[16:]
     exact_refs, lse_refs, rest = rest[0:2], rest[2:4], rest[4:]
     mine_ref, away_ref, q_ref, k_ref, v_ref, g_ref, kt_ref, dk_acc, dv_acc, dqt_ref, bias_ref, tail_ref = rest
-    pair = pl.program_id(0)
-    turn = pl.program_id(1)
+    turn = pl.program_id(0)
     me = me_ref[0]
     step = turn ^ me
     length = k_ref.shape[0]
@@ -693,21 +723,22 @@
             away_ref[part] = ref[2 * block:].astype(BF)
 
 
-def attend_pull(blocks, grads, exacts, log_totals, slopes, starts, me):
+def attend_pull(pair, blocks, grads, exacts, log_totals, slopes, starts, me):
     block, width = blocks[0].shape[0], blocks[0].shape[1] // 3
     pairs = width // (2 * HD)
     length = 4 * block
     smem = pl.BlockSpec(memory_space=pltpu.SMEM)
-    rows = pl.BlockSpec((block, 2 * HD), lambda p, i: (0, p))
-    wide = pl.BlockSpec((2 * HD, 2 * block), lambda p, i: (p, 0))
-    sums = pl.BlockSpec((1, 8, 2 * block), lambda p, i: (p, 0, 0))
-    out = pl.BlockSpec((3, 2 * block, 2 * HD), lambda p, i: (0, 0, p))
+    triples = [pl.BlockSpec((block, 2 * HD), functools.partial(lambda part, i: (0, part * pairs + pair), part)) for part in range(3)]
+    rows = pl.BlockSpec((block, 2 * HD), lambda i: (0, pair))
+    wide = pl.BlockSpec((2 * HD, 2 * block), lambda i: (pair, 0))
+    sums = pl.BlockSpec((1, 8, 2 * block), lambda i: (pair, 0, 0))
+    out = pl.BlockSpec((3, 2 * block, 2 * HD), lambda i: (0, 0, 0))
     return pl.pallas_call(
-        functools.partial(pull_kernel, block),
-        grid=(pairs, 4),
-        in_specs=[smem, smem, smem] + triple_specs(block, pairs) + [rows] * 4 + [wide] * 2 + [sums] * 2,
+        functools.partial(pull_kernel, block, pair),
+        grid=(4,),
+        in_specs=[smem, smem, smem] + triples * 4 + [rows] * 4 + [wide] * 2 + [sums] * 2,
         out_specs=[out, out],
-        out_shape=[jax.ShapeDtypeStruct((3, 2 * block, width), BF)] * 2,
+        out_shape=[jax.ShapeDtypeStruct((3, 2 * block, 2 * HD), BF)] * 2,
         scratch_shapes=[
             pltpu.VMEM((length, 2 * HD), BF),
             pltpu.VMEM((length, 2 * HD), BF),
@@ -721,9 +752,162 @@
             pltpu.VMEM((PIECE, block), F32),
         ],
         compiler_params=pltpu.CompilerParams(vmem_limit_bytes=VMEM_LIMIT),
-        cost_estimate=pl.CostEstimate(flops=25 * length * length * width // 2, bytes_accessed=30 * block * width, transcendentals=0),
+        cost_estimate=took(22),
         name="attend_pull",
     )(slopes, starts, me, *[b for b in blocks for _ in range(3)], *grads, *exacts, *log_totals)
+
+
+def head_columns(refs, quarter, first, last):
+    return jnp.concatenate(
+        [refs[odd][chip, 1 - quarter if odd else quarter, :, first:last] for chip in range(4) for odd in range(2)], axis=0
+    )
+
+
+def in_vmem(count):
+    return [pl.BlockSpec(memory_space=pltpu.VMEM)] * count
+
+
+def call_once(kernel, name, outs, args, us, scalars=0):
+    return pl.pallas_call(
+        kernel,
+        in_specs=[pl.BlockSpec(memory_space=pltpu.SMEM)] * scalars + in_vmem(len(args) - scalars),
+        out_specs=in_vmem(len(outs)),
+        out_shape=outs,
+        compiler_params=pltpu.CompilerParams(vmem_limit_bytes=VMEM_LIMIT),
+        cost_estimate=took(us),
+        name=name,
+    )(*args)
+
+
+def project_kernel(rows_ref, bias_ref, *rest):
+    weight_refs, out_refs = rest[:2], rest[2:]
+    rows = rows_ref[...]
+    for quarter in (1, 0):
+        out = dot_nn(rows, head_columns(weight_refs, quarter, 0, 768)) + bias_ref[quarter:quarter + 1]
+        out_refs[quarter][...] = out.astype(BF)
+
+
+def project(rows, bias, pieces):
+    out = jax.ShapeDtypeStruct((rows.shape[0], 768), BF)
+    return call_once(project_kernel, "project", [out, out], [rows, bias, *pieces], 5)
+
+
+def mix_term(mixed_refs, weight_refs):
+    rows = jnp.concatenate([ref[...] for ref in mixed_refs], axis=1)
+    weight = jnp.concatenate([head_columns(weight_refs, quarter, 768, 1024) for quarter in range(2)], axis=1)
+    return dot_nt(rows, weight)
+
+
+def mix_far_kernel(mine_ref, other_ref, *rest):
+    rest[2][...] = mix_term((mine_ref, other_ref), rest[:2]).astype(BF)
+
+
+def mix_far(mine, other, pieces):
+    out = jax.ShapeDtypeStruct((mine.shape[0], 1024), BF)
+    return call_once(mix_far_kernel, "mix_far", [out], [mine, other, *pieces], 4)[0]
+
+
+def mix_near_kernel(mine_ref, other_ref, far_ref, resid_ref, vector_ref, *rest):
+    weight_refs, (mid_ref, normed_ref, flip_ref) = rest[:2], rest[2:]
+    term = mix_term((mine_ref, other_ref), weight_refs)
+    mid = resid_ref[...] + (term + far_ref[...].astype(F32) + vector_ref[2:3])
+    mid_ref[...] = mid
+    normed = (normalize(mid)[0] * vector_ref[3:4] + vector_ref[4:5]).astype(BF)
+    normed_ref[...] = normed
+    flip_ref[...] = flipped(normed)
+
+
+def mix_near(mine, other, far, resid, vectors, pieces):
+    outs = [
+        jax.ShapeDtypeStruct(resid.shape, F32),
+        jax.ShapeDtypeStruct(resid.shape, BF),
+        jax.ShapeDtypeStruct(resid.shape, BF),
+    ]
+    return call_once(mix_near_kernel, "mix_near", outs, [mine, other, far, resid, vectors, *pieces], 6)
+
+
+def unmix_kernel(grad_ref, *rest):
+    weight_refs, out_refs = rest[:2], rest[2:]
+    grad = grad_ref[...]
+    for quarter in (1, 0):
+        out_refs[quarter][...] = dot_nn(grad, head_columns(weight_refs, quarter, 768, 1024)).astype(BF)
+
+
+def unmix(grad, pieces):
+    out = jax.ShapeDtypeStruct((grad.shape[0], 256), BF)
+    return call_once(unmix_kernel, "unmix", [out, out], [grad, *pieces], 4)
+
+
+def unproject_term(grad_refs, weight_refs, first):
+    rows = jnp.concatenate(
+        [ref[part, first:first + 512] for pair in grad_refs for part in range(3) for ref in pair], axis=1
+    )
+    weight = jnp.concatenate([head_columns(weight_refs, quarter, 0, 768) for quarter in range(2)], axis=1)
+    return dot_nt(rows, weight)
+
+
+def unproject_far_kernel(*rest):
+    rest[6][...] = unproject_term((rest[0:2], rest[2:4]), rest[4:6], 512).astype(BF)
+
+
+def unproject_far(mine, other, pieces):
+    out = jax.ShapeDtypeStruct((512, 1024), BF)
+    return call_once(unproject_far_kernel, "unproject_far", [out], [*mine, *other, *pieces], 6)[0]
+
+
+def unproject_near_kernel(last, own_ref, *rest):
+    mine, other, rest = rest[0:2], rest[2:4], rest[4:]
+    far_ref, resid_ref, grad_mid_ref, vector_ref, rest = *rest[:4], rest[4:]
+    weight_refs, (grad_ref, low_ref, sums_ref) = rest[:2], rest[2:]
+    term = unproject_term((mine, other), weight_refs, 0) + far_ref[...].astype(F32)
+    grad_norm, grad_gain, grad_shift = norm_pull(resid_ref[...], vector_ref[0:1], term)
+    grad = grad_mid_ref[...] + grad_norm
+    grad_ref[...] = grad
+    if last:
+        put_turned(low_ref, own_ref[0], grad.astype(BF))
+    else:
+        low_ref[...] = flipped(grad).astype(BF)
+    sums_ref[...] = jnp.concatenate([grad_gain, grad_shift, jnp.zeros((6, grad.shape[1]), F32)], axis=0)
+
+
+def unproject_near(last, own_keep, mine, other, far, resid, grad_mid, vectors, pieces):
+    outs = [
+        jax.ShapeDtypeStruct(resid.shape, F32),
+        jax.ShapeDtypeStruct(resid.shape, BF),
+        jax.ShapeDtypeStruct((8, resid.shape[1]), F32),
+    ]
+    args = [own_keep, *mine, *other, far, resid, grad_mid, vectors, *pieces]
+    kernel = functools.partial(unproject_near_kernel, last)
+    return call_once(kernel, "unproject_near", outs, args, 9, scalars=1)
+
+
+def head_grads_kernel(near_ref, far_ref, grad_near_ref, grad_far_ref, *rest):
+    pairs, rest = (rest[0:2], rest[2:4]), rest[4:]
+    mixed_refs, out_refs, bias_ref = (rest[0:2], rest[2:4]), rest[4:6], rest[6]
+    rows_t = jnp.concatenate([near_ref[...], far_ref[...]], axis=0).T
+    grad_t = jnp.concatenate([grad_near_ref[...], grad_far_ref[...]], axis=0).T
+    for quarter, refs in enumerate(pairs):
+        grads = [jnp.concatenate([ref[part] for ref in refs], axis=1) for part in range(3)]
+        for part in range(4):
+            if part < 3:
+                term = dot_nn(rows_t, grads[part])
+            else:
+                term = dot_nn(grad_t, jnp.concatenate([m[...] for m in mixed_refs[quarter]], axis=0))
+            term = term.astype(BF)
+            for index in range(8):
+                chip, odd = index // 2, index % 2
+                place = 1 - quarter if odd else quarter
+                out_refs[odd][chip, place, :, part * 256:(part + 1) * 256] = term[index * 128:(index + 1) * 128]
+        for row, part in ((0, 0), (1, 2)):
+            total = jnp.sum(grads[part].astype(F32), axis=0, keepdims=True)
+            bias_ref[2 * quarter + row:2 * quarter + row + 1, :] = total
+    bias_ref[4:8, :] = jnp.zeros((4, 256), F32)
+
+
+def head_grads(near, far, grad_near, grad_far, mine, other, mixed_mine, mixed_other):
+    outs = [jax.ShapeDtypeStruct((4, 2, 128, 1024), BF)] * 2 + [jax.ShapeDtypeStruct((8, 256), F32)]
+    args = [near, far, grad_near, grad_far, *mine, *other, *mixed_mine, *mixed_other]
+    return call_once(head_grads_kernel, "head_grads", outs, args, 10)
 
 
 GELU_A = 0.7978845608028654
@@ -748,323 +932,303 @@
     return jnp.concatenate([ref[0, :, first:last] for ref in refs], axis=0)
 
 
-def mlp_kernel(normed_ref, mid_ref, vector_ref, bias_ref, *rest):
-    weight_refs, (hidden_ref, active_ref, out_ref, next_ref, acc_ref) = rest[:8], rest[8:]
-    tile = hidden_ref.shape[1]
+def flipped(values):
+    return jnp.concatenate([values[:, (block ^ 1) * 128:(block ^ 1) * 128 + 128] for block in range(8)], axis=1)
+
+
+def put_turned(out_ref, own, values):
+    for block in range(8):
+        here = pl.ds(pl.multiple_of((block ^ own) * 128, 128), 128)
+        out_ref[:, here] = values[:, block * 128:(block + 1) * 128]
+
+
+def enter_kernel(own_ref, direct_ref, moved_ref, vector_ref, resid_ref, normed_ref, flip_ref):
+    own, keep = own_ref[0], own_ref[1]
+    for block in range(8):
+        here = pl.ds(pl.multiple_of((block ^ own) * 128, 128), 128)
+        rows = jnp.where(keep > 0, direct_ref[:, here].astype(F32), moved_ref[:, here].astype(F32))
+        resid_ref[:, block * 128:(block + 1) * 128] = rows
+    values = resid_ref[...]
+    normed_ref[...] = (normalize(values)[0] * vector_ref[0:1] + vector_ref[1:2]).astype(BF)
+    flip_ref[...] = flipped(values).astype(BF)
+
+
+def enter(own_keep, direct, moved, vectors):
+    rows, features = direct.shape
+    smem = pl.BlockSpec(memory_space=pltpu.SMEM)
+    vmem = pl.BlockSpec(memory_space=pltpu.VMEM)
+    return pl.pallas_call(
+        enter_kernel,
+        in_specs=[smem, vmem, vmem, vmem],
+        out_specs=[vmem, vmem, vmem],
+        out_shape=[
+            jax.ShapeDtypeStruct((rows, features), F32),
+            jax.ShapeDtypeStruct((rows, features), BF),
+            jax.ShapeDtypeStruct((rows, features), BF),
+        ],
+        compiler_params=pltpu.CompilerParams(vmem_limit_bytes=VMEM_LIMIT),
+        cost_estimate=took(4),
+        name="enter",
+    )(own_keep, direct, moved, vectors)
+
+
+def half_specs(tile):
+    def spec(half):
+        return pl.BlockSpec((2, 128, 2 * tile), lambda f: (0, 0, jnp.clip(f - 2 * half, 0, 1)))
+
+    return [spec(half) for half in range(2) for _ in range(4)]
+
+
+def by_half(step, weight_refs, body):
+    @pl.when(step < 2)
+    def _():
+        body(weight_refs[:4])
+
+    @pl.when(step >= 2)
+    def _():
+        body(weight_refs[4:])
+
+
+def joined(refs, first, last):
+    return jnp.concatenate([ref[core, :, first:last] for ref in refs for core in range(2)], axis=0)
+
+
+GELU_A = 0.7978845608028654
+GELU_B = 0.044715
+
+
+def normalize(values):
+    centred = values - jnp.mean(values, axis=-1, keepdims=True)
+    spread = lax.rsqrt(jnp.mean(centred * centred, axis=-1, keepdims=True) + NORM_EPS)
+    return centred * spread, spread
+
+
+def norm_pull(values, gain, grad):
+    unit, spread = normalize(values)
+    grad_unit = grad * gain
+    inner = grad_unit - jnp.mean(grad_unit, axis=-1, keepdims=True)
+    inner = inner - unit * jnp.mean(grad_unit * unit, axis=-1, keepdims=True)
+    return spread * inner, jnp.sum(grad * unit, axis=0, keepdims=True), jnp.sum(grad, axis=0, keepdims=True)
+
+
+def mlp_kernel(normed_ref, other_ref, bias_ref, *rest):
+    weight_refs, (hidden_ref, active_ref, near_ref, away_ref, acc_ref) = rest[:8], rest[8:]
+    rows, tile = normed_ref.shape[0], hidden_ref.shape[1]
     step = pl.program_id(0)
-    hidden = dot_nn(normed_ref[...], joined(weight_refs, 0, tile)) + bias_ref[...]
-    inner = jnp.tanh(GELU_A * (hidden + GELU_B * hidden * hidden * hidden))
-    active = (0.5 * hidden * (1.0 + inner)).astype(BF)
-    hidden_ref[...] = hidden.astype(BF)
-    active_ref[...] = active
-    term = dot_nt(active, joined(weight_refs, tile, 2 * tile))
 
     @pl.when(step == 0)
     def _():
-        acc_ref[...] = term
-
-    @pl.when(step > 0)
-    def _():
-        acc_ref[...] += term
+        acc_ref[...] = jnp.zeros_like(acc_ref)
+
+    def body(refs):
+        expand, reduce = joined(refs, 0, tile), joined(refs, tile, 2 * tile)
+        for first, ref in ((0, normed_ref), (rows, other_ref)):
+            hidden = dot_nn(ref[...], expand) + bias_ref[...]
+            inner = jnp.tanh(GELU_A * (hidden + GELU_B * hidden * hidden * hidden))
+            active = (0.5 * hidden * (1.0 + inner)).astype(BF)
+            hidden_ref[first:first + rows] = hidden.astype(BF)
+            active_ref[first:first + rows] = active
+            acc_ref[first:first + rows] += dot_nt(active, reduce)
+
+    by_half(step, weight_refs, body)
 
     @pl.when(step == pl.num_programs(0) - 1)
     def _():
-        out = mid_ref[...] + (acc_ref[...] + vector_ref[5:6])
-        out_ref[...] = out
-        next_ref[...] = (normalize(out)[0] * vector_ref[6:7] + vector_ref[7:8]).astype(BF)
-
-
-def mlp_forward(normed, mid, vectors, bias, bundles):
+        near_ref[...] = acc_ref[:rows]
+        away_ref[...] = flipped(acc_ref[rows:]).astype(BF)
+
+
+def mlp_forward(normed, other, bias, weights):
     rows, features = normed.shape
     units = bias.shape[1]
     tile = 512
     whole = pl.BlockSpec((rows, features), lambda f: (0, 0))
-    tiles = pl.BlockSpec((rows, tile), lambda f: (0, f))
-    weight_spec = pl.BlockSpec((1, 128, 2 * tile), lambda f: (f // 2, 0, f % 2))
+    tiles = pl.BlockSpec((2 * rows, tile), lambda f: (0, f))
     return pl.pallas_call(
         mlp_kernel,
         grid=(units // tile,),
-        in_specs=[whole, whole, pl.BlockSpec((8, features), lambda f: (0, 0)), pl.BlockSpec((1, tile), lambda f: (0, f))]
-        + [weight_spec] * 8,
+        in_specs=[whole, whole, pl.BlockSpec((1, tile), lambda f: (0, f))] + half_specs(tile),
         out_specs=[tiles, tiles, whole, whole],
         out_shape=[
-            jax.ShapeDtypeStruct((rows, units), BF),
-            jax.ShapeDtypeStruct((rows, units), BF),
+            jax.ShapeDtypeStruct((2 * rows, units), BF),
+            jax.ShapeDtypeStruct((2 * rows, units), BF),
             jax.ShapeDtypeStruct((rows, features), F32),
             jax.ShapeDtypeStruct((rows, features), BF),
         ],
-        scratch_shapes=[pltpu.VMEM((rows, features), F32)],
+        scratch_shapes=[pltpu.VMEM((2 * rows, features), F32)],
         compiler_params=pltpu.CompilerParams(vmem_limit_bytes=VMEM_LIMIT),
-        cost_estimate=pl.CostEstimate(flops=4 * rows * features * units, bytes_accessed=6 * features * units, transcendentals=0),
+        cost_estimate=took(18),
         name="mlp_forward",
-    )(normed, mid, vectors, bias, *bundles)
-
-
-def mlp_pull_kernel(grad_ref, mid_ref, vector_ref, hidden_ref, *rest):
+    )(normed, other, bias, *weights)
+
+
+def mlp_close_kernel(last, own_ref, near_ref, got_ref, mid_ref, vector_ref, out_ref, next_ref):
+    out = mid_ref[...] + (near_ref[...] + got_ref[...].astype(F32) + vector_ref[5:6])
+    out_ref[...] = out
+    if last:
+        put_turned(next_ref, own_ref[0], out.astype(BF))
+    else:
+        next_ref[...] = (normalize(out)[0] * vector_ref[6:7] + vector_ref[7:8]).astype(BF)
+
+
+def mlp_close(last, own_keep, near, got, mid, vectors):
+    outs = [jax.ShapeDtypeStruct(mid.shape, F32), jax.ShapeDtypeStruct(mid.shape, BF)]
+    args = [own_keep, near, got, mid, vectors]
+    return call_once(functools.partial(mlp_close_kernel, last), "mlp_close", outs, args, 3, scalars=1)
+
+
+def mlp_pull_kernel(grad_ref, other_ref, hidden_ref, *rest):
     weight_refs = rest[:8]
-    grad_hidden_ref, grad_bias_ref, grad_mid_ref, grad_low_ref, sums_ref, acc_ref, low_ref = rest[8:]
-    tile = hidden_ref.shape[1]
+    grad_hidden_ref, grad_bias_ref, near_ref, away_ref, acc_ref, low_ref = rest[8:]
+    rows, tile = grad_ref.shape[0], hidden_ref.shape[1]
     step = pl.program_id(0)
 
     @pl.when(step == 0)
     def _():
-        low_ref[...] = grad_ref[...].astype(BF)
-
-    hidden = hidden_ref[...].astype(F32)
-    squared = hidden * hidden
-    inner = jnp.tanh(GELU_A * hidden * (1.0 + GELU_B * squared))
-    slope = 0.5 * (1.0 + inner) + 0.5 * hidden * (1.0 - inner * inner) * (GELU_A * (1.0 + 3.0 * GELU_B * squared))
-    grad_hidden = dot_nn(low_ref[...], joined(weight_refs, tile, 2 * tile)) * slope
-    grad_bias_ref[...] = jnp.sum(grad_hidden, axis=0, keepdims=True)
-    grad_hidden = grad_hidden.astype(BF)
-    grad_hidden_ref[...] = grad_hidden
-    term = dot_nt(grad_hidden, joined(weight_refs, 0, tile))
-
-    @pl.when(step == 0)
-    def _():
-        acc_ref[...] = term
-
-    @pl.when(step > 0)
-    def _():
-        acc_ref[...] += term
+        low_ref[:rows] = grad_ref[...].astype(BF)
+        low_ref[rows:] = other_ref[...]
+        acc_ref[...] = jnp.zeros_like(acc_ref)
+
+    def body(refs):
+        expand, reduce = joined(refs, 0, tile), joined(refs, tile, 2 * tile)
+        total = jnp.zeros((1, tile), F32)
+        for first in (0, rows):
+            here = slice(first, first + rows)
+            hidden = hidden_ref[here].astype(F32)
+            squared = hidden * hidden
+            inner = jnp.tanh(GELU_A * hidden * (1.0 + GELU_B * squared))
+            slope = 0.5 * (1.0 + inner) + 0.5 * hidden * (1.0 - inner * inner) * (GELU_A * (1.0 + 3.0 * GELU_B * squared))
+            grad_hidden = dot_nn(low_ref[here], reduce) * slope
+            total = total + jnp.sum(grad_hidden, axis=0, keepdims=True)
+            grad_hidden = grad_hidden.astype(BF)
+            grad_hidden_ref[here] = grad_hidden
+            acc_ref[here] += dot_nt(grad_hidden, expand)
+        grad_bias_ref[...] = total
+
+    by_half(step, weight_refs, body)
 
     @pl.when(step == pl.num_programs(0) - 1)
     def _():
-        grad = grad_ref[...]
-        grad_norm, grad_gain, grad_shift = norm_pull(mid_ref[...], vector_ref[3:4], acc_ref[...])
-        grad_mid = grad + grad_norm
-        grad_mid_ref[...] = grad_mid
-        grad_low_ref[...] = grad_mid.astype(BF)
-        sums_ref[...] = jnp.concatenate(
-            [
-                jnp.sum(grad_mid, axis=0, keepdims=True),
-                grad_gain,
-                grad_shift,
-                jnp.sum(grad, axis=0, keepdims=True),
-                jnp.zeros((4, grad.shape[1]), F32),
-            ],
-            axis=0,
-        )
-
-
-def mlp_backward(grad, mid, vectors, hidden, bundles):
+        near_ref[...] = acc_ref[:rows]
+        away_ref[...] = flipped(acc_ref[rows:]).astype(BF)
+
+
+def mlp_backward(grad, other, hidden, weights):
     rows, features = grad.shape
     units = hidden.shape[1]
     tile = 512
     whole = pl.BlockSpec((rows, features), lambda f: (0, 0))
-    tiles = pl.BlockSpec((rows, tile), lambda f: (0, f))
-    eight = pl.BlockSpec((8, features), lambda f: (0, 0))
-    weight_spec = pl.BlockSpec((1, 128, 2 * tile), lambda f: (f // 2, 0, f % 2))
+    tiles = pl.BlockSpec((2 * rows, tile), lambda f: (0, f))
     return pl.pallas_call(
         mlp_pull_kernel,
         grid=(units // tile,),
-        in_specs=[whole, whole, eight, tiles] + [weight_spec] * 8,
-        out_specs=[tiles, pl.BlockSpec((1, tile), lambda f: (0, f)), whole, whole, eight],
+        in_specs=[whole, whole, tiles] + half_specs(tile),
+        out_specs=[tiles, pl.BlockSpec((1, tile), lambda f: (0, f)), whole, whole],
         out_shape=[
-            jax.ShapeDtypeStruct((rows, units), BF),
+            jax.ShapeDtypeStruct((2 * rows, units), BF),
             jax.ShapeDtypeStruct((1, units), F32),
             jax.ShapeDtypeStruct((rows, features), F32),
             jax.ShapeDtypeStruct((rows, features), BF),
-            jax.ShapeDtypeStruct((8, features), F32),
         ],
-        scratch_shapes=[pltpu.VMEM((rows, features), F32), pltpu.VMEM((rows, features), BF)],
+        scratch_shapes=[pltpu.VMEM((2 * rows, features), F32), pltpu.VMEM((2 * rows, features), BF)],
         compiler_params=pltpu.CompilerParams(vmem_limit_bytes=VMEM_LIMIT),
-        cost_estimate=pl.CostEstimate(flops=4 * rows * features * units, bytes_accessed=6 * features * units, transcendentals=0),
+        cost_estimate=took(22),
         name="mlp_backward",
-    )(grad, mid, vectors, hidden, *bundles)
-
-
-def mlp_weights_kernel(grad_ref, normed_ref, active_ref, grad_hidden_ref, *rest):
-    out_refs, (grad_t_ref, normed_t_ref) = rest[:8], rest[8:]
-    tile = active_ref.shape[1]
-
+    )(grad, other, hidden, *weights)
+
+
+def mlp_open_kernel(near_ref, got_ref, mid_ref, grad_ref, vector_ref, grad_mid_ref, grad_low_ref, sums_ref):
+    grad = grad_ref[...]
+    term = near_ref[...] + got_ref[...].astype(F32)
+    grad_norm, grad_gain, grad_shift = norm_pull(mid_ref[...], vector_ref[3:4], term)
+    grad_mid = grad + grad_norm
+    grad_mid_ref[...] = grad_mid
+    grad_low_ref[...] = grad_mid.astype(BF)
+    rows = [jnp.sum(grad_mid, axis=0, keepdims=True), grad_gain, grad_shift, jnp.sum(grad, axis=0, keepdims=True)]
+    sums_ref[...] = jnp.concatenate(rows + [jnp.zeros((4, grad.shape[1]), F32)], axis=0)
+
+
+def mlp_open(near, got, mid, grad, vectors):
+    outs = [
+        jax.ShapeDtypeStruct(mid.shape, F32),
+        jax.ShapeDtypeStruct(mid.shape, BF),
+        jax.ShapeDtypeStruct((8, mid.shape[1]), F32),
+    ]
+    return call_once(mlp_open_kernel, "mlp_open", outs, [near, got, mid, grad, vectors], 5)
+
+
+def unit_grads_kernel(second, left_ref, other_ref, right_ref, own_ref, pair_ref, single_ref, left_t_ref):
     @pl.when(pl.program_id(0) == 0)
     def _():
-        grad_t_ref[...] = grad_ref[...].astype(BF).T
-        normed_t_ref[...] = normed_ref[...].T
-
-    grad_expand = dot_nn(normed_t_ref[...], grad_hidden_ref[...]).astype(BF)
-    grad_reduce = dot_nn(grad_t_ref[...], active_ref[...]).astype(BF)
-    for index, out_ref in enumerate(out_refs):
-        here = slice(index * 128, (index + 1) * 128)
-        out_ref[0, :, :tile] = grad_expand[here]
-        out_ref[0, :, tile:] = grad_reduce[here]
-
-
-def mlp_weight_grads(grad, normed, active, grad_hidden):
-    rows, features = grad.shape
-    units = active.shape[1]
+        left_t_ref[...] = jnp.concatenate([left_ref[...].astype(BF), other_ref[...]], axis=0).T
+
+    grad = dot_nn(left_t_ref[...], right_ref[...]).astype(BF)
+    single, direct = (1, 2) if second == "x" else (2, 1)
+    for core in range(2):
+        own_ref[0, core] = grad[core * 128:(core + 1) * 128]
+        single_ref[0, core] = grad[(2 * single + core) * 128:(2 * single + core + 1) * 128]
+        pair_ref[0, 0, core] = grad[(2 * direct + core) * 128:(2 * direct + core + 1) * 128]
+        pair_ref[0, 1, core] = grad[(6 + core) * 128:(7 + core) * 128]
+
+
+def unit_grads(second, left, other, right):
+    rows, features = left.shape
+    units = right.shape[1]
     tile = 512
     whole = pl.BlockSpec((rows, features), lambda f: (0, 0))
-    tiles = pl.BlockSpec((rows, tile), lambda f: (0, f))
-    weight_spec = pl.BlockSpec((1, 128, 2 * tile), lambda f: (f // 2, 0, f % 2))
+    out = pl.BlockSpec((1, 2, 128, tile), lambda f: (f // 2, 0, 0, f % 2))
+    one = jax.ShapeDtypeStruct((2, 2, 128, 1024), BF)
     return pl.pallas_call(
-        mlp_weights_kernel,
+        functools.partial(unit_grads_kernel, second),
         grid=(units // tile,),
-        in_specs=[whole, whole, tiles, tiles],
-        out_specs=[weight_spec] * 8,
-        out_shape=[jax.ShapeDtypeStruct((units // 1024, 128, 2048), BF)] * 8,
-        scratch_shapes=[pltpu.VMEM((features, rows), BF), pltpu.VMEM((features, rows), BF)],
+        in_specs=[whole, whole, pl.BlockSpec((2 * rows, tile), lambda f: (0, f))],
+        out_specs=[out, pl.BlockSpec((1, 2, 2, 128, tile), lambda f: (f // 2, 0, 0, 0, f % 2)), out],
+        out_shape=[one, jax.ShapeDtypeStruct((2, 2, 2, 128, 1024), BF), one],
+        scratch_shapes=[pltpu.VMEM((features, 2 * rows), BF)],
         compiler_params=pltpu.CompilerParams(vmem_limit_bytes=VMEM_LIMIT),
-        cost_estimate=pl.CostEstimate(flops=4 * rows * features * units, bytes_accessed=8 * features * units, transcendentals=0),
-        name="mlp_weight_grads",
-    )(grad, normed, active, grad_hidden)
-
-
-def head_columns(refs, quarter, first, last):
-    return jnp.concatenate(
-        [ref[quarter if index % 2 == 0 else 1 - quarter, :, first:last] for index, ref in enumerate(refs)], axis=0
-    )
-
-
-def in_vmem(count):
-    return [pl.BlockSpec(memory_space=pltpu.VMEM)] * count
-
-
-def call_once(kernel, name, outs, args, flops):
-    moved = sum(a.size * a.dtype.itemsize for a in args) + sum(a.size * a.dtype.itemsize for a in outs)
-    return pl.pallas_call(
-        kernel,
-        in_specs=in_vmem(len(args)),
-        out_specs=in_vmem(len(outs)),
-        out_shape=outs,
-        compiler_params=pltpu.CompilerParams(vmem_limit_bytes=VMEM_LIMIT),
-        cost_estimate=pl.CostEstimate(flops=flops, bytes_accessed=moved, transcendentals=0),
-        name=name,
-    )(*args)
-
-
-def project_kernel(rows_ref, bias_ref, *rest):
-    weight_refs, out_refs = rest[:8], rest[8:]
-    rows = rows_ref[...]
-    for quarter in (1, 0):
-        out = dot_nn(rows, head_columns(weight_refs, quarter, 0, 768)) + bias_ref[quarter:quarter + 1]
-        out_refs[quarter][...] = out.astype(BF)
-
-
-def project(rows, bias, pieces):
-    out = jax.ShapeDtypeStruct((rows.shape[0], 768), BF)
-    return call_once(project_kernel, "project", [out, out], [rows, bias, *pieces], 2 * rows.shape[0] * 1024 * 1536)
-
-
-def mix_term(mixed_refs, weight_refs):
-    rows = jnp.concatenate([ref[...] for ref in mixed_refs], axis=1)
-    weight = jnp.concatenate([head_columns(weight_refs, quarter, 768, 1024) for quarter in range(2)], axis=1)
-    return dot_nt(rows, weight)
-
-
-def mix_far_kernel(mine_ref, other_ref, *rest):
-    rest[8][...] = mix_term((mine_ref, other_ref), rest[:8]).astype(BF)
-
-
-def mix_far(mine, other, pieces):
-    out = jax.ShapeDtypeStruct((mine.shape[0], 1024), BF)
-    return call_once(mix_far_kernel, "mix_far", [out], [mine, other, *pieces], 2 * mine.shape[0] * 512 * 1024)[0]
-
-
-def mix_near_kernel(mine_ref, other_ref, far_ref, resid_ref, vector_ref, *rest):
-    weight_refs, (mid_ref, normed_ref) = rest[:8], rest[8:]
-    term = mix_term((mine_ref, other_ref), weight_refs)
-    mid = resid_ref[...] + (term + far_ref[...].astype(F32) + vector_ref[2:3])
-    mid_ref[...] = mid
-    normed_ref[...] = (normalize(mid)[0] * vector_ref[3:4] + vector_ref[4:5]).astype(BF)
-
-
-def mix_near(mine, other, far, resid, vectors, pieces):
-    outs = [jax.ShapeDtypeStruct(resid.shape, F32), jax.ShapeDtypeStruct(resid.shape, BF)]
-    return call_once(mix_near_kernel, "mix_near", outs, [mine, other, far, resid, vectors, *pieces], 2 * mine.shape[0] * 512 * 1024)
-
-
-def unmix_kernel(grad_ref, *rest):
-    weight_refs, out_refs = rest[:8], rest[8:]
-    grad = grad_ref[...]
-    for quarter in (1, 0):
-        out_refs[quarter][...] = dot_nn(grad, head_columns(weight_refs, quarter, 768, 1024)).astype(BF)
-
-
-def unmix(grad, pieces):
-    out = jax.ShapeDtypeStruct((grad.shape[0], 256), BF)
-    return call_once(unmix_kernel, "unmix", [out, out], [grad, *pieces], 2 * grad.shape[0] * 512 * 1024)
-
-
-def unproject_term(grad_refs, weight_refs, first):
-    rows = jnp.concatenate([ref[part, first:first + 512] for ref in grad_refs for part in range(3)], axis=1)
-    weight = jnp.concatenate([head_columns(weight_refs, quarter, 0, 768) for quarter in range(2)], axis=1)
-    return dot_nt(rows, weight)
-
-
-def unproject_far_kernel(mine_ref, other_ref, *rest):
-    rest[8][...] = unproject_term((mine_ref, other_ref), rest[:8], 512).astype(BF)
-
-
-def unproject_far(mine, other, pieces):
-    out = jax.ShapeDtypeStruct((512, 1024), BF)
-    return call_once(unproject_far_kernel, "unproject_far", [out], [mine, other, *pieces], 2 * 512 * 1536 * 1024)[0]
-
-
-def unproject_near_kernel(mine_ref, other_ref, far_ref, resid_ref, grad_mid_ref, vector_ref, *rest):
-    weight_refs, (grad_ref, low_ref, sums_ref) = rest[:8], rest[8:]
-    term = unproject_term((mine_ref, other_ref), weight_refs, 0) + far_ref[...].astype(F32)
-    grad_norm, grad_gain, grad_shift = norm_pull(resid_ref[...], vector_ref[0:1], term)
-    grad = grad_mid_ref[...] + grad_norm
-    grad_ref[...] = grad
-    low_ref[...] = grad.astype(BF)
-    sums_ref[...] = jnp.concatenate([grad_gain, grad_shift, jnp.zeros((6, grad.shape[1]), F32)], axis=0)
-
-
-def unproject_near(mine, other, far, resid, grad_mid, vectors, pieces):
-    outs = [
-        jax.ShapeDtypeStruct(resid.shape, F32),
-        jax.ShapeDtypeStruct(resid.shape, BF),
-        jax.ShapeDtypeStruct((8, resid.shape[1]), F32),
-    ]
-    args = [mine, other, far, resid, grad_mid, vectors, *pieces]
-    return call_once(unproject_near_kernel, "unproject_near", outs, args, 2 * 512 * 1536 * 1024)
-
-
-def head_grads_kernel(near_ref, far_ref, grad_near_ref, grad_far_ref, mine_ref, other_ref, *rest):
-    mixed_refs, out_refs, bias_ref = (rest[0:2], rest[2:4]), rest[4:12], rest[12]
-    rows_t = jnp.concatenate([near_ref[...], far_ref[...]], axis=0).T
-    grad_t = jnp.concatenate([grad_near_ref[...], grad_far_ref[...]], axis=0).T
-    for quarter, ref in enumerate((mine_ref, other_ref)):
-        for part in range(4):
-            if part < 3:
-                term = dot_nn(rows_t, ref[part])
-            else:
-                term = dot_nn(grad_t, jnp.concatenate([m[...] for m in mixed_refs[quarter]], axis=0))
-            term = term.astype(BF)
-            for index, out_ref in enumerate(out_refs):
-                place = quarter if index % 2 == 0 else 1 - quarter
-                out_ref[place, :, part * 256:(part + 1) * 256] = term[index * 128:(index + 1) * 128]
-        for row, part in ((0, 0), (1, 2)):
-            total = jnp.sum(ref[part].astype(F32), axis=0, keepdims=True)
-            bias_ref[2 * quarter + row:2 * quarter + row + 1, :] = total
-    bias_ref[4:8, :] = jnp.zeros((4, 256), F32)
-
-
-def head_grads(near, far, grad_near, grad_far, mine, other, mixed_mine, mixed_other):
-    outs = [jax.ShapeDtypeStruct((2, 128, 1024), BF)] * 8 + [jax.ShapeDtypeStruct((8, 256), F32)]
-    args = [near, far, grad_near, grad_far, mine, other, *mixed_mine, *mixed_other]
-    return call_once(head_grads_kernel, "head_grads", outs, args, 2 * 1024 * 1024 * 2048)
-
-
-def gather_plane(own):
-    half = own.shape[0] // 2
+        cost_estimate=took(10),
+        name="unit_grads",
+    )(left, other, right)
+
+
+def fetch_heads(piece, core, out):
+    token = yield
+    far = swap(after(piece, token), Z1)
+    token = yield []
+    far = after(far, token)
+    own = jnp.stack([jnp.where(core == 0, piece, far), jnp.where(core == 0, far, piece)])
     from_x = swap(own, XBIT)
     from_y = swap(own, YBIT)
-    across = jnp.concatenate([swap(from_x[:half], YBIT), swap(from_y[half:], XBIT)], axis=0)
-    out = []
-    for quad in (own, from_x, from_y, across):
-        out += [quad, swap(quad, CORE)]
-    return out
-
-
-def scatter_plane(pieces):
-    own, to_x, to_y, across = [pieces[2 * i] + swap(pieces[2 * i + 1], CORE) for i in range(4)]
-    half = own.shape[0] // 2
-    first = own[:half] + swap(to_y[:half], YBIT) + swap(to_x[:half] + swap(across[:half], YBIT), XBIT)
-    second = own[half:] + swap(to_x[half:], XBIT) + swap(to_y[half:] + swap(across[half:], XBIT), YBIT)
-    return first, second
+    token = yield [own]
+    from_x, from_y = after_all((from_x, from_y), token)
+    across = swap(from_y, XBIT)
+    token = yield [from_x, from_y]
+    quads = jnp.stack([own, from_x, from_y, after(across, token)])
+    other = swap(quads, CORE)
+    token = yield [quads]
+    out += [quads, other]
+
+
+def fetch_units(piece, core, first_out, second_out):
+    token = yield
+    piece = after(piece, token)
+    same, cross = swap_some(piece, (0, Z1)), swap_some(piece, (CORE | Z1, CORE))
+    token = yield []
+    same, cross = after_all((same, cross), token)
+    first = jnp.stack([jnp.where(core == 0, piece, same), cross])
+    first_x, first_y = swap(first, XBIT), swap(first, YBIT)
+    second = swap(first, Z0)
+    token = yield [first]
+    first_x, first_y, second = after_all((first_x, first_y, second), token)
+    second_x, second_y = swap(second, XBIT), swap(second, YBIT)
+    token = yield [first_x, first_y, second]
+    second_x, second_y = after_all((second_x, second_y), token)
+    first_across, second_across = swap(first_x, YBIT), swap(second_y, XBIT)
+    token = yield [second_x, second_y]
+    first_across, second_across = after_all((first_across, second_across), token)
+    first_out += [first, first_x, first_y, first_across]
+    second_out += [second, second_x, second_y, second_across]
+    yield [first_across, second_across]
 
 
 def pack_heads(project, output):
@@ -1080,76 +1244,108 @@
     return jnp.stack(parts, axis=2).reshape(128, 2048)
 
 
-def unpack_units(values):
-    shaped = values.reshape(128, 2, 2, 512)
-    return shaped[:, :, 0].reshape(128, 1024), shaped[:, :, 1].reshape(128, 1024).T
-
-
-def fetch_heads(piece, core):
-    far = swap(piece, Z1)
-    return gather_plane(jnp.stack([jnp.where(core == 0, piece, far), jnp.where(core == 0, far, piece)]))
-
-
-def fetch_units(piece):
-    own = jnp.stack([piece, swap(piece, 1), swap(piece, 2), swap(piece, 3)])
-    return own, gather_plane(own)
-
-
-def fetch_small(six, project_bias, expand_bias, own, place, core):
+def fetch_small(six, project_bias, expand_bias, own, core):
     layers = six.shape[1]
     wide = jnp.pad(project_bias, ((0, 0), (0, 0), (0, 96)))
-    piece = jnp.concatenate([six.transpose(1, 0, 2), wide, expand_bias[:, None, :], jnp.zeros((layers, 7, 128), BF)], axis=1)
-    every = lax.all_gather(piece, AXES, axis=0, tiled=False).reshape(8, 4, layers, 16, 128).astype(F32)
-    turned = every[jnp.arange(8) ^ own, 0]
-    native = every[:, place ^ jnp.arange(4)]
+    rows = jnp.concatenate([six.transpose(1, 0, 2), wide, expand_bias[:, None, :]], axis=1).astype(F32)[None]
+    for mask in (CORE, XBIT, YBIT):
+        rows = jnp.concatenate([rows, swap(rows, mask)], axis=0)
+    vectors = rows[:, :, :6].transpose(1, 2, 0, 3).reshape(layers, 6, 1024)
+    local = turn_index(rows[:, :, 6:], own).transpose(1, 2, 0, 3)[None]
+    for mask in (Z0, Z1):
+        local = jnp.concatenate([local, swap(local, mask)], axis=0)
+    native = local.transpose(1, 0, 2, 3, 4)
     out = []
     for layer in range(layers):
-        vectors = turned[:, layer, :6].transpose(1, 0, 2).reshape(6, 1024)
-        following = turned[:, min(layer + 1, layers - 1), :2].transpose(1, 0, 2).reshape(2, 1024)
-        pair = native[:, ::2, layer, 6:8, :32].transpose(1, 2, 0, 3).reshape(2, 2, 256)
+        pair = native[layer, ::2, :2, :, :32].reshape(2, 2, 256)
         pair = jnp.where(core == 0, pair, pair[::-1])
         head_bias = jnp.concatenate([pair[:, 0], jnp.zeros((2, 256), F32), pair[:, 1]], axis=1)
-        unit_bias = native[:, :, layer, 8].transpose(1, 0, 2).reshape(1, 4096)
-        out.append((jnp.concatenate([vectors, following], axis=0), head_bias, unit_bias))
+        unit_bias = native[layer, :, 2].reshape(2, 1, 2048)
+        unit_bias = jnp.where(core == 0, unit_bias[0], unit_bias[1])
+        following = vectors[min(layer + 1, layers - 1), :2]
+        out.append((jnp.concatenate([vectors[layer], following], axis=0), head_bias, unit_bias))
     return out
 
 
-def sum_small(layers, own, core):
-    turn = jnp.arange(8) ^ own
-    rows = []
-    for first_sums, second_sums, unit_sums, head_sums in layers:
-        six = jnp.stack([first_sums[0], first_sums[1], second_sums[0], second_sums[1], second_sums[2], second_sums[3]])
-        heads = head_sums[:4].reshape(2, 2, 256)
-        heads = jnp.where(core == 0, heads, heads[::-1]).reshape(4, 8, 32)[:, turn]
-        heads = jnp.pad(heads, ((0, 0), (0, 0), (0, 96)))
-        rows += [six.reshape(6, 8, 128), unit_sums.reshape(4, 8, 128)[:, turn], heads]
-    rows = jnp.concatenate(rows, axis=0).transpose(1, 0, 2)
+def spread_sums(rows):
     rows = rows.reshape(2, 2, 2, rows.shape[1], 128)
     rows = rows[:, :, 0] + swap(rows[:, :, 1], CORE)
     rows = rows[:, 0] + swap(rows[:, 1], XBIT)
-    rows = rows[0] + swap(rows[1], YBIT)
-    rows = rows.reshape(len(layers), 14, 128)
+    return rows[0] + swap(rows[1], YBIT)
+
+
+def sum_small(layers, own, core):
+    count = len(layers)
+    vectors, biases = [], []
+    for first_sums, second_sums, unit_sums, head_sums in layers:
+        vectors += [first_sums[:2], second_sums[:4]]
+        heads = head_sums[:4].reshape(2, 2, 256)
+        heads = jnp.where(core == 0, heads, heads[::-1]).reshape(4, 8, 32)
+        heads = jnp.pad(heads, ((0, 0), (0, 0), (0, 96)))
+        units = unit_sums.reshape(2, 8, 128)
+        none = jnp.zeros_like(units)
+        biases += [jnp.where(core == 0, units, none), jnp.where(core == 0, none, units), heads]
+    vectors = jnp.concatenate(vectors, axis=0).reshape(6 * count, 8, 128).transpose(1, 0, 2)
+    biases = turn_index(jnp.concatenate(biases, axis=0).transpose(1, 0, 2), own)
+    rows = spread_sums(jnp.concatenate([vectors, biases], axis=1))
+    vectors, biases = rows[:6 * count].reshape(count, 6, 128), rows[6 * count:].reshape(count, 8, 128)
 
     def part(offset):
-        return jnp.concatenate([rows[:, :6], rows[:, 6 + offset:7 + offset], rows[:, 12:14]], axis=1)
+        return jnp.concatenate([vectors, biases[:, offset:offset + 1], biases[:, 6:8]], axis=1)
 
     two = swap(part(2), 2)
-    base = jnp.concatenate([rows[:, :7], rows[:, 10:12]], axis=1)
-    whole = base[:, :7] + two[:, :7] + swap(part(1), 1)[:, :7] + swap(part(3), 3)[:, :7]
-    return whole[:, :6], whole[:, 6], base[:, 7:, :32] + two[:, 7:, :32]
-
-
-def reduce_heads(pieces, core):
-    first, second = (part[0].astype(F32) for part in scatter_plane(pieces))
-    near = jnp.where(core == 0, first, second)
-    away = jnp.where(core == 0, second, first)
-    return unpack_heads(near + swap(away.astype(BF), Z1).astype(F32))
-
-
-def reduce_units(pieces):
-    first, second = scatter_plane(pieces)
-    terms = [first[0], swap(first[1], 1), swap(second[0], 2), swap(second[1], 3)]
-    return unpack_units(sum(term.astype(F32) for term in terms))
+    whole = jnp.concatenate([vectors, biases[:, :1]], axis=1) + two[:, :7] + swap(part(1), 1)[:, :7] + swap(part(3), 3)[:, :7]
+    return whole[:, :6], whole[:, 6], biases[:, 4:6, :32] + two[:, 7:, :32]
+
+
+def reduce_heads(even, odd, core, out):
+    token = yield
+    got = swap(odd, CORE)
+    token = yield []
+    got = after(got, token)
+    low, high = even[:2] + got[:2], even[2:] + got[2:]
+    from_y = swap(high, YBIT)
+    token = yield [low, high]
+    from_y = after(from_y, token)
+    relayed = low[1] + from_y[1]
+    relay = swap(relayed, XBIT)
+    token = yield [relayed]
+    total = low[0] + from_y[0] + after(relay, token)
+    near = jnp.where(core == 0, total[0], total[1])
+    away = jnp.where(core == 0, total[1], total[0])
+    far = swap(away, Z1)
+    token = yield [near, away]
+    out.append(unpack_heads(near.astype(F32) + after(far, token).astype(F32)))
+
+
+def reduce_units(reduce_parts, expand_parts, core, out):
+    yield
+    own_r, pair_r, single_r = reduce_parts
+    from_y = swap(pair_r, YBIT)
+    yield []
+    own_e, pair_e, single_e = expand_parts
+    from_x = swap(pair_e, XBIT)
+    token = yield []
+    from_y = after(from_y, token)
+    relayed_r = single_r + from_y[:, 1]
+    relay_r = swap(relayed_r, XBIT)
+    token = yield [relayed_r]
+    from_x = after(from_x, token)
+    relayed_e = single_e + from_x[:, 1]
+    relay_e = swap(relayed_e, YBIT)
+    token = yield [relayed_e]
+    relay_r, relay_e = after_all((relay_r, relay_e), token)
+    here, away = [
+        jnp.stack([own_r[i] + from_y[i, 0] + relay_r[i], own_e[i] + from_x[i, 0] + relay_e[i]]) for i in range(2)
+    ]
+    got = swap(away, Z0)
+    token = yield [here, away]
+    here = here + after(got, token)
+    same, cross = here[:, 0], here[:, 1]
+    same_got, cross_got = swap_some(same, (0, Z1)), swap_some(cross, (CORE, CORE | Z1))
+    token = yield [same, cross]
+    same_got, cross_got = after_all((same_got, cross_got), token)
+    out.append(jnp.where(core == 0, same, same_got).astype(F32) + cross_got.astype(F32))
 
 
 def fast_device(
@@ -1172,85 +1368,148 @@
     own = lax.axis_index("dp")
     place = lax.axis_index("tensor")
     core = own & 1
+    keep = core == (place >> 1)
+    own_keep = jnp.stack([own, keep.astype(jnp.int32)]).astype(jnp.int32)
     me = (2 * core + (place & 1)).astype(jnp.int32).reshape(1)
     slopes = head_slopes((place ^ (2 * core)) * 4, 4)
-    starts = redeal(picture_start)[0]
+
     six = jnp.stack([first_gain, first_shift, output_bias, second_gain, second_shift, reduce_bias])
-    small = fetch_small(six, project_bias, expand_bias, own, place, core)
     head_piece = [pack_heads(project_weight[i], output_weight[i]) for i in range(LAYERS)]
     unit_piece = [pack_units(expand_weight[i], reduce_weight[i]) for i in range(LAYERS)]
+    heads, units = [[] for i in range(LAYERS)], [([], []) for i in range(LAYERS)]
+    head_tasks = [task(fetch_heads(head_piece[i], core, heads[i])) for i in range(LAYERS)]
+    unit_tasks = [task(fetch_units(unit_piece[i], core, *units[i])) for i in range(LAYERS)]
+
+    advance(layer_input, head_tasks[0])
+    small = fetch_small(six, project_bias, expand_bias, own, core)
     dealt = redeal(layer_input)
-    heads, units = [None] * LAYERS, [None] * LAYERS
-    heads[0] = fetch_heads(head_piece[0], core)
-    quad, units[0] = fetch_units(after(unit_piece[0], dealt))
-    resid = turn_blocks(dealt.astype(F32), own)
-    normed = layer_norm(resid, small[0][0][0], small[0][0][1]).astype(BF)
+    starts = jnp.where(keep, picture_start, redeal(picture_start))[0]
+    advance(layer_input, unit_tasks[0])
+    made = advance(layer_input, head_tasks[0])
+    resid, normed, unused = enter(own_keep, layer_input, after(dealt, *made), small[0][0])
+    made = advance(normed, head_tasks[0])
+    normed = after(normed, *made)
+    advance(normed, head_tasks[0])
     saved = []
     for layer in range(LAYERS):
         vectors, head_bias, unit_bias = small[layer]
+        first, last = layer == 0, layer + 1 == LAYERS
+        far = swap(normed, Z0)
+        if not heads[layer]:
+            advance(normed, head_tasks[layer])
         pieces = heads[layer]
-        far = swap(normed, Z0)
-        if layer + 1 < LAYERS:
-            heads[layer + 1] = fetch_heads(after(head_piece[layer + 1], quad), core)
-            quad, units[layer + 1] = fetch_units(after(unit_piece[layer + 1], far))
         near_mine, near_other = project(normed, head_bias, pieces)
         got_near = swap(near_other, CORE)
-        far_mine, far_other = project(far, head_bias, pieces)
+        made = advance(near_mine, unit_tasks[layer])
+        far_mine, far_other = project(after(far, near_mine, *made), head_bias, pieces)
         got_far = swap(far_other, CORE)
-        blocks = (near_mine, far_mine, got_near, got_far)
+        made = []
+        if first:
+            made += advance(far_mine, head_tasks[1], unit_tasks[1])
+        else:
+            made += advance(far_mine, unit_tasks[layer])
+        blocks = after_all((near_mine, far_mine, got_near, got_far), *made)
         far_mixed, far_send, far_exact, far_log = attend(blocks, 1, slopes, starts, me)
         far_got = swap(far_send, CORE)
-        far_term = swap(mix_far(far_mixed, far_got, pieces), Z0)
-        near_mixed, near_send, near_exact, near_log = attend(blocks, 0, slopes, starts, me)
+        far_part = mix_far(far_mixed, far_got, pieces)
+        far_term = swap(far_part, Z0)
+        made = advance(far_part, unit_tasks[layer])
+        near_blocks = after_all(blocks, far_part, *made)
+        near_mixed, near_send, near_exact, near_log = attend(near_blocks, 0, slopes, starts, me)
         near_got = swap(near_send, CORE)
-        mid, normed_two = mix_near(near_mixed, near_got, far_term, resid, vectors, pieces)
-        hidden, active, out, following = mlp_forward(normed_two, mid, vectors, unit_bias, units[layer])
+        made = []
+        if first:
+            made += advance(near_mixed, unit_tasks[0])
+        else:
+            cotangent_far = redeal(after(cotangent, near_mixed))
+        mid, normed_two, flip_two = mix_near(near_mixed, near_got, after(far_term, near_mixed, *made), resid, vectors, pieces)
+        normed_other = swap(flip_two, CORE)
+        if first:
+            made = advance(mid, unit_tasks[0], head_tasks[1], unit_tasks[1])
+            normed_two = after(normed_two, *made)
+        hidden, active, near_out, away_out = mlp_forward(normed_two, normed_other, unit_bias, units[layer][0] + units[layer][1])
+        got_out = swap(away_out, CORE)
+        if not last:
+            made = advance(near_out, head_tasks[layer + 1])
+            got_out = after(got_out, *made)
+        out, following = mlp_close(last, own_keep, near_out, got_out, mid, vectors)
+        if not last:
+            advance(out, head_tasks[layer + 1])
+        else:
+            grad, unused, flip_grad = enter(own_keep, cotangent, after(cotangent_far, out), vectors)
+            grad_other = swap(flip_grad, CORE)
         saved.append((
-            resid, normed, far, blocks, (near_exact, far_exact), (near_log, far_log),
-            (near_mixed, far_mixed), (near_got, far_got), mid, normed_two, hidden, active,
+            resid, normed, far, blocks, (near_exact, far_exact), (near_log, far_log), (near_mixed, far_mixed),
+            (near_got, far_got), mid, normed_two, normed_other, hidden, active,
         ))
         resid, normed = out, following
-        if layer == 0:
-            grad = turn_blocks(redeal(after(cotangent, far_term)).astype(F32), own)
-    layer_output = redeal(turn_blocks(resid.astype(BF), own))
-    sums, head_grad, unit_grad = [None] * LAYERS, [None] * LAYERS, [None] * LAYERS
+    layer_output = jnp.where(keep, normed, redeal(normed))
+    sums = [None] * LAYERS
+    head_grad, unit_grad = ([[] for i in range(LAYERS)] for j in range(2))
+    pending = []
     for layer in reversed(range(LAYERS)):
         vectors, pieces = small[layer][0], heads[layer]
         (
-            resid, normed, far, blocks, exacts, logs, mixed, mixed_got, mid, normed_two, hidden, active,
+            resid, normed, far, blocks, exacts, logs, mixed, mixed_got, mid, normed_two, normed_other, hidden, active,
         ) = saved[layer]
-        grad_hidden, unit_sums, grad_mid, grad_low, second_sums = mlp_backward(grad, mid, vectors, hidden, units[layer])
+        grad_hidden, unit_sums, near_term, away_term = mlp_backward(grad, grad_other, hidden, units[layer][0] + units[layer][1])
+        got_term = after(swap(away_term, CORE), *advance(near_term, *pending[:1]))
+        grad_mid, grad_low, second_sums = mlp_open(near_term, got_term, mid, grad, vectors)
         grad_far = swap(grad_low, Z0)
-        unit_pieces = mlp_weight_grads(grad, normed_two, active, grad_hidden)
-        near_mine, near_other = unmix(grad_low, pieces)
+        made = advance(grad_low, *pending[1:])
+        reduce_parts = unit_grads("x", grad, grad_other, after(active, grad_low, *made))
+        near_mine, near_other = unmix(after(grad_low, reduce_parts[0]), pieces)
         got_near = swap(near_other, CORE)
-        far_mine, far_other = unmix(grad_far, pieces)
+        expand_parts = unit_grads("y", normed_two, normed_other, after(grad_hidden, near_mine))
+        unit_task = task(reduce_units(reduce_parts, expand_parts, core, unit_grad[layer]))
+        advance(None, unit_task)
+        advance(None, unit_task)
+        far_mine, far_other = unmix(after(grad_far, expand_parts[0]), pieces)
         got_far = swap(far_other, CORE)
-        grads_mixed = (near_mine, far_mine, got_near, got_far)
-        mine, away = attend_pull(blocks, grads_mixed, exacts, logs, slopes, starts, me)
-        other = swap(away, CORE)
-        far_term = swap(unproject_far(mine, other, pieces), Z0)
-        *head_pieces, head_sums = head_grads(normed, far, grad_low, grad_far, mine, other, mixed, mixed_got)
-        grad, grad_low, first_sums = unproject_near(mine, other, far_term, resid, grad_mid, vectors, pieces)
+        made = advance(far_mine, *pending)
+        grads_mixed = after_all((near_mine, far_mine, got_near, got_far), *made)
+        mine_0, away_0 = attend_pull(0, blocks, grads_mixed, exacts, logs, slopes, starts, me)
+        other_0 = swap(away_0, CORE)
+        made = advance(mine_0, unit_task, *pending)
+        grads_mixed = after_all(grads_mixed, mine_0, *made)
+        mine_1, away_1 = attend_pull(1, blocks, grads_mixed, exacts, logs, slopes, starts, me)
+        other_1 = swap(away_1, CORE)
+        other_1 = after(other_1, *advance(mine_1, unit_task))
+        mine, other = (mine_0, mine_1), (other_0, other_1)
+        far_part = unproject_far(mine, other, pieces)
+        far_term = swap(far_part, Z0)
+        even, odd, head_sums = head_grads(normed, far, grad_low, after(grad_far, far_part), mine, other, mixed, mixed_got)
+        head_task = task(reduce_heads(even, odd, core, head_grad[layer]))
+        advance(None, head_task)
+        made = advance(head_sums, unit_task) if layer == 0 else [head_sums]
+        grad, grad_low, first_sums = unproject_near(
+            layer == 0, own_keep, mine, other, after(far_term, *made), resid, grad_mid, vectors, pieces
+        )
         sums[layer] = (first_sums, second_sums, unit_sums, head_sums)
-        head_grad[layer] = reduce_heads(head_pieces, core)
-        unit_grad[layer] = reduce_units(unit_pieces)
-    input_grad = redeal(turn_blocks(grad_low, own))
-    six, unit_sum, head_sum = sum_small(sums, own, core)
+        if layer > 0:
+            grad_other = swap(grad_low, CORE)
+            grad = after(grad, *advance(grad, head_task))
+        pending = [unit_task, head_task]
+    input_far = redeal(grad_low)
+    sums = after_all([row for layer in sums for row in layer], grad)
+    while len(head_grad[0]) + len(unit_grad[0]) < 2:
+        made = advance(grad, *pending)
+    input_grad = jnp.where(keep, grad_low, input_far)
+    six, unit_sum, head_sum = sum_small([sums[4 * i:4 * i + 4] for i in range(LAYERS)], own, core)
     return (
         layer_output,
         input_grad,
         six[:, 0],
         six[:, 1],
-        jnp.stack([g[0] for g in head_grad]),
+        jnp.stack([g[0][0] for g in head_grad]),
         head_sum,
-        jnp.stack([g[1] for g in head_grad]),
+        jnp.stack([g[0][1] for g in head_grad]),
         six[:, 2],
         six[:, 3],
         six[:, 4],
-        jnp.stack([g[0] for g in unit_grad]),
+        jnp.stack([g[0][1] for g in unit_grad]),
         unit_sum,
-        jnp.stack([g[1] for g in unit_grad]),
+        jnp.stack([g[0][0].T for g in unit_grad]),
         six[:, 5],
     )
 

time: 1140 us -> 944 us (0.83)
  blocking collectives: 86.8 us -> 0 us
  starting transfers between devices: 171 us -> 96.8 us
  local copies, waits for them, and re-layouts: 108 us -> 44.4 us
  waiting for transfers between devices: 310 us -> 352 us
  other arithmetic: 72.5 us -> 38.7 us
  Pallas kernels: 370 us -> 403 us
    all_gather x1 -> x0, blocking collectives: 86.8 us -> none  [fetch_small(): lax.all_gather(piece, AXES, axis=0, tiled=False)]
    ppermute x116 -> x85, starting transfers between devices: 141 us -> 75.4 us  [swap(): return lax.ppermute(values, AXES, [(i, i ^ mask) for i in range(32)])]
    pallas_call x22 -> x32, Pallas kernels: 218 us -> 260 us  [the longest x22 131 us: call_once(): pl.pallas_call(kernel, in_specs=[pl.BlockSpec(memory_space=pltpu.SMEM)] *...]
    ppermute x5 -> x13, waiting for transfers between devices: 0.01 us -> 42.1 us  [the longest x8 42.1 us: swap_some(): lax.ppermute(values, AXES, [pair for pair in pairs if pair[0] != pair[1]])]
    add x31 -> x24, other arithmetic: 47.4 us -> 22.8 us  [the longest x2 4.51 us: reduce_units(): own_e[i] + from_x[i, 0] + relay_e[i]]
    slice x28 -> x19, local copies, waits for them, and re-layouts: 24.4 us -> 2.3 us  [the longest x4 1.53 us: sum_small(): vectors += [first_sums[:2], second_sums[:4]]]
    unnamed x264 -> x155, local copies, waits for them, and re-layouts: 38.7 us -> 29.4 us
    ppermute x5 -> x13, starting transfers between devices: 30.3 us -> 21.3 us  [the longest x8 14.3 us: swap_some(): lax.ppermute(values, AXES, [pair for pair in pairs if pair[0] != pair[1]])]
  transfers between devices with their start and end apart: 121 -> 98, of which waited for: 24 -> 43; matrix products, arithmetic and copies ran while one was open for 15% -> 6% of each run, Pallas kernels for 29% -> 38%
where the time goes in v3:
time: 944 us; the launch traced here: 937 us
  Pallas kernels  403 us (43%)
  waiting for transfers between devices  352 us (37%)
  starting transfers between devices  96.8 us (10%)
  local copies, waits for them, and re-layouts  44.4 us (5%)
  other arithmetic  38.7 us (4%)
    ppermute x85, waiting for transfers between devices, swap(): return lax.ppermute(values, AXES, [(i, i ^ mask) for i in range(32)])  310 us
    pallas_call x22, Pallas kernels, call_once(): pl.pallas_call(kernel, in_specs=[pl.BlockSpec(memory_space=pltpu.SMEM)] *...  131 us
    pallas_call x4, Pallas kernels, attend_pull(): pl.pallas_call(functools.partial(pull_kernel, block, pair), grid=(4,), in...  85 us
    ppermute x85, starting transfers between devices, swap(): return lax.ppermute(values, AXES, [(i, i ^ mask) for i in range(32)])  75.4 us
    pallas_call x4, Pallas kernels, attend(): pl.pallas_call(functools.partial(attend_kernel, block, rest_bit), grid=(p...  66.8 us
    ppermute x8, waiting for transfers between devices, swap_some(): lax.ppermute(values, AXES, [pair for pair in pairs if pair[0] != pair[1]])  42.1 us
    pallas_call x2, Pallas kernels, mlp_backward(): pl.pallas_call(mlp_pull_kernel, grid=(units // tile,), in_specs=[whole, w...  41.3 us
    pallas_call x4, Pallas kernels, unit_grads(): pl.pallas_call(functools.partial(unit_grads_kernel, second), grid=(units...  36 us
  transfers between devices with their start and end apart: 98, of which 43 were waited for; matrix products, arithmetic and copies ran while one was open for 6% of the time, Pallas kernels for 38%

profile of v3, /device:TPU:0, one launch (start us, length us, event | category | flops | bytes accessed | tf_op | source)
XLA Modules:
  0.0 936.9 jit_solution(16861222392771580426)
XLA Ops:
  22.9 19.3 %collective-permute-done.2 = bf16[128,1024]{1,0:T(8,128)(2,1)S(1)} collective-permute-done((bf16[128,1024]{1,0:T(8,128)(2,1)S(1)}, bf16[128,1024]{1,0:T(8,128)(2,1)S(1)}, u32[]{:S(2)}, u32[]{:S(2)}) %collective-permute-start.2) | collective-permute-done | bytes 262176 | tf_op jit(solution)/shard_map/ppermute | solution.py:426
  50.2 7.0 collective-permute-done.6
  58.7 7.6 collective-permute-done.10
  91.4 22.7 %collective-permute-done.12.rows_ref.far_ref = bf16[512,1024]{1,0:T(8,128)(2,1)S(1)} collective-permute-done((bf16[512,1024]{1,0:T(8,128)(2,1)}, bf16[512,1024]{1,0:T(8,128)(2,1)S(1)}, u32[]{:S(2)}, u32[]{:S(2)}) %collective-permute-start.12) | collective-permute-done | bytes 1048608 | tf_op jit(solution)/shard_map/ppermute | solution.py:426
  125.4 18.8 %attend.4 = (bf16[512,256]{1,0:T(8,128)(2,1)}, bf16[512,256]{1,0:T(8,128)(2,1)}, f32[256,1024]{1,0:T(8,128)}, f32[2,8,1024]{2,1,0:T(8,128)}) custom-call(f32[4]{0:T(128)} %multiply_exponential_fusion.slope_ref, s32[2]{0:T(128)} %fusion.22.start_ref, s32[1]{0:T(128)} %bitcast.3.me_ref, bf16[512,768]{1,0:T(8,128)(2,1)} %get-tuple-element.243.rest_0_.rest_1_.rest_2_, ...), custom_call_target="tpu_custom_call" | custom-call | flops 8499999744 | bytes 1 | tf_op jit(solution)/shard_map/attend/pallas_call | solution.py:603
  164.4 14.2 %attend.5 = (bf16[512,256]{1,0:T(8,128)(2,1)}, bf16[512,256]{1,0:T(8,128)(2,1)}, f32[256,1024]{1,0:T(8,128)}, f32[2,8,1024]{2,1,0:T(8,128)}) custom-call(f32[4]{0:T(128)} %multiply_exponential_fusion.slope_ref, s32[2]{0:T(128)} %fusion.22.start_ref, s32[1]{0:T(128)} %bitcast.3.me_ref, bf16[512,768]{1,0:T(8,128)(2,1)} %get-tuple-element.243.rest_0_.rest_1_.rest_2_, ...), custom_call_target="tpu_custom_call" | custom-call | flops 8499999744 | bytes 1 | tf_op jit(solution)/shard_map/attend/pallas_call | solution.py:603
  181.2 6.9 collective-permute-done.24.rest_6_
  189.6 15.0 %collective-permute-done.22.far_ref = bf16[512,1024]{1,0:T(8,128)(2,1)S(1)} collective-permute-done((bf16[512,1024]{1,0:T(8,128)(2,1)}, bf16[512,1024]{1,0:T(8,128)(2,1)S(1)}, u32[]{:S(2)}, u32[]{:S(2)}) %collective-permute-start.22) | collective-permute-done | bytes 1048608 | tf_op jit(solution)/shard_map/ppermute | solution.py:426
  206.0 6.2 mix_near.2
  212.7 15.1 %collective-permute-done.25.rest_3_ = bf16[2,128,2048]{2,1,0:T(8,128)(2,1)} collective-permute-done((bf16[2,128,2048]{2,1,0:T(8,128)(2,1)S(1)}, bf16[2,128,2048]{2,1,0:T(8,128)(2,1)}, u32[]{:S(2)}, u32[]{:S(2)}) %collective-permute-start.25) | collective-permute-done | bytes 1048608 | tf_op jit(solution)/shard_map/ppermute | solution.py:426
  229.3 17.1 %mlp_forward.2 = (bf16[1024,2048]{1,0:T(8,128)(2,1)}, bf16[1024,2048]{1,0:T(8,128)(2,1)}, f32[512,1024]{1,0:T(8,128)}, bf16[512,1024]{1,0:T(8,128)(2,1)}) custom-call(bf16[512,1024]{1,0:T(8,128)(2,1)} %get-tuple-element.262.normed_ref.left_ref, bf16[512,1024]{1,0:T(8,128)(2,1)} %copy-done.39, f32[1,2048]{1,0:T(1,128)} %bitcast.349, ...), custom_call_target="tpu_custom_call" | custom-call | flops 8999999488 | bytes 1 | tf_op jit(solution)/shard_map/mlp_forward/pallas_call | solution.py:1047
  248.8 11.9 %collective-permute-done.32 = bf16[2,128,1024]{2,1,0:T(8,128)(2,1)S(1)} collective-permute-done((bf16[2,128,1024]{2,1,0:T(8,128)(2,1)S(1)}, bf16[2,128,1024]{2,1,0:T(8,128)(2,1)S(1)}, u32[]{:S(2)}, u32[]{:S(2)}) %collective-permute-start.32) | collective-permute-done | bytes 524320 | tf_op jit(solution)/shard_map/ppermute | solution.py:426
  268.1 6.4 collective-permute-done.34
  286.3 14.3 %collective-permute-done.37.rest_1_ = bf16[2,128,2048]{2,1,0:T(8,128)(2,1)} collective-permute-done((bf16[2,128,2048]{2,1,0:T(8,128)(2,1)S(1)}, bf16[2,128,2048]{2,1,0:T(8,128)(2,1)}, u32[]{:S(2)}, u32[]{:S(2)}) %collective-permute-start.37) | collective-permute-done | bytes 1048608 | tf_op jit(solution)/shard_map/ppermute | solution.py:426
  305.1 19.9 %collective-permute-done.36.rows_ref.far_ref = bf16[512,1024]{1,0:T(8,128)(2,1)S(1)} collective-permute-done((bf16[512,1024]{1,0:T(8,128)(2,1)S(1)}, bf16[512,1024]{1,0:T(8,128)(2,1)S(1)}, u32[]{:S(2)}, u32[]{:S(2)}) %collective-permute-start.36) | collective-permute-done | bytes 1048608 | tf_op jit(solution)/shard_map/ppermute | solution.py:426
  334.7 18.8 %attend.6 = (bf16[512,256]{1,0:T(8,128)(2,1)}, bf16[512,256]{1,0:T(8,128)(2,1)}, f32[256,1024]{1,0:T(8,128)}, f32[2,8,1024]{2,1,0:T(8,128)}) custom-call(f32[4]{0:T(128)} %multiply_exponential_fusion.slope_ref, s32[2]{0:T(128)} %fusion.22.start_ref, s32[1]{0:T(128)} %bitcast.3.me_ref, bf16[512,768]{1,0:T(8,128)(2,1)} %get-tuple-element.290.rest_0_.rest_1_.rest_2_, ...), custom_call_target="tpu_custom_call" | custom-call | flops 8499999744 | bytes 1 | tf_op jit(solution)/shard_map/attend/pallas_call | solution.py:603
  360.2 15.0 %attend.7 = (bf16[512,256]{1,0:T(8,128)(2,1)}, bf16[512,256]{1,0:T(8,128)(2,1)}, f32[256,1024]{1,0:T(8,128)}, f32[2,8,1024]{2,1,0:T(8,128)}) custom-call(f32[4]{0:T(128)} %multiply_exponential_fusion.slope_ref, s32[2]{0:T(128)} %fusion.22.start_ref, s32[1]{0:T(128)} %bitcast.3.me_ref, bf16[512,768]{1,0:T(8,128)(2,1)} %get-tuple-element.290.rest_0_.rest_1_.rest_2_, ...), custom_call_target="tpu_custom_call" | custom-call | flops 8499999744 | bytes 1 | tf_op jit(solution)/shard_map/attend/pallas_call | solution.py:603
  376.2 14.8 %collective-permute-done.48.far_ref = bf16[512,1024]{1,0:T(8,128)(2,1)S(1)} collective-permute-done((bf16[512,1024]{1,0:T(8,128)(2,1)}, bf16[512,1024]{1,0:T(8,128)(2,1)S(1)}, u32[]{:S(2)}, u32[]{:S(2)}) %collective-permute-start.48) | collective-permute-done | bytes 1048608 | tf_op jit(solution)/shard_map/ppermute | solution.py:426
  392.1 6.2 mix_near.3
  403.4 6.4 collective-permute-start.53
  410.8 17.4 %mlp_forward.3 = (bf16[1024,2048]{1,0:T(8,128)(2,1)}, bf16[1024,2048]{1,0:T(8,128)(2,1)}, f32[512,1024]{1,0:T(8,128)}, bf16[512,1024]{1,0:T(8,128)(2,1)}) custom-call(bf16[512,1024]{1,0:T(8,128)(2,1)} %get-tuple-element.297.normed_ref.left_ref, bf16[512,1024]{1,0:T(8,128)(2,1)} %copy-done.49, f32[1,2048]{1,0:T(1,128)} %bitcast.348, ...), custom_call_target="tpu_custom_call" | custom-call | flops 8999999488 | bytes 1 | tf_op jit(solution)/shard_map/mlp_forward/pallas_call | solution.py:1047
  429.2 20.4 %mlp_backward.2 = (bf16[1024,2048]{1,0:T(8,128)(2,1)}, f32[1,2048]{1,0:T(1,128)}, f32[512,1024]{1,0:T(8,128)}, bf16[512,1024]{1,0:T(8,128)(2,1)}) custom-call(f32[512,1024]{1,0:T(8,128)} %get-tuple-element.304.grad_ref.left_ref, bf16[512,1024]{1,0:T(8,128)(2,1)} %copy-done.50, bf16[1024,2048]{1,0:T(8,128)(2,1)} %get-tuple-element.306.hidden_ref, ...), custom_call_target="tpu_custom_call" | custom-call | flops 11000000512 | bytes 1 | tf_op jit(solution)/shard_map/mlp_backward/pallas_call | solution.py:1122
  453.6 6.6 mlp_open.2
  462.5 9.1 unit_grads.4
  477.1 8.8 unit_grads.5
  495.5 21.2 %attend_pull.4 = (bf16[3,1024,128]{2,1,0:T(8,128)(2,1)}, bf16[3,1024,128]{2,1,0:T(8,128)(2,1)}) custom-call(f32[4]{0:T(128)} %multiply_exponential_fusion.slope_ref, s32[2]{0:T(128)} %fusion.22.start_ref, s32[1]{0:T(128)} %bitcast.3.me_ref, bf16[512,768]{1,0:T(8,128)(2,1)} %get-tuple-element.290.rest_0_.rest_1_.rest_2_, ...), custom_call_target="tpu_custom_call" | custom-call | flops 11000000512 | bytes 1 | tf_op jit(solution)/shard_map/attend_pull/pallas_call | solution.py:736
  519.3 21.4 %attend_pull.5 = (bf16[3,1024,128]{2,1,0:T(8,128)(2,1)}, bf16[3,1024,128]{2,1,0:T(8,128)(2,1)}) custom-call(f32[4]{0:T(128)} %multiply_exponential_fusion.slope_ref, s32[2]{0:T(128)} %fusion.22.start_ref, s32[1]{0:T(128)} %bitcast.3.me_ref, bf16[512,768]{1,0:T(8,128)(2,1)} %get-tuple-element.290.rest_0_.rest_1_.rest_2_, ...), custom_call_target="tpu_custom_call" | custom-call | flops 11000000512 | bytes 1 | tf_op jit(solution)/shard_map/attend_pull/pallas_call | solution.py:736
  544.5 6.0 unproject_far.2
  550.8 9.9 %head_grads.2 = (bf16[4,2,128,1024]{3,2,1,0:T(8,128)(2,1)}, bf16[4,2,128,1024]{3,2,1,0:T(8,128)(2,1)}, f32[8,256]{1,0:T(8,128)}) custom-call(bf16[512,1024]{1,0:T(8,128)(2,1)} %get-tuple-element.269.rows_ref.near_ref, bf16[512,1024]{1,0:T(8,128)(2,1)} %copy-done.41, bf16[512,1024]{1,0:T(8,128)(2,1)} %get-tuple-element.313.grad_ref.grad_near_ref, ...), custom_call_target="tpu_custom_call" | custom-call | flops 5000000000 | bytes 1 | tf_op jit(solution)/shard_map/head_grads/pallas_call | solution.py:771
  560.7 15.2 %collective-permute-done.62.rest_4_ = bf16[512,1024]{1,0:T(8,128)(2,1)S(1)} collective-permute-done((bf16[512,1024]{1,0:T(8,128)(2,1)}, bf16[512,1024]{1,0:T(8,128)(2,1)S(1)}, u32[]{:S(2)}, u32[]{:S(2)}) %collective-permute-start.62) | collective-permute-done | bytes 1048608 | tf_op jit(solution)/shard_map/ppermute | solution.py:426
  576.9 9.2 unproject_near.2
  595.5 20.8 %mlp_backward.3 = (bf16[1024,2048]{1,0:T(8,128)(2,1)}, f32[1,2048]{1,0:T(1,128)}, f32[512,1024]{1,0:T(8,128)}, bf16[512,1024]{1,0:T(8,128)(2,1)}) custom-call(f32[512,1024]{1,0:T(8,128)} %get-tuple-element.349.grad_ref.left_ref, bf16[512,1024]{1,0:T(8,128)(2,1)} %copy-done.47, bf16[1024,2048]{1,0:T(8,128)(2,1)} %get-tuple-element.351.hidden_ref, ...), custom_call_target="tpu_custom_call" | custom-call | flops 11000000512 | bytes 1 | tf_op jit(solution)/shard_map/mlp_backward/pallas_call | solution.py:1122
  623.1 6.7 mlp_open.3
  630.0 12.3 %collective-permute-done.68 = bf16[2,2,128,1024]{3,2,1,0:T(8,128)(2,1)} collective-permute-done((bf16[2,2,128,1024]{3,2,1,0:T(8,128)(2,1)}, bf16[2,2,128,1024]{3,2,1,0:T(8,128)(2,1)}, u32[]{:S(2)}, u32[]{:S(2)}) %collective-permute-start.68) | collective-permute-done | bytes 1048608 | tf_op jit(solution)/shard_map/ppermute | solution.py:426
  643.6 9.3 unit_grads.6
  656.9 8.8 unit_grads.7
  679.3 21.2 %attend_pull.6 = (bf16[3,1024,128]{2,1,0:T(8,128)(2,1)}, bf16[3,1024,128]{2,1,0:T(8,128)(2,1)}) custom-call(f32[4]{0:T(128)} %multiply_exponential_fusion.slope_ref, s32[2]{0:T(128)} %fusion.22.start_ref, s32[1]{0:T(128)} %bitcast.3.me_ref, bf16[512,768]{1,0:T(8,128)(2,1)} %get-tuple-element.243.rest_0_.rest_1_.rest_2_, ...), custom_call_target="tpu_custom_call" | custom-call | flops 11000000512 | bytes 1 | tf_op jit(solution)/shard_map/attend_pull/pallas_call | solution.py:736
  700.5 17.0 %collective-permute-done.74 = bf16[2,2,2,128,1024]{4,3,2,1,0:T(8,128)(2,1)S(1)} collective-permute-done((bf16[2,2,2,128,1024]{4,3,2,1,0:T(8,128)(2,1)}, bf16[2,2,2,128,1024]{4,3,2,1,0:T(8,128)(2,1)S(1)}, u32[]{:S(2)}, u32[]{:S(2)}) %collective-permute-start.74) | collective-permute-done | bytes 2097184 | tf_op jit(solution)/shard_map/ppermute | solution.py:426
  717.6 21.2 %attend_pull.7 = (bf16[3,1024,128]{2,1,0:T(8,128)(2,1)}, bf16[3,1024,128]{2,1,0:T(8,128)(2,1)}) custom-call(f32[4]{0:T(128)} %multiply_exponential_fusion.slope_ref, s32[2]{0:T(128)} %fusion.22.start_ref, s32[1]{0:T(128)} %bitcast.3.me_ref, bf16[512,768]{1,0:T(8,128)(2,1)} %get-tuple-element.243.rest_0_.rest_1_.rest_2_, ...), custom_call_target="tpu_custom_call" | custom-call | flops 11000000512 | bytes 1 | tf_op jit(solution)/shard_map/attend_pull/pallas_call | solution.py:736
  751.2 6.0 unproject_far.3
  758.9 9.8 %head_grads.3 = (bf16[4,2,128,1024]{3,2,1,0:T(8,128)(2,1)}, bf16[4,2,128,1024]{3,2,1,0:T(8,128)(2,1)}, f32[8,256]{1,0:T(8,128)}) custom-call(bf16[512,1024]{1,0:T(8,128)(2,1)} %get-tuple-element.228.rows_ref.near_ref, bf16[512,1024]{1,0:T(8,128)(2,1)} %copy-done.35, bf16[512,1024]{1,0:T(8,128)(2,1)} %get-tuple-element.362.grad_ref.grad_near_ref, ...), custom_call_target="tpu_custom_call" | custom-call | flops 5000000000 | bytes 1 | tf_op jit(solution)/shard_map/head_grads/pallas_call | solution.py:771
  774.3 18.2 %collective-permute-done.78.rest_4_ = bf16[512,1024]{1,0:T(8,128)(2,1)} collective-permute-done((bf16[512,1024]{1,0:T(8,128)(2,1)}, bf16[512,1024]{1,0:T(8,128)(2,1)}, u32[]{:S(2)}, u32[]{:S(2)}) %collective-permute-start.78) | collective-permute-done | bytes 1048608 | tf_op jit(solution)/shard_map/ppermute | solution.py:426
  792.6 9.3 unproject_near.3
  811.5 19.3 %collective-permute-done.92 = bf16[128,1024]{1,0:T(8,128)(2,1)S(1)} collective-permute-done((bf16[128,1024]{1,0:T(8,128)(2,1)S(1)}, bf16[128,1024]{1,0:T(8,128)(2,1)S(1)}, u32[]{:S(2)}, u32[]{:S(2)}) %collective-permute-start.92) | collective-permute-done | bytes 262176 | tf_op jit(solution)/shard_map/ppermute | solution.py:426
  845.8 14.1 %collective-permute-done.87 = f32[2,9,128]{2,1,0:T(8,128)} collective-permute-done((f32[2,9,128]{2,1,0:T(8,128)}, f32[2,9,128]{2,1,0:T(8,128)}, u32[]{:S(2)}, u32[]{:S(2)}) %collective-permute-start.87) | collective-permute-done | bytes 9248 | tf_op jit(solution)/shard_map/ppermute | solution.py:426
  877.8 32.2 %collective-permute-done.95 = bf16[2,128,1024]{2,1,0:T(8,128)(2,1)S(1)} collective-permute-done((bf16[2,128,1024]{2,1,0:T(8,128)(2,1)S(1)}, bf16[2,128,1024]{2,1,0:T(8,128)(2,1)S(1)}, u32[]{:S(2)}, u32[]{:S(2)}) %collective-permute-start.95) | collective-permute-done | bytes 524320 | tf_op jit(solution)/shard_map/ppermute | solution.py:431
  915.5 6.7 collective-permute-done.90
  924.6 9.6 %collective-permute-done.91 = bf16[128,1024]{1,0:T(8,128)(2,1)S(1)} collective-permute-done((bf16[128,1024]{1,0:T(8,128)(2,1)S(1)}, bf16[128,1024]{1,0:T(8,128)(2,1)S(1)}, u32[]{:S(2)}, u32[]{:S(2)}) %collective-permute-start.91) | collective-permute-done | bytes 262176 | tf_op jit(solution)/shard_map/ppermute | solution.py:426
  (499 shorter events, 282.7 us)
Async XLA Ops:
  0.7 45.5 %collective-permute-start.1 = (bf16[512,1024]{1,0:T(8,128)(2,1)}, bf16[512,1024]{1,0:T(8,128)(2,1)}, u32[]{:S(2)}, u32[]{:S(2)}) collective-permute-start(bf16[512,1024]{1,0:T(8,128)(2,1)} %direct_ref.2), channel_id=1, source_target_pairs={{2,4},{3,5},{4,2},{5,3},{10,12},{11,13},{12,10},{13,11},{18,20},{1... | collective-permute-start | bytes 3145736 | tf_op jit(solution)/shard_map/ppermute | solution.py:439
  14.6 27.6 %collective-permute-start.2 = (bf16[128,1024]{1,0:T(8,128)(2,1)S(1)}, bf16[128,1024]{1,0:T(8,128)(2,1)S(1)}, u32[]{:S(2)}, u32[]{:S(2)}) collective-permute-start(bf16[128,1024]{1,0:T(8,128)(2,1)S(1)} %pad_maximum_fusion.15), channel_id=1, source_target_pairs={{0,2},{1,3},{2,0},{3,1},{4,6},{5,7},{6,4},{7,5},{8,10},{9,11},{10,... | collective-permute-start | bytes 786440 | tf_op jit(solution)/shard_map/ppermute | solution.py:426
  77.6 36.5 %collective-permute-start.12 = (bf16[512,1024]{1,0:T(8,128)(2,1)}, bf16[512,1024]{1,0:T(8,128)(2,1)S(1)}, u32[]{:S(2)}, u32[]{:S(2)}) collective-permute-start(bf16[512,1024]{1,0:T(8,128)(2,1)} %get-tuple-element.228.rows_ref.near_ref), channel_id=1, source_target_pairs={{0,1},{1,0},{2,3},{3,2},{4,5},{5,4},{6,7},{7,6},{8,9},{9,8},{10,11... | collective-permute-start | bytes 3145736 | tf_op jit(solution)/shard_map/ppermute | solution.py:426
  122.3 32.3 %collective-permute-start.18 = (bf16[2,128,2048]{2,1,0:T(8,128)(2,1)S(1)}, bf16[2,128,2048]{2,1,0:T(8,128)(2,1)S(1)}, u32[]{:S(2)}, u32[]{:S(2)}) collective-permute-start(bf16[2,128,2048]{2,1,0:T(8,128)(2,1)S(1)} %pad_maximum_fusion.2.rest_0_), channel_id=1, source_target_pairs={{0,8},{1,9},{2,10},{3,11},{4,12},{5,13},{6,14},{7,15},{8,0},{9,1},... | collective-permute-start | bytes 3145736 | tf_op jit(solution)/shard_map/ppermute | solution.py:426
  123.8 30.8 %collective-permute-start.19 = (bf16[2,128,2048]{2,1,0:T(8,128)(2,1)S(1)}, bf16[2,128,2048]{2,1,0:T(8,128)(2,1)S(1)}, u32[]{:S(2)}, u32[]{:S(2)}) collective-permute-start(bf16[2,128,2048]{2,1,0:T(8,128)(2,1)S(1)} %pad_maximum_fusion.2.rest_0_), channel_id=1, source_target_pairs={{0,16},{1,17},{2,18},{3,19},{4,20},{5,21},{6,22},{7,23},{8,24},{9,... | collective-permute-start | bytes 3145736 | tf_op jit(solution)/shard_map/ppermute | solution.py:426
  125.4 29.3 %collective-permute-start.20 = (bf16[2,128,2048]{2,1,0:T(8,128)(2,1)S(1)}, bf16[2,128,2048]{2,1,0:T(8,128)(2,1)}, u32[]{:S(2)}, u32[]{:S(2)}) collective-permute-start(bf16[2,128,2048]{2,1,0:T(8,128)(2,1)S(1)} %pad_maximum_fusion.2.rest_0_), channel_id=1, source_target_pairs={{0,1},{1,0},{2,3},{3,2},{4,5},{5,4},{6,7},{7,6},{8,9},{9,8},{10,11... | collective-permute-start | bytes 3145736 | tf_op jit(solution)/shard_map/ppermute | solution.py:426
  154.7 25.8 %collective-permute-start.23 = (bf16[2,128,2048]{2,1,0:T(8,128)(2,1)}, bf16[2,128,2048]{2,1,0:T(8,128)(2,1)}, u32[]{:S(2)}, u32[]{:S(2)}) collective-permute-start(bf16[2,128,2048]{2,1,0:T(8,128)(2,1)} %collective-permute-done.20.rest_4_), channel_id=1, source_target_pairs={{0,8},{1,9},{2,10},{3,11},{4,12},{5,13},{6,14},{7,15},{8,0},{9,1},... | collective-permute-start | bytes 3145736 | tf_op jit(solution)/shard_map/ppermute | solution.py:426
  158.5 53.7 %collective-permute-start.28 = (bf16[128,2048]{1,0:T(8,128)(2,1)S(1)}, bf16[128,2048]{1,0:T(8,128)(2,1)S(1)}, u32[]{:S(2)}, u32[]{:S(2)}) collective-permute-start(bf16[128,2048]{1,0:T(8,128)(2,1)S(1)} %reshape.355), channel_id=1, source_target_pairs={{4,6},{5,7},{6,4},{7,5},{12,14},{13,15},{14,12},{15,13},{20,22},{2... | collective-permute-start | bytes 1572872 | tf_op jit(solution)/shard_map/ppermute | solution.py:431
  159.3 52.9 %collective-permute-start.29 = (bf16[128,2048]{1,0:T(8,128)(2,1)S(1)}, bf16[128,2048]{1,0:T(8,128)(2,1)S(1)}, u32[]{:S(2)}, u32[]{:S(2)}) collective-permute-start(bf16[128,2048]{1,0:T(8,128)(2,1)S(1)} %reshape.355), channel_id=1, source_target_pairs={{0,6},{1,7},{2,4},{3,5},{4,0},{5,1},{6,2},{7,3},{8,14},{9,15},{10,... | collective-permute-start | bytes 1572872 | tf_op jit(solution)/shard_map/ppermute | solution.py:431
  163.7 40.9 %collective-permute-start.22 = (bf16[512,1024]{1,0:T(8,128)(2,1)}, bf16[512,1024]{1,0:T(8,128)(2,1)S(1)}, u32[]{:S(2)}, u32[]{:S(2)}) collective-permute-start(bf16[512,1024]{1,0:T(8,128)(2,1)} %mix_far.2), channel_id=1, source_target_pairs={{0,1},{1,0},{2,3},{3,2},{4,5},{5,4},{6,7},{7,6},{8,9},{9,8},{10,11... | collective-permute-start | bytes 3145736 | tf_op jit(solution)/shard_map/ppermute | solution.py:426
  180.5 24.7 %collective-permute-start.21 = (bf16[512,256]{1,0:T(8,128)(2,1)}, bf16[512,256]{1,0:T(8,128)(2,1)S(1)}, u32[]{:S(2)}, u32[]{:S(2)}) collective-permute-start(bf16[512,256]{1,0:T(8,128)(2,1)} %get-tuple-element.248), channel_id=1, source_target_pairs={{0,4},{1,5},{2,6},{3,7},{4,0},{5,1},{6,2},{7,3},{8,12},{9,13},{10,... | collective-permute-start | bytes 786440 | tf_op jit(solution)/shard_map/ppermute | solution.py:426
  274.9 25.7 %collective-permute-start.37 = (bf16[2,128,2048]{2,1,0:T(8,128)(2,1)S(1)}, bf16[2,128,2048]{2,1,0:T(8,128)(2,1)}, u32[]{:S(2)}, u32[]{:S(2)}) collective-permute-start(bf16[2,128,2048]{2,1,0:T(8,128)(2,1)S(1)} %pad_maximum_fusion.3.rest_0_), channel_id=1, source_target_pairs={{0,8},{1,9},{2,10},{3,11},{4,12},{5,13},{6,14},{7,15},{8,0},{9,1},... | collective-permute-start | bytes 3145736 | tf_op jit(solution)/shard_map/ppermute | solution.py:426
  276.1 25.3 %collective-permute-start.38 = (bf16[2,128,2048]{2,1,0:T(8,128)(2,1)S(1)}, bf16[2,128,2048]{2,1,0:T(8,128)(2,1)}, u32[]{:S(2)}, u32[]{:S(2)}) collective-permute-start(bf16[2,128,2048]{2,1,0:T(8,128)(2,1)S(1)} %pad_maximum_fusion.3.rest_0_), channel_id=1, source_target_pairs={{0,16},{1,17},{2,18},{3,19},{4,20},{5,21},{6,22},{7,23},{8,24},{9,... | collective-permute-start | bytes 3145736 | tf_op jit(solution)/shard_map/ppermute | solution.py:426
  277.6 26.1 %collective-permute-start.39 = (bf16[2,128,2048]{2,1,0:T(8,128)(2,1)S(1)}, bf16[2,128,2048]{2,1,0:T(8,128)(2,1)}, u32[]{:S(2)}, u32[]{:S(2)}) collective-permute-start(bf16[2,128,2048]{2,1,0:T(8,128)(2,1)S(1)} %pad_maximum_fusion.3.rest_0_), channel_id=1, source_target_pairs={{0,1},{1,0},{2,3},{3,2},{4,5},{5,4},{6,7},{7,6},{8,9},{9,8},{10,11... | collective-permute-start | bytes 3145736 | tf_op jit(solution)/shard_map/ppermute | solution.py:426
  277.6 47.4 %collective-permute-start.36 = (bf16[512,1024]{1,0:T(8,128)(2,1)S(1)}, bf16[512,1024]{1,0:T(8,128)(2,1)S(1)}, u32[]{:S(2)}, u32[]{:S(2)}) collective-permute-start(bf16[512,1024]{1,0:T(8,128)(2,1)S(1)} %copy-done.40), channel_id=1, source_target_pairs={{0,1},{1,0},{2,3},{3,2},{4,5},{5,4},{6,7},{7,6},{8,9},{9,8},{10,11... | collective-permute-start | bytes 3145736 | tf_op jit(solution)/shard_map/ppermute | solution.py:426
  303.8 28.1 %collective-permute-start.42 = (bf16[2,128,2048]{2,1,0:T(8,128)(2,1)}, bf16[2,128,2048]{2,1,0:T(8,128)(2,1)S(1)}, u32[]{:S(2)}, u32[]{:S(2)}) collective-permute-start(bf16[2,128,2048]{2,1,0:T(8,128)(2,1)} %collective-permute-done.39.rest_4_), channel_id=1, source_target_pairs={{0,8},{1,9},{2,10},{3,11},{4,12},{5,13},{6,14},{7,15},{8,0},{9,1},... | collective-permute-start | bytes 3145736 | tf_op jit(solution)/shard_map/ppermute | solution.py:426
  304.6 27.2 %collective-permute-start.43 = (bf16[2,128,2048]{2,1,0:T(8,128)(2,1)}, bf16[2,128,2048]{2,1,0:T(8,128)(2,1)S(1)}, u32[]{:S(2)}, u32[]{:S(2)}) collective-permute-start(bf16[2,128,2048]{2,1,0:T(8,128)(2,1)} %collective-permute-done.39.rest_4_), channel_id=1, source_target_pairs={{0,16},{1,17},{2,18},{3,19},{4,20},{5,21},{6,22},{7,23},{8,24},{9,... | collective-permute-start | bytes 3145736 | tf_op jit(solution)/shard_map/ppermute | solution.py:426
  331.3 28.9 %collective-permute-start.45 = (bf16[2,128,2048]{2,1,0:T(8,128)(2,1)}, bf16[2,128,2048]{2,1,0:T(8,128)(2,1)S(1)}, u32[]{:S(2)}, u32[]{:S(2)}) collective-permute-start(bf16[2,128,2048]{2,1,0:T(8,128)(2,1)} %collective-permute-done.37.rest_1_), channel_id=1, source_target_pairs={{0,16},{1,17},{2,18},{3,19},{4,20},{5,21},{6,22},{7,23},{8,24},{9,... | collective-permute-start | bytes 3145736 | tf_op jit(solution)/shard_map/ppermute | solution.py:426
  331.9 28.4 %collective-permute-start.46 = (bf16[2,128,2048]{2,1,0:T(8,128)(2,1)S(1)}, bf16[2,128,2048]{2,1,0:T(8,128)(2,1)S(1)}, u32[]{:S(2)}, u32[]{:S(2)}) collective-permute-start(bf16[2,128,2048]{2,1,0:T(8,128)(2,1)S(1)} %collective-permute-done.43.rest_6_), channel_id=1, source_target_pairs={{0,8},{1,9},{2,10},{3,11},{4,12},{5,13},{6,14},{7,15},{8,0},{9,1},... | collective-permute-start | bytes 3145736 | tf_op jit(solution)/shard_map/ppermute | solution.py:426
  360.2 30.9 %collective-permute-start.48 = (bf16[512,1024]{1,0:T(8,128)(2,1)}, bf16[512,1024]{1,0:T(8,128)(2,1)S(1)}, u32[]{:S(2)}, u32[]{:S(2)}) collective-permute-start(bf16[512,1024]{1,0:T(8,128)(2,1)} %mix_far.3), channel_id=1, source_target_pairs={{0,1},{1,0},{2,3},{3,2},{4,5},{5,4},{6,7},{7,6},{8,9},{9,8},{10,11... | collective-permute-start | bytes 3145736 | tf_op jit(solution)/shard_map/ppermute | solution.py:426
  403.4 24.8 %collective-permute-start.53 = (bf16[512,1024]{1,0:T(8,128)(2,1)}, bf16[512,1024]{1,0:T(8,128)(2,1)S(1)}, u32[]{:S(2)}, u32[]{:S(2)}) collective-permute-start(bf16[512,1024]{1,0:T(8,128)(2,1)} %get-tuple-element.305), channel_id=1, source_target_pairs={{0,4},{1,5},{2,6},{3,7},{4,0},{5,1},{6,2},{7,3},{8,12},{9,13},{10,... | collective-permute-start | bytes 3145736 | tf_op jit(solution)/shard_map/ppermute | solution.py:426
  460.1 26.0 %collective-permute-start.55 = (bf16[512,1024]{1,0:T(8,128)(2,1)}, bf16[512,1024]{1,0:T(8,128)(2,1)S(1)}, u32[]{:S(2)}, u32[]{:S(2)}) collective-permute-start(bf16[512,1024]{1,0:T(8,128)(2,1)} %get-tuple-element.313.grad_ref.grad_near_ref), channel_id=1, source_target_pairs={{0,1},{1,0},{2,3},{3,2},{4,5},{5,4},{6,7},{7,6},{8,9},{9,8},{10,11... | collective-permute-start | bytes 3145736 | tf_op jit(solution)/shard_map/ppermute | solution.py:426
  471.6 47.6 %collective-permute-start.58 = (bf16[2,2,2,128,1024]{4,3,2,1,0:T(8,128)(2,1)}, bf16[2,2,2,128,1024]{4,3,2,1,0:T(8,128)(2,1)S(1)}, u32[]{:S(2)}, u32[]{:S(2)}) collective-permute-start(bf16[2,2,2,128,1024]{4,3,2,1,0:T(8,128)(2,1)} %get-tuple-element.328), channel_id=1, source_target_pairs={{0,16},{1,17},{2,18},{3,19},{4,20},{5,21},{6,22},{7,23},{8,24},{9,... | collective-permute-start | bytes 6291464 | tf_op jit(solution)/shard_map/ppermute | solution.py:426
  491.4 49.9 %collective-permute-start.61 = (bf16[2,2,2,128,1024]{4,3,2,1,0:T(8,128)(2,1)}, bf16[2,2,2,128,1024]{4,3,2,1,0:T(8,128)(2,1)S(1)}, u32[]{:S(2)}, u32[]{:S(2)}) collective-permute-start(bf16[2,2,2,128,1024]{4,3,2,1,0:T(8,128)(2,1)} %get-tuple-element.338), channel_id=1, source_target_pairs={{0,8},{1,9},{2,10},{3,11},{4,12},{5,13},{6,14},{7,15},{8,0},{9,1},... | collective-permute-start | bytes 6291464 | tf_op jit(solution)/shard_map/ppermute | solution.py:426
  550.5 25.4 %collective-permute-start.62 = (bf16[512,1024]{1,0:T(8,128)(2,1)}, bf16[512,1024]{1,0:T(8,128)(2,1)S(1)}, u32[]{:S(2)}, u32[]{:S(2)}) collective-permute-start(bf16[512,1024]{1,0:T(8,128)(2,1)} %unproject_far.2), channel_id=1, source_target_pairs={{0,1},{1,0},{2,3},{3,2},{4,5},{5,4},{6,7},{7,6},{8,9},{9,8},{10,11... | collective-permute-start | bytes 3145736 | tf_op jit(solution)/shard_map/ppermute | solution.py:426
  560.7 32.6 %collective-permute-start.63 = (bf16[4,2,128,1024]{3,2,1,0:T(8,128)(2,1)}, bf16[4,2,128,1024]{3,2,1,0:T(8,128)(2,1)S(1)}, u32[]{:S(2)}, u32[]{:S(2)}) collective-permute-start(bf16[4,2,128,1024]{3,2,1,0:T(8,128)(2,1)} %get-tuple-element.347), channel_id=1, source_target_pairs={{0,4},{1,5},{2,6},{3,7},{4,0},{5,1},{6,2},{7,3},{8,12},{9,13},{10,... | collective-permute-start | bytes 6291464 | tf_op jit(solution)/shard_map/ppermute | solution.py:426
  587.2 30.0 %collective-permute-start.66 = (bf16[2,2,128,1024]{3,2,0,1:T(8,128)(2,1)}, bf16[2,2,128,1024]{3,2,0,1:T(8,128)(2,1)S(1)}, u32[]{:S(2)}, u32[]{:S(2)}) collective-permute-start(bf16[2,2,128,1024]{3,2,0,1:T(8,128)(2,1)} %copy.119), channel_id=1, source_target_pairs={{0,8},{1,9},{2,10},{3,11},{4,12},{5,13},{6,14},{7,15},{8,0},{9,1},... | collective-permute-start | bytes 3145736 | tf_op jit(solution)/shard_map/ppermute | solution.py:426
  591.8 25.4 %collective-permute-start.67 = (bf16[2,2,128,1024]{3,2,0,1:T(8,128)(2,1)S(1)}, bf16[2,2,128,1024]{3,2,0,1:T(8,128)(2,1)}, u32[]{:S(2)}, u32[]{:S(2)}) collective-permute-start(bf16[2,2,128,1024]{3,2,0,1:T(8,128)(2,1)S(1)} %copy.120), channel_id=1, source_target_pairs={{0,16},{1,17},{2,18},{3,19},{4,20},{5,21},{6,22},{7,23},{8,24},{9,... | collective-permute-start | bytes 3145736 | tf_op jit(solution)/shard_map/ppermute | solution.py:426
  616.5 25.9 %collective-permute-start.68 = (bf16[2,2,128,1024]{3,2,1,0:T(8,128)(2,1)}, bf16[2,2,128,1024]{3,2,1,0:T(8,128)(2,1)}, u32[]{:S(2)}, u32[]{:S(2)}) collective-permute-start(bf16[2,2,128,1024]{3,2,1,0:T(8,128)(2,1)} %get-tuple-element.478), channel_id=1, source_target_pairs={{0,16},{1,17},{2,18},{3,19},{4,20},{5,21},{6,22},{7,23},{8,24},{9,... | collective-permute-start | bytes 3145736 | tf_op jit(solution)/shard_map/ppermute | solution.py:426
  617.1 127.4 %collective-permute-start.50 = (bf16[512,1024]{1,0:T(8,128)(2,1)}, bf16[512,1024]{1,0:T(8,128)(2,1)}, u32[]{:S(2)}, u32[]{:S(2)}) collective-permute-start(bf16[512,1024]{1,0:T(8,128)(2,1)} %get-tuple-element.300), channel_id=1, source_target_pairs={{0,4},{1,5},{2,6},{3,7},{4,0},{5,1},{6,2},{7,3},{8,12},{9,13},{10,... | collective-permute-start | bytes 3145736 | tf_op jit(solution)/shard_map/ppermute | solution.py:426
  621.3 54.5 %collective-permute-start.72 = (bf16[2,2,128,1024]{3,2,0,1:T(8,128)(2,1)S(1)}, bf16[2,2,128,1024]{3,2,0,1:T(8,128)(2,1)S(1)}, u32[]{:S(2)}, u32[]{:S(2)}) collective-permute-start(bf16[2,2,128,1024]{3,2,0,1:T(8,128)(2,1)S(1)} %pad_maximum_fusion.5), channel_id=1, source_target_pairs={{0,1},{1,0},{2,3},{3,2},{4,5},{5,4},{6,7},{7,6},{8,9},{9,8},{10,11... | collective-permute-start | bytes 3145736 | tf_op jit(solution)/shard_map/ppermute | solution.py:426
  629.7 39.5 %collective-permute-start.69 = (bf16[512,1024]{1,0:T(8,128)(2,1)}, bf16[512,1024]{1,0:T(8,128)(2,1)S(1)}, u32[]{:S(2)}, u32[]{:S(2)}) collective-permute-start(bf16[512,1024]{1,0:T(8,128)(2,1)} %get-tuple-element.362.grad_ref.grad_near_ref), channel_id=1, source_target_pairs={{0,1},{1,0},{2,3},{3,2},{4,5},{5,4},{6,7},{7,6},{8,9},{9,8},{10,11... | collective-permute-start | bytes 3145736 | tf_op jit(solution)/shard_map/ppermute | solution.py:426
  643.5 32.5 %collective-permute-start.73 = (bf16[2,128,1024]{2,1,0:T(8,128)(2,1)S(1)}, bf16[2,128,1024]{2,1,0:T(8,128)(2,1)}, u32[]{:S(2)}, u32[]{:S(2)}) collective-permute-start(bf16[2,128,1024]{2,1,0:T(8,128)(2,1)S(1)} %fusion.5), channel_id=1, source_target_pairs={{0,8},{1,9},{2,10},{3,11},{4,12},{5,13},{6,14},{7,15},{8,0},{9,1},... | collective-permute-start | bytes 1572872 | tf_op jit(solution)/shard_map/ppermute | solution.py:426
  670.2 47.3 %collective-permute-start.74 = (bf16[2,2,2,128,1024]{4,3,2,1,0:T(8,128)(2,1)}, bf16[2,2,2,128,1024]{4,3,2,1,0:T(8,128)(2,1)S(1)}, u32[]{:S(2)}, u32[]{:S(2)}) collective-permute-start(bf16[2,2,2,128,1024]{4,3,2,1,0:T(8,128)(2,1)} %get-tuple-element.383), channel_id=1, source_target_pairs={{0,16},{1,17},{2,18},{3,19},{4,20},{5,21},{6,22},{7,23},{8,24},{9,... | collective-permute-start | bytes 6291464 | tf_op jit(solution)/shard_map/ppermute | solution.py:426
  675.8 66.1 %collective-permute-start.77 = (bf16[2,2,2,128,1024]{4,3,2,1,0:T(8,128)(2,1)}, bf16[2,2,2,128,1024]{4,3,2,1,0:T(8,128)(2,1)S(1)}, u32[]{:S(2)}, u32[]{:S(2)}) collective-permute-start(bf16[2,2,2,128,1024]{4,3,2,1,0:T(8,128)(2,1)} %get-tuple-element.393), channel_id=1, source_target_pairs={{0,8},{1,9},{2,10},{3,11},{4,12},{5,13},{6,14},{7,15},{8,0},{9,1},... | collective-permute-start | bytes 6291464 | tf_op jit(solution)/shard_map/ppermute | solution.py:426
  739.4 29.4 %collective-permute-start.79 = (bf16[2,2,128,1024]{3,2,1,0:T(8,128)(2,1)S(1)}, bf16[2,2,128,1024]{3,2,1,0:T(8,128)(2,1)}, u32[]{:S(2)}, u32[]{:S(2)}) collective-permute-start(bf16[2,2,128,1024]{3,2,1,0:T(8,128)(2,1)S(1)} %bitcast_add_fusion.1), channel_id=1, source_target_pairs={{0,8},{1,9},{2,10},{3,11},{4,12},{5,13},{6,14},{7,15},{8,0},{9,1},... | collective-permute-start | bytes 3145736 | tf_op jit(solution)/shard_map/ppermute | solution.py:426
  743.0 25.7 %collective-permute-start.80 = (bf16[2,2,128,1024]{3,2,1,0:T(8,128)(2,1)}, bf16[2,2,128,1024]{3,2,1,0:T(8,128)(2,1)}, u32[]{:S(2)}, u32[]{:S(2)}) collective-permute-start(bf16[2,2,128,1024]{3,2,1,0:T(8,128)(2,1)} %bitcast_add_fusion), channel_id=1, source_target_pairs={{0,16},{1,17},{2,18},{3,19},{4,20},{5,21},{6,22},{7,23},{8,24},{9,... | collective-permute-start | bytes 3145736 | tf_op jit(solution)/shard_map/ppermute | solution.py:426
  749.3 57.8 %collective-permute-start.51 = (bf16[512,1024]{1,0:T(8,128)(2,1)}, bf16[512,1024]{1,0:T(8,128)(2,1)}, u32[]{:S(2)}, u32[]{:S(2)}) collective-permute-start(bf16[512,1024]{1,0:T(8,128)(2,1)} %get-tuple-element.302), channel_id=1, source_target_pairs={{2,4},{3,5},{4,2},{5,3},{10,12},{11,13},{12,10},{13,11},{18,20},{1... | collective-permute-start | bytes 3145736 | tf_op jit(solution)/shard_map/ppermute | solution.py:439
  757.2 35.3 %collective-permute-start.78 = (bf16[512,1024]{1,0:T(8,128)(2,1)}, bf16[512,1024]{1,0:T(8,128)(2,1)}, u32[]{:S(2)}, u32[]{:S(2)}) collective-permute-start(bf16[512,1024]{1,0:T(8,128)(2,1)} %unproject_far.3), channel_id=1, source_target_pairs={{0,1},{1,0},{2,3},{3,2},{4,5},{5,4},{6,7},{7,6},{8,9},{9,8},{10,11... | collective-permute-start | bytes 3145736 | tf_op jit(solution)/shard_map/ppermute | solution.py:426
  805.4 25.4 %collective-permute-start.92 = (bf16[128,1024]{1,0:T(8,128)(2,1)S(1)}, bf16[128,1024]{1,0:T(8,128)(2,1)S(1)}, u32[]{:S(2)}, u32[]{:S(2)}) collective-permute-start(bf16[128,1024]{1,0:T(8,128)(2,1)S(1)} %get-tuple-element.492), channel_id=1, source_target_pairs={{0,2},{1,3},{2,0},{3,1},{4,6},{5,7},{6,4},{7,5},{8,10},{9,11},{10,... | collective-permute-start | bytes 786440 | tf_op jit(solution)/shard_map/ppermute | solution.py:426
  808.3 29.5 %collective-permute-start.96 = (bf16[2,128,1024]{2,1,0:T(8,128)(2,1)}, bf16[2,128,1024]{2,1,0:T(8,128)(2,1)}, u32[]{:S(2)}, u32[]{:S(2)}) collective-permute-start(bf16[2,128,1024]{2,1,0:T(8,128)(2,1)} %get-tuple-element.491), channel_id=1, source_target_pairs={{4,6},{5,7},{6,4},{7,5},{12,14},{13,15},{14,12},{15,13},{20,22},{2... | collective-permute-start | bytes 1572872 | tf_op jit(solution)/shard_map/ppermute | solution.py:431
  809.7 32.6 %collective-permute-start.97 = (bf16[2,128,1024]{2,1,0:T(8,128)(2,1)}, bf16[2,128,1024]{2,1,0:T(8,128)(2,1)}, u32[]{:S(2)}, u32[]{:S(2)}) collective-permute-start(bf16[2,128,1024]{2,1,0:T(8,128)(2,1)} %get-tuple-element.490), channel_id=1, source_target_pairs={{0,4},{1,5},{2,6},{3,7},{4,2},{5,3},{6,0},{7,1},{8,12},{9,13},{10,... | collective-permute-start | bytes 1572872 | tf_op jit(solution)/shard_map/ppermute | solution.py:431
  830.8 40.3 %collective-permute-start.88 = (bf16[4,2,128,1024]{3,2,1,0:T(8,128)(2,1)}, bf16[4,2,128,1024]{3,2,1,0:T(8,128)(2,1)S(1)}, u32[]{:S(2)}, u32[]{:S(2)}) collective-permute-start(bf16[4,2,128,1024]{3,2,1,0:T(8,128)(2,1)} %get-tuple-element.419), channel_id=1, source_target_pairs={{0,4},{1,5},{2,6},{3,7},{4,0},{5,1},{6,2},{7,3},{8,12},{9,13},{10,... | collective-permute-start | bytes 6291464 | tf_op jit(solution)/shard_map/ppermute | solution.py:426
  833.4 33.5 %collective-permute-start.93 = (bf16[2,2,128,1024]{3,2,1,0:T(8,128)(2,1)}, bf16[2,2,128,1024]{3,2,1,0:T(8,128)(2,1)}, u32[]{:S(2)}, u32[]{:S(2)}) collective-permute-start(bf16[2,2,128,1024]{3,2,1,0:T(8,128)(2,1)} %pad_maximum_fusion.7), channel_id=1, source_target_pairs={{0,1},{1,0},{2,3},{3,2},{4,5},{5,4},{6,7},{7,6},{8,9},{9,8},{10,11... | collective-permute-start | bytes 3145736 | tf_op jit(solution)/shard_map/ppermute | solution.py:426
  837.7 28.4 %collective-permute-start.86 = (f32[2,9,128]{2,1,0:T(8,128)}, f32[2,9,128]{2,1,0:T(8,128)}, u32[]{:S(2)}, u32[]{:S(2)}) collective-permute-start(f32[2,9,128]{2,1,0:T(8,128)} %get-tuple-element.533), channel_id=1, source_target_pairs={{0,1},{1,0},{2,3},{3,2},{4,5},{5,4},{6,7},{7,6},{8,9},{9,8},{10,11... | collective-permute-start | bytes 27656 | tf_op jit(solution)/shard_map/ppermute | solution.py:426
  860.0 63.5 %collective-permute-start.81 = (bf16[512,1024]{1,0:T(8,128)(2,1)}, bf16[512,1024]{1,0:T(8,128)(2,1)}, u32[]{:S(2)}, u32[]{:S(2)}) collective-permute-start(bf16[512,1024]{1,0:T(8,128)(2,1)} %get-tuple-element.402), channel_id=1, source_target_pairs={{2,4},{3,5},{4,2},{5,3},{10,12},{11,13},{12,10},{13,11},{18,20},{1... | collective-permute-start | bytes 3145736 | tf_op jit(solution)/shard_map/ppermute | solution.py:439
  869.5 40.5 %collective-permute-start.95 = (bf16[2,128,1024]{2,1,0:T(8,128)(2,1)S(1)}, bf16[2,128,1024]{2,1,0:T(8,128)(2,1)S(1)}, u32[]{:S(2)}, u32[]{:S(2)}) collective-permute-start(bf16[2,128,1024]{2,1,0:T(8,128)(2,1)S(1)} %get-tuple-element.488), channel_id=1, source_target_pairs={{0,4},{1,5},{2,6},{3,7},{4,2},{5,3},{6,0},{7,1},{8,12},{9,13},{10,... | collective-permute-start | bytes 1572872 | tf_op jit(solution)/shard_map/ppermute | solution.py:431
  874.2 37.6 %collective-permute-start.89 = (bf16[2,2,128,1024]{3,2,1,0:T(8,128)(2,1)S(1)}, bf16[2,2,128,1024]{3,2,1,0:T(8,128)(2,1)S(1)}, u32[]{:S(2)}, u32[]{:S(2)}) collective-permute-start(bf16[2,2,128,1024]{3,2,1,0:T(8,128)(2,1)S(1)} %get-tuple-element.476), channel_id=1, source_target_pairs={{0,16},{1,17},{2,18},{3,19},{4,20},{5,21},{6,22},{7,23},{8,24},{9,... | collective-permute-start | bytes 3145736 | tf_op jit(solution)/shard_map/ppermute | solution.py:426
  (117 other events, 1109.3 us)

commit v4 on v3

--- a/solution.py
+++ b/solution.py
@@ -437,6 +437,17 @@
         return (i & ~6) | (z1 << 2) | (core << 1)
 
     return lax.ppermute(values, AXES, [(i, target(i)) for i in range(32) if target(i) != i])
+
+
+CHIPS = [[0, 2, 4, 6], [1, 3, 5, 7]]
+
+
+def plane_gather(values):
+    return lax.all_gather(values, "dp", axis_index_groups=CHIPS, axis=0, tiled=False)
+
+
+def plane_scatter(values):
+    return lax.psum_scatter(values, "dp", axis_index_groups=CHIPS, scatter_dimension=0, tiled=False)
 
 
 def turn_index(values, own):
@@ -759,19 +770,22 @@
 
 def head_columns(refs, quarter, first, last):
     return jnp.concatenate(
-        [refs[odd][chip, 1 - quarter if odd else quarter, :, first:last] for chip in range(4) for odd in range(2)], axis=0
-    )
-
-
-def in_vmem(count):
-    return [pl.BlockSpec(memory_space=pltpu.VMEM)] * count
-
-
-def call_once(kernel, name, outs, args, us, scalars=0):
+        [refs[odd][chip ^ refs[2][0], 1 - quarter if odd else quarter, :, first:last] for chip in range(4) for odd in range(2)],
+        axis=0,
+    )
+
+
+def placed(arrays):
+    return [
+        pl.BlockSpec(memory_space=pltpu.SMEM if a.dtype == jnp.int32 else pltpu.VMEM) for a in arrays
+    ]
+
+
+def call_once(kernel, name, outs, args, us):
     return pl.pallas_call(
         kernel,
-        in_specs=[pl.BlockSpec(memory_space=pltpu.SMEM)] * scalars + in_vmem(len(args) - scalars),
-        out_specs=in_vmem(len(outs)),
+        in_specs=placed(args),
+        out_specs=placed(outs),
         out_shape=outs,
         compiler_params=pltpu.CompilerParams(vmem_limit_bytes=VMEM_LIMIT),
         cost_estimate=took(us),
@@ -780,7 +794,7 @@
 
 
 def project_kernel(rows_ref, bias_ref, *rest):
-    weight_refs, out_refs = rest[:2], rest[2:]
+    weight_refs, out_refs = rest[:3], rest[3:]
     rows = rows_ref[...]
     for quarter in (1, 0):
         out = dot_nn(rows, head_columns(weight_refs, quarter, 0, 768)) + bias_ref[quarter:quarter + 1]
@@ -799,7 +813,7 @@
 
 
 def mix_far_kernel(mine_ref, other_ref, *rest):
-    rest[2][...] = mix_term((mine_ref, other_ref), rest[:2]).astype(BF)
+    rest[3][...] = mix_term((mine_ref, other_ref), rest[:3]).astype(BF)
 
 
 def mix_far(mine, other, pieces):
@@ -808,7 +822,7 @@
 
 
 def mix_near_kernel(mine_ref, other_ref, far_ref, resid_ref, vector_ref, *rest):
-    weight_refs, (mid_ref, normed_ref, flip_ref) = rest[:2], rest[2:]
+    weight_refs, (mid_ref, normed_ref, flip_ref) = rest[:3], rest[3:]
     term = mix_term((mine_ref, other_ref), weight_refs)
     mid = resid_ref[...] + (term + far_ref[...].astype(F32) + vector_ref[2:3])
     mid_ref[...] = mid
@@ -827,7 +841,7 @@
 
 
 def unmix_kernel(grad_ref, *rest):
-    weight_refs, out_refs = rest[:2], rest[2:]
+    weight_refs, out_refs = rest[:3], rest[3:]
     grad = grad_ref[...]
     for quarter in (1, 0):
         out_refs[quarter][...] = dot_nn(grad, head_columns(weight_refs, quarter, 768, 1024)).astype(BF)
@@ -847,7 +861,7 @@
 
 
 def unproject_far_kernel(*rest):
-    rest[6][...] = unproject_term((rest[0:2], rest[2:4]), rest[4:6], 512).astype(BF)
+    rest[7][...] = unproject_term((rest[0:2], rest[2:4]), rest[4:7], 512).astype(BF)
 
 
 def unproject_far(mine, other, pieces):
@@ -858,7 +872,7 @@
 def unproject_near_kernel(last, own_ref, *rest):
     mine, other, rest = rest[0:2], rest[2:4], rest[4:]
     far_ref, resid_ref, grad_mid_ref, vector_ref, rest = *rest[:4], rest[4:]
-    weight_refs, (grad_ref, low_ref, sums_ref) = rest[:2], rest[2:]
+    weight_refs, (grad_ref, low_ref, sums_ref) = rest[:3], rest[3:]
     term = unproject_term((mine, other), weight_refs, 0) + far_ref[...].astype(F32)
     grad_norm, grad_gain, grad_shift = norm_pull(resid_ref[...], vector_ref[0:1], term)
     grad = grad_mid_ref[...] + grad_norm
@@ -878,10 +892,10 @@
     ]
     args = [own_keep, *mine, *other, far, resid, grad_mid, vectors, *pieces]
     kernel = functools.partial(unproject_near_kernel, last)
-    return call_once(kernel, "unproject_near", outs, args, 9, scalars=1)
-
-
-def head_grads_kernel(near_ref, far_ref, grad_near_ref, grad_far_ref, *rest):
+    return call_once(kernel, "unproject_near", outs, args, 9)
+
+
+def head_grads_kernel(turn_ref, near_ref, far_ref, grad_near_ref, grad_far_ref, *rest):
     pairs, rest = (rest[0:2], rest[2:4]), rest[4:]
     mixed_refs, out_refs, bias_ref = (rest[0:2], rest[2:4]), rest[4:6], rest[6]
     rows_t = jnp.concatenate([near_ref[...], far_ref[...]], axis=0).T
@@ -897,16 +911,16 @@
             for index in range(8):
                 chip, odd = index // 2, index % 2
                 place = 1 - quarter if odd else quarter
-                out_refs[odd][chip, place, :, part * 256:(part + 1) * 256] = term[index * 128:(index + 1) * 128]
+                out_refs[odd][chip ^ turn_ref[0], place, :, part * 256:(part + 1) * 256] = term[index * 128:(index + 1) * 128]
         for row, part in ((0, 0), (1, 2)):
             total = jnp.sum(grads[part].astype(F32), axis=0, keepdims=True)
             bias_ref[2 * quarter + row:2 * quarter + row + 1, :] = total
     bias_ref[4:8, :] = jnp.zeros((4, 256), F32)
 
 
-def head_grads(near, far, grad_near, grad_far, mine, other, mixed_mine, mixed_other):
+def head_grads(turn, near, far, grad_near, grad_far, mine, other, mixed_mine, mixed_other):
     outs = [jax.ShapeDtypeStruct((4, 2, 128, 1024), BF)] * 2 + [jax.ShapeDtypeStruct((8, 256), F32)]
-    args = [near, far, grad_near, grad_far, *mine, *other, *mixed_mine, *mixed_other]
+    args = [turn, near, far, grad_near, grad_far, *mine, *other, *mixed_mine, *mixed_other]
     return call_once(head_grads_kernel, "head_grads", outs, args, 10)
 
 
@@ -926,10 +940,6 @@
     inner = grad_unit - jnp.mean(grad_unit, axis=-1, keepdims=True)
     inner = inner - unit * jnp.mean(grad_unit * unit, axis=-1, keepdims=True)
     return spread * inner, jnp.sum(grad * unit, axis=0, keepdims=True), jnp.sum(grad, axis=0, keepdims=True)
-
-
-def joined(refs, first, last):
-    return jnp.concatenate([ref[0, :, first:last] for ref in refs], axis=0)
 
 
 def flipped(values):
@@ -972,11 +982,19 @@
     )(own_keep, direct, moved, vectors)
 
 
-def half_specs(tile):
-    def spec(half):
-        return pl.BlockSpec((2, 128, 2 * tile), lambda f: (0, 0, jnp.clip(f - 2 * half, 0, 1)))
-
-    return [spec(half) for half in range(2) for _ in range(4)]
+def half_specs(tile, weights):
+    def spec(half, chip, whole):
+        def index(f, turn):
+            column = jnp.clip(f - 2 * half, 0, 1)
+            return (chip ^ turn[0], 0, 0, column) if whole else (0, 0, column)
+
+        return pl.BlockSpec((None, 2, 128, 2 * tile) if whole else (2, 128, 2 * tile), index)
+
+    return [spec(half, chip, len(weights[half]) == 1) for half in range(2) for chip in range(4)]
+
+
+def half_arrays(weights):
+    return [array for half in weights for array in (half if len(half) == 4 else half * 4)]
 
 
 def by_half(step, weight_refs, body):
@@ -993,25 +1011,7 @@
     return jnp.concatenate([ref[core, :, first:last] for ref in refs for core in range(2)], axis=0)
 
 
-GELU_A = 0.7978845608028654
-GELU_B = 0.044715
-
-
-def normalize(values):
-    centred = values - jnp.mean(values, axis=-1, keepdims=True)
-    spread = lax.rsqrt(jnp.mean(centred * centred, axis=-1, keepdims=True) + NORM_EPS)
-    return centred * spread, spread
-
-
-def norm_pull(values, gain, grad):
-    unit, spread = normalize(values)
-    grad_unit = grad * gain
-    inner = grad_unit - jnp.mean(grad_unit, axis=-1, keepdims=True)
-    inner = inner - unit * jnp.mean(grad_unit * unit, axis=-1, keepdims=True)
-    return spread * inner, jnp.sum(grad * unit, axis=0, keepdims=True), jnp.sum(grad, axis=0, keepdims=True)
-
-
-def mlp_kernel(normed_ref, other_ref, bias_ref, *rest):
+def mlp_kernel(turn_ref, normed_ref, other_ref, bias_ref, *rest):
     weight_refs, (hidden_ref, active_ref, near_ref, away_ref, acc_ref) = rest[:8], rest[8:]
     rows, tile = normed_ref.shape[0], hidden_ref.shape[1]
     step = pl.program_id(0)
@@ -1038,28 +1038,31 @@
         away_ref[...] = flipped(acc_ref[rows:]).astype(BF)
 
 
-def mlp_forward(normed, other, bias, weights):
+def mlp_forward(turn, normed, other, bias, weights):
     rows, features = normed.shape
     units = bias.shape[1]
     tile = 512
-    whole = pl.BlockSpec((rows, features), lambda f: (0, 0))
-    tiles = pl.BlockSpec((2 * rows, tile), lambda f: (0, f))
+    whole = pl.BlockSpec((rows, features), lambda f, turn: (0, 0))
+    tiles = pl.BlockSpec((2 * rows, tile), lambda f, turn: (0, f))
     return pl.pallas_call(
         mlp_kernel,
-        grid=(units // tile,),
-        in_specs=[whole, whole, pl.BlockSpec((1, tile), lambda f: (0, f))] + half_specs(tile),
-        out_specs=[tiles, tiles, whole, whole],
+        grid_spec=pltpu.PrefetchScalarGridSpec(
+            num_scalar_prefetch=1,
+            grid=(units // tile,),
+            in_specs=[whole, whole, pl.BlockSpec((1, tile), lambda f, turn: (0, f))] + half_specs(tile, weights),
+            out_specs=[tiles, tiles, whole, whole],
+            scratch_shapes=[pltpu.VMEM((2 * rows, features), F32)],
+        ),
         out_shape=[
             jax.ShapeDtypeStruct((2 * rows, units), BF),
             jax.ShapeDtypeStruct((2 * rows, units), BF),
             jax.ShapeDtypeStruct((rows, features), F32),
             jax.ShapeDtypeStruct((rows, features), BF),
         ],
-        scratch_shapes=[pltpu.VMEM((2 * rows, features), F32)],
         compiler_params=pltpu.CompilerParams(vmem_limit_bytes=VMEM_LIMIT),
         cost_estimate=took(18),
         name="mlp_forward",
-    )(normed, other, bias, *weights)
+    )(turn, normed, other, bias, *half_arrays(weights))
 
 
 def mlp_close_kernel(last, own_ref, near_ref, got_ref, mid_ref, vector_ref, out_ref, next_ref):
@@ -1074,10 +1077,10 @@
 def mlp_close(last, own_keep, near, got, mid, vectors):
     outs = [jax.ShapeDtypeStruct(mid.shape, F32), jax.ShapeDtypeStruct(mid.shape, BF)]
     args = [own_keep, near, got, mid, vectors]
-    return call_once(functools.partial(mlp_close_kernel, last), "mlp_close", outs, args, 3, scalars=1)
-
-
-def mlp_pull_kernel(grad_ref, other_ref, hidden_ref, *rest):
+    return call_once(functools.partial(mlp_close_kernel, last), "mlp_close", outs, args, 3)
+
+
+def mlp_pull_kernel(turn_ref, grad_ref, other_ref, hidden_ref, *rest):
     weight_refs = rest[:8]
     grad_hidden_ref, grad_bias_ref, near_ref, away_ref, acc_ref, low_ref = rest[8:]
     rows, tile = grad_ref.shape[0], hidden_ref.shape[1]
@@ -1113,28 +1116,31 @@
         away_ref[...] = flipped(acc_ref[rows:]).astype(BF)
 
 
-def mlp_backward(grad, other, hidden, weights):
+def mlp_backward(turn, grad, other, hidden, weights):
     rows, features = grad.shape
     units = hidden.shape[1]
     tile = 512
-    whole = pl.BlockSpec((rows, features), lambda f: (0, 0))
-    tiles = pl.BlockSpec((2 * rows, tile), lambda f: (0, f))
+    whole = pl.BlockSpec((rows, features), lambda f, turn: (0, 0))
+    tiles = pl.BlockSpec((2 * rows, tile), lambda f, turn: (0, f))
     return pl.pallas_call(
         mlp_pull_kernel,
-        grid=(units // tile,),
-        in_specs=[whole, whole, tiles] + half_specs(tile),
-        out_specs=[tiles, pl.BlockSpec((1, tile), lambda f: (0, f)), whole, whole],
+        grid_spec=pltpu.PrefetchScalarGridSpec(
+            num_scalar_prefetch=1,
+            grid=(units // tile,),
+            in_specs=[whole, whole, tiles] + half_specs(tile, weights),
+            out_specs=[tiles, pl.BlockSpec((1, tile), lambda f, turn: (0, f)), whole, whole],
+            scratch_shapes=[pltpu.VMEM((2 * rows, features), F32), pltpu.VMEM((2 * rows, features), BF)],
+        ),
         out_shape=[
             jax.ShapeDtypeStruct((2 * rows, units), BF),
             jax.ShapeDtypeStruct((1, units), F32),
             jax.ShapeDtypeStruct((rows, features), F32),
             jax.ShapeDtypeStruct((rows, features), BF),
         ],
-        scratch_shapes=[pltpu.VMEM((2 * rows, features), F32), pltpu.VMEM((2 * rows, features), BF)],
         compiler_params=pltpu.CompilerParams(vmem_limit_bytes=VMEM_LIMIT),
         cost_estimate=took(22),
         name="mlp_backward",
-    )(grad, other, hidden, *weights)
+    )(turn, grad, other, hidden, *half_arrays(weights))
 
 
 def mlp_open_kernel(near_ref, got_ref, mid_ref, grad_ref, vector_ref, grad_mid_ref, grad_low_ref, sums_ref):
@@ -1191,7 +1197,263 @@
     )(left, other, right)
 
 
-def fetch_heads(piece, core, out):
+def unit_grads_whole_kernel(turn_ref, left_ref, other_ref, right_ref, out_ref, left_t_ref):
+    @pl.when(pl.program_id(0) == 0)
+    def _():
+        left_t_ref[...] = jnp.concatenate([left_ref[...].astype(BF), other_ref[...]], axis=0).T
+
+    grad = dot_nn(left_t_ref[...], right_ref[...]).astype(BF)
+    for chip in range(4):
+        for core in range(2):
+            first = (2 * chip + core) * 128
+            out_ref[chip ^ turn_ref[0], 0, core] = grad[first:first + 128]
+
+
+def unit_grads_whole(turn, left, other, right):
+    rows, features = left.shape
+    units = right.shape[1]
+    tile = 512
+    whole = pl.BlockSpec((rows, features), lambda f: (0, 0))
+    return pl.pallas_call(
+        unit_grads_whole_kernel,
+        grid=(units // tile,),
+        in_specs=[
+            pl.BlockSpec(memory_space=pltpu.SMEM),
+            whole,
+            whole,
+            pl.BlockSpec((2 * rows, tile), lambda f: (0, f)),
+        ],
+        out_specs=pl.BlockSpec((4, 1, 2, 128, tile), lambda f: (0, f // 2, 0, 0, f % 2)),
+        out_shape=jax.ShapeDtypeStruct((4, 2, 2, 128, 1024), BF),
+        scratch_shapes=[pltpu.VMEM((features, 2 * rows), BF)],
+        compiler_params=pltpu.CompilerParams(vmem_limit_bytes=VMEM_LIMIT),
+        cost_estimate=took(10),
+        name="unit_grads_whole",
+    )(turn, left, other, right)
+
+
+MESH = pl.DeviceIdType.MESH
+
+
+def flip(index, bit):
+    return index + bit - 2 * bit * ((index // bit) % 2)
+
+
+def peer(mask):
+    dp, tensor = lax.axis_index("dp"), lax.axis_index("tensor")
+    for bit in (1, 2):
+        tensor = flip(tensor, bit) if mask & bit else tensor
+        dp = flip(dp, bit) if mask & (CORE * bit) else dp
+    dp = flip(dp, 4) if mask & YBIT else dp
+    return {"dp": dp, "tensor": tensor}
+
+
+def xor_block(block, own):
+    return sum(bit * ((block // bit + own // bit) % 2) for bit in (1, 2, 4))
+
+
+def greet(masks):
+    barrier = pltpu.get_barrier_semaphore()
+    for mask in masks:
+        pl.semaphore_signal(barrier, inc=1, device_id=peer(mask), device_id_type=MESH)
+    pl.semaphore_wait(barrier, len(masks))
+
+
+def project_rows(rows, weight_refs, bias_ref, layer, out_refs):
+    for quarter in (1, 0):
+        weight = jnp.concatenate(
+            [weight_refs[odd][chip, 1 - quarter if odd else quarter, :, 0:768] for chip in range(4) for odd in range(2)],
+            axis=0,
+        )
+        out_refs[quarter][...] = (dot_nn(rows, weight) + bias_ref[layer, quarter:quarter + 1]).astype(BF)
+
+
+SMALL_ROWS = 11
+
+
+def start_kernel(
+    layers, x_ref, project_ref, output_ref, expand_ref, reduce_ref, small_ref,
+    resid_ref, normed_ref, far_ref, even_ref, odd_ref, first_ref, vector_ref, head_bias_ref, unit_bias_ref,
+    near_mine_ref, far_mine_ref, got_near_ref, got_far_ref,
+    came_ref, piece_ref, every_ref, near_other_ref, far_other_ref, local_sem, send_sem, recv_sem,
+):
+    own, place = lax.axis_index("dp"), lax.axis_index("tensor")
+    core = own % 2
+    keep = core == place // 2
+    count = [0]
+
+    def copy(source, target, device):
+        index = count[0]
+        count[0] += 1
+        return pltpu.make_async_remote_copy(
+            src_ref=source, dst_ref=target, send_sem=send_sem.at[index], recv_sem=recv_sem.at[index],
+            device_id=device, device_id_type=MESH,
+        )
+
+    greet((1, 2, 4, 6, 8, 16))
+    tokens = copy(x_ref, came_ref, peer(CORE | Z1))
+    stay = pltpu.make_async_copy(x_ref, came_ref, local_sem)
+
+    @pl.when(keep)
+    def _():
+        stay.start()
+
+    @pl.when(jnp.logical_not(keep))
+    def _():
+        tokens.start()
+
+    for part in range(3):
+        even_ref[0, core, :, part * 256:(part + 1) * 256] = project_ref[0, part]
+    even_ref[0, core, :, 768:1024] = output_ref[0].T
+    along = copy(even_ref.at[0, core], even_ref.at[0, 1 - core], peer(Z1))
+    along.start()
+    every_ref[0, 0] = small_ref[...]
+    smalls = [
+        (copy(every_ref.at[0, pl.ds(0, width)], every_ref.at[0, pl.ds(width, width)], peer(mask)))
+        for width, mask in ((1, CORE), (2, XBIT), (4, YBIT))
+    ]
+    smalls += [
+        copy(every_ref.at[pl.ds(0, width)], every_ref.at[pl.ds(width, width)], peer(mask)) for width, mask in ((1, Z0), (2, Z1))
+    ]
+    smalls[0].start()
+    for half in range(2):
+        here = slice(half * 512, (half + 1) * 512)
+        piece_ref[:, half * 1024:half * 1024 + 512] = expand_ref[0, :, here]
+        piece_ref[:, half * 1024 + 512:half * 1024 + 1024] = reduce_ref[0, here, :].T
+    cross = copy(piece_ref, first_ref.at[1], {
+        "dp": flip(own, 1), "tensor": place + (1 - core) * (flip(place, 2) - place)
+    })
+    same = copy(piece_ref, first_ref.at[0], peer(Z1))
+
+    @pl.when(core == 0)
+    def _():
+        first_ref[0] = piece_ref[...]
+
+    for step in range(1, 5):
+        smalls[step - 1].wait()
+        smalls[step].start()
+    along.wait()
+    over_x = copy(even_ref.at[0], even_ref.at[1], peer(XBIT))
+    over_y = copy(even_ref.at[0], even_ref.at[2], peer(YBIT))
+    over_x.start()
+    over_y.start()
+    cores = [copy(even_ref.at[chip], odd_ref.at[chip], peer(CORE)) for chip in range(4)]
+    cores[0].start()
+    smalls[4].wait()
+    for layer in range(layers):
+        base = layer * SMALL_ROWS
+        later = min(layer + 1, layers - 1) * SMALL_ROWS
+        rows = [base + row for row in range(6)] + [later, later + 1]
+        for row, source in enumerate(rows):
+            vector_ref[layer, row:row + 1, :] = jnp.concatenate(
+                [every_ref[0, block, source:source + 1, :] for block in range(8)], axis=1
+            )
+        for quarter in range(2):
+            which = 2 * (core + quarter - 2 * core * quarter)
+            total = every_ref[which, 0, base + 6:base + 10, :]
+            for block in range(1, 8):
+                total = total + every_ref[which, block, base + 6:base + 10, :]
+            head_bias_ref[layer, quarter:quarter + 1, :] = jnp.concatenate(
+                [total[0:1], total[1:2], jnp.zeros((1, 256), F32), total[2:3], total[3:4]], axis=1
+            )
+            for block in range(8):
+                unit_bias_ref[layer, :, quarter * 1024 + block * 128:quarter * 1024 + (block + 1) * 128] = every_ref[
+                    2 * core + quarter, xor_block(block, own), base + 10:base + 11, :
+                ]
+    over_y.wait()
+    over_x.wait()
+    across = copy(even_ref.at[2], even_ref.at[3], peer(XBIT))
+    across.start()
+    cores[1].start()
+    cores[2].start()
+
+    @pl.when(keep)
+    def _():
+        stay.wait()
+
+    @pl.when(jnp.logical_not(keep))
+    def _():
+        tokens.wait()
+
+    for block in range(8):
+        here = pl.ds(pl.multiple_of(xor_block(block, own) * 128, 128), 128)
+        resid_ref[:, block * 128:(block + 1) * 128] = came_ref[:, here].astype(F32)
+    normed = (normalize(resid_ref[...])[0] * vector_ref[0, 0:1] + vector_ref[0, 1:2]).astype(BF)
+    normed_ref[...] = normed
+    beside = copy(normed_ref, far_ref, peer(Z0))
+    beside.start()
+    cross.start()
+
+    @pl.when(core == 1)
+    def _():
+        same.start()
+
+    across.wait()
+    cores[3].start()
+    for one in cores:
+        one.wait()
+    weights = (even_ref, odd_ref)
+    project_rows(normed_ref[...], weights, head_bias_ref, 0, (near_mine_ref, near_other_ref))
+    back_near = copy(near_other_ref, got_near_ref, peer(CORE))
+    back_near.start()
+    beside.wait()
+    project_rows(far_ref[...], weights, head_bias_ref, 0, (far_mine_ref, far_other_ref))
+    back_far = copy(far_other_ref, got_far_ref, peer(CORE))
+    back_far.start()
+    cross.wait()
+
+    @pl.when(core == 1)
+    def _():
+        same.wait()
+
+    back_near.wait()
+    back_far.wait()
+
+
+def start(x, project_weight, output_weight, expand_weight, reduce_weight, small, layers):
+    rows, features = x.shape
+    vmem = pl.BlockSpec(memory_space=pltpu.VMEM)
+
+    triple = jax.ShapeDtypeStruct((rows, 768), BF)
+    heads = jax.ShapeDtypeStruct((4, 2, 128, 1024), BF)
+    outs = [
+        jax.ShapeDtypeStruct((rows, features), F32),
+        jax.ShapeDtypeStruct((rows, features), BF),
+        jax.ShapeDtypeStruct((rows, features), BF),
+        heads,
+        heads,
+        jax.ShapeDtypeStruct((2, 128, 2048), BF),
+        jax.ShapeDtypeStruct((layers, 8, features), F32),
+        jax.ShapeDtypeStruct((layers, 2, 768), F32),
+        jax.ShapeDtypeStruct((layers, 1, 2048), F32),
+        triple,
+        triple,
+        triple,
+        triple,
+    ]
+    copies = 19
+    return pl.pallas_call(
+        functools.partial(start_kernel, layers),
+        in_specs=[vmem] * 6,
+        out_specs=[vmem] * len(outs),
+        out_shape=outs,
+        scratch_shapes=[
+            pltpu.VMEM((rows, features), BF),
+            pltpu.VMEM((128, 2048), BF),
+            pltpu.VMEM((4, 8, *small.shape), F32),
+            pltpu.VMEM((rows, 768), BF),
+            pltpu.VMEM((rows, 768), BF),
+            pltpu.SemaphoreType.DMA,
+            pltpu.SemaphoreType.DMA((copies,)),
+            pltpu.SemaphoreType.DMA((copies,)),
+        ],
+        compiler_params=pltpu.CompilerParams(vmem_limit_bytes=VMEM_LIMIT, collective_id=0, has_side_effects=True),
+        cost_estimate=took(60),
+        name="start",
+    )(x, project_weight, output_weight, expand_weight, reduce_weight, small)
+
+
+def fetch_heads(piece, core, turn, out):
     token = yield
     far = swap(after(piece, token), Z1)
     token = yield []
@@ -1206,20 +1468,36 @@
     quads = jnp.stack([own, from_x, from_y, after(across, token)])
     other = swap(quads, CORE)
     token = yield [quads]
-    out += [quads, other]
+    out += [quads, other, turn]
+
+
+def fetch_units_near(first, first_out, second_out):
+    token = yield
+    first = after(first, token)
+    first_x, first_y, second = swap(first, XBIT), swap(first, YBIT), swap(first, Z0)
+    token = yield []
+    first_x, first_y, second = after_all((first_x, first_y, second), token)
+    yield from join_units(first, first_x, first_y, second, first_out, second_out)
 
 
 def fetch_units(piece, core, first_out, second_out):
     token = yield
     piece = after(piece, token)
-    same, cross = swap_some(piece, (0, Z1)), swap_some(piece, (CORE | Z1, CORE))
+    pair = jnp.stack([piece, swap(piece, CORE)])
+    far = swap_some(pair, (0, Z1))
+    token = yield [pair]
+    first = jnp.where(core == 0, pair, after(far, token))
+    token = yield [first]
+    second = swap(after(first, token), Z0)
     token = yield []
-    same, cross = after_all((same, cross), token)
-    first = jnp.stack([jnp.where(core == 0, piece, same), cross])
+    first, second = after_all((first, second), token)
     first_x, first_y = swap(first, XBIT), swap(first, YBIT)
-    second = swap(first, Z0)
-    token = yield [first]
-    first_x, first_y, second = after_all((first_x, first_y, second), token)
+    token = yield [second]
+    first_x, first_y = after_all((first_x, first_y), token)
+    yield from join_units(first, first_x, first_y, second, first_out, second_out)
+
+
+def join_units(first, first_x, first_y, second, first_out, second_out):
     second_x, second_y = swap(second, XBIT), swap(second, YBIT)
     token = yield [first_x, first_y, second]
     second_x, second_y = after_all((second_x, second_y), token)
@@ -1244,58 +1522,57 @@
     return jnp.stack(parts, axis=2).reshape(128, 2048)
 
 
-def fetch_small(six, project_bias, expand_bias, own, core):
+def small_rows(six, project_bias, expand_bias, own):
     layers = six.shape[1]
-    wide = jnp.pad(project_bias, ((0, 0), (0, 0), (0, 96)))
-    rows = jnp.concatenate([six.transpose(1, 0, 2), wide, expand_bias[:, None, :]], axis=1).astype(F32)[None]
+    wide = jnp.zeros((layers, 2, 256), F32)
+    wide = lax.dynamic_update_slice(wide, project_bias.astype(F32), (0, 0, own * 32))
+    rows = jnp.concatenate(
+        [six.transpose(1, 0, 2).astype(F32), wide.reshape(layers, 4, 128), expand_bias[:, None, :].astype(F32)], axis=1
+    )
+    return jnp.pad(rows.reshape(layers * SMALL_ROWS, 128), ((0, -layers * SMALL_ROWS % 8), (0, 0)))
+
+
+def pack_kernel(count, own_ref, *rest):
+    out_ref, own = rest[-1], own_ref[0]
+    core = own % 2
+    out_ref[...] = jnp.zeros_like(out_ref)
+    for layer in range(count):
+        first_ref, second_ref, unit_ref, head_ref = rest[4 * layer:4 * layer + 4]
+        for place in range(8):
+            here = slice(place * 128, (place + 1) * 128)
+            out_ref[place, 6 * layer:6 * layer + 2, :] = first_ref[0:2, here]
+            out_ref[place, 6 * layer + 2:6 * layer + 6, :] = second_ref[0:4, here]
+            base = 6 * count + 12 * layer
+            for quarter in range(2):
+                lane = pl.multiple_of(quarter * 1024 + (place ^ own) * 128, 128)
+                out_ref[place, pl.ds(base + 2 * core + quarter, 1), :] = unit_ref[0:1, pl.ds(lane, 128)]
+                row = base + 4 + 4 * (quarter ^ core)
+                for half in range(2):
+                    out_ref[place, pl.ds(row + 2 * half, 2), :] = head_ref[2 * quarter:2 * quarter + 2, half * 128:(half + 1) * 128]
+
+
+def sum_small(layers, own, own_keep, token):
+    count = len(layers)
+    rows = 18 * count
+    args = [own_keep] + [array for layer in layers for array in layer]
+    rows = call_once(
+        functools.partial(pack_kernel, count), "pack", [jax.ShapeDtypeStruct((8, rows, 128), F32)], args, 3
+    )[0]
+    rows = after(rows, token)
     for mask in (CORE, XBIT, YBIT):
-        rows = jnp.concatenate([rows, swap(rows, mask)], axis=0)
-    vectors = rows[:, :, :6].transpose(1, 2, 0, 3).reshape(layers, 6, 1024)
-    local = turn_index(rows[:, :, 6:], own).transpose(1, 2, 0, 3)[None]
-    for mask in (Z0, Z1):
-        local = jnp.concatenate([local, swap(local, mask)], axis=0)
-    native = local.transpose(1, 0, 2, 3, 4)
-    out = []
-    for layer in range(layers):
-        pair = native[layer, ::2, :2, :, :32].reshape(2, 2, 256)
-        pair = jnp.where(core == 0, pair, pair[::-1])
-        head_bias = jnp.concatenate([pair[:, 0], jnp.zeros((2, 256), F32), pair[:, 1]], axis=1)
-        unit_bias = native[layer, :, 2].reshape(2, 1, 2048)
-        unit_bias = jnp.where(core == 0, unit_bias[0], unit_bias[1])
-        following = vectors[min(layer + 1, layers - 1), :2]
-        out.append((jnp.concatenate([vectors[layer], following], axis=0), head_bias, unit_bias))
-    return out
-
-
-def spread_sums(rows):
-    rows = rows.reshape(2, 2, 2, rows.shape[1], 128)
-    rows = rows[:, :, 0] + swap(rows[:, :, 1], CORE)
-    rows = rows[:, 0] + swap(rows[:, 1], XBIT)
-    return rows[0] + swap(rows[1], YBIT)
-
-
-def sum_small(layers, own, core):
-    count = len(layers)
-    vectors, biases = [], []
-    for first_sums, second_sums, unit_sums, head_sums in layers:
-        vectors += [first_sums[:2], second_sums[:4]]
-        heads = head_sums[:4].reshape(2, 2, 256)
-        heads = jnp.where(core == 0, heads, heads[::-1]).reshape(4, 8, 32)
-        heads = jnp.pad(heads, ((0, 0), (0, 0), (0, 96)))
-        units = unit_sums.reshape(2, 8, 128)
-        none = jnp.zeros_like(units)
-        biases += [jnp.where(core == 0, units, none), jnp.where(core == 0, none, units), heads]
-    vectors = jnp.concatenate(vectors, axis=0).reshape(6 * count, 8, 128).transpose(1, 0, 2)
-    biases = turn_index(jnp.concatenate(biases, axis=0).transpose(1, 0, 2), own)
-    rows = spread_sums(jnp.concatenate([vectors, biases], axis=1))
-    vectors, biases = rows[:6 * count].reshape(count, 6, 128), rows[6 * count:].reshape(count, 8, 128)
-
-    def part(offset):
-        return jnp.concatenate([vectors, biases[:, offset:offset + 1], biases[:, 6:8]], axis=1)
-
-    two = swap(part(2), 2)
-    whole = jnp.concatenate([vectors, biases[:, :1]], axis=1) + two[:, :7] + swap(part(1), 1)[:, :7] + swap(part(3), 3)[:, :7]
-    return whole[:, :6], whole[:, 6], biases[:, 4:6, :32] + two[:, 7:, :32]
+        bit = rows.reshape(-1, 2, 18 * count, 128)
+        rows = bit[:, 0] + swap(bit[:, 1], mask)
+    vectors, biases = rows[0, :6 * count], rows[0, 6 * count:].reshape(count, 12, 128)
+
+    def part(offset, *more):
+        return jnp.concatenate([vectors, biases[:, offset], *more], axis=0)
+
+    two = swap(part(2, biases[:, 8:].reshape(4 * count, 128)), 2)
+    whole = part(0) + two[:7 * count] + swap(part(1), 1) + swap(part(3), 3)
+    heads = biases[:, 4:8] + two[7 * count:].reshape(count, 4, 128)
+    heads = heads.reshape(count, 2, 2, 128).transpose(0, 2, 1, 3).reshape(count, 2, 256)
+    heads = lax.dynamic_slice_in_dim(heads, own * 32, 32, 2)
+    return whole[:6 * count].reshape(count, 6, 128), whole[6 * count:], heads
 
 
 def reduce_heads(even, odd, core, out):
@@ -1311,11 +1588,16 @@
     relay = swap(relayed, XBIT)
     token = yield [relayed]
     total = low[0] + from_y[0] + after(relay, token)
+    yield from close_heads(total, core, out)
+
+
+def close_heads(total, core, out):
     near = jnp.where(core == 0, total[0], total[1])
     away = jnp.where(core == 0, total[1], total[0])
     far = swap(away, Z1)
     token = yield [near, away]
     out.append(unpack_heads(near.astype(F32) + after(far, token).astype(F32)))
+    yield list(out[-1])
 
 
 def reduce_units(reduce_parts, expand_parts, core, out):
@@ -1335,9 +1617,13 @@
     relay_e = swap(relayed_e, YBIT)
     token = yield [relayed_e]
     relay_r, relay_e = after_all((relay_r, relay_e), token)
-    here, away = [
+    totals = [
         jnp.stack([own_r[i] + from_y[i, 0] + relay_r[i], own_e[i] + from_x[i, 0] + relay_e[i]]) for i in range(2)
     ]
+    yield from close_units(*totals, core, out)
+
+
+def close_units(here, away, core, out):
     got = swap(away, Z0)
     token = yield [here, away]
     here = here + after(got, token)
@@ -1346,6 +1632,7 @@
     token = yield [same, cross]
     same_got, cross_got = after_all((same_got, cross_got), token)
     out.append(jnp.where(core == 0, same, same_got).astype(F32) + cross_got.astype(F32))
+    yield [out[-1]]
 
 
 def fast_device(
@@ -1374,40 +1661,39 @@
     slopes = head_slopes((place ^ (2 * core)) * 4, 4)
 
     six = jnp.stack([first_gain, first_shift, output_bias, second_gain, second_shift, reduce_bias])
-    head_piece = [pack_heads(project_weight[i], output_weight[i]) for i in range(LAYERS)]
-    unit_piece = [pack_units(expand_weight[i], reduce_weight[i]) for i in range(LAYERS)]
+    turn = jnp.zeros((1,), jnp.int32)
+    resid, normed, far, even, odd, ready, vectors_of, head_bias_of, unit_bias_of, *blocks = start(
+        layer_input, project_weight, output_weight, expand_weight, reduce_weight,
+        small_rows(six, project_bias, expand_bias, own), LAYERS,
+    )
+    near_mine, far_mine, got_near, got_far = blocks
+    small = [(vectors_of[i], head_bias_of[i], unit_bias_of[i]) for i in range(LAYERS)]
+    starts = jnp.where(keep, picture_start, redeal(picture_start))[0]
     heads, units = [[] for i in range(LAYERS)], [([], []) for i in range(LAYERS)]
-    head_tasks = [task(fetch_heads(head_piece[i], core, heads[i])) for i in range(LAYERS)]
-    unit_tasks = [task(fetch_units(unit_piece[i], core, *units[i])) for i in range(LAYERS)]
-
-    advance(layer_input, head_tasks[0])
-    small = fetch_small(six, project_bias, expand_bias, own, core)
-    dealt = redeal(layer_input)
-    starts = jnp.where(keep, picture_start, redeal(picture_start))[0]
-    advance(layer_input, unit_tasks[0])
-    made = advance(layer_input, head_tasks[0])
-    resid, normed, unused = enter(own_keep, layer_input, after(dealt, *made), small[0][0])
-    made = advance(normed, head_tasks[0])
-    normed = after(normed, *made)
-    advance(normed, head_tasks[0])
+    heads[0] += [even, odd, turn]
+    head_tasks, unit_tasks = [None], [task(fetch_units_near(ready, *units[0]))]
+    for layer in range(1, LAYERS):
+        weights = after_all((project_weight, output_weight, expand_weight, reduce_weight), far_mine)
+        head_piece = pack_heads(weights[0][layer], weights[1][layer])
+        unit_piece = pack_units(weights[2][layer], weights[3][layer])
+        head_tasks.append(task(fetch_heads(head_piece, core, turn, heads[layer])))
+        unit_tasks.append(task(fetch_units(unit_piece, core, *units[layer])))
     saved = []
     for layer in range(LAYERS):
         vectors, head_bias, unit_bias = small[layer]
         first, last = layer == 0, layer + 1 == LAYERS
-        far = swap(normed, Z0)
-        if not heads[layer]:
-            advance(normed, head_tasks[layer])
+        if not first:
+            far = swap(normed, Z0)
+            while not heads[layer]:
+                advance(normed, head_tasks[layer])
+            near_mine, near_other = project(normed, head_bias, heads[layer])
+            got_near = swap(near_other, CORE)
+            far_mine, far_other = project(after(far, near_mine), head_bias, heads[layer])
+            got_far = swap(far_other, CORE)
         pieces = heads[layer]
-        near_mine, near_other = project(normed, head_bias, pieces)
-        got_near = swap(near_other, CORE)
-        made = advance(near_mine, unit_tasks[layer])
-        far_mine, far_other = project(after(far, near_mine, *made), head_bias, pieces)
-        got_far = swap(far_other, CORE)
-        made = []
+        made = advance(far_mine, unit_tasks[layer])
         if first:
-            made += advance(far_mine, head_tasks[1], unit_tasks[1])
-        else:
-            made += advance(far_mine, unit_tasks[layer])
+            made += advance(far_mine, unit_tasks[1])
         blocks = after_all((near_mine, far_mine, got_near, got_far), *made)
         far_mixed, far_send, far_exact, far_log = attend(blocks, 1, slopes, starts, me)
         far_got = swap(far_send, CORE)
@@ -1417,33 +1703,36 @@
         near_blocks = after_all(blocks, far_part, *made)
         near_mixed, near_send, near_exact, near_log = attend(near_blocks, 0, slopes, starts, me)
         near_got = swap(near_send, CORE)
-        made = []
+        made = advance(near_mixed, unit_tasks[layer])
         if first:
-            made += advance(near_mixed, unit_tasks[0])
-        else:
+            made += advance(near_mixed, unit_tasks[1])
+        if last:
             cotangent_far = redeal(after(cotangent, near_mixed))
         mid, normed_two, flip_two = mix_near(near_mixed, near_got, after(far_term, near_mixed, *made), resid, vectors, pieces)
         normed_other = swap(flip_two, CORE)
+        if last:
+            grad, unused, flip_grad = enter(own_keep, cotangent, after(cotangent_far, mid), vectors)
+            grad_other = swap(flip_grad, CORE)
+            normed_two = after(normed_two, grad)
         if first:
-            made = advance(mid, unit_tasks[0], head_tasks[1], unit_tasks[1])
+            made = advance(mid, unit_tasks[0])
+            advance(mid, unit_tasks[1], head_tasks[1])
             normed_two = after(normed_two, *made)
-        hidden, active, near_out, away_out = mlp_forward(normed_two, normed_other, unit_bias, units[layer][0] + units[layer][1])
+        hidden, active, near_out, away_out = mlp_forward(turn, normed_two, normed_other, unit_bias, units[layer])
         got_out = swap(away_out, CORE)
         if not last:
-            made = advance(near_out, head_tasks[layer + 1])
-            got_out = after(got_out, *made)
+            got_out = after(got_out, *advance(near_out, head_tasks[layer + 1]))
         out, following = mlp_close(last, own_keep, near_out, got_out, mid, vectors)
         if not last:
             advance(out, head_tasks[layer + 1])
-        else:
-            grad, unused, flip_grad = enter(own_keep, cotangent, after(cotangent_far, out), vectors)
-            grad_other = swap(flip_grad, CORE)
+            advance(out, unit_tasks[layer + 1])
         saved.append((
             resid, normed, far, blocks, (near_exact, far_exact), (near_log, far_log), (near_mixed, far_mixed),
             (near_got, far_got), mid, normed_two, normed_other, hidden, active,
         ))
         resid, normed = out, following
     layer_output = jnp.where(keep, normed, redeal(normed))
+    grad = after(grad, normed)
     sums = [None] * LAYERS
     head_grad, unit_grad = ([[] for i in range(LAYERS)] for j in range(2))
     pending = []
@@ -1452,13 +1741,14 @@
         (
             resid, normed, far, blocks, exacts, logs, mixed, mixed_got, mid, normed_two, normed_other, hidden, active,
         ) = saved[layer]
-        grad_hidden, unit_sums, near_term, away_term = mlp_backward(grad, grad_other, hidden, units[layer][0] + units[layer][1])
-        got_term = after(swap(away_term, CORE), *advance(near_term, *pending[:1]))
+        grad_hidden, unit_sums, near_term, away_term = mlp_backward(turn, grad, grad_other, hidden, units[layer])
+        got_term = after(swap(away_term, CORE), *advance(near_term, *pending))
         grad_mid, grad_low, second_sums = mlp_open(near_term, got_term, mid, grad, vectors)
         grad_far = swap(grad_low, Z0)
-        made = advance(grad_low, *pending[1:])
-        reduce_parts = unit_grads("x", grad, grad_other, after(active, grad_low, *made))
-        near_mine, near_other = unmix(after(grad_low, reduce_parts[0]), pieces)
+        first = layer == 0
+        reduce_parts = unit_grads("x", grad, grad_other, after(active, grad_low))
+        made = advance(reduce_parts[0], *pending)
+        near_mine, near_other = unmix(after(grad_low, reduce_parts[0], *made), pieces)
         got_near = swap(near_other, CORE)
         expand_parts = unit_grads("y", normed_two, normed_other, after(grad_hidden, near_mine))
         unit_task = task(reduce_units(reduce_parts, expand_parts, core, unit_grad[layer]))
@@ -1470,7 +1760,7 @@
         grads_mixed = after_all((near_mine, far_mine, got_near, got_far), *made)
         mine_0, away_0 = attend_pull(0, blocks, grads_mixed, exacts, logs, slopes, starts, me)
         other_0 = swap(away_0, CORE)
-        made = advance(mine_0, unit_task, *pending)
+        made = advance(mine_0, unit_task)
         grads_mixed = after_all(grads_mixed, mine_0, *made)
         mine_1, away_1 = attend_pull(1, blocks, grads_mixed, exacts, logs, slopes, starts, me)
         other_1 = swap(away_1, CORE)
@@ -1478,24 +1768,26 @@
         mine, other = (mine_0, mine_1), (other_0, other_1)
         far_part = unproject_far(mine, other, pieces)
         far_term = swap(far_part, Z0)
-        even, odd, head_sums = head_grads(normed, far, grad_low, after(grad_far, far_part), mine, other, mixed, mixed_got)
+        even, odd, head_sums = head_grads(
+            turn, normed, far, grad_low, after(grad_far, far_part), mine, other, mixed, mixed_got
+        )
         head_task = task(reduce_heads(even, odd, core, head_grad[layer]))
         advance(None, head_task)
-        made = advance(head_sums, unit_task) if layer == 0 else [head_sums]
+        made = advance(head_sums, unit_task)
         grad, grad_low, first_sums = unproject_near(
-            layer == 0, own_keep, mine, other, after(far_term, *made), resid, grad_mid, vectors, pieces
+            first, own_keep, mine, other, after(far_term, *made), resid, grad_mid, vectors, pieces
         )
         sums[layer] = (first_sums, second_sums, unit_sums, head_sums)
-        if layer > 0:
+        if not first:
             grad_other = swap(grad_low, CORE)
             grad = after(grad, *advance(grad, head_task))
         pending = [unit_task, head_task]
     input_far = redeal(grad_low)
-    sums = after_all([row for layer in sums for row in layer], grad)
+    made = advance(grad, *pending)
+    six, unit_sum, head_sum = sum_small(sums, own, own_keep, made[0])
     while len(head_grad[0]) + len(unit_grad[0]) < 2:
-        made = advance(grad, *pending)
+        advance(grad, *pending)
     input_grad = jnp.where(keep, grad_low, input_far)
-    six, unit_sum, head_sum = sum_small([sums[4 * i:4 * i + 4] for i in range(LAYERS)], own, core)
     return (
         layer_output,
         input_grad,

time: 944 us -> 912 us (0.966)
  waiting for transfers between devices: 352 us -> 213 us
  Pallas kernels: 403 us -> 492 us
  starting transfers between devices: 96.8 us -> 124 us
    ppermute x85 -> x73, waiting for transfers between devices: 310 us -> 212 us  [swap(): return lax.ppermute(values, AXES, [(i, i ^ mask) for i in range(32)])]
    pallas_call x26, Pallas kernels: 207 us -> 301 us  [the longest x21 123 us: call_once(): pl.pallas_call(kernel, in_specs=placed(args), out_specs=placed(outs), out...]
    ppermute x8 -> x5, waiting for transfers between devices: 42.1 us -> 0.53 us  [swap_some(): lax.ppermute(values, AXES, [pair for pair in pairs if pair[0] != pair[1]])]
    ppermute x85 -> x73, starting transfers between devices: 75.4 us -> 109 us  [swap(): return lax.ppermute(values, AXES, [(i, i ^ mask) for i in range(32)])]
    unnamed x155 -> x124, local copies, waits for them, and re-layouts: 29.4 us -> 28.6 us
  transfers between devices with their start and end apart: 98 -> 82, of which waited for: 43 -> 38; matrix products, arithmetic and copies ran while one was open for 6% -> 4% of each run, Pallas kernels for 38% -> 36%
where the time goes in v4:
time: 912 us; the launch traced here: 902 us
  Pallas kernels  492 us (54%)
  waiting for transfers between devices  213 us (23%)
  starting transfers between devices  124 us (14%)
  local copies, waits for them, and re-layouts  40.4 us (4%)
  other arithmetic  30.2 us (3%)
    ppermute x73, waiting for transfers between devices, swap(): return lax.ppermute(values, AXES, [(i, i ^ mask) for i in range(32)])  212 us
    pallas_call x21, Pallas kernels, call_once(): pl.pallas_call(kernel, in_specs=placed(args), out_specs=placed(outs), out...  123 us
    ppermute x73, starting transfers between devices, swap(): return lax.ppermute(values, AXES, [(i, i ^ mask) for i in range(32)])  109 us
    pallas_call x1, Pallas kernels, start(): pl.pallas_call(functools.partial(start_kernel, layers), in_specs=[vmem] *...  92.4 us
    pallas_call x4, Pallas kernels, attend_pull(): pl.pallas_call(functools.partial(pull_kernel, block, pair), grid=(4,), in...  84.9 us
    pallas_call x4, Pallas kernels, attend(): pl.pallas_call(functools.partial(attend_kernel, block, rest_bit), grid=(p...  66 us
    pallas_call x2, Pallas kernels, mlp_forward(): pl.pallas_call(mlp_kernel, grid_spec=pltpu.PrefetchScalarGridSpec(num_sca...  45.2 us
    pallas_call x2, Pallas kernels, mlp_backward(): pl.pallas_call(mlp_pull_kernel, grid_spec=pltpu.PrefetchScalarGridSpec(nu...  41.1 us
  transfers between devices with their start and end apart: 82, of which 38 were waited for; matrix products, arithmetic and copies ran while one was open for 4% of the time, Pallas kernels for 36%

profile of v4, /device:TPU:0, one launch (start us, length us, event | category | flops | bytes accessed | tf_op | source)
XLA Modules:
  0.0 902.3 jit_solution(15739789908049624617)
XLA Ops:
  6.8 92.4 %start.1 = (f32[512,1024]{1,0:T(8,128)}, bf16[512,1024]{1,0:T(8,128)(2,1)}, bf16[512,1024]{1,0:T(8,128)(2,1)}, bf16[4,2,128,1024]{3,2,1,0:T(8,128)(2,1)}, bf16[4...) custom-call(bf16[512,1024]{1,0:T(8,128)(2,1)} %x_ref.1, ...), custom_call_target="tpu_custom_call" | custom-call | flops 30000001024 | bytes 1 | tf_op jit(solution)/shard_map/start/pallas_call | solution.py:1435
  106.6 18.8 %attend.4 = (bf16[512,256]{1,0:T(8,128)(2,1)}, bf16[512,256]{1,0:T(8,128)(2,1)}, f32[256,1024]{1,0:T(8,128)}, f32[2,8,1024]{2,1,0:T(8,128)}) custom-call(f32[4]{0:T(128)} %multiply_exponential_fusion.slope_ref, s32[2]{0:T(128)} %fusion.16.start_ref, s32[1]{0:T(128)} %bitcast.3.me_ref, bf16[512,768]{1,0:T(8,128)(2,1)} %get-tuple-element.244.rest_0_.rest_1_.rest_2_, ...), custom_call_target="tpu_custom_call" | custom-call | flops 8499999744 | bytes 1 | tf_op jit(solution)/shard_map/attend/pallas_call | solution.py:614
  125.4 19.2 %collective-permute-start.2 = (bf16[512,256]{1,0:T(8,128)(2,1)}, bf16[512,256]{1,0:T(8,128)(2,1)S(1)}, u32[]{:S(2)}, u32[]{:S(2)}) collective-permute-start(bf16[512,256]{1,0:T(8,128)(2,1)} %get-tuple-element.236), channel_id=1, source_target_pairs={{0,4},{1,5},{2,6},{3,7},{4,0},{5,1},{6,2},{7,3},{8,12},{9,13},{10,... | collective-permute-start | bytes 786440 | tf_op jit(solution)/shard_map/ppermute | solution.py:426
  155.9 14.2 %attend.5 = (bf16[512,256]{1,0:T(8,128)(2,1)}, bf16[512,256]{1,0:T(8,128)(2,1)}, f32[256,1024]{1,0:T(8,128)}, f32[2,8,1024]{2,1,0:T(8,128)}) custom-call(f32[4]{0:T(128)} %multiply_exponential_fusion.slope_ref, s32[2]{0:T(128)} %fusion.16.start_ref, s32[1]{0:T(128)} %bitcast.3.me_ref, bf16[512,768]{1,0:T(8,128)(2,1)} %get-tuple-element.244.rest_0_.rest_1_.rest_2_, ...), custom_call_target="tpu_custom_call" | custom-call | flops 8499999744 | bytes 1 | tf_op jit(solution)/shard_map/attend/pallas_call | solution.py:614
  179.4 5.8 collective-permute-done.7.far_ref
  186.2 6.3 mix_near.2
  201.7 27.9 %mlp_forward.2 = (bf16[1024,2048]{1,0:T(8,128)(2,1)}, bf16[1024,2048]{1,0:T(8,128)(2,1)}, f32[512,1024]{1,0:T(8,128)}, bf16[512,1024]{1,0:T(8,128)(2,1)}) custom-call(s32[1]{0:T(128)} %constant.9.clone.1.rest_2_.turn_ref.rest_6_.rest_10_, bf16[512,1024]{1,0:T(8,128)(2,1)} %get-tuple-element.260.normed_ref.left_ref, bf16[512,1024]{1,0:T(8,128)(2,1)} %copy-done.27, ...), custom_call_target="tpu_custom_call" | custom-call | flops 8999999488 | bytes 1 | tf_op jit(solution)/shard_map/mlp_forward/pallas_call | solution.py:1047
  236.8 12.6 %collective-permute-done.15 = bf16[128,1024]{1,0:T(8,128)(2,1)S(1)} collective-permute-done((bf16[128,1024]{1,0:T(8,128)(2,1)S(1)}, bf16[128,1024]{1,0:T(8,128)(2,1)S(1)}, u32[]{:S(2)}, u32[]{:S(2)}) %collective-permute-start.15) | collective-permute-done | bytes 262176 | tf_op jit(solution)/shard_map/ppermute | solution.py:426
  256.8 6.5 collective-permute-done.16
  265.1 12.0 %collective-permute-done.18 = bf16[2,128,1024]{2,1,0:T(8,128)(2,1)S(1)} collective-permute-done((bf16[2,128,1024]{2,1,0:T(8,128)(2,1)S(1)}, bf16[2,128,1024]{2,1,0:T(8,128)(2,1)S(1)}, u32[]{:S(2)}, u32[]{:S(2)}) %collective-permute-start.18) | collective-permute-done | bytes 524320 | tf_op jit(solution)/shard_map/ppermute | solution.py:426
  280.2 23.3 %collective-permute-done.23.rest_4_ = bf16[2,128,2048]{2,1,0:T(8,128)(2,1)S(1)} collective-permute-done((bf16[2,128,2048]{2,1,0:T(8,128)(2,1)S(1)}, bf16[2,128,2048]{2,1,0:T(8,128)(2,1)S(1)}, u32[]{:S(2)}, u32[]{:S(2)}) %collective-permute-start.23) | collective-permute-done | bytes 1048608 | tf_op jit(solution)/shard_map/ppermute | solution.py:426
  306.1 5.3 project.2
  311.3 14.2 %collective-permute-done.20.rows_ref.far_ref = bf16[512,1024]{1,0:T(8,128)(2,1)S(1)} collective-permute-done((bf16[512,1024]{1,0:T(8,128)(2,1)}, bf16[512,1024]{1,0:T(8,128)(2,1)S(1)}, u32[]{:S(2)}, u32[]{:S(2)}) %collective-permute-start.20) | collective-permute-done | bytes 1048608 | tf_op jit(solution)/shard_map/ppermute | solution.py:426
  326.5 5.3 project.3
  335.2 18.8 %attend.6 = (bf16[512,256]{1,0:T(8,128)(2,1)}, bf16[512,256]{1,0:T(8,128)(2,1)}, f32[256,1024]{1,0:T(8,128)}, f32[2,8,1024]{2,1,0:T(8,128)}) custom-call(f32[4]{0:T(128)} %multiply_exponential_fusion.slope_ref, s32[2]{0:T(128)} %fusion.16.start_ref, s32[1]{0:T(128)} %bitcast.3.me_ref, bf16[512,768]{1,0:T(8,128)(2,1)} %get-tuple-element.294.rest_0_.rest_1_.rest_2_, ...), custom_call_target="tpu_custom_call" | custom-call | flops 8499999744 | bytes 1 | tf_op jit(solution)/shard_map/attend/pallas_call | solution.py:614
  361.8 14.2 %attend.7 = (bf16[512,256]{1,0:T(8,128)(2,1)}, bf16[512,256]{1,0:T(8,128)(2,1)}, f32[256,1024]{1,0:T(8,128)}, f32[2,8,1024]{2,1,0:T(8,128)}) custom-call(f32[4]{0:T(128)} %multiply_exponential_fusion.slope_ref, s32[2]{0:T(128)} %fusion.16.start_ref, s32[1]{0:T(128)} %bitcast.3.me_ref, bf16[512,768]{1,0:T(8,128)(2,1)} %get-tuple-element.294.rest_0_.rest_1_.rest_2_, ...), custom_call_target="tpu_custom_call" | custom-call | flops 8499999744 | bytes 1 | tf_op jit(solution)/shard_map/attend/pallas_call | solution.py:614
  379.9 6.1 collective-permute-done.32.rest_7_
  386.0 6.2 collective-permute-done.30.far_ref
  393.2 6.2 mix_near.3
  405.6 17.4 %mlp_forward.3 = (bf16[1024,2048]{1,0:T(8,128)(2,1)}, bf16[1024,2048]{1,0:T(8,128)(2,1)}, f32[512,1024]{1,0:T(8,128)}, bf16[512,1024]{1,0:T(8,128)(2,1)}) custom-call(s32[1]{0:T(128)} %constant.9.clone.1.rest_2_.turn_ref.rest_6_.rest_10_, bf16[512,1024]{1,0:T(8,128)(2,1)} %get-tuple-element.308.normed_ref.left_ref, bf16[512,1024]{1,0:T(8,128)(2,1)} %copy-done.35, ...), custom_call_target="tpu_custom_call" | custom-call | flops 8999999488 | bytes 1 | tf_op jit(solution)/shard_map/mlp_forward/pallas_call | solution.py:1047
  422.9 5.4 collective-permute-start.35
  432.5 4.8 mlp_close.3
  438.3 20.5 %mlp_backward.2 = (bf16[1024,2048]{1,0:T(8,128)(2,1)}, f32[1,2048]{1,0:T(1,128)}, f32[512,1024]{1,0:T(8,128)}, bf16[512,1024]{1,0:T(8,128)(2,1)}) custom-call(s32[1]{0:T(128)} %constant.9.clone.1.rest_2_.turn_ref.rest_6_.rest_10_, f32[512,1024]{1,0:T(8,128)} %get-tuple-element.313.grad_ref.left_ref, bf16[512,1024]{1,0:T(8,128)(2,1)} %copy-done.38, ...), custom_call_target="tpu_custom_call" | custom-call | flops 11000000512 | bytes 1 | tf_op jit(solution)/shard_map/mlp_backward/pallas_call | solution.py:1125
  462.7 6.6 mlp_open.2
  472.4 9.2 %unit_grads.4 = (bf16[2,2,128,1024]{3,2,1,0:T(8,128)(2,1)}, bf16[2,2,2,128,1024]{4,3,2,1,0:T(8,128)(2,1)}, bf16[2,2,128,1024]{3,2,1,0:T(8,128)(2,1)}) custom-call(f32[512,1024]{1,0:T(8,128)} %get-tuple-element.313.grad_ref.left_ref, bf16[512,1024]{1,0:T(8,128)(2,1)} %copy-done.38, bf16[1024,2048]{1,0:T(8,128)(2,1)} %get-tuple-element.320.right_ref), custom_call_target="tpu_custom_call" | custom-call | flops 5000000000 | bytes 1 | tf_op jit(solution)/shard_map/unit_grads/pallas_call | solution.py:1187
  486.7 8.9 unit_grads.5
  503.8 21.2 %attend_pull.4 = (bf16[3,1024,128]{2,1,0:T(8,128)(2,1)}, bf16[3,1024,128]{2,1,0:T(8,128)(2,1)}) custom-call(f32[4]{0:T(128)} %multiply_exponential_fusion.slope_ref, s32[2]{0:T(128)} %fusion.16.start_ref, s32[1]{0:T(128)} %bitcast.3.me_ref, bf16[512,768]{1,0:T(8,128)(2,1)} %get-tuple-element.294.rest_0_.rest_1_.rest_2_, ...), custom_call_target="tpu_custom_call" | custom-call | flops 11000000512 | bytes 1 | tf_op jit(solution)/shard_map/attend_pull/pallas_call | solution.py:747
  529.5 21.4 %attend_pull.5 = (bf16[3,1024,128]{2,1,0:T(8,128)(2,1)}, bf16[3,1024,128]{2,1,0:T(8,128)(2,1)}) custom-call(f32[4]{0:T(128)} %multiply_exponential_fusion.slope_ref, s32[2]{0:T(128)} %fusion.16.start_ref, s32[1]{0:T(128)} %bitcast.3.me_ref, bf16[512,768]{1,0:T(8,128)(2,1)} %get-tuple-element.294.rest_0_.rest_1_.rest_2_, ...), custom_call_target="tpu_custom_call" | custom-call | flops 11000000512 | bytes 1 | tf_op jit(solution)/shard_map/attend_pull/pallas_call | solution.py:747
  558.4 6.0 unproject_far.2
  565.1 10.2 %head_grads.2 = (bf16[4,2,128,1024]{3,2,1,0:T(8,128)(2,1)}, bf16[4,2,128,1024]{3,2,1,0:T(8,128)(2,1)}, f32[8,256]{1,0:T(8,128)}) custom-call(s32[1]{0:T(128)} %constant.9.clone.1.rest_2_.turn_ref.rest_6_.rest_10_, bf16[512,1024]{1,0:T(8,128)(2,1)} %get-tuple-element.270.rows_ref.near_ref, bf16[512,1024]{1,0:T(8,128)(2,1)} %copy-done.29, ...), custom_call_target="tpu_custom_call" | custom-call | flops 5000000000 | bytes 1 | tf_op jit(solution)/shard_map/head_grads/pallas_call | solution.py:785
  589.3 9.3 %unproject_near.2 = (f32[512,1024]{1,0:T(8,128)}, bf16[512,1024]{1,0:T(8,128)(2,1)}, f32[8,1024]{1,0:T(8,128)}) custom-call(s32[2]{0:T(128)} %pad_add_fusion.own_ref, bf16[3,1024,128]{2,1,0:T(8,128)(2,1)} %get-tuple-element.335.rest_0_, bf16[3,1024,128]{2,1,0:T(8,128)(2,1)} %get-tuple-element.343.rest_1_, bf16[3,1024,128]{2,1,0:T(8,128)(2,1)} %copy-done.48, ...), custom_call_target="tpu_custom_call" | custom-call | flops 4499999744 | bytes 1 | tf_op jit(solution)/shard_map/unproject_near/pallas_call | solution.py:785
  601.6 20.7 %mlp_backward.3 = (bf16[1024,2048]{1,0:T(8,128)(2,1)}, f32[1,2048]{1,0:T(1,128)}, f32[512,1024]{1,0:T(8,128)}, bf16[512,1024]{1,0:T(8,128)(2,1)}) custom-call(s32[1]{0:T(128)} %constant.9.clone.1.rest_2_.turn_ref.rest_6_.rest_10_, f32[512,1024]{1,0:T(8,128)} %get-tuple-element.360.grad_ref.left_ref, bf16[512,1024]{1,0:T(8,128)(2,1)} %collective-permute-done.50.other_ref, ...), custom_call_target="tpu_custom_call" | custom-call | flops 11000000512 | bytes 1 | tf_op jit(solution)/shard_map/mlp_backward/pallas_call | solution.py:1125
  628.2 6.6 mlp_open.3
  635.6 9.3 %unit_grads.6 = (bf16[2,2,128,1024]{3,2,1,0:T(8,128)(2,1)}, bf16[2,2,2,128,1024]{4,3,2,1,0:T(8,128)(2,1)}, bf16[2,2,128,1024]{3,2,1,0:T(8,128)(2,1)}) custom-call(f32[512,1024]{1,0:T(8,128)} %get-tuple-element.360.grad_ref.left_ref, bf16[512,1024]{1,0:T(8,128)(2,1)} %collective-permute-done.50.other_ref, bf16[1024,2048]{1,0:T(8,128)(2,1)} %get-tuple-element.370.right_ref), custom_call_target="tpu_custom_call" | custom-call | flops 5000000000 | bytes 1 | tf_op jit(solution)/shard_map/unit_grads/pallas_call | solution.py:1187
  651.6 5.2 collective-permute-start.58
  656.8 8.8 unit_grads.7
  665.6 5.0 collective-permute-done.57.grad_ref.grad_far_ref
  678.3 21.2 %attend_pull.6 = (bf16[3,1024,128]{2,1,0:T(8,128)(2,1)}, bf16[3,1024,128]{2,1,0:T(8,128)(2,1)}) custom-call(f32[4]{0:T(128)} %multiply_exponential_fusion.slope_ref, s32[2]{0:T(128)} %fusion.16.start_ref, s32[1]{0:T(128)} %bitcast.3.me_ref, bf16[512,768]{1,0:T(8,128)(2,1)} %get-tuple-element.244.rest_0_.rest_1_.rest_2_, ...), custom_call_target="tpu_custom_call" | custom-call | flops 11000000512 | bytes 1 | tf_op jit(solution)/shard_map/attend_pull/pallas_call | solution.py:747
  699.7 21.2 %attend_pull.7 = (bf16[3,1024,128]{2,1,0:T(8,128)(2,1)}, bf16[3,1024,128]{2,1,0:T(8,128)(2,1)}) custom-call(f32[4]{0:T(128)} %multiply_exponential_fusion.slope_ref, s32[2]{0:T(128)} %fusion.16.start_ref, s32[1]{0:T(128)} %bitcast.3.me_ref, bf16[512,768]{1,0:T(8,128)(2,1)} %get-tuple-element.244.rest_0_.rest_1_.rest_2_, ...), custom_call_target="tpu_custom_call" | custom-call | flops 11000000512 | bytes 1 | tf_op jit(solution)/shard_map/attend_pull/pallas_call | solution.py:747
  728.3 6.0 unproject_far.3
  734.3 10.1 %head_grads.3 = (bf16[4,2,128,1024]{3,2,1,0:T(8,128)(2,1)}, bf16[4,2,128,1024]{3,2,1,0:T(8,128)(2,1)}, f32[8,256]{1,0:T(8,128)}) custom-call(s32[1]{0:T(128)} %constant.9.clone.1.rest_2_.turn_ref.rest_6_.rest_10_, bf16[512,1024]{1,0:T(8,128)(2,1)} %get-tuple-element.408.near_ref, bf16[512,1024]{1,0:T(8,128)(2,1)} %get-tuple-element.409.far_ref, ...), custom_call_target="tpu_custom_call" | custom-call | flops 5000000000 | bytes 1 | tf_op jit(solution)/shard_map/head_grads/pallas_call | solution.py:785
  760.5 16.4 %collective-permute-done.65.rest_4_ = bf16[512,1024]{1,0:T(8,128)(2,1)} collective-permute-done((bf16[512,1024]{1,0:T(8,128)(2,1)}, bf16[512,1024]{1,0:T(8,128)(2,1)}, u32[]{:S(2)}, u32[]{:S(2)}) %collective-permute-start.65) | collective-permute-done | bytes 1048608 | tf_op jit(solution)/shard_map/ppermute | solution.py:426
  776.9 9.2 %unproject_near.3 = (f32[512,1024]{1,0:T(8,128)}, bf16[512,1024]{1,0:T(8,128)(2,1)}, f32[8,1024]{1,0:T(8,128)}) custom-call(s32[2]{0:T(128)} %pad_add_fusion.own_ref, bf16[3,1024,128]{2,1,0:T(8,128)(2,1)} %get-tuple-element.393.rest_0_, bf16[3,1024,128]{2,1,0:T(8,128)(2,1)} %get-tuple-element.401.rest_1_, ...), custom_call_target="tpu_custom_call" | custom-call | flops 4499999744 | bytes 1 | tf_op jit(solution)/shard_map/unproject_near/pallas_call | solution.py:785
  787.7 11.4 %collective-permute-done.69 = bf16[2,2,128,1024]{3,2,1,0:T(8,128)(2,1)S(1)} collective-permute-done((bf16[2,2,128,1024]{3,2,1,0:T(8,128)(2,1)S(1)}, bf16[2,2,128,1024]{3,2,1,0:T(8,128)(2,1)S(1)}, u32[]{:S(2)}, u32[]{:S(2)}) %collective-permute-start.69) | collective-permute-done | bytes 1048608 | tf_op jit(solution)/shard_map/ppermute | solution.py:426
  821.6 7.9 collective-permute-start.81
  833.8 26.0 %collective-permute-done.73 = f32[22,128]{1,0:T(8,128)S(1)} collective-permute-done((f32[22,128]{1,0:T(8,128)S(1)}, f32[22,128]{1,0:T(8,128)S(1)}, u32[]{:S(2)}, u32[]{:S(2)}) %collective-permute-start.73) | collective-permute-done | bytes 11296 | tf_op jit(solution)/shard_map/ppermute | solution.py:426
  865.7 11.3 %collective-permute-done.78 = bf16[2,128,1024]{2,1,0:T(8,128)(2,1)S(1)} collective-permute-done((bf16[2,128,1024]{2,1,0:T(8,128)(2,1)S(1)}, bf16[2,128,1024]{2,1,0:T(8,128)(2,1)S(1)}, u32[]{:S(2)}, u32[]{:S(2)}) %collective-permute-start.78) | collective-permute-done | bytes 524320 | tf_op jit(solution)/shard_map/ppermute | solution.py:426
  878.1 14.2 %collective-permute-start.79 = (bf16[128,1024]{1,0:T(8,128)(2,1)S(1)}, bf16[128,1024]{1,0:T(8,128)(2,1)S(1)}, u32[]{:S(2)}, u32[]{:S(2)}) collective-permute-start(bf16[128,1024]{1,0:T(8,128)(2,1)S(1)} %select_bitcast_fusion), channel_id=1, source_target_pairs={{0,2},{1,3},{2,0},{3,1},{4,6},{5,7},{6,4},{7,5},{8,10},{9,11},{10,... | collective-permute-start | bytes 786440 | tf_op jit(solution)/shard_map/ppermute | solution.py:426
  (377 shorter events, 233.9 us)
Async XLA Ops:
  101.8 49.3 %collective-permute-start.5 = (bf16[2,128,2048]{2,1,0:T(8,128)(2,1)}, bf16[2,128,2048]{2,1,0:T(8,128)(2,1)}, u32[]{:S(2)}, u32[]{:S(2)}) collective-permute-start(bf16[2,128,2048]{2,1,0:T(8,128)(2,1)} %get-tuple-element.240.rest_0_), channel_id=1, source_target_pairs={{0,1},{1,0},{2,3},{3,2},{4,5},{5,4},{6,7},{7,6},{8,9},{9,8},{10,11... | collective-permute-start | bytes 3145736 | tf_op jit(solution)/shard_map/ppermute | solution.py:426
  101.8 49.3 %collective-permute-start.4 = (bf16[2,128,2048]{2,1,0:T(8,128)(2,1)}, bf16[2,128,2048]{2,1,0:T(8,128)(2,1)}, u32[]{:S(2)}, u32[]{:S(2)}) collective-permute-start(bf16[2,128,2048]{2,1,0:T(8,128)(2,1)} %get-tuple-element.240.rest_0_), channel_id=1, source_target_pairs={{0,16},{1,17},{2,18},{3,19},{4,20},{5,21},{6,22},{7,23},{8,24},{9,... | collective-permute-start | bytes 3145736 | tf_op jit(solution)/shard_map/ppermute | solution.py:426
  103.3 47.8 %collective-permute-start.3 = (bf16[2,128,2048]{2,1,0:T(8,128)(2,1)}, bf16[2,128,2048]{2,1,0:T(8,128)(2,1)}, u32[]{:S(2)}, u32[]{:S(2)}) collective-permute-start(bf16[2,128,2048]{2,1,0:T(8,128)(2,1)} %get-tuple-element.240.rest_0_), channel_id=1, source_target_pairs={{0,8},{1,9},{2,10},{3,11},{4,12},{5,13},{6,14},{7,15},{8,0},{9,1},... | collective-permute-start | bytes 3145736 | tf_op jit(solution)/shard_map/ppermute | solution.py:426
  144.6 25.4 %collective-permute-start.10 = (bf16[2,128,2048]{2,1,0:T(8,128)(2,1)S(1)}, bf16[2,128,2048]{2,1,0:T(8,128)(2,1)S(1)}, u32[]{:S(2)}, u32[]{:S(2)}) collective-permute-start(bf16[2,128,2048]{2,1,0:T(8,128)(2,1)S(1)} %pad_maximum_fusion.1), channel_id=1, source_target_pairs={{4,6},{5,7},{6,4},{7,5},{12,14},{13,15},{14,12},{15,13},{20,22},{2... | collective-permute-start | bytes 3145736 | tf_op jit(solution)/shard_map/ppermute | solution.py:431
  151.1 34.1 %collective-permute-start.7 = (bf16[512,1024]{1,0:T(8,128)(2,1)}, bf16[512,1024]{1,0:T(8,128)(2,1)S(1)}, u32[]{:S(2)}, u32[]{:S(2)}) collective-permute-start(bf16[512,1024]{1,0:T(8,128)(2,1)} %mix_far.2), channel_id=1, source_target_pairs={{0,1},{1,0},{2,3},{3,2},{4,5},{5,4},{6,7},{7,6},{8,9},{9,8},{10,11... | collective-permute-start | bytes 3145736 | tf_op jit(solution)/shard_map/ppermute | solution.py:426
  151.1 23.7 %collective-permute-start.9 = (bf16[2,128,2048]{2,1,0:T(8,128)(2,1)}, bf16[2,128,2048]{2,1,0:T(8,128)(2,1)}, u32[]{:S(2)}, u32[]{:S(2)}) collective-permute-start(bf16[2,128,2048]{2,1,0:T(8,128)(2,1)} %collective-permute-done.5.rest_4_), channel_id=1, source_target_pairs={{0,16},{1,17},{2,18},{3,19},{4,20},{5,21},{6,22},{7,23},{8,24},{9,... | collective-permute-start | bytes 3145736 | tf_op jit(solution)/shard_map/ppermute | solution.py:426
  153.6 23.8 %collective-permute-start.8 = (bf16[2,128,2048]{2,1,0:T(8,128)(2,1)}, bf16[2,128,2048]{2,1,0:T(8,128)(2,1)S(1)}, u32[]{:S(2)}, u32[]{:S(2)}) collective-permute-start(bf16[2,128,2048]{2,1,0:T(8,128)(2,1)} %collective-permute-done.5.rest_4_), channel_id=1, source_target_pairs={{0,8},{1,9},{2,10},{3,11},{4,12},{5,13},{6,14},{7,15},{8,0},{9,1},... | collective-permute-start | bytes 3145736 | tf_op jit(solution)/shard_map/ppermute | solution.py:426
  155.3 41.9 %collective-permute-start.11 = (bf16[2,128,2048]{2,1,0:T(8,128)(2,1)}, bf16[2,128,2048]{2,1,0:T(8,128)(2,1)}, u32[]{:S(2)}, u32[]{:S(2)}) collective-permute-start(bf16[2,128,2048]{2,1,0:T(8,128)(2,1)} %collective-permute-done.3.rest_1_), channel_id=1, source_target_pairs={{0,16},{1,17},{2,18},{3,19},{4,20},{5,21},{6,22},{7,23},{8,24},{9,... | collective-permute-start | bytes 3145736 | tf_op jit(solution)/shard_map/ppermute | solution.py:426
  177.4 23.3 %collective-permute-start.12 = (bf16[2,128,2048]{2,1,0:T(8,128)(2,1)}, bf16[2,128,2048]{2,1,0:T(8,128)(2,1)}, u32[]{:S(2)}, u32[]{:S(2)}) collective-permute-start(bf16[2,128,2048]{2,1,0:T(8,128)(2,1)} %collective-permute-done.9.rest_6_), channel_id=1, source_target_pairs={{0,8},{1,9},{2,10},{3,11},{4,12},{5,13},{6,14},{7,15},{8,0},{9,1},... | collective-permute-start | bytes 3145736 | tf_op jit(solution)/shard_map/ppermute | solution.py:426
  229.6 22.7 %collective-permute-start.14 = (bf16[512,1024]{1,0:T(8,128)(2,1)}, bf16[512,1024]{1,0:T(8,128)(2,1)}, u32[]{:S(2)}, u32[]{:S(2)}) collective-permute-start(bf16[512,1024]{1,0:T(8,128)(2,1)} %get-tuple-element.264), channel_id=1, source_target_pairs={{0,4},{1,5},{2,6},{3,7},{4,0},{5,1},{6,2},{7,3},{8,12},{9,13},{10,... | collective-permute-start | bytes 3145736 | tf_op jit(solution)/shard_map/ppermute | solution.py:426
  277.4 27.3 %collective-permute-start.19 = (bf16[4,2,128,1024]{3,2,1,0:T(8,128)(2,1)S(1)}, bf16[4,2,128,1024]{3,2,1,0:T(8,128)(2,1)S(1)}, u32[]{:S(2)}, u32[]{:S(2)}) collective-permute-start(bf16[4,2,128,1024]{3,2,1,0:T(8,128)(2,1)S(1)} %pad_maximum_fusion.rest_0_.rest_4_.rest_8_), channel_id=1, source_target_pairs={{0,4},{1,5},{2,6},{3,7},{4,0},{5,1},{6,2},{7,3},{8,12},{9,13},{10,... | collective-permute-start | bytes 6291464 | tf_op jit(solution)/shard_map/ppermute | solution.py:426
  277.5 26.0 %collective-permute-start.23 = (bf16[2,128,2048]{2,1,0:T(8,128)(2,1)S(1)}, bf16[2,128,2048]{2,1,0:T(8,128)(2,1)S(1)}, u32[]{:S(2)}, u32[]{:S(2)}) collective-permute-start(bf16[2,128,2048]{2,1,0:T(8,128)(2,1)S(1)} %broadcast_select_fusion.rest_0_), channel_id=1, source_target_pairs={{0,1},{1,0},{2,3},{3,2},{4,5},{5,4},{6,7},{7,6},{8,9},{9,8},{10,11... | collective-permute-start | bytes 3145736 | tf_op jit(solution)/shard_map/ppermute | solution.py:426
  278.6 47.0 %collective-permute-start.20 = (bf16[512,1024]{1,0:T(8,128)(2,1)}, bf16[512,1024]{1,0:T(8,128)(2,1)S(1)}, u32[]{:S(2)}, u32[]{:S(2)}) collective-permute-start(bf16[512,1024]{1,0:T(8,128)(2,1)} %get-tuple-element.270.rows_ref.near_ref), channel_id=1, source_target_pairs={{0,1},{1,0},{2,3},{3,2},{4,5},{5,4},{6,7},{7,6},{8,9},{9,8},{10,11... | collective-permute-start | bytes 3145736 | tf_op jit(solution)/shard_map/ppermute | solution.py:426
  303.5 28.8 %collective-permute-start.25 = (bf16[2,128,2048]{2,1,0:T(8,128)(2,1)S(1)}, bf16[2,128,2048]{2,1,0:T(8,128)(2,1)}, u32[]{:S(2)}, u32[]{:S(2)}) collective-permute-start(bf16[2,128,2048]{2,1,0:T(8,128)(2,1)S(1)} %broadcast_select_fusion.rest_0_), channel_id=1, source_target_pairs={{0,16},{1,17},{2,18},{3,19},{4,20},{5,21},{6,22},{7,23},{8,24},{9,... | collective-permute-start | bytes 3145736 | tf_op jit(solution)/shard_map/ppermute | solution.py:426
  304.1 28.9 %collective-permute-start.24 = (bf16[2,128,2048]{2,1,0:T(8,128)(2,1)S(1)}, bf16[2,128,2048]{2,1,0:T(8,128)(2,1)}, u32[]{:S(2)}, u32[]{:S(2)}) collective-permute-start(bf16[2,128,2048]{2,1,0:T(8,128)(2,1)S(1)} %broadcast_select_fusion.rest_0_), channel_id=1, source_target_pairs={{0,8},{1,9},{2,10},{3,11},{4,12},{5,13},{6,14},{7,15},{8,0},{9,1},... | collective-permute-start | bytes 3145736 | tf_op jit(solution)/shard_map/ppermute | solution.py:426
  331.8 28.9 %collective-permute-start.28 = (bf16[2,128,2048]{2,1,0:T(8,128)(2,1)S(1)}, bf16[2,128,2048]{2,1,0:T(8,128)(2,1)S(1)}, u32[]{:S(2)}, u32[]{:S(2)}) collective-permute-start(bf16[2,128,2048]{2,1,0:T(8,128)(2,1)S(1)} %collective-permute-done.23.rest_4_), channel_id=1, source_target_pairs={{0,16},{1,17},{2,18},{3,19},{4,20},{5,21},{6,22},{7,23},{8,24},{9,... | collective-permute-start | bytes 3145736 | tf_op jit(solution)/shard_map/ppermute | solution.py:426
  332.4 28.3 %collective-permute-start.27 = (bf16[2,128,2048]{2,1,0:T(8,128)(2,1)S(1)}, bf16[2,128,2048]{2,1,0:T(8,128)(2,1)S(1)}, u32[]{:S(2)}, u32[]{:S(2)}) collective-permute-start(bf16[2,128,2048]{2,1,0:T(8,128)(2,1)S(1)} %collective-permute-done.23.rest_4_), channel_id=1, source_target_pairs={{0,8},{1,9},{2,10},{3,11},{4,12},{5,13},{6,14},{7,15},{8,0},{9,1},... | collective-permute-start | bytes 3145736 | tf_op jit(solution)/shard_map/ppermute | solution.py:426
  354.3 25.6 %collective-permute-start.31 = (bf16[2,128,2048]{2,1,0:T(8,128)(2,1)}, bf16[2,128,2048]{2,1,0:T(8,128)(2,1)S(1)}, u32[]{:S(2)}, u32[]{:S(2)}) collective-permute-start(bf16[2,128,2048]{2,1,0:T(8,128)(2,1)} %collective-permute-done.24.rest_1_), channel_id=1, source_target_pairs={{0,16},{1,17},{2,18},{3,19},{4,20},{5,21},{6,22},{7,23},{8,24},{9,... | collective-permute-start | bytes 3145736 | tf_op jit(solution)/shard_map/ppermute | solution.py:426
  360.7 31.5 %collective-permute-start.30 = (bf16[512,1024]{1,0:T(8,128)(2,1)}, bf16[512,1024]{1,0:T(8,128)(2,1)S(1)}, u32[]{:S(2)}, u32[]{:S(2)}) collective-permute-start(bf16[512,1024]{1,0:T(8,128)(2,1)} %mix_far.3), channel_id=1, source_target_pairs={{0,1},{1,0},{2,3},{3,2},{4,5},{5,4},{6,7},{7,6},{8,9},{9,8},{10,11... | collective-permute-start | bytes 3145736 | tf_op jit(solution)/shard_map/ppermute | solution.py:426
  360.7 25.3 %collective-permute-start.32 = (bf16[2,128,2048]{2,1,0:T(8,128)(2,1)S(1)}, bf16[2,128,2048]{2,1,0:T(8,128)(2,1)S(1)}, u32[]{:S(2)}, u32[]{:S(2)}) collective-permute-start(bf16[2,128,2048]{2,1,0:T(8,128)(2,1)S(1)} %collective-permute-done.28.rest_6_), channel_id=1, source_target_pairs={{0,8},{1,9},{2,10},{3,11},{4,12},{5,13},{6,14},{7,15},{8,0},{9,1},... | collective-permute-start | bytes 3145736 | tf_op jit(solution)/shard_map/ppermute | solution.py:426
  376.2 23.3 %collective-permute-start.33 = (bf16[512,1024]{1,0:T(8,128)(2,1)S(1)}, bf16[512,1024]{1,0:T(8,128)(2,1)S(1)}, u32[]{:S(2)}, u32[]{:S(2)}) collective-permute-start(bf16[512,1024]{1,0:T(8,128)(2,1)S(1)} %copy-done.26), channel_id=1, source_target_pairs={{2,4},{3,5},{4,2},{5,3},{10,12},{11,13},{12,10},{13,11},{18,20},{1... | collective-permute-start | bytes 3145736 | tf_op jit(solution)/shard_map/ppermute | solution.py:439
  469.3 27.0 %collective-permute-start.39 = (bf16[512,1024]{1,0:T(8,128)(2,1)}, bf16[512,1024]{1,0:T(8,128)(2,1)S(1)}, u32[]{:S(2)}, u32[]{:S(2)}) collective-permute-start(bf16[512,1024]{1,0:T(8,128)(2,1)} %get-tuple-element.322.grad_ref.grad_near_ref), channel_id=1, source_target_pairs={{0,1},{1,0},{2,3},{3,2},{4,5},{5,4},{6,7},{7,6},{8,9},{9,8},{10,11... | collective-permute-start | bytes 3145736 | tf_op jit(solution)/shard_map/ppermute | solution.py:426
  481.6 47.8 %collective-permute-start.42 = (bf16[2,2,2,128,1024]{4,3,2,1,0:T(8,128)(2,1)}, bf16[2,2,2,128,1024]{4,3,2,1,0:T(8,128)(2,1)S(1)}, u32[]{:S(2)}, u32[]{:S(2)}) collective-permute-start(bf16[2,2,2,128,1024]{4,3,2,1,0:T(8,128)(2,1)} %get-tuple-element.337), channel_id=1, source_target_pairs={{0,16},{1,17},{2,18},{3,19},{4,20},{5,21},{6,22},{7,23},{8,24},{9,... | collective-permute-start | bytes 6291464 | tf_op jit(solution)/shard_map/ppermute | solution.py:426
  501.3 50.2 %collective-permute-start.45 = (bf16[2,2,2,128,1024]{4,3,2,1,0:T(8,128)(2,1)}, bf16[2,2,2,128,1024]{4,3,2,1,0:T(8,128)(2,1)S(1)}, u32[]{:S(2)}, u32[]{:S(2)}) collective-permute-start(bf16[2,2,2,128,1024]{4,3,2,1,0:T(8,128)(2,1)} %get-tuple-element.347), channel_id=1, source_target_pairs={{0,8},{1,9},{2,10},{3,11},{4,12},{5,13},{6,14},{7,15},{8,0},{9,1},... | collective-permute-start | bytes 6291464 | tf_op jit(solution)/shard_map/ppermute | solution.py:426
  552.9 25.7 %collective-permute-start.47 = (bf16[2,2,128,1024]{3,2,0,1:T(8,128)(2,1)S(1)}, bf16[2,2,128,1024]{3,2,0,1:T(8,128)(2,1)}, u32[]{:S(2)}, u32[]{:S(2)}) collective-permute-start(bf16[2,2,128,1024]{3,2,0,1:T(8,128)(2,1)S(1)} %copy.54), channel_id=1, source_target_pairs={{0,8},{1,9},{2,10},{3,11},{4,12},{5,13},{6,14},{7,15},{8,0},{9,1},... | collective-permute-start | bytes 3145736 | tf_op jit(solution)/shard_map/ppermute | solution.py:426
  555.1 24.9 %collective-permute-start.48 = (bf16[2,2,128,1024]{3,2,0,1:T(8,128)(2,1)S(1)}, bf16[2,2,128,1024]{3,2,0,1:T(8,128)(2,1)S(1)}, u32[]{:S(2)}, u32[]{:S(2)}) collective-permute-start(bf16[2,2,128,1024]{3,2,0,1:T(8,128)(2,1)S(1)} %copy.55), channel_id=1, source_target_pairs={{0,16},{1,17},{2,18},{3,19},{4,20},{5,21},{6,22},{7,23},{8,24},{9,... | collective-permute-start | bytes 3145736 | tf_op jit(solution)/shard_map/ppermute | solution.py:426
  564.4 24.9 %collective-permute-start.46 = (bf16[512,1024]{1,0:T(8,128)(2,1)}, bf16[512,1024]{1,0:T(8,128)(2,1)}, u32[]{:S(2)}, u32[]{:S(2)}) collective-permute-start(bf16[512,1024]{1,0:T(8,128)(2,1)} %unproject_far.2), channel_id=1, source_target_pairs={{0,1},{1,0},{2,3},{3,2},{4,5},{5,4},{6,7},{7,6},{8,9},{9,8},{10,11... | collective-permute-start | bytes 3145736 | tf_op jit(solution)/shard_map/ppermute | solution.py:426
  575.3 24.1 %collective-permute-start.49 = (bf16[4,2,128,1024]{3,2,1,0:T(8,128)(2,1)}, bf16[4,2,128,1024]{3,2,1,0:T(8,128)(2,1)S(1)}, u32[]{:S(2)}, u32[]{:S(2)}) collective-permute-start(bf16[4,2,128,1024]{3,2,1,0:T(8,128)(2,1)} %get-tuple-element.358), channel_id=1, source_target_pairs={{0,4},{1,5},{2,6},{3,7},{4,0},{5,1},{6,2},{7,3},{8,12},{9,13},{10,... | collective-permute-start | bytes 6291464 | tf_op jit(solution)/shard_map/ppermute | solution.py:426
  598.6 25.8 %collective-permute-start.52 = (bf16[2,2,128,1024]{3,2,0,1:T(8,128)(2,1)}, bf16[2,2,128,1024]{3,2,0,1:T(8,128)(2,1)S(1)}, u32[]{:S(2)}, u32[]{:S(2)}) collective-permute-start(bf16[2,2,128,1024]{3,2,0,1:T(8,128)(2,1)} %pad_maximum_fusion.3), channel_id=1, source_target_pairs={{0,1},{1,0},{2,3},{3,2},{4,5},{5,4},{6,7},{7,6},{8,9},{9,8},{10,11... | collective-permute-start | bytes 3145736 | tf_op jit(solution)/shard_map/ppermute | solution.py:426
  600.5 25.5 %collective-permute-start.53 = (bf16[2,2,128,1024]{3,2,1,0:T(8,128)(2,1)}, bf16[2,2,128,1024]{3,2,1,0:T(8,128)(2,1)S(1)}, u32[]{:S(2)}, u32[]{:S(2)}) collective-permute-start(bf16[2,2,128,1024]{3,2,1,0:T(8,128)(2,1)} %get-tuple-element.468), channel_id=1, source_target_pairs={{0,16},{1,17},{2,18},{3,19},{4,20},{5,21},{6,22},{7,23},{8,24},{9,... | collective-permute-start | bytes 3145736 | tf_op jit(solution)/shard_map/ppermute | solution.py:426
  624.6 20.9 %collective-permute-start.55 = (bf16[2,128,1024]{2,1,0:T(8,128)(2,1)S(1)}, bf16[2,128,1024]{2,1,0:T(8,128)(2,1)S(1)}, u32[]{:S(2)}, u32[]{:S(2)}) collective-permute-start(bf16[2,128,1024]{2,1,0:T(8,128)(2,1)S(1)} %get-tuple-element.480), channel_id=1, source_target_pairs={{0,4},{1,5},{2,6},{3,7},{4,2},{5,3},{6,0},{7,1},{8,12},{9,13},{10,... | collective-permute-start | bytes 1572872 | tf_op jit(solution)/shard_map/ppermute | solution.py:431
  624.7 20.8 %collective-permute-start.54 = (bf16[2,128,1024]{2,1,0:T(8,128)(2,1)S(1)}, bf16[2,128,1024]{2,1,0:T(8,128)(2,1)S(1)}, u32[]{:S(2)}, u32[]{:S(2)}) collective-permute-start(bf16[2,128,1024]{2,1,0:T(8,128)(2,1)S(1)} %get-tuple-element.481), channel_id=1, source_target_pairs={{4,6},{5,7},{6,4},{7,5},{12,14},{13,15},{14,12},{15,13},{20,22},{2... | collective-permute-start | bytes 1572872 | tf_op jit(solution)/shard_map/ppermute | solution.py:431
  634.9 35.8 %collective-permute-start.57 = (bf16[512,1024]{1,0:T(8,128)(2,1)}, bf16[512,1024]{1,0:T(8,128)(2,1)}, u32[]{:S(2)}, u32[]{:S(2)}) collective-permute-start(bf16[512,1024]{1,0:T(8,128)(2,1)} %get-tuple-element.375.grad_ref.grad_near_ref), channel_id=1, source_target_pairs={{0,1},{1,0},{2,3},{3,2},{4,5},{5,4},{6,7},{7,6},{8,9},{9,8},{10,11... | collective-permute-start | bytes 3145736 | tf_op jit(solution)/shard_map/ppermute | solution.py:426
  645.5 54.0 %collective-permute-start.61 = (bf16[2,2,2,128,1024]{4,3,2,1,0:T(8,128)(2,1)}, bf16[2,2,2,128,1024]{4,3,2,1,0:T(8,128)(2,1)S(1)}, u32[]{:S(2)}, u32[]{:S(2)}) collective-permute-start(bf16[2,2,2,128,1024]{4,3,2,1,0:T(8,128)(2,1)} %get-tuple-element.395), channel_id=1, source_target_pairs={{0,16},{1,17},{2,18},{3,19},{4,20},{5,21},{6,22},{7,23},{8,24},{9,... | collective-permute-start | bytes 6291464 | tf_op jit(solution)/shard_map/ppermute | solution.py:426
  651.6 25.0 %collective-permute-start.58 = (bf16[512,256]{1,0:T(8,128)(2,1)}, bf16[512,256]{1,0:T(8,128)(2,1)S(1)}, u32[]{:S(2)}, u32[]{:S(2)}) collective-permute-start(bf16[512,256]{1,0:T(8,128)(2,1)} %get-tuple-element.382), channel_id=1, source_target_pairs={{0,4},{1,5},{2,6},{3,7},{4,0},{5,1},{6,2},{7,3},{8,12},{9,13},{10,... | collective-permute-start | bytes 786440 | tf_op jit(solution)/shard_map/ppermute | solution.py:426
  676.2 48.3 %collective-permute-start.64 = (bf16[2,2,2,128,1024]{4,3,2,1,0:T(8,128)(2,1)}, bf16[2,2,2,128,1024]{4,3,2,1,0:T(8,128)(2,1)S(1)}, u32[]{:S(2)}, u32[]{:S(2)}) collective-permute-start(bf16[2,2,2,128,1024]{4,3,2,1,0:T(8,128)(2,1)} %get-tuple-element.405), channel_id=1, source_target_pairs={{0,8},{1,9},{2,10},{3,11},{4,12},{5,13},{6,14},{7,15},{8,0},{9,1},... | collective-permute-start | bytes 6291464 | tf_op jit(solution)/shard_map/ppermute | solution.py:426
  721.4 26.7 %collective-permute-start.66 = (bf16[2,2,128,1024]{3,2,1,0:T(8,128)(2,1)S(1)}, bf16[2,2,128,1024]{3,2,1,0:T(8,128)(2,1)}, u32[]{:S(2)}, u32[]{:S(2)}) collective-permute-start(bf16[2,2,128,1024]{3,2,1,0:T(8,128)(2,1)S(1)} %bitcast_add_fusion.1), channel_id=1, source_target_pairs={{0,8},{1,9},{2,10},{3,11},{4,12},{5,13},{6,14},{7,15},{8,0},{9,1},... | collective-permute-start | bytes 3145736 | tf_op jit(solution)/shard_map/ppermute | solution.py:426
  725.7 25.1 %collective-permute-start.67 = (bf16[2,2,128,1024]{3,2,1,0:T(8,128)(2,1)}, bf16[2,2,128,1024]{3,2,1,0:T(8,128)(2,1)S(1)}, u32[]{:S(2)}, u32[]{:S(2)}) collective-permute-start(bf16[2,2,128,1024]{3,2,1,0:T(8,128)(2,1)} %bitcast_add_fusion), channel_id=1, source_target_pairs={{0,16},{1,17},{2,18},{3,19},{4,20},{5,21},{6,22},{7,23},{8,24},{9,... | collective-permute-start | bytes 3145736 | tf_op jit(solution)/shard_map/ppermute | solution.py:426
  726.5 28.7 %collective-permute-start.36 = (bf16[512,1024]{1,0:T(8,128)(2,1)}, bf16[512,1024]{1,0:T(8,128)(2,1)}, u32[]{:S(2)}, u32[]{:S(2)}) collective-permute-start(bf16[512,1024]{1,0:T(8,128)(2,1)} %get-tuple-element.312), channel_id=1, source_target_pairs={{2,4},{3,5},{4,2},{5,3},{10,12},{11,13},{12,10},{13,11},{18,20},{1... | collective-permute-start | bytes 3145736 | tf_op jit(solution)/shard_map/ppermute | solution.py:439
  734.3 42.5 %collective-permute-start.65 = (bf16[512,1024]{1,0:T(8,128)(2,1)}, bf16[512,1024]{1,0:T(8,128)(2,1)}, u32[]{:S(2)}, u32[]{:S(2)}) collective-permute-start(bf16[512,1024]{1,0:T(8,128)(2,1)} %unproject_far.3), channel_id=1, source_target_pairs={{0,1},{1,0},{2,3},{3,2},{4,5},{5,4},{6,7},{7,6},{8,9},{9,8},{10,11... | collective-permute-start | bytes 3145736 | tf_op jit(solution)/shard_map/ppermute | solution.py:426
  755.1 43.9 %collective-permute-start.69 = (bf16[2,2,128,1024]{3,2,1,0:T(8,128)(2,1)S(1)}, bf16[2,2,128,1024]{3,2,1,0:T(8,128)(2,1)S(1)}, u32[]{:S(2)}, u32[]{:S(2)}) collective-permute-start(bf16[2,2,128,1024]{3,2,1,0:T(8,128)(2,1)S(1)} %pad_maximum_fusion.5), channel_id=1, source_target_pairs={{0,1},{1,0},{2,3},{3,2},{4,5},{5,4},{6,7},{7,6},{8,9},{9,8},{10,11... | collective-permute-start | bytes 3145736 | tf_op jit(solution)/shard_map/ppermute | solution.py:426
  757.5 44.0 %collective-permute-start.60 = (bf16[128,1024]{1,0:T(8,128)(2,1)S(1)}, bf16[128,1024]{1,0:T(8,128)(2,1)S(1)}, u32[]{:S(2)}, u32[]{:S(2)}) collective-permute-start(bf16[128,1024]{1,0:T(8,128)(2,1)S(1)} %get-tuple-element.482), channel_id=1, source_target_pairs={{0,2},{1,3},{2,0},{3,1},{4,6},{5,7},{6,4},{7,5},{8,10},{9,11},{10,... | collective-permute-start | bytes 786440 | tf_op jit(solution)/shard_map/ppermute | solution.py:426
  809.8 51.9 %collective-permute-start.68 = (bf16[512,1024]{1,0:T(8,128)(2,1)}, bf16[512,1024]{1,0:T(8,128)(2,1)}, u32[]{:S(2)}, u32[]{:S(2)}) collective-permute-start(bf16[512,1024]{1,0:T(8,128)(2,1)} %get-tuple-element.416), channel_id=1, source_target_pairs={{2,4},{3,5},{4,2},{5,3},{10,12},{11,13},{12,10},{13,11},{18,20},{1... | collective-permute-start | bytes 3145736 | tf_op jit(solution)/shard_map/ppermute | solution.py:439
  811.4 51.4 %collective-permute-start.80 = (bf16[2,128,1024]{2,1,0:T(8,128)(2,1)}, bf16[2,128,1024]{2,1,0:T(8,128)(2,1)}, u32[]{:S(2)}, u32[]{:S(2)}) collective-permute-start(bf16[2,128,1024]{2,1,0:T(8,128)(2,1)} %get-tuple-element.479), channel_id=1, source_target_pairs={{4,6},{5,7},{6,4},{7,5},{12,14},{13,15},{14,12},{15,13},{20,22},{2... | collective-permute-start | bytes 1572872 | tf_op jit(solution)/shard_map/ppermute | solution.py:431
  816.8 43.0 %collective-permute-start.73 = (f32[22,128]{1,0:T(8,128)S(1)}, f32[22,128]{1,0:T(8,128)S(1)}, u32[]{:S(2)}, u32[]{:S(2)}) collective-permute-start(f32[22,128]{1,0:T(8,128)S(1)} %pad_maximum_fusion.13), channel_id=1, source_target_pairs={{0,2},{1,3},{2,0},{3,1},{4,6},{5,7},{6,4},{7,5},{8,10},{9,11},{10,... | collective-permute-start | bytes 33800 | tf_op jit(solution)/shard_map/ppermute | solution.py:426
  821.6 41.2 %collective-permute-start.81 = (bf16[2,128,1024]{2,1,0:T(8,128)(2,1)}, bf16[2,128,1024]{2,1,0:T(8,128)(2,1)}, u32[]{:S(2)}, u32[]{:S(2)}) collective-permute-start(bf16[2,128,1024]{2,1,0:T(8,128)(2,1)} %get-tuple-element.478), channel_id=1, source_target_pairs={{0,4},{1,5},{2,6},{3,7},{4,2},{5,3},{6,0},{7,1},{8,12},{9,13},{10,... | collective-permute-start | bytes 1572872 | tf_op jit(solution)/shard_map/ppermute | solution.py:431
  833.6 29.2 %collective-permute-start.77 = (bf16[2,2,128,1024]{3,2,1,0:T(8,128)(2,1)}, bf16[2,2,128,1024]{3,2,1,0:T(8,128)(2,1)}, u32[]{:S(2)}, u32[]{:S(2)}) collective-permute-start(bf16[2,2,128,1024]{3,2,1,0:T(8,128)(2,1)} %get-tuple-element.462), channel_id=1, source_target_pairs={{0,16},{1,17},{2,18},{3,19},{4,20},{5,21},{6,22},{7,23},{8,24},{9,... | collective-permute-start | bytes 3145736 | tf_op jit(solution)/shard_map/ppermute | solution.py:426
  878.1 21.4 %collective-permute-start.79 = (bf16[128,1024]{1,0:T(8,128)(2,1)S(1)}, bf16[128,1024]{1,0:T(8,128)(2,1)S(1)}, u32[]{:S(2)}, u32[]{:S(2)}) collective-permute-start(bf16[128,1024]{1,0:T(8,128)(2,1)S(1)} %select_bitcast_fusion), channel_id=1, source_target_pairs={{0,2},{1,3},{2,0},{3,1},{4,6},{5,7},{6,4},{7,5},{8,10},{9,11},{10,... | collective-permute-start | bytes 786440 | tf_op jit(solution)/shard_map/ppermute | solution.py:426
  (93 other events, 1063.3 us)

commit v5 on v4

--- a/solution.py
+++ b/solution.py
@@ -411,7 +411,7 @@
 NEG = -1e30
 BF = jnp.bfloat16
 F32 = jnp.float32
-VMEM_LIMIT = 56 * 1024 * 1024
+VMEM_LIMIT = 24 * 1024 * 1024
 
 
 def took(us):
@@ -1273,7 +1273,7 @@
 
 def start_kernel(
     layers, x_ref, project_ref, output_ref, expand_ref, reduce_ref, small_ref,
-    resid_ref, normed_ref, far_ref, even_ref, odd_ref, first_ref, vector_ref, head_bias_ref, unit_bias_ref,
+    resid_ref, normed_ref, far_ref, even_ref, odd_ref, first_ref, first_x_ref, first_y_ref, second_ref, vector_ref, head_bias_ref, unit_bias_ref,
     near_mine_ref, far_mine_ref, got_near_ref, got_far_ref,
     came_ref, piece_ref, every_ref, near_other_ref, far_other_ref, local_sem, send_sem, recv_sem,
 ):
@@ -1360,13 +1360,6 @@
                 unit_bias_ref[layer, :, quarter * 1024 + block * 128:quarter * 1024 + (block + 1) * 128] = every_ref[
                     2 * core + quarter, xor_block(block, own), base + 10:base + 11, :
                 ]
-    over_y.wait()
-    over_x.wait()
-    across = copy(even_ref.at[2], even_ref.at[3], peer(XBIT))
-    across.start()
-    cores[1].start()
-    cores[2].start()
-
     @pl.when(keep)
     def _():
         stay.wait()
@@ -1388,6 +1381,12 @@
     def _():
         same.start()
 
+    over_y.wait()
+    over_x.wait()
+    across = copy(even_ref.at[2], even_ref.at[3], peer(XBIT))
+    across.start()
+    cores[1].start()
+    cores[2].start()
     across.wait()
     cores[3].start()
     for one in cores:
@@ -1396,18 +1395,23 @@
     project_rows(normed_ref[...], weights, head_bias_ref, 0, (near_mine_ref, near_other_ref))
     back_near = copy(near_other_ref, got_near_ref, peer(CORE))
     back_near.start()
+    cross.wait()
+
+    @pl.when(core == 1)
+    def _():
+        same.wait()
+
+    units = [copy(first_ref, target, peer(mask)) for target, mask in ((first_x_ref, XBIT), (first_y_ref, YBIT), (second_ref, Z0))]
+    for one in units:
+        one.start()
     beside.wait()
     project_rows(far_ref[...], weights, head_bias_ref, 0, (far_mine_ref, far_other_ref))
     back_far = copy(far_other_ref, got_far_ref, peer(CORE))
     back_far.start()
-    cross.wait()
-
-    @pl.when(core == 1)
-    def _():
-        same.wait()
-
     back_near.wait()
     back_far.wait()
+    for one in units:
+        one.wait()
 
 
 def start(x, project_weight, output_weight, expand_weight, reduce_weight, small, layers):
@@ -1422,7 +1426,7 @@
         jax.ShapeDtypeStruct((rows, features), BF),
         heads,
         heads,
-        jax.ShapeDtypeStruct((2, 128, 2048), BF),
+        *[jax.ShapeDtypeStruct((2, 128, 2048), BF)] * 4,
         jax.ShapeDtypeStruct((layers, 8, features), F32),
         jax.ShapeDtypeStruct((layers, 2, 768), F32),
         jax.ShapeDtypeStruct((layers, 1, 2048), F32),
@@ -1431,7 +1435,7 @@
         triple,
         triple,
     ]
-    copies = 19
+    copies = 22
     return pl.pallas_call(
         functools.partial(start_kernel, layers),
         in_specs=[vmem] * 6,
@@ -1453,6 +1457,207 @@
     )(x, project_weight, output_weight, expand_weight, reduce_weight, small)
 
 
+def finish_kernel(
+    layers, grad_ref, even_ref, odd_ref, here_ref, away_ref, *rest,
+):
+    sums, rest = rest[:4 * layers], rest[4 * layers:]
+    grad_out_ref, project_ref, output_ref, reduce_ref, expand_ref, small_ref, rest = *rest[:6], rest[6:]
+    odd_got, y_send, y_got, x_send, x_got, relay_send, relay_got, z_send, z_got, away_got, part_ref, part_got, rest = *rest[:12], rest[12:]
+    rows_ref, core_got, x_rows, y_rows, near_send, near_got, far_send, far_got, local_sem, send_sem, recv_sem = rest
+    own, place = lax.axis_index("dp"), lax.axis_index("tensor")
+    core = own % 2
+    keep = core == place // 2
+    count = [0]
+
+    def copy(source, target, device):
+        index = count[0]
+        count[0] += 1
+        return pltpu.make_async_remote_copy(
+            src_ref=source, dst_ref=target, send_sem=send_sem.at[index], recv_sem=recv_sem.at[index],
+            device_id=device, device_id_type=MESH,
+        )
+
+    greet((1, 2, 4, 6, 8, 16))
+    across = copy(odd_ref, odd_got, peer(CORE))
+    across.start()
+    beside = copy(away_ref, away_got, peer(Z0))
+    beside.start()
+    tokens = copy(grad_ref, grad_out_ref, peer(CORE | Z1))
+    stay = pltpu.make_async_copy(grad_ref, grad_out_ref, local_sem)
+
+    @pl.when(keep)
+    def _():
+        stay.start()
+
+    @pl.when(jnp.logical_not(keep))
+    def _():
+        tokens.start()
+
+    vectors = 6 * layers
+    rows_ref[...] = jnp.zeros_like(rows_ref)
+    for layer in range(layers):
+        first_ref, second_ref, unit_ref, head_ref = sums[4 * layer:4 * layer + 4]
+        base = vectors + 12 * layer
+        for block in range(8):
+            slot = (block % 2) * 4 + (block // 2 % 2) * 2 + block // 4
+            lanes = slice(block * 128, (block + 1) * 128)
+            rows_ref[slot, 6 * layer:6 * layer + 2, :] = first_ref[0:2, lanes]
+            rows_ref[slot, 6 * layer + 2:6 * layer + 6, :] = second_ref[0:4, lanes]
+            for quarter in range(2):
+                lane = pl.multiple_of(quarter * 1024 + xor_block(block, own) * 128, 128)
+                rows_ref[slot, pl.ds(base + 2 * core + quarter, 1), :] = unit_ref[0:1, pl.ds(lane, 128)]
+                row = base + 4 + 4 * (quarter + core - 2 * quarter * core)
+                for half in range(2):
+                    rows_ref[slot, pl.ds(row + 2 * half, 2), :] = head_ref[
+                        2 * quarter:2 * quarter + 2, half * 128:(half + 1) * 128
+                    ]
+    hop = copy(rows_ref.at[pl.ds(4, 4)], core_got, peer(CORE))
+    hop.start()
+    hop.wait()
+    rows_ref[0:4] = rows_ref[0:4] + core_got[...]
+    hop = copy(rows_ref.at[pl.ds(2, 2)], x_rows, peer(XBIT))
+    hop.start()
+    across.wait()
+    for chip in range(4):
+        for quarter in range(2):
+            odd_got[chip, quarter] = odd_got[chip, quarter] + even_ref[chip, quarter]
+    y_send[0], y_send[1] = odd_got[2, 0], odd_got[3, 0]
+    x_send[0], x_send[1] = odd_got[1, 1], odd_got[3, 1]
+    over_y = copy(y_send, y_got, peer(YBIT))
+    over_x = copy(x_send, x_got, peer(XBIT))
+    over_y.start()
+    over_x.start()
+    hop.wait()
+    rows_ref[0:2] = rows_ref[0:2] + x_rows[...]
+    hop = copy(rows_ref.at[pl.ds(1, 1)], y_rows, peer(YBIT))
+    hop.start()
+    hop.wait()
+    rows_ref[0] = rows_ref[0] + y_rows[0]
+    near_send[...] = jnp.zeros_like(near_send)
+    far_send[...] = jnp.zeros_like(far_send)
+    near_send[0:vectors, :] = rows_ref[0, 0:vectors, :]
+    for layer in range(layers):
+        base = vectors + 12 * layer
+        near_send[vectors + 2 * layer:vectors + 2 * layer + 1, :] = rows_ref[0, base + 1:base + 2, :]
+        near_send[vectors + 2 * layer + 1:vectors + 2 * layer + 2, :] = rows_ref[0, base + 3:base + 4, :]
+    hop = copy(near_send, near_got, peer(Z0))
+    hop.start()
+    over_y.wait()
+    over_x.wait()
+    relay_send[0] = odd_got[1, 0] + y_got[1]
+    relay_send[1] = odd_got[2, 1] + x_got[1]
+    relays = [copy(relay_send.at[i], relay_got.at[i], peer(mask)) for i, mask in ((0, XBIT), (1, YBIT))]
+    for one in relays:
+        one.start()
+    beside.wait()
+    for kind in range(2):
+        for side in range(2):
+            part_ref[side, kind] = here_ref[kind, side] + away_got[kind, side]
+    crossing = copy(part_ref.at[1], part_got.at[1], {
+        "dp": flip(own, 1), "tensor": place + core * (flip(place, 2) - place)
+    })
+    crossing.start()
+    along = copy(part_ref.at[0], part_got.at[0], peer(Z1))
+
+    @pl.when(core == 1)
+    def _():
+        along.start()
+
+    @pl.when(core == 0)
+    def _():
+        part_got[0] = part_ref[0]
+
+    for one in relays:
+        one.wait()
+    total = [odd_got[0, 0] + y_got[0] + relay_got[0], odd_got[0, 1] + x_got[0] + relay_got[1]]
+    z_send[core] = total[0]
+    z_send[1 - core] = total[1]
+    heads = copy(z_send.at[1], z_got, peer(Z1))
+    heads.start()
+    hop.wait()
+    far_send[0:vectors, :] = rows_ref[0, 0:vectors, :] + near_got[0:vectors, :]
+    for layer in range(layers):
+        base = vectors + 12 * layer
+        far_send[vectors + layer:vectors + layer + 1, :] = (
+            rows_ref[0, base + 2:base + 3, :] + near_got[vectors + 2 * layer + 1:vectors + 2 * layer + 2, :]
+        )
+        far_send[vectors + layers + 4 * layer:vectors + layers + 4 * layer + 4, :] = rows_ref[0, base + 8:base + 12, :]
+    hop = copy(far_send, far_got, peer(Z1))
+    hop.start()
+    crossing.wait()
+
+    @pl.when(core == 1)
+    def _():
+        along.wait()
+
+    reduce_ref[...] = (part_got[0, 0].astype(F32) + part_got[1, 0].astype(F32)).T
+    expand_ref[...] = part_got[0, 1].astype(F32) + part_got[1, 1].astype(F32)
+    hop.wait()
+    small_ref[0:vectors, :] = far_send[0:vectors, :] + far_got[0:vectors, :]
+    for layer in range(layers):
+        base = vectors + 12 * layer
+        row = vectors + layer
+        small_ref[row:row + 1, :] = (
+            rows_ref[0, base:base + 1, :] + near_got[vectors + 2 * layer:vectors + 2 * layer + 1, :] + far_got[row:row + 1, :]
+        )
+        row = vectors + layers + 4 * layer
+        small_ref[row:row + 4, :] = rows_ref[0, base + 4:base + 8, :] + far_got[row:row + 4, :]
+    heads.wait()
+    for part in range(3):
+        here = slice(part * 256, (part + 1) * 256)
+        project_ref[part] = z_send[0, :, here].astype(F32) + z_got[:, here].astype(F32)
+    output_ref[...] = (z_send[0, :, 768:].astype(F32) + z_got[:, 768:].astype(F32)).T
+
+    @pl.when(keep)
+    def _():
+        stay.wait()
+
+    @pl.when(jnp.logical_not(keep))
+    def _():
+        tokens.wait()
+
+
+def finish(grad, even, odd, here, away, sums):
+    layers = len(sums)
+    vmem = pl.BlockSpec(memory_space=pltpu.VMEM)
+    rows = 18 * layers
+    args = [grad, even, odd, here, away, *[array for layer in sums for array in layer]]
+    small = 8 * (-(-11 * layers // 8))
+    outs = [
+        jax.ShapeDtypeStruct(grad.shape, BF),
+        jax.ShapeDtypeStruct((3, 128, 256), F32),
+        jax.ShapeDtypeStruct((256, 128), F32),
+        jax.ShapeDtypeStruct((1024, 128), F32),
+        jax.ShapeDtypeStruct((128, 1024), F32),
+        jax.ShapeDtypeStruct((small, 128), F32),
+    ]
+    one = (128, 1024)
+    copies = 15
+    return pl.pallas_call(
+        functools.partial(finish_kernel, layers),
+        in_specs=[vmem] * len(args),
+        out_specs=[vmem] * len(outs),
+        out_shape=outs,
+        scratch_shapes=[
+            pltpu.VMEM((4, 2, *one), BF),
+            *[pltpu.VMEM((2, *one), BF)] * 7,
+            pltpu.VMEM(one, BF),
+            *[pltpu.VMEM((2, 2, *one), BF)] * 3,
+            pltpu.VMEM((8, rows, 128), F32),
+            pltpu.VMEM((4, rows, 128), F32),
+            pltpu.VMEM((2, rows, 128), F32),
+            pltpu.VMEM((1, rows, 128), F32),
+            *[pltpu.VMEM((small, 128), F32)] * 4,
+            pltpu.SemaphoreType.DMA,
+            pltpu.SemaphoreType.DMA((copies,)),
+            pltpu.SemaphoreType.DMA((copies,)),
+        ],
+        compiler_params=pltpu.CompilerParams(vmem_limit_bytes=VMEM_LIMIT, collective_id=1, has_side_effects=True),
+        cost_estimate=took(50),
+        name="finish",
+    )(*args)
+
+
 def fetch_heads(piece, core, turn, out):
     token = yield
     far = swap(after(piece, token), Z1)
@@ -1471,15 +1676,6 @@
     out += [quads, other, turn]
 
 
-def fetch_units_near(first, first_out, second_out):
-    token = yield
-    first = after(first, token)
-    first_x, first_y, second = swap(first, XBIT), swap(first, YBIT), swap(first, Z0)
-    token = yield []
-    first_x, first_y, second = after_all((first_x, first_y, second), token)
-    yield from join_units(first, first_x, first_y, second, first_out, second_out)
-
-
 def fetch_units(piece, core, first_out, second_out):
     token = yield
     piece = after(piece, token)
@@ -1490,14 +1686,29 @@
     token = yield [first]
     second = swap(after(first, token), Z0)
     token = yield []
-    first, second = after_all((first, second), token)
+    second = after(second, token)
+    token = yield [second]
+    first = after(first, token)
     first_x, first_y = swap(first, XBIT), swap(first, YBIT)
-    token = yield [second]
-    first_x, first_y = after_all((first_x, first_y), token)
-    yield from join_units(first, first_x, first_y, second, first_out, second_out)
+    token = yield []
+    steps = join_units(first, first_x, first_y, second, first_out, second_out)
+    next(steps)
+    made = steps.send(token)
+    while made is not None:
+        token = yield made
+        made = next_made(steps, token)
+
+
+def next_made(steps, token):
+    try:
+        return steps.send(token)
+    except StopIteration:
+        return None
 
 
 def join_units(first, first_x, first_y, second, first_out, second_out):
+    token = yield
+    first, first_x, first_y, second = after_all((first, first_x, first_y, second), token)
     second_x, second_y = swap(second, XBIT), swap(second, YBIT)
     token = yield [first_x, first_y, second]
     second_x, second_y = after_all((second_x, second_y), token)
@@ -1530,49 +1741,6 @@
         [six.transpose(1, 0, 2).astype(F32), wide.reshape(layers, 4, 128), expand_bias[:, None, :].astype(F32)], axis=1
     )
     return jnp.pad(rows.reshape(layers * SMALL_ROWS, 128), ((0, -layers * SMALL_ROWS % 8), (0, 0)))
-
-
-def pack_kernel(count, own_ref, *rest):
-    out_ref, own = rest[-1], own_ref[0]
-    core = own % 2
-    out_ref[...] = jnp.zeros_like(out_ref)
-    for layer in range(count):
-        first_ref, second_ref, unit_ref, head_ref = rest[4 * layer:4 * layer + 4]
-        for place in range(8):
-            here = slice(place * 128, (place + 1) * 128)
-            out_ref[place, 6 * layer:6 * layer + 2, :] = first_ref[0:2, here]
-            out_ref[place, 6 * layer + 2:6 * layer + 6, :] = second_ref[0:4, here]
-            base = 6 * count + 12 * layer
-            for quarter in range(2):
-                lane = pl.multiple_of(quarter * 1024 + (place ^ own) * 128, 128)
-                out_ref[place, pl.ds(base + 2 * core + quarter, 1), :] = unit_ref[0:1, pl.ds(lane, 128)]
-                row = base + 4 + 4 * (quarter ^ core)
-                for half in range(2):
-                    out_ref[place, pl.ds(row + 2 * half, 2), :] = head_ref[2 * quarter:2 * quarter + 2, half * 128:(half + 1) * 128]
-
-
-def sum_small(layers, own, own_keep, token):
-    count = len(layers)
-    rows = 18 * count
-    args = [own_keep] + [array for layer in layers for array in layer]
-    rows = call_once(
-        functools.partial(pack_kernel, count), "pack", [jax.ShapeDtypeStruct((8, rows, 128), F32)], args, 3
-    )[0]
-    rows = after(rows, token)
-    for mask in (CORE, XBIT, YBIT):
-        bit = rows.reshape(-1, 2, 18 * count, 128)
-        rows = bit[:, 0] + swap(bit[:, 1], mask)
-    vectors, biases = rows[0, :6 * count], rows[0, 6 * count:].reshape(count, 12, 128)
-
-    def part(offset, *more):
-        return jnp.concatenate([vectors, biases[:, offset], *more], axis=0)
-
-    two = swap(part(2, biases[:, 8:].reshape(4 * count, 128)), 2)
-    whole = part(0) + two[:7 * count] + swap(part(1), 1) + swap(part(3), 3)
-    heads = biases[:, 4:8] + two[7 * count:].reshape(count, 4, 128)
-    heads = heads.reshape(count, 2, 2, 128).transpose(0, 2, 1, 3).reshape(count, 2, 256)
-    heads = lax.dynamic_slice_in_dim(heads, own * 32, 32, 2)
-    return whole[:6 * count].reshape(count, 6, 128), whole[6 * count:], heads
 
 
 def reduce_heads(even, odd, core, out):
@@ -1620,6 +1788,10 @@
     totals = [
         jnp.stack([own_r[i] + from_y[i, 0] + relay_r[i], own_e[i] + from_x[i, 0] + relay_e[i]]) for i in range(2)
     ]
+    if core is None:
+        out += totals
+        yield totals
+        return
     yield from close_units(*totals, core, out)
 
 
@@ -1662,7 +1834,7 @@
 
     six = jnp.stack([first_gain, first_shift, output_bias, second_gain, second_shift, reduce_bias])
     turn = jnp.zeros((1,), jnp.int32)
-    resid, normed, far, even, odd, ready, vectors_of, head_bias_of, unit_bias_of, *blocks = start(
+    resid, normed, far, even, odd, first_pieces, first_x, first_y, second, vectors_of, head_bias_of, unit_bias_of, *blocks = start(
         layer_input, project_weight, output_weight, expand_weight, reduce_weight,
         small_rows(six, project_bias, expand_bias, own), LAYERS,
     )
@@ -1671,7 +1843,7 @@
     starts = jnp.where(keep, picture_start, redeal(picture_start))[0]
     heads, units = [[] for i in range(LAYERS)], [([], []) for i in range(LAYERS)]
     heads[0] += [even, odd, turn]
-    head_tasks, unit_tasks = [None], [task(fetch_units_near(ready, *units[0]))]
+    head_tasks, unit_tasks = [None], [task(join_units(first_pieces, first_x, first_y, second, *units[0]))]
     for layer in range(1, LAYERS):
         weights = after_all((project_weight, output_weight, expand_weight, reduce_weight), far_mine)
         head_piece = pack_heads(weights[0][layer], weights[1][layer])
@@ -1694,6 +1866,7 @@
         made = advance(far_mine, unit_tasks[layer])
         if first:
             made += advance(far_mine, unit_tasks[1])
+            made += [far_piece for far_piece in (head_piece,)]
         blocks = after_all((near_mine, far_mine, got_near, got_far), *made)
         far_mixed, far_send, far_exact, far_log = attend(blocks, 1, slopes, starts, me)
         far_got = swap(far_send, CORE)
@@ -1715,13 +1888,11 @@
             grad_other = swap(flip_grad, CORE)
             normed_two = after(normed_two, grad)
         if first:
-            made = advance(mid, unit_tasks[0])
             advance(mid, unit_tasks[1], head_tasks[1])
-            normed_two = after(normed_two, *made)
         hidden, active, near_out, away_out = mlp_forward(turn, normed_two, normed_other, unit_bias, units[layer])
         got_out = swap(away_out, CORE)
         if not last:
-            got_out = after(got_out, *advance(near_out, head_tasks[layer + 1]))
+            got_out = after(got_out, *advance(near_out, head_tasks[layer + 1], unit_tasks[layer + 1]))
         out, following = mlp_close(last, own_keep, near_out, got_out, mid, vectors)
         if not last:
             advance(out, head_tasks[layer + 1])
@@ -1751,7 +1922,7 @@
         near_mine, near_other = unmix(after(grad_low, reduce_parts[0], *made), pieces)
         got_near = swap(near_other, CORE)
         expand_parts = unit_grads("y", normed_two, normed_other, after(grad_hidden, near_mine))
-        unit_task = task(reduce_units(reduce_parts, expand_parts, core, unit_grad[layer]))
+        unit_task = task(reduce_units(reduce_parts, expand_parts, None if first else core, unit_grad[layer]))
         advance(None, unit_task)
         advance(None, unit_task)
         far_mine, far_other = unmix(after(grad_far, expand_parts[0]), pieces)
@@ -1771,8 +1942,9 @@
         even, odd, head_sums = head_grads(
             turn, normed, far, grad_low, after(grad_far, far_part), mine, other, mixed, mixed_got
         )
-        head_task = task(reduce_heads(even, odd, core, head_grad[layer]))
-        advance(None, head_task)
+        if not first:
+            head_task = task(reduce_heads(even, odd, core, head_grad[layer]))
+            advance(None, head_task)
         made = advance(head_sums, unit_task)
         grad, grad_low, first_sums = unproject_near(
             first, own_keep, mine, other, after(far_term, *made), resid, grad_mid, vectors, pieces
@@ -1782,12 +1954,13 @@
             grad_other = swap(grad_low, CORE)
             grad = after(grad, *advance(grad, head_task))
         pending = [unit_task, head_task]
-    input_far = redeal(grad_low)
-    made = advance(grad, *pending)
-    six, unit_sum, head_sum = sum_small(sums, own, own_keep, made[0])
-    while len(head_grad[0]) + len(unit_grad[0]) < 2:
-        advance(grad, *pending)
-    input_grad = jnp.where(keep, grad_low, input_far)
+    input_grad, *grads, small_sums = finish(grad_low, even, odd, *unit_grad[0], sums)
+    head_grad[0], unit_grad[0] = [grads[:2]], [grads[2:]]
+    unit_grad[1:] = [[(g[0][0].T, g[0][1])] for g in unit_grad[1:]]
+    six = small_sums[:6 * LAYERS].reshape(LAYERS, 6, 128)
+    unit_sum = small_sums[6 * LAYERS:7 * LAYERS]
+    head_sum = small_sums[7 * LAYERS:11 * LAYERS].reshape(LAYERS, 2, 2, 128).transpose(0, 2, 1, 3).reshape(LAYERS, 2, 256)
+    head_sum = lax.dynamic_slice_in_dim(head_sum, own * 32, 32, 2)
     return (
         layer_output,
         input_grad,
@@ -1801,7 +1974,7 @@
         six[:, 4],
         jnp.stack([g[0][1] for g in unit_grad]),
         unit_sum,
-        jnp.stack([g[0][0].T for g in unit_grad]),
+        jnp.stack([g[0][0] for g in unit_grad]),
         six[:, 5],
     )
 

time: 912 us -> 834 us (0.914)
  starting transfers between devices: 124 us -> 60.8 us
  local copies, waits for them, and re-layouts: 40.4 us -> 96.2 us
  waiting for transfers between devices: 213 us -> 160 us
  Pallas kernels: 492 us -> 465 us
    ppermute x73 -> x59, waiting for transfers between devices: 212 us -> 125 us  [swap(): return lax.ppermute(values, AXES, [(i, i ^ mask) for i in range(32)])]
    pallas_call x21 -> x20, Pallas kernels: 123 us -> 46.4 us  [call_once(): pl.pallas_call(kernel, in_specs=placed(args), out_specs=placed(outs), out...]
    pallas_call x0 -> x1, Pallas kernels: none -> 65.3 us  [finish(): pl.pallas_call(functools.partial(finish_kernel, layers), in_specs=[vmem]...]
    ppermute x73 -> x59, starting transfers between devices: 109 us -> 53.3 us  [swap(): return lax.ppermute(values, AXES, [(i, i ^ mask) for i in range(32)])]
    unnamed x124 -> x321, local copies, waits for them, and re-layouts: 28.6 us -> 73.7 us
    ppermute x5 -> x3, waiting for transfers between devices: 0.53 us -> 34.9 us  [swap_some(): lax.ppermute(values, AXES, [pair for pair in pairs if pair[0] != pair[1]])]
    pallas_call x2, Pallas kernels: 45.2 us -> 28.7 us  [mlp_forward(): pl.pallas_call(mlp_kernel, grid_spec=pltpu.PrefetchScalarGridSpec(num_sca...]
    pallas_call x1, Pallas kernels: 92.4 us -> 107 us  [start(): pl.pallas_call(functools.partial(start_kernel, layers), in_specs=[vmem] *...]
  transfers between devices with their start and end apart: 82 -> 65, of which waited for: 38 -> 25; matrix products, arithmetic and copies ran while one was open for 4% -> 5% of each run, Pallas kernels for 36% -> 31%
where the time goes in v5:
time: 834 us; the launch traced here: 817 us
  Pallas kernels  465 us (56%)
  waiting for transfers between devices  160 us (19%)
  local copies, waits for them, and re-layouts  96.2 us (12%)
  starting transfers between devices  60.8 us (7%)
  other arithmetic  32.8 us (4%)
    ppermute x59, waiting for transfers between devices, swap(): return lax.ppermute(values, AXES, [(i, i ^ mask) for i in range(32)])  125 us
    pallas_call x1, Pallas kernels, start(): pl.pallas_call(functools.partial(start_kernel, layers), in_specs=[vmem] *...  107 us
    pallas_call x4, Pallas kernels, attend_pull(): pl.pallas_call(functools.partial(pull_kernel, block, pair), grid=(4,), in...  86.1 us
    unnamed x321, local copies, waits for them, and re-layouts  73.7 us
    pallas_call x4, Pallas kernels, attend(): pl.pallas_call(functools.partial(attend_kernel, block, rest_bit), grid=(p...  69.1 us
    pallas_call x1, Pallas kernels, finish(): pl.pallas_call(functools.partial(finish_kernel, layers), in_specs=[vmem]...  65.3 us
    ppermute x59, starting transfers between devices, swap(): return lax.ppermute(values, AXES, [(i, i ^ mask) for i in range(32)])  53.3 us
    pallas_call x20, Pallas kernels, call_once(): pl.pallas_call(kernel, in_specs=placed(args), out_specs=placed(outs), out...  46.4 us
  transfers between devices with their start and end apart: 65, of which 25 were waited for; matrix products, arithmetic and copies ran while one was open for 5% of the time, Pallas kernels for 31%

profile of v5, /device:TPU:0, one launch (start us, length us, event | category | flops | bytes accessed | tf_op | source)
XLA Modules:
  0.0 817.0 jit_solution(1519408463793445594)
XLA Ops:
  11.4 107.0 %start.1 = (f32[512,1024]{1,0:T(8,128)S(1)}, bf16[512,1024]{1,0:T(8,128)(2,1)S(1)}, bf16[512,1024]{1,0:T(8,128)(2,1)S(1)}, bf16[4,2,128,1024]{3,2,1,0:T(8,128)(2...) custom-call(bf16[512,1024]{1,0:T(8,128)(2,1)S(1)} %copy-done.14, ...), custom_call_target="tpu_custom_call" | custom-call | flops 30000001024 | bytes 1 | tf_op jit(solution)/shard_map/start/pallas_call | solution.py:1439
  135.4 3.1 pad_maximum_fusion.9
  150.3 17.7 %attend.4 = (bf16[512,256]{1,0:T(8,128)(2,1)S(1)}, bf16[512,256]{1,0:T(8,128)(2,1)S(1)}, f32[256,1024]{1,0:T(8,128)S(1)}, f32[2,8,1024]{2,1,0:T(8,128)S(1)}) custom-call(f32[4]{0:T(128)S(1)} %multiply_exponential_fusion.slope_ref, s32[2]{0:T(128)S(1)} %fusion.9.start_ref, s32[1]{0:T(128)} %bitcast.3.me_ref, bf16[512,768]{1,0:T(8,128)(2,1)S(1)} %copy-done.118, ...), custom_call_target="tpu_custom_call" | custom-call | flops 8499999744 | bytes 1 | tf_op jit(solution)/shard_map/attend/pallas_call | solution.py:614
  177.4 16.7 %attend.5 = (bf16[512,256]{1,0:T(8,128)(2,1)S(1)}, bf16[512,256]{1,0:T(8,128)(2,1)S(1)}, f32[256,1024]{1,0:T(8,128)S(1)}, f32[2,8,1024]{2,1,0:T(8,128)S(1)}) custom-call(f32[4]{0:T(128)S(1)} %multiply_exponential_fusion.slope_ref, s32[2]{0:T(128)S(1)} %fusion.9.start_ref, s32[1]{0:T(128)} %bitcast.3.me_ref, bf16[512,768]{1,0:T(8,128)(2,1)S(1)} %copy-done.119, ...), custom_call_target="tpu_custom_call" | custom-call | flops 8499999744 | bytes 1 | tf_op jit(solution)/shard_map/attend/pallas_call | solution.py:614
  197.6 5.3 collective-permute-done.8.rest_7_
  202.9 9.0 %collective-permute-done.6.far_ref = bf16[512,1024]{1,0:T(8,128)(2,1)S(1)} collective-permute-done((bf16[512,1024]{1,0:T(8,128)(2,1)S(1)}, bf16[512,1024]{1,0:T(8,128)(2,1)S(1)}, u32[]{:S(2)}, u32[]{:S(2)}) %collective-permute-start.6) | collective-permute-done | bytes 1048608 | tf_op jit(solution)/shard_map/ppermute | solution.py:426
  218.2 15.3 %mlp_forward.2 = (bf16[1024,2048]{1,0:T(8,128)(2,1)S(1)}, bf16[1024,2048]{1,0:T(8,128)(2,1)S(1)}, f32[512,1024]{1,0:T(8,128)S(1)}, bf16[512,1024]{1,0:T(8,128)(2,1)}) custom-call(s32[1]{0:T(128)} %constant.9.clone.1.rest_2_.turn_ref.rest_6_.rest_10_, bf16[512,1024]{1,0:T(8,128)(2,1)S(1)} %get-tuple-element.263.normed_ref.left_ref, ...), custom_call_target="tpu_custom_call" | custom-call | flops 8999999488 | bytes 1 | tf_op jit(solution)/shard_map/mlp_forward/pallas_call | solution.py:1047
  239.1 14.1 %collective-permute-done.12 = bf16[128,1024]{1,0:T(8,128)(2,1)S(1)} collective-permute-done((bf16[128,1024]{1,0:T(8,128)(2,1)S(1)}, bf16[128,1024]{1,0:T(8,128)(2,1)S(1)}, u32[]{:S(2)}, u32[]{:S(2)}) %collective-permute-start.12) | collective-permute-done | bytes 262176 | tf_op jit(solution)/shard_map/ppermute | solution.py:426
  261.5 6.7 collective-permute-done.14
  270.0 11.9 %collective-permute-done.16 = bf16[2,128,1024]{2,1,0:T(8,128)(2,1)S(1)} collective-permute-done((bf16[2,128,1024]{2,1,0:T(8,128)(2,1)}, bf16[2,128,1024]{2,1,0:T(8,128)(2,1)S(1)}, u32[]{:S(2)}, u32[]{:S(2)}) %collective-permute-start.16) | collective-permute-done | bytes 524320 | tf_op jit(solution)/shard_map/ppermute | solution.py:426
  289.4 19.6 %collective-permute-done.18.rows_ref.far_ref = bf16[512,1024]{1,0:T(8,128)(2,1)S(1)} collective-permute-done((bf16[512,1024]{1,0:T(8,128)(2,1)S(1)}, bf16[512,1024]{1,0:T(8,128)(2,1)S(1)}, u32[]{:S(2)}, u32[]{:S(2)}) %collective-permute-start.18) | collective-permute-done | bytes 1048608 | tf_op jit(solution)/shard_map/ppermute | solution.py:426
  313.5 17.7 %attend.6 = (bf16[512,256]{1,0:T(8,128)(2,1)S(1)}, bf16[512,256]{1,0:T(8,128)(2,1)S(1)}, f32[256,1024]{1,0:T(8,128)S(1)}, f32[2,8,1024]{2,1,0:T(8,128)S(1)}) custom-call(f32[4]{0:T(128)S(1)} %multiply_exponential_fusion.slope_ref, s32[2]{0:T(128)S(1)} %fusion.9.start_ref, s32[1]{0:T(128)} %bitcast.3.me_ref, ...), custom_call_target="tpu_custom_call" | custom-call | flops 8499999744 | bytes 1 | tf_op jit(solution)/shard_map/attend/pallas_call | solution.py:614
  333.9 2.9 collective-permute-done.24.rest_5_
  339.7 16.9 %attend.7 = (bf16[512,256]{1,0:T(8,128)(2,1)S(1)}, bf16[512,256]{1,0:T(8,128)(2,1)S(1)}, f32[256,1024]{1,0:T(8,128)S(1)}, f32[2,8,1024]{2,1,0:T(8,128)S(1)}) custom-call(f32[4]{0:T(128)S(1)} %multiply_exponential_fusion.slope_ref, s32[2]{0:T(128)S(1)} %fusion.9.start_ref, s32[1]{0:T(128)} %bitcast.3.me_ref, ...), custom_call_target="tpu_custom_call" | custom-call | flops 8499999744 | bytes 1 | tf_op jit(solution)/shard_map/attend/pallas_call | solution.py:614
  357.5 2.5 collective-permute-done.28.rest_3_
  363.1 2.6 enter.1
  365.8 13.4 %mlp_forward.3 = (bf16[1024,2048]{1,0:T(8,128)(2,1)S(1)}, bf16[1024,2048]{1,0:T(8,128)(2,1)S(1)}, f32[512,1024]{1,0:T(8,128)S(1)}, bf16[512,1024]{1,0:T(8,128)(2,1)S(1)}) custom-call(s32[1]{0:T(128)} %constant.9.clone.1.rest_2_.turn_ref.rest_6_.rest_10_, bf16[512,1024]{1,0:T(8,128)(2,1)S(1)} %get-tuple-element.312.normed_ref.left_ref, ...), custom_call_target="tpu_custom_call" | custom-call | flops 8999999488 | bytes 1 | tf_op jit(solution)/shard_map/mlp_forward/pallas_call | solution.py:1047
  383.1 22.4 %collective-permute-start.32 = (bf16[512,1024]{1,0:T(8,128)(2,1)S(1)}, bf16[512,1024]{1,0:T(8,128)(2,1)S(1)}, u32[]{:S(2)}, u32[]{:S(2)}) collective-permute-start(bf16[512,1024]{1,0:T(8,128)(2,1)S(1)} %get-tuple-element.316), channel_id=1, source_target_pairs={{0,4},{1,5},{2,6},{3,7},{4,0},{5,1},{6,2},{7,3},{8,12},{9,13},{10,... | collective-permute-start | bytes 3145736 | tf_op jit(solution)/shard_map/ppermute | solution.py:426
  407.7 2.4 mlp_close.3
  411.0 16.5 %mlp_backward.2 = (bf16[1024,2048]{1,0:T(8,128)(2,1)S(1)}, f32[1,2048]{1,0:T(1,128)S(1)}, f32[512,1024]{1,0:T(8,128)S(1)}, bf16[512,1024]{1,0:T(8,128)(2,1)S(1)}) custom-call(s32[1]{0:T(128)} %constant.9.clone.1.rest_2_.turn_ref.rest_6_.rest_10_, f32[512,1024]{1,0:T(8,128)S(1)} %get-tuple-element.318.grad_ref.left_ref, ...), custom_call_target="tpu_custom_call" | custom-call | flops 11000000512 | bytes 1 | tf_op jit(solution)/shard_map/mlp_backward/pallas_call | solution.py:1125
  435.3 6.4 unit_grads.4
  444.7 6.8 unit_grads.5
  451.5 9.2 %collective-permute-done.36.grad_ref.grad_far_ref = bf16[512,1024]{1,0:T(8,128)(2,1)S(1)} collective-permute-done((bf16[512,1024]{1,0:T(8,128)(2,1)S(1)}, bf16[512,1024]{1,0:T(8,128)(2,1)S(1)}, u32[]{:S(2)}, u32[]{:S(2)}) %collective-permute-start.36) | collective-permute-done | bytes 1048608 | tf_op jit(solution)/shard_map/ppermute | solution.py:426
  463.2 21.0 %attend_pull.4 = (bf16[3,1024,128]{2,1,0:T(8,128)(2,1)S(1)}, bf16[3,1024,128]{2,1,0:T(8,128)(2,1)S(1)}) custom-call(f32[4]{0:T(128)S(1)} %multiply_exponential_fusion.slope_ref, s32[2]{0:T(128)S(1)} %fusion.9.start_ref, s32[1]{0:T(128)} %bitcast.3.me_ref, bf16[512,768]{1,0:T(8,128)(2,1)S(1)} %copy-done.84, bf16[512,768]{1,0:T(8,128)(2,1)S(1)} %copy-done.84, ...), custom_call_target="tpu_custom_call" | custom-call | flops 11000000512 | bytes 1 | tf_op jit(solution)/shard_map/attend_pull/pallas_call | solution.py:747
  484.2 5.6 collective-permute-done.39
  489.9 21.2 %attend_pull.5 = (bf16[3,1024,128]{2,1,0:T(8,128)(2,1)S(1)}, bf16[3,1024,128]{2,1,0:T(8,128)(2,1)S(1)}) custom-call(f32[4]{0:T(128)S(1)} %multiply_exponential_fusion.slope_ref, s32[2]{0:T(128)S(1)} %fusion.9.start_ref, s32[1]{0:T(128)} %bitcast.3.me_ref, bf16[512,768]{1,0:T(8,128)(2,1)S(1)} %copy-done.84, bf16[512,768]{1,0:T(8,128)(2,1)S(1)} %copy-done.84, ...), custom_call_target="tpu_custom_call" | custom-call | flops 11000000512 | bytes 1 | tf_op jit(solution)/shard_map/attend_pull/pallas_call | solution.py:747
  514.6 2.8 unproject_far.2
  519.2 4.9 head_grads.2
  526.8 4.3 copy.67
  531.2 7.0 collective-permute-done.44
  539.9 5.5 fusion.4
  547.4 5.1 unproject_near.2
  553.8 4.0 copy.66
  559.6 2.5 slice_add_fusion
  567.4 16.7 %mlp_backward.3 = (bf16[1024,2048]{1,0:T(8,128)(2,1)S(1)}, f32[1,2048]{1,0:T(1,128)S(1)}, f32[512,1024]{1,0:T(8,128)S(1)}, bf16[512,1024]{1,0:T(8,128)(2,1)S(1)}) custom-call(s32[1]{0:T(128)} %constant.9.clone.1.rest_2_.turn_ref.rest_6_.rest_10_, f32[512,1024]{1,0:T(8,128)S(1)} %copy-done.63, bf16[512,1024]{1,0:T(8,128)(2,1)S(1)} %collective-permute-done.47.other_ref, ...), custom_call_target="tpu_custom_call" | custom-call | flops 11000000512 | bytes 1 | tf_op jit(solution)/shard_map/mlp_backward/pallas_call | solution.py:1125
  586.2 2.8 collective-permute-start.52
  593.8 6.6 unit_grads.6
  600.5 34.9 %collective-permute-done.52 = bf16[2,128,1024]{2,1,0:T(8,128)(2,1)S(1)} collective-permute-done((bf16[2,128,1024]{2,1,0:T(8,128)(2,1)S(1)}, bf16[2,128,1024]{2,1,0:T(8,128)(2,1)S(1)}, u32[]{:S(2)}, u32[]{:S(2)}) %collective-permute-start.52) | collective-permute-done | bytes 524320 | tf_op jit(solution)/shard_map/ppermute | solution.py:431
  639.8 6.4 unit_grads.7
  649.8 21.9 %attend_pull.6 = (bf16[3,1024,128]{2,1,0:T(8,128)(2,1)S(1)}, bf16[3,1024,128]{2,1,0:T(8,128)(2,1)}) custom-call(f32[4]{0:T(128)S(1)} %multiply_exponential_fusion.slope_ref, s32[2]{0:T(128)S(1)} %fusion.9.start_ref, s32[1]{0:T(128)} %bitcast.3.me_ref, bf16[512,768]{1,0:T(8,128)(2,1)S(1)} %copy-done.120, bf16[512,768]{1,0:T(8,128)(2,1)S(1)} %copy-done.120, ...), custom_call_target="tpu_custom_call" | custom-call | flops 11000000512 | bytes 1 | tf_op jit(solution)/shard_map/attend_pull/pallas_call | solution.py:747
  673.9 22.0 %attend_pull.7 = (bf16[3,1024,128]{2,1,0:T(8,128)(2,1)S(1)}, bf16[3,1024,128]{2,1,0:T(8,128)(2,1)}) custom-call(f32[4]{0:T(128)S(1)} %multiply_exponential_fusion.slope_ref, s32[2]{0:T(128)S(1)} %fusion.9.start_ref, s32[1]{0:T(128)} %bitcast.3.me_ref, bf16[512,768]{1,0:T(8,128)(2,1)S(1)} %copy-done.120, bf16[512,768]{1,0:T(8,128)(2,1)S(1)} %copy-done.120, ...), custom_call_target="tpu_custom_call" | custom-call | flops 11000000512 | bytes 1 | tf_op jit(solution)/shard_map/attend_pull/pallas_call | solution.py:747
  706.7 3.3 unproject_far.3
  710.6 6.4 head_grads.3
  717.0 6.1 collective-permute-done.63
  727.9 7.2 collective-permute-done.62.rest_4_
  735.2 5.7 unproject_near.3
  740.8 65.3 %finish.1 = (bf16[512,1024]{1,0:T(8,128)(2,1)S(1)}, f32[3,128,256]{2,1,0:T(8,128)S(1)}, f32[256,128]{1,0:T(8,128)S(1)}, f32[1024,128]{1,0:T(8,128)S(1)}, f32[128,1024]{1,0:T(8,128)S(1)}, /*index=5*/f32[24,128]{1,0:T(8,128)S(1)}) custom-call(bf16[512,1024]{1,0:T(8,128)(2,1)S(1)} %get-tuple-element.421.grad_ref, ...), custom_call_target="tpu_custom_call" | custom-call | flops 24999999488 | bytes 1 | tf_op jit(solution)/shard_map/finish/pallas_call | solution.py:1636
  810.4 2.6 copy.72
  (517 shorter events, 176.2 us)
Async XLA Ops:
  130.0 47.2 %collective-permute-start.3 = (bf16[2,128,2048]{2,1,0:T(8,128)(2,1)S(1)}, bf16[2,128,2048]{2,1,0:T(8,128)(2,1)}, u32[]{:S(2)}, u32[]{:S(2)}) collective-permute-start(bf16[2,128,2048]{2,1,0:T(8,128)(2,1)S(1)} %get-tuple-element.235.rest_4_), channel_id=1, source_target_pairs={{0,8},{1,9},{2,10},{3,11},{4,12},{5,13},{6,14},{7,15},{8,0},{9,1},... | collective-permute-start | bytes 3145736 | tf_op jit(solution)/shard_map/ppermute | solution.py:426
  131.5 45.7 %collective-permute-start.4 = (bf16[2,128,2048]{2,1,0:T(8,128)(2,1)S(1)}, bf16[2,128,2048]{2,1,0:T(8,128)(2,1)}, u32[]{:S(2)}, u32[]{:S(2)}) collective-permute-start(bf16[2,128,2048]{2,1,0:T(8,128)(2,1)S(1)} %get-tuple-element.235.rest_4_), channel_id=1, source_target_pairs={{0,16},{1,17},{2,18},{3,19},{4,20},{5,21},{6,22},{7,23},{8,24},{9,... | collective-permute-start | bytes 3145736 | tf_op jit(solution)/shard_map/ppermute | solution.py:426
  132.7 10.8 %collective-permute-start = (s32[1,2]{1,0:T(1,128)S(1)}, s32[1,2]{1,0:T(1,128)S(1)}, u32[]{:S(2)}, u32[]{:S(2)}) collective-permute-start(s32[1,2]{1,0:T(1,128)S(1)} %copy-done.156), channel_id=1, source_target_pairs={{2,4},{3,5},{4,2},{5,3},{10,12},{11,13},{12,10},{13,11},{18,20},{1... | collective-permute-start | bytes 32 | tf_op jit(solution)/shard_map/ppermute | solution.py:439
  169.6 28.0 %collective-permute-start.7 = (bf16[2,128,2048]{2,1,0:T(8,128)(2,1)S(1)}, bf16[2,128,2048]{2,1,0:T(8,128)(2,1)}, u32[]{:S(2)}, u32[]{:S(2)}) collective-permute-start(bf16[2,128,2048]{2,1,0:T(8,128)(2,1)S(1)} %get-tuple-element.233.rest_1_), channel_id=1, source_target_pairs={{0,16},{1,17},{2,18},{3,19},{4,20},{5,21},{6,22},{7,23},{8,24},{9,... | collective-permute-start | bytes 3145736 | tf_op jit(solution)/shard_map/ppermute | solution.py:426
  170.4 26.0 %collective-permute-start.9 = (bf16[2,128,2048]{2,1,0:T(8,128)(2,1)}, bf16[2,128,2048]{2,1,0:T(8,128)(2,1)}, u32[]{:S(2)}, u32[]{:S(2)}) collective-permute-start(bf16[2,128,2048]{2,1,0:T(8,128)(2,1)} %pad_maximum_fusion.1), channel_id=1, source_target_pairs={{4,6},{5,7},{6,4},{7,5},{12,14},{13,15},{14,12},{15,13},{20,22},{2... | collective-permute-start | bytes 3145736 | tf_op jit(solution)/shard_map/ppermute | solution.py:431
  176.4 35.5 %collective-permute-start.6 = (bf16[512,1024]{1,0:T(8,128)(2,1)S(1)}, bf16[512,1024]{1,0:T(8,128)(2,1)S(1)}, u32[]{:S(2)}, u32[]{:S(2)}) collective-permute-start(bf16[512,1024]{1,0:T(8,128)(2,1)S(1)} %mix_far.2), channel_id=1, source_target_pairs={{0,1},{1,0},{2,3},{3,2},{4,5},{5,4},{6,7},{7,6},{8,9},{9,8},{10,11... | collective-permute-start | bytes 3145736 | tf_op jit(solution)/shard_map/ppermute | solution.py:426
  177.2 25.8 %collective-permute-start.8 = (bf16[2,128,2048]{2,1,0:T(8,128)(2,1)}, bf16[2,128,2048]{2,1,0:T(8,128)(2,1)S(1)}, u32[]{:S(2)}, u32[]{:S(2)}) collective-permute-start(bf16[2,128,2048]{2,1,0:T(8,128)(2,1)} %collective-permute-done.4.rest_6_), channel_id=1, source_target_pairs={{0,8},{1,9},{2,10},{3,11},{4,12},{5,13},{6,14},{7,15},{8,0},{9,1},... | collective-permute-start | bytes 3145736 | tf_op jit(solution)/shard_map/ppermute | solution.py:426
  194.2 17.7 %collective-permute-start.5 = (bf16[512,256]{1,0:T(8,128)(2,1)S(1)}, bf16[512,256]{1,0:T(8,128)(2,1)S(1)}, u32[]{:S(2)}, u32[]{:S(2)}) collective-permute-start(bf16[512,256]{1,0:T(8,128)(2,1)S(1)} %get-tuple-element.256), channel_id=1, source_target_pairs={{0,4},{1,5},{2,6},{3,7},{4,0},{5,1},{6,2},{7,3},{8,12},{9,13},{10,... | collective-permute-start | bytes 786440 | tf_op jit(solution)/shard_map/ppermute | solution.py:426
  215.8 41.0 %collective-permute-start.13 = (bf16[2,128,2048]{2,1,0:T(8,128)(2,1)S(1)}, bf16[2,128,2048]{2,1,0:T(8,128)(2,1)}, u32[]{:S(2)}, u32[]{:S(2)}) collective-permute-start(bf16[2,128,2048]{2,1,0:T(8,128)(2,1)S(1)} %broadcast_select_fusion.rest_0_), channel_id=1, source_target_pairs={{0,1},{1,0},{2,3},{3,2},{4,5},{5,4},{6,7},{7,6},{8,9},{9,8},{10,11... | collective-permute-start | bytes 3145736 | tf_op jit(solution)/shard_map/ppermute | solution.py:426
  238.8 18.1 %collective-permute-start.11 = (bf16[512,1024]{1,0:T(8,128)(2,1)}, bf16[512,1024]{1,0:T(8,128)(2,1)S(1)}, u32[]{:S(2)}, u32[]{:S(2)}) collective-permute-start(bf16[512,1024]{1,0:T(8,128)(2,1)} %get-tuple-element.268), channel_id=1, source_target_pairs={{0,4},{1,5},{2,6},{3,7},{4,0},{5,1},{6,2},{7,3},{8,12},{9,13},{10,... | collective-permute-start | bytes 3145736 | tf_op jit(solution)/shard_map/ppermute | solution.py:426
  239.1 14.1 %collective-permute-start.12 = (bf16[128,1024]{1,0:T(8,128)(2,1)S(1)}, bf16[128,1024]{1,0:T(8,128)(2,1)S(1)}, u32[]{:S(2)}, u32[]{:S(2)}) collective-permute-start(bf16[128,1024]{1,0:T(8,128)(2,1)S(1)} %copy-done.155), channel_id=1, source_target_pairs={{0,2},{1,3},{2,0},{3,1},{4,6},{5,7},{6,4},{7,5},{8,10},{9,11},{10,... | collective-permute-start | bytes 786440 | tf_op jit(solution)/shard_map/ppermute | solution.py:426
  254.3 13.9 %collective-permute-start.14 = (bf16[2,128,1024]{2,1,0:T(8,128)(2,1)S(1)}, bf16[2,128,1024]{2,1,0:T(8,128)(2,1)S(1)}, u32[]{:S(2)}, u32[]{:S(2)}) collective-permute-start(bf16[2,128,1024]{2,1,0:T(8,128)(2,1)S(1)} %get-tuple-element.481), channel_id=1, source_target_pairs={{0,8},{1,9},{2,10},{3,11},{4,12},{5,13},{6,14},{7,15},{8,0},{9,1},... | collective-permute-start | bytes 1572872 | tf_op jit(solution)/shard_map/ppermute | solution.py:426
  255.3 13.7 %collective-permute-start.15 = (bf16[2,128,1024]{2,1,0:T(8,128)(2,1)S(1)}, bf16[2,128,1024]{2,1,0:T(8,128)(2,1)}, u32[]{:S(2)}, u32[]{:S(2)}) collective-permute-start(bf16[2,128,1024]{2,1,0:T(8,128)(2,1)S(1)} %get-tuple-element.481), channel_id=1, source_target_pairs={{0,16},{1,17},{2,18},{3,19},{4,20},{5,21},{6,22},{7,23},{8,24},{9,... | collective-permute-start | bytes 1572872 | tf_op jit(solution)/shard_map/ppermute | solution.py:426
  269.0 12.9 %collective-permute-start.16 = (bf16[2,128,1024]{2,1,0:T(8,128)(2,1)}, bf16[2,128,1024]{2,1,0:T(8,128)(2,1)S(1)}, u32[]{:S(2)}, u32[]{:S(2)}) collective-permute-start(bf16[2,128,1024]{2,1,0:T(8,128)(2,1)} %collective-permute-done.15), channel_id=1, source_target_pairs={{0,8},{1,9},{2,10},{3,11},{4,12},{5,13},{6,14},{7,15},{8,0},{9,1},... | collective-permute-start | bytes 1572872 | tf_op jit(solution)/shard_map/ppermute | solution.py:426
  283.5 25.6 %collective-permute-start.18 = (bf16[512,1024]{1,0:T(8,128)(2,1)S(1)}, bf16[512,1024]{1,0:T(8,128)(2,1)S(1)}, u32[]{:S(2)}, u32[]{:S(2)}) collective-permute-start(bf16[512,1024]{1,0:T(8,128)(2,1)S(1)} %get-tuple-element.275.rows_ref.near_ref), channel_id=1, source_target_pairs={{0,1},{1,0},{2,3},{3,2},{4,5},{5,4},{6,7},{7,6},{8,9},{9,8},{10,11... | collective-permute-start | bytes 3145736 | tf_op jit(solution)/shard_map/ppermute | solution.py:426
  283.5 27.9 %collective-permute-start.21 = (bf16[2,128,2048]{2,1,0:T(8,128)(2,1)S(1)}, bf16[2,128,2048]{2,1,0:T(8,128)(2,1)S(1)}, u32[]{:S(2)}, u32[]{:S(2)}) collective-permute-start(bf16[2,128,2048]{2,1,0:T(8,128)(2,1)S(1)} %broadcast_select_fusion.rest_0_), channel_id=1, source_target_pairs={{0,8},{1,9},{2,10},{3,11},{4,12},{5,13},{6,14},{7,15},{8,0},{9,1},... | collective-permute-start | bytes 3145736 | tf_op jit(solution)/shard_map/ppermute | solution.py:426
  284.6 26.8 %collective-permute-start.22 = (bf16[2,128,2048]{2,1,0:T(8,128)(2,1)S(1)}, bf16[2,128,2048]{2,1,0:T(8,128)(2,1)S(1)}, u32[]{:S(2)}, u32[]{:S(2)}) collective-permute-start(bf16[2,128,2048]{2,1,0:T(8,128)(2,1)S(1)} %broadcast_select_fusion.rest_0_), channel_id=1, source_target_pairs={{0,16},{1,17},{2,18},{3,19},{4,20},{5,21},{6,22},{7,23},{8,24},{9,... | collective-permute-start | bytes 3145736 | tf_op jit(solution)/shard_map/ppermute | solution.py:426
  311.4 25.4 %collective-permute-start.24 = (bf16[2,128,2048]{2,1,0:T(8,128)(2,1)}, bf16[2,128,2048]{2,1,0:T(8,128)(2,1)S(1)}, u32[]{:S(2)}, u32[]{:S(2)}) collective-permute-start(bf16[2,128,2048]{2,1,0:T(8,128)(2,1)} %collective-permute-done.13.rest_4_), channel_id=1, source_target_pairs={{0,8},{1,9},{2,10},{3,11},{4,12},{5,13},{6,14},{7,15},{8,0},{9,1},... | collective-permute-start | bytes 3145736 | tf_op jit(solution)/shard_map/ppermute | solution.py:426
  312.5 26.3 %collective-permute-start.25 = (bf16[2,128,2048]{2,1,0:T(8,128)(2,1)}, bf16[2,128,2048]{2,1,0:T(8,128)(2,1)S(1)}, u32[]{:S(2)}, u32[]{:S(2)}) collective-permute-start(bf16[2,128,2048]{2,1,0:T(8,128)(2,1)} %collective-permute-done.13.rest_4_), channel_id=1, source_target_pairs={{0,16},{1,17},{2,18},{3,19},{4,20},{5,21},{6,22},{7,23},{8,24},{9,... | collective-permute-start | bytes 3145736 | tf_op jit(solution)/shard_map/ppermute | solution.py:426
  331.5 28.5 %collective-permute-start.28 = (bf16[2,128,2048]{2,1,0:T(8,128)(2,1)S(1)}, bf16[2,128,2048]{2,1,0:T(8,128)(2,1)S(1)}, u32[]{:S(2)}, u32[]{:S(2)}) collective-permute-start(bf16[2,128,2048]{2,1,0:T(8,128)(2,1)S(1)} %collective-permute-done.21.rest_1_), channel_id=1, source_target_pairs={{0,16},{1,17},{2,18},{3,19},{4,20},{5,21},{6,22},{7,23},{8,24},{9,... | collective-permute-start | bytes 3145736 | tf_op jit(solution)/shard_map/ppermute | solution.py:426
  333.8 27.7 %collective-permute-start.27 = (bf16[512,1024]{1,0:T(8,128)(2,1)S(1)}, bf16[512,1024]{1,0:T(8,128)(2,1)S(1)}, u32[]{:S(2)}, u32[]{:S(2)}) collective-permute-start(bf16[512,1024]{1,0:T(8,128)(2,1)S(1)} %mix_far.3), channel_id=1, source_target_pairs={{0,1},{1,0},{2,3},{3,2},{4,5},{5,4},{6,7},{7,6},{8,9},{9,8},{10,11... | collective-permute-start | bytes 3145736 | tf_op jit(solution)/shard_map/ppermute | solution.py:426
  338.7 22.8 %collective-permute-start.29 = (bf16[2,128,2048]{2,1,0:T(8,128)(2,1)S(1)}, bf16[2,128,2048]{2,1,0:T(8,128)(2,1)S(1)}, u32[]{:S(2)}, u32[]{:S(2)}) collective-permute-start(bf16[2,128,2048]{2,1,0:T(8,128)(2,1)S(1)} %collective-permute-done.25.rest_6_), channel_id=1, source_target_pairs={{0,8},{1,9},{2,10},{3,11},{4,12},{5,13},{6,14},{7,15},{8,0},{9,1},... | collective-permute-start | bytes 3145736 | tf_op jit(solution)/shard_map/ppermute | solution.py:426
  356.8 6.4 collective-permute-start.30
  383.1 24.6 %collective-permute-start.32 = (bf16[512,1024]{1,0:T(8,128)(2,1)S(1)}, bf16[512,1024]{1,0:T(8,128)(2,1)S(1)}, u32[]{:S(2)}, u32[]{:S(2)}) collective-permute-start(bf16[512,1024]{1,0:T(8,128)(2,1)S(1)} %get-tuple-element.316), channel_id=1, source_target_pairs={{0,4},{1,5},{2,6},{3,7},{4,0},{5,1},{6,2},{7,3},{8,12},{9,13},{10,... | collective-permute-start | bytes 3145736 | tf_op jit(solution)/shard_map/ppermute | solution.py:426
  435.3 25.4 %collective-permute-start.36 = (bf16[512,1024]{1,0:T(8,128)(2,1)S(1)}, bf16[512,1024]{1,0:T(8,128)(2,1)S(1)}, u32[]{:S(2)}, u32[]{:S(2)}) collective-permute-start(bf16[512,1024]{1,0:T(8,128)(2,1)S(1)} %get-tuple-element.327.grad_ref.grad_near_ref), channel_id=1, source_target_pairs={{0,1},{1,0},{2,3},{3,2},{4,5},{5,4},{6,7},{7,6},{8,9},{9,8},{10,11... | collective-permute-start | bytes 3145736 | tf_op jit(solution)/shard_map/ppermute | solution.py:426
  441.8 48.0 %collective-permute-start.39 = (bf16[2,2,2,128,1024]{4,3,2,1,0:T(8,128)(2,1)S(1)}, bf16[2,2,2,128,1024]{4,3,2,1,0:T(8,128)(2,1)S(1)}, u32[]{:S(2)}, u32[]{:S(2)}) collective-permute-start(bf16[2,2,2,128,1024]{4,3,2,1,0:T(8,128)(2,1)S(1)} %get-tuple-element.342), channel_id=1, source_target_pairs={{0,16},{1,17},{2,18},{3,19},{4,20},{5,21},{6,22},{7,23},{8,24},{9,... | collective-permute-start | bytes 6291464 | tf_op jit(solution)/shard_map/ppermute | solution.py:426
  442.8 18.9 %collective-permute-start.37 = (bf16[512,256]{1,0:T(8,128)(2,1)S(1)}, bf16[512,256]{1,0:T(8,128)(2,1)S(1)}, u32[]{:S(2)}, u32[]{:S(2)}) collective-permute-start(bf16[512,256]{1,0:T(8,128)(2,1)S(1)} %get-tuple-element.334), channel_id=1, source_target_pairs={{0,4},{1,5},{2,6},{3,7},{4,0},{5,1},{6,2},{7,3},{8,12},{9,13},{10,... | collective-permute-start | bytes 786440 | tf_op jit(solution)/shard_map/ppermute | solution.py:426
  461.6 51.2 %collective-permute-start.42 = (bf16[2,2,2,128,1024]{4,3,2,1,0:T(8,128)(2,1)S(1)}, bf16[2,2,2,128,1024]{4,3,2,1,0:T(8,128)(2,1)S(1)}, u32[]{:S(2)}, u32[]{:S(2)}) collective-permute-start(bf16[2,2,2,128,1024]{4,3,2,1,0:T(8,128)(2,1)S(1)} %get-tuple-element.352), channel_id=1, source_target_pairs={{0,8},{1,9},{2,10},{3,11},{4,12},{5,13},{6,14},{7,15},{8,0},{9,1},... | collective-permute-start | bytes 6291464 | tf_op jit(solution)/shard_map/ppermute | solution.py:426
  512.8 25.5 %collective-permute-start.44 = (bf16[2,2,128,1024]{3,2,0,1:T(8,128)(2,1)}, bf16[2,2,128,1024]{3,2,0,1:T(8,128)(2,1)}, u32[]{:S(2)}, u32[]{:S(2)}) collective-permute-start(bf16[2,2,128,1024]{3,2,0,1:T(8,128)(2,1)} %copy.60), channel_id=1, source_target_pairs={{0,8},{1,9},{2,10},{3,11},{4,12},{5,13},{6,14},{7,15},{8,0},{9,1},... | collective-permute-start | bytes 3145736 | tf_op jit(solution)/shard_map/ppermute | solution.py:426
  514.4 25.5 %collective-permute-start.45 = (bf16[2,2,128,1024]{3,2,0,1:T(8,128)(2,1)}, bf16[2,2,128,1024]{3,2,0,1:T(8,128)(2,1)}, u32[]{:S(2)}, u32[]{:S(2)}) collective-permute-start(bf16[2,2,128,1024]{3,2,0,1:T(8,128)(2,1)} %copy.61), channel_id=1, source_target_pairs={{0,16},{1,17},{2,18},{3,19},{4,20},{5,21},{6,22},{7,23},{8,24},{9,... | collective-permute-start | bytes 3145736 | tf_op jit(solution)/shard_map/ppermute | solution.py:426
  517.4 29.0 %collective-permute-start.43 = (bf16[512,1024]{1,0:T(8,128)(2,1)}, bf16[512,1024]{1,0:T(8,128)(2,1)}, u32[]{:S(2)}, u32[]{:S(2)}) collective-permute-start(bf16[512,1024]{1,0:T(8,128)(2,1)} %unproject_far.2), channel_id=1, source_target_pairs={{0,1},{1,0},{2,3},{3,2},{4,5},{5,4},{6,7},{7,6},{8,9},{9,8},{10,11... | collective-permute-start | bytes 3145736 | tf_op jit(solution)/shard_map/ppermute | solution.py:426
  531.1 28.5 %collective-permute-start.46 = (bf16[4,2,128,1024]{2,3,1,0:T(8,128)(2,1)}, bf16[4,2,128,1024]{2,3,1,0:T(8,128)(2,1)}, u32[]{:S(2)}, u32[]{:S(2)}) collective-permute-start(bf16[4,2,128,1024]{2,3,1,0:T(8,128)(2,1)} %copy.67), channel_id=1, source_target_pairs={{0,4},{1,5},{2,6},{3,7},{4,0},{5,1},{6,2},{7,3},{8,12},{9,13},{10,... | collective-permute-start | bytes 6291464 | tf_op jit(solution)/shard_map/ppermute | solution.py:426
  553.8 8.7 %collective-permute-start.47 = (bf16[512,1024]{1,0:T(8,128)(2,1)}, bf16[512,1024]{1,0:T(8,128)(2,1)S(1)}, u32[]{:S(2)}, u32[]{:S(2)}) collective-permute-start(bf16[512,1024]{1,0:T(8,128)(2,1)} %get-tuple-element.366), channel_id=1, source_target_pairs={{0,4},{1,5},{2,6},{3,7},{4,0},{5,1},{6,2},{7,3},{8,12},{9,13},{10,... | collective-permute-start | bytes 3145736 | tf_op jit(solution)/shard_map/ppermute | solution.py:426
  557.8 27.3 %collective-permute-start.49 = (bf16[2,2,128,1024]{3,2,0,1:T(8,128)(2,1)}, bf16[2,2,128,1024]{3,2,0,1:T(8,128)(2,1)S(1)}, u32[]{:S(2)}, u32[]{:S(2)}) collective-permute-start(bf16[2,2,128,1024]{3,2,0,1:T(8,128)(2,1)} %pad_maximum_fusion.3), channel_id=1, source_target_pairs={{0,1},{1,0},{2,3},{3,2},{4,5},{5,4},{6,7},{7,6},{8,9},{9,8},{10,11... | collective-permute-start | bytes 3145736 | tf_op jit(solution)/shard_map/ppermute | solution.py:426
  562.1 26.9 %collective-permute-start.50 = (bf16[2,2,128,1024]{2,3,1,0:T(8,128)(2,1)S(1)}, bf16[2,2,128,1024]{2,3,1,0:T(8,128)(2,1)S(1)}, u32[]{:S(2)}, u32[]{:S(2)}) collective-permute-start(bf16[2,2,128,1024]{2,3,1,0:T(8,128)(2,1)S(1)} %get-tuple-element.468), channel_id=1, source_target_pairs={{0,16},{1,17},{2,18},{3,19},{4,20},{5,21},{6,22},{7,23},{8,24},{9,... | collective-permute-start | bytes 3145736 | tf_op jit(solution)/shard_map/ppermute | solution.py:426
  584.4 63.0 %collective-permute-start.33 = (bf16[512,1024]{1,0:T(8,128)(2,1)S(1)}, bf16[512,1024]{1,0:T(8,128)(2,1)S(1)}, u32[]{:S(2)}, u32[]{:S(2)}) collective-permute-start(bf16[512,1024]{1,0:T(8,128)(2,1)S(1)} %get-tuple-element.317), channel_id=1, source_target_pairs={{2,4},{3,5},{4,2},{5,3},{10,12},{11,13},{12,10},{13,11},{18,20},{1... | collective-permute-start | bytes 3145736 | tf_op jit(solution)/shard_map/ppermute | solution.py:439
  585.4 15.1 %collective-permute-start.51 = (bf16[2,128,1024]{2,1,0:T(8,128)(2,1)S(1)}, bf16[2,128,1024]{2,1,0:T(8,128)(2,1)S(1)}, u32[]{:S(2)}, u32[]{:S(2)}) collective-permute-start(bf16[2,128,1024]{2,1,0:T(8,128)(2,1)S(1)} %get-tuple-element.477), channel_id=1, source_target_pairs={{4,6},{5,7},{6,4},{7,5},{12,14},{13,15},{14,12},{15,13},{20,22},{2... | collective-permute-start | bytes 1572872 | tf_op jit(solution)/shard_map/ppermute | solution.py:431
  586.2 49.1 %collective-permute-start.52 = (bf16[2,128,1024]{2,1,0:T(8,128)(2,1)S(1)}, bf16[2,128,1024]{2,1,0:T(8,128)(2,1)S(1)}, u32[]{:S(2)}, u32[]{:S(2)}) collective-permute-start(bf16[2,128,1024]{2,1,0:T(8,128)(2,1)S(1)} %get-tuple-element.476), channel_id=1, source_target_pairs={{0,4},{1,5},{2,6},{3,7},{4,2},{5,3},{6,0},{7,1},{8,12},{9,13},{10,... | collective-permute-start | bytes 1572872 | tf_op jit(solution)/shard_map/ppermute | solution.py:431
  589.1 47.2 %collective-permute-start.53 = (bf16[2,128,1024]{1,2,0:T(8,128)(2,1)S(1)}, bf16[2,128,1024]{1,2,0:T(8,128)(2,1)S(1)}, u32[]{:S(2)}, u32[]{:S(2)}) collective-permute-start(bf16[2,128,1024]{1,2,0:T(8,128)(2,1)S(1)} %fusion.2), channel_id=1, source_target_pairs={{0,8},{1,9},{2,10},{3,11},{4,12},{5,13},{6,14},{7,15},{8,0},{9,1},... | collective-permute-start | bytes 1572872 | tf_op jit(solution)/shard_map/ppermute | solution.py:426
  593.6 52.7 %collective-permute-start.54 = (bf16[512,1024]{1,0:T(8,128)(2,1)S(1)}, bf16[512,1024]{1,0:T(8,128)(2,1)S(1)}, u32[]{:S(2)}, u32[]{:S(2)}) collective-permute-start(bf16[512,1024]{1,0:T(8,128)(2,1)S(1)} %get-tuple-element.380.grad_ref.grad_near_ref), channel_id=1, source_target_pairs={{0,1},{1,0},{2,3},{3,2},{4,5},{5,4},{6,7},{7,6},{8,9},{9,8},{10,11... | collective-permute-start | bytes 3145736 | tf_op jit(solution)/shard_map/ppermute | solution.py:426
  635.4 37.4 %collective-permute-start.58 = (bf16[2,2,2,128,1024]{4,3,2,1,0:T(8,128)(2,1)S(1)}, bf16[2,2,2,128,1024]{4,3,2,1,0:T(8,128)(2,1)S(1)}, u32[]{:S(2)}, u32[]{:S(2)}) collective-permute-start(bf16[2,2,2,128,1024]{4,3,2,1,0:T(8,128)(2,1)S(1)} %get-tuple-element.400), channel_id=1, source_target_pairs={{0,16},{1,17},{2,18},{3,19},{4,20},{5,21},{6,22},{7,23},{8,24},{9,... | collective-permute-start | bytes 6291464 | tf_op jit(solution)/shard_map/ppermute | solution.py:426
  639.0 10.7 %collective-permute-start.55 = (bf16[512,256]{1,0:T(8,128)(2,1)S(1)}, bf16[512,256]{1,0:T(8,128)(2,1)S(1)}, u32[]{:S(2)}, u32[]{:S(2)}) collective-permute-start(bf16[512,256]{1,0:T(8,128)(2,1)S(1)} %get-tuple-element.387), channel_id=1, source_target_pairs={{0,4},{1,5},{2,6},{3,7},{4,0},{5,1},{6,2},{7,3},{8,12},{9,13},{10,... | collective-permute-start | bytes 786440 | tf_op jit(solution)/shard_map/ppermute | solution.py:426
  648.5 49.0 %collective-permute-start.57 = (bf16[128,1024]{0,1:T(8,128)(2,1)S(1)}, bf16[128,1024]{0,1:T(8,128)(2,1)S(1)}, u32[]{:S(2)}, u32[]{:S(2)}) collective-permute-start(bf16[128,1024]{0,1:T(8,128)(2,1)S(1)} %get-tuple-element.478), channel_id=1, source_target_pairs={{0,2},{1,3},{2,0},{3,1},{4,6},{5,7},{6,4},{7,5},{8,10},{9,11},{10,... | collective-permute-start | bytes 786440 | tf_op jit(solution)/shard_map/ppermute | solution.py:426
  648.5 49.0 %collective-permute-start.61 = (bf16[2,2,2,128,1024]{4,3,2,1,0:T(8,128)(2,1)S(1)}, bf16[2,2,2,128,1024]{4,3,2,1,0:T(8,128)(2,1)S(1)}, u32[]{:S(2)}, u32[]{:S(2)}) collective-permute-start(bf16[2,2,2,128,1024]{4,3,2,1,0:T(8,128)(2,1)S(1)} %get-tuple-element.410), channel_id=1, source_target_pairs={{0,8},{1,9},{2,10},{3,11},{4,12},{5,13},{6,14},{7,15},{8,0},{9,1},... | collective-permute-start | bytes 6291464 | tf_op jit(solution)/shard_map/ppermute | solution.py:426
  672.5 28.6 %collective-permute-start.59 = (bf16[3,1024,128]{2,1,0:T(8,128)(2,1)}, bf16[3,1024,128]{2,1,0:T(8,128)(2,1)}, u32[]{:S(2)}, u32[]{:S(2)}) collective-permute-start(bf16[3,1024,128]{2,1,0:T(8,128)(2,1)} %get-tuple-element.407), channel_id=1, source_target_pairs={{0,4},{1,5},{2,6},{3,7},{4,0},{5,1},{6,2},{7,3},{8,12},{9,13},{10,... | collective-permute-start | bytes 2359304 | tf_op jit(solution)/shard_map/ppermute | solution.py:426
  697.5 25.6 %collective-permute-start.63 = (bf16[2,2,128,1024]{3,2,1,0:T(8,128)(2,1)}, bf16[2,2,128,1024]{3,2,1,0:T(8,128)(2,1)}, u32[]{:S(2)}, u32[]{:S(2)}) collective-permute-start(bf16[2,2,128,1024]{3,2,1,0:T(8,128)(2,1)} %bitcast_add_fusion.1), channel_id=1, source_target_pairs={{0,8},{1,9},{2,10},{3,11},{4,12},{5,13},{6,14},{7,15},{8,0},{9,1},... | collective-permute-start | bytes 3145736 | tf_op jit(solution)/shard_map/ppermute | solution.py:426
  698.7 25.6 %collective-permute-start.64 = (bf16[2,2,128,1024]{3,2,1,0:T(8,128)(2,1)}, bf16[2,2,128,1024]{3,2,1,0:T(8,128)(2,1)}, u32[]{:S(2)}, u32[]{:S(2)}) collective-permute-start(bf16[2,2,128,1024]{3,2,1,0:T(8,128)(2,1)} %bitcast_add_fusion), channel_id=1, source_target_pairs={{0,16},{1,17},{2,18},{3,19},{4,20},{5,21},{6,22},{7,23},{8,24},{9,... | collective-permute-start | bytes 3145736 | tf_op jit(solution)/shard_map/ppermute | solution.py:426
  710.1 25.0 %collective-permute-start.62 = (bf16[512,1024]{1,0:T(8,128)(2,1)S(1)}, bf16[512,1024]{1,0:T(8,128)(2,1)S(1)}, u32[]{:S(2)}, u32[]{:S(2)}) collective-permute-start(bf16[512,1024]{1,0:T(8,128)(2,1)S(1)} %unproject_far.3), channel_id=1, source_target_pairs={{0,1},{1,0},{2,3},{3,2},{4,5},{5,4},{6,7},{7,6},{8,9},{9,8},{10,11... | collective-permute-start | bytes 3145736 | tf_op jit(solution)/shard_map/ppermute | solution.py:426
  (176 other events, 2001.2 us)

commit v6 on v5

--- a/solution.py
+++ b/solution.py
@@ -1272,11 +1272,15 @@
 
 
 def start_kernel(
-    layers, x_ref, project_ref, output_ref, expand_ref, reduce_ref, small_ref,
-    resid_ref, normed_ref, far_ref, even_ref, odd_ref, first_ref, first_x_ref, first_y_ref, second_ref, vector_ref, head_bias_ref, unit_bias_ref,
+    layers, x_ref, project_ref, output_ref, expand_ref, reduce_ref,
+    *rest,
+):
+    six_refs, bias_ref, unit_row_ref, rest = rest[:6], rest[6], rest[7], rest[8:]
+    (
+    resid_ref, normed_ref, far_ref, even_ref, odd_ref, first_ref, heads_ref, pairs_ref, vector_ref, head_bias_ref, unit_bias_ref,
     near_mine_ref, far_mine_ref, got_near_ref, got_far_ref,
     came_ref, piece_ref, every_ref, near_other_ref, far_other_ref, local_sem, send_sem, recv_sem,
-):
+    ) = rest
     own, place = lax.axis_index("dp"), lax.axis_index("tensor")
     core = own % 2
     keep = core == place // 2
@@ -1302,12 +1306,30 @@
     def _():
         tokens.start()
 
-    for part in range(3):
-        even_ref[0, core, :, part * 256:(part + 1) * 256] = project_ref[0, part]
-    even_ref[0, core, :, 768:1024] = output_ref[0].T
+    def pack_heads_into(target, layer):
+        for part in range(3):
+            target[:, part * 256:(part + 1) * 256] = project_ref[layer, part]
+        target[:, 768:1024] = output_ref[layer].T
+
+    def pack_units_into(target, layer):
+        for half in range(2):
+            here = slice(half * 512, (half + 1) * 512)
+            target[:, half * 1024:half * 1024 + 512] = expand_ref[layer, :, here]
+            target[:, half * 1024 + 512:half * 1024 + 1024] = reduce_ref[layer, here, :].T
+
+    pack_heads_into(even_ref.at[0, core], 0)
     along = copy(even_ref.at[0, core], even_ref.at[0, 1 - core], peer(Z1))
     along.start()
-    every_ref[0, 0] = small_ref[...]
+    every_ref[0, 0] = jnp.zeros(every_ref.shape[2:], F32)
+    lane = lax.broadcasted_iota(jnp.int32, (1, 128), 1)
+    for layer in range(layers):
+        base = layer * SMALL_ROWS
+        for row, ref in enumerate(six_refs):
+            every_ref[0, 0, base + row:base + row + 1, :] = ref[layer:layer + 1, :].astype(F32)
+        for part in range(2):
+            ours = jnp.where(lane // 32 == own % 4, bias_ref[layer, part:part + 1, :].astype(F32), 0.0)
+            every_ref[0, 0, pl.ds(base + 6 + 2 * part + own // 4, 1), :] = ours
+        every_ref[0, 0, base + 10:base + 11, :] = unit_row_ref[layer:layer + 1, :].astype(F32)
     smalls = [
         (copy(every_ref.at[0, pl.ds(0, width)], every_ref.at[0, pl.ds(width, width)], peer(mask)))
         for width, mask in ((1, CORE), (2, XBIT), (4, YBIT))
@@ -1316,10 +1338,7 @@
         copy(every_ref.at[pl.ds(0, width)], every_ref.at[pl.ds(width, width)], peer(mask)) for width, mask in ((1, Z0), (2, Z1))
     ]
     smalls[0].start()
-    for half in range(2):
-        here = slice(half * 512, (half + 1) * 512)
-        piece_ref[:, half * 1024:half * 1024 + 512] = expand_ref[0, :, here]
-        piece_ref[:, half * 1024 + 512:half * 1024 + 1024] = reduce_ref[0, here, :].T
+    pack_units_into(piece_ref, 0)
     cross = copy(piece_ref, first_ref.at[1], {
         "dp": flip(own, 1), "tensor": place + (1 - core) * (flip(place, 2) - place)
     })
@@ -1381,6 +1400,13 @@
     def _():
         same.start()
 
+    ahead = []
+    for layer in range(1, layers):
+        pack_heads_into(heads_ref.at[layer - 1], layer)
+        pack_units_into(pairs_ref.at[layer - 1, 0], layer)
+        ahead.append(copy(pairs_ref.at[layer - 1, 0], pairs_ref.at[layer - 1, 1], peer(CORE)))
+    for one in ahead:
+        one.start()
     over_y.wait()
     over_x.wait()
     across = copy(even_ref.at[2], even_ref.at[3], peer(XBIT))
@@ -1395,27 +1421,27 @@
     project_rows(normed_ref[...], weights, head_bias_ref, 0, (near_mine_ref, near_other_ref))
     back_near = copy(near_other_ref, got_near_ref, peer(CORE))
     back_near.start()
-    cross.wait()
-
-    @pl.when(core == 1)
-    def _():
-        same.wait()
-
-    units = [copy(first_ref, target, peer(mask)) for target, mask in ((first_x_ref, XBIT), (first_y_ref, YBIT), (second_ref, Z0))]
-    for one in units:
-        one.start()
     beside.wait()
     project_rows(far_ref[...], weights, head_bias_ref, 0, (far_mine_ref, far_other_ref))
     back_far = copy(far_other_ref, got_far_ref, peer(CORE))
     back_far.start()
     back_near.wait()
     back_far.wait()
-    for one in units:
+    cross.wait()
+
+    @pl.when(core == 1)
+    def _():
+        same.wait()
+
+    for one in ahead:
         one.wait()
 
 
-def start(x, project_weight, output_weight, expand_weight, reduce_weight, small, layers):
+def start(x, project_weight, output_weight, expand_weight, reduce_weight, six, project_bias, expand_bias):
     rows, features = x.shape
+    layers = expand_bias.shape[0]
+    small = 8 * (-(-SMALL_ROWS * layers // 8))
+    project_bias = jnp.tile(project_bias, (1, 1, 4))
     vmem = pl.BlockSpec(memory_space=pltpu.VMEM)
 
     triple = jax.ShapeDtypeStruct((rows, 768), BF)
@@ -1426,7 +1452,9 @@
         jax.ShapeDtypeStruct((rows, features), BF),
         heads,
         heads,
-        *[jax.ShapeDtypeStruct((2, 128, 2048), BF)] * 4,
+        jax.ShapeDtypeStruct((2, 128, 2048), BF),
+        jax.ShapeDtypeStruct((layers - 1, 128, 1024), BF),
+        jax.ShapeDtypeStruct((layers - 1, 2, 128, 2048), BF),
         jax.ShapeDtypeStruct((layers, 8, features), F32),
         jax.ShapeDtypeStruct((layers, 2, 768), F32),
         jax.ShapeDtypeStruct((layers, 1, 2048), F32),
@@ -1435,16 +1463,16 @@
         triple,
         triple,
     ]
-    copies = 22
+    copies = 19 + layers - 1
     return pl.pallas_call(
         functools.partial(start_kernel, layers),
-        in_specs=[vmem] * 6,
+        in_specs=[vmem] * 13,
         out_specs=[vmem] * len(outs),
         out_shape=outs,
         scratch_shapes=[
             pltpu.VMEM((rows, features), BF),
             pltpu.VMEM((128, 2048), BF),
-            pltpu.VMEM((4, 8, *small.shape), F32),
+            pltpu.VMEM((4, 8, small, 128), F32),
             pltpu.VMEM((rows, 768), BF),
             pltpu.VMEM((rows, 768), BF),
             pltpu.SemaphoreType.DMA,
@@ -1454,7 +1482,7 @@
         compiler_params=pltpu.CompilerParams(vmem_limit_bytes=VMEM_LIMIT, collective_id=0, has_side_effects=True),
         cost_estimate=took(60),
         name="start",
-    )(x, project_weight, output_weight, expand_weight, reduce_weight, small)
+    )(x, project_weight, output_weight, expand_weight, reduce_weight, *six, project_bias, expand_bias)
 
 
 def finish_kernel(
@@ -1676,42 +1704,10 @@
     out += [quads, other, turn]
 
 
-def fetch_units(piece, core, first_out, second_out):
-    token = yield
-    piece = after(piece, token)
-    pair = jnp.stack([piece, swap(piece, CORE)])
-    far = swap_some(pair, (0, Z1))
-    token = yield [pair]
-    first = jnp.where(core == 0, pair, after(far, token))
-    token = yield [first]
-    second = swap(after(first, token), Z0)
-    token = yield []
-    second = after(second, token)
-    token = yield [second]
-    first = after(first, token)
-    first_x, first_y = swap(first, XBIT), swap(first, YBIT)
-    token = yield []
-    steps = join_units(first, first_x, first_y, second, first_out, second_out)
-    next(steps)
-    made = steps.send(token)
-    while made is not None:
-        token = yield made
-        made = next_made(steps, token)
-
-
-def next_made(steps, token):
-    try:
-        return steps.send(token)
-    except StopIteration:
-        return None
-
-
 def join_units(first, first_x, first_y, second, first_out, second_out):
-    token = yield
-    first, first_x, first_y, second = after_all((first, first_x, first_y, second), token)
     second_x, second_y = swap(second, XBIT), swap(second, YBIT)
     token = yield [first_x, first_y, second]
-    second_x, second_y = after_all((second_x, second_y), token)
+    first_x, second_x, second_y = after_all((first_x, second_x, second_y), token)
     first_across, second_across = swap(first_x, YBIT), swap(second_y, XBIT)
     token = yield [second_x, second_y]
     first_across, second_across = after_all((first_across, second_across), token)
@@ -1720,27 +1716,33 @@
     yield [first_across, second_across]
 
 
-def pack_heads(project, output):
-    return jnp.concatenate([project.transpose(1, 0, 2).reshape(128, 768), output.T], axis=1)
+def fetch_units_near(first, first_out, second_out):
+    token = yield
+    first = after(first, token)
+    first_x, first_y, second = swap(first, XBIT), swap(first, YBIT), swap(first, Z0)
+    token = yield []
+    first_x, first_y, second = after_all((first_x, first_y, second), token)
+    yield from join_units(first, first_x, first_y, second, first_out, second_out)
+
+
+def fetch_units(pair, core, first_out, second_out):
+    token = yield
+    far = swap_some(after(pair, token), (0, Z1))
+    token = yield []
+    first = jnp.where(core == 0, pair, after(far, token))
+    second = swap(first, Z0)
+    token = yield [first]
+    second = after(second, token)
+    token = yield [second]
+    first = after(first, token)
+    first_x, first_y = swap(first, XBIT), swap(first, YBIT)
+    token = yield []
+    first_x, first_y = after_all((first_x, first_y), token)
+    yield from join_units(first, first_x, first_y, second, first_out, second_out)
 
 
 def unpack_heads(values):
     return values[:, :768].reshape(128, 3, 256).transpose(1, 0, 2), values[:, 768:].T
-
-
-def pack_units(expand, reduce):
-    parts = (expand.reshape(128, 2, 512), reduce.T.reshape(128, 2, 512))
-    return jnp.stack(parts, axis=2).reshape(128, 2048)
-
-
-def small_rows(six, project_bias, expand_bias, own):
-    layers = six.shape[1]
-    wide = jnp.zeros((layers, 2, 256), F32)
-    wide = lax.dynamic_update_slice(wide, project_bias.astype(F32), (0, 0, own * 32))
-    rows = jnp.concatenate(
-        [six.transpose(1, 0, 2).astype(F32), wide.reshape(layers, 4, 128), expand_bias[:, None, :].astype(F32)], axis=1
-    )
-    return jnp.pad(rows.reshape(layers * SMALL_ROWS, 128), ((0, -layers * SMALL_ROWS % 8), (0, 0)))
 
 
 def reduce_heads(even, odd, core, out):
@@ -1799,6 +1801,8 @@
     got = swap(away, Z0)
     token = yield [here, away]
     here = here + after(got, token)
+    token = yield [here]
+    here = after(here, token)
     same, cross = here[:, 0], here[:, 1]
     same_got, cross_got = swap_some(same, (0, Z1)), swap_some(cross, (CORE, CORE | Z1))
     token = yield [same, cross]
@@ -1832,24 +1836,20 @@
     me = (2 * core + (place & 1)).astype(jnp.int32).reshape(1)
     slopes = head_slopes((place ^ (2 * core)) * 4, 4)
 
-    six = jnp.stack([first_gain, first_shift, output_bias, second_gain, second_shift, reduce_bias])
     turn = jnp.zeros((1,), jnp.int32)
-    resid, normed, far, even, odd, first_pieces, first_x, first_y, second, vectors_of, head_bias_of, unit_bias_of, *blocks = start(
+    resid, normed, far, even, odd, first_pieces, own_heads, own_units, vectors_of, head_bias_of, unit_bias_of, *blocks = start(
         layer_input, project_weight, output_weight, expand_weight, reduce_weight,
-        small_rows(six, project_bias, expand_bias, own), LAYERS,
+        (first_gain, first_shift, output_bias, second_gain, second_shift, reduce_bias), project_bias, expand_bias,
     )
     near_mine, far_mine, got_near, got_far = blocks
     small = [(vectors_of[i], head_bias_of[i], unit_bias_of[i]) for i in range(LAYERS)]
     starts = jnp.where(keep, picture_start, redeal(picture_start))[0]
     heads, units = [[] for i in range(LAYERS)], [([], []) for i in range(LAYERS)]
     heads[0] += [even, odd, turn]
-    head_tasks, unit_tasks = [None], [task(join_units(first_pieces, first_x, first_y, second, *units[0]))]
+    head_tasks, unit_tasks = [None], [task(fetch_units_near(first_pieces, *units[0]))]
     for layer in range(1, LAYERS):
-        weights = after_all((project_weight, output_weight, expand_weight, reduce_weight), far_mine)
-        head_piece = pack_heads(weights[0][layer], weights[1][layer])
-        unit_piece = pack_units(weights[2][layer], weights[3][layer])
-        head_tasks.append(task(fetch_heads(head_piece, core, turn, heads[layer])))
-        unit_tasks.append(task(fetch_units(unit_piece, core, *units[layer])))
+        head_tasks.append(task(fetch_heads(own_heads[layer - 1], core, turn, heads[layer])))
+        unit_tasks.append(task(fetch_units(own_units[layer - 1], core, *units[layer])))
     saved = []
     for layer in range(LAYERS):
         vectors, head_bias, unit_bias = small[layer]
@@ -1864,31 +1864,30 @@
             got_far = swap(far_other, CORE)
         pieces = heads[layer]
         made = advance(far_mine, unit_tasks[layer])
-        if first:
-            made += advance(far_mine, unit_tasks[1])
-            made += [far_piece for far_piece in (head_piece,)]
         blocks = after_all((near_mine, far_mine, got_near, got_far), *made)
+        if last:
+            cotangent_far = redeal(after(cotangent, far_mine))
         far_mixed, far_send, far_exact, far_log = attend(blocks, 1, slopes, starts, me)
         far_got = swap(far_send, CORE)
         far_part = mix_far(far_mixed, far_got, pieces)
         far_term = swap(far_part, Z0)
         made = advance(far_part, unit_tasks[layer])
+        if last:
+            grad, unused, flip_grad = enter(own_keep, cotangent, after(cotangent_far, far_part), vectors)
+            grad_other = swap(flip_grad, CORE)
+            made.append(grad)
         near_blocks = after_all(blocks, far_part, *made)
         near_mixed, near_send, near_exact, near_log = attend(near_blocks, 0, slopes, starts, me)
         near_got = swap(near_send, CORE)
         made = advance(near_mixed, unit_tasks[layer])
         if first:
-            made += advance(near_mixed, unit_tasks[1])
-        if last:
-            cotangent_far = redeal(after(cotangent, near_mixed))
+            advance(near_mixed, unit_tasks[1], head_tasks[1])
         mid, normed_two, flip_two = mix_near(near_mixed, near_got, after(far_term, near_mixed, *made), resid, vectors, pieces)
         normed_other = swap(flip_two, CORE)
-        if last:
-            grad, unused, flip_grad = enter(own_keep, cotangent, after(cotangent_far, mid), vectors)
-            grad_other = swap(flip_grad, CORE)
-            normed_two = after(normed_two, grad)
         if first:
-            advance(mid, unit_tasks[1], head_tasks[1])
+            made = advance(mid, unit_tasks[0])
+            made += advance(mid, unit_tasks[1], head_tasks[1])
+            normed_two = after(normed_two, *made)
         hidden, active, near_out, away_out = mlp_forward(turn, normed_two, normed_other, unit_bias, units[layer])
         got_out = swap(away_out, CORE)
         if not last:
@@ -1918,8 +1917,7 @@
         grad_far = swap(grad_low, Z0)
         first = layer == 0
         reduce_parts = unit_grads("x", grad, grad_other, after(active, grad_low))
-        made = advance(reduce_parts[0], *pending)
-        near_mine, near_other = unmix(after(grad_low, reduce_parts[0], *made), pieces)
+        near_mine, near_other = unmix(after(grad_low, reduce_parts[0]), pieces)
         got_near = swap(near_other, CORE)
         expand_parts = unit_grads("y", normed_two, normed_other, after(grad_hidden, near_mine))
         unit_task = task(reduce_units(reduce_parts, expand_parts, None if first else core, unit_grad[layer]))
@@ -1935,7 +1933,8 @@
         grads_mixed = after_all(grads_mixed, mine_0, *made)
         mine_1, away_1 = attend_pull(1, blocks, grads_mixed, exacts, logs, slopes, starts, me)
         other_1 = swap(away_1, CORE)
-        other_1 = after(other_1, *advance(mine_1, unit_task))
+        made = advance(mine_1, unit_task, *pending)
+        other_1 = after(other_1, *made, *([layer_output] if layer == LAYERS - 1 else []))
         mine, other = (mine_0, mine_1), (other_0, other_1)
         far_part = unproject_far(mine, other, pieces)
         far_term = swap(far_part, Z0)

time: 834 us -> 784 us (0.940)
  Pallas kernels: 465 us -> 426 us
  starting transfers between devices: 60.8 us -> 90.7 us
  waiting for transfers between devices: 160 us -> 134 us
  local copies, waits for them, and re-layouts: 96.2 us -> 87.3 us
    ppermute x3, waiting for transfers between devices: 34.9 us -> 0.01 us  [swap_some(): lax.ppermute(values, AXES, [pair for pair in pairs if pair[0] != pair[1]])]
    ppermute x59 -> x61, starting transfers between devices: 53.3 us -> 84 us  [swap(): return lax.ppermute(values, AXES, [(i, i ^ mask) for i in range(32)])]
    pallas_call x1, Pallas kernels: 107 us -> 85.8 us  [start(): pl.pallas_call(functools.partial(start_kernel, layers), in_specs=[vmem] *...]
    pallas_call x4, Pallas kernels: 86.1 us -> 76.2 us  [attend_pull(): pl.pallas_call(functools.partial(pull_kernel, block, pair), grid=(4,), in...]
    ppermute x59 -> x61, waiting for transfers between devices: 125 us -> 134 us  [swap(): return lax.ppermute(values, AXES, [(i, i ^ mask) for i in range(32)])]
    unnamed x321 -> x274, local copies, waits for them, and re-layouts: 73.7 us -> 68.6 us
  transfers between devices with their start and end apart: 65 -> 67, of which waited for: 25 -> 25; matrix products, arithmetic and copies ran while one was open for 5% -> 5% of each run, Pallas kernels for 31% -> 31%
where the time goes in v6:
time: 784 us; the launch traced here: 771 us
  Pallas kernels  426 us (54%)
  waiting for transfers between devices  134 us (17%)
  starting transfers between devices  90.7 us (12%)
  local copies, waits for them, and re-layouts  87.3 us (11%)
  other arithmetic  31.1 us (4%)
    ppermute x61, waiting for transfers between devices, swap(): return lax.ppermute(values, AXES, [(i, i ^ mask) for i in range(32)])  134 us
    pallas_call x1, Pallas kernels, start(): pl.pallas_call(functools.partial(start_kernel, layers), in_specs=[vmem] *...  85.8 us
    ppermute x61, starting transfers between devices, swap(): return lax.ppermute(values, AXES, [(i, i ^ mask) for i in range(32)])  84 us
    pallas_call x4, Pallas kernels, attend_pull(): pl.pallas_call(functools.partial(pull_kernel, block, pair), grid=(4,), in...  76.2 us
    unnamed x274, local copies, waits for them, and re-layouts  68.6 us
    pallas_call x1, Pallas kernels, finish(): pl.pallas_call(functools.partial(finish_kernel, layers), in_specs=[vmem]...  64 us
    pallas_call x4, Pallas kernels, attend(): pl.pallas_call(functools.partial(attend_kernel, block, rest_bit), grid=(p...  61.7 us
    pallas_call x20, Pallas kernels, call_once(): pl.pallas_call(kernel, in_specs=placed(args), out_specs=placed(outs), out...  46.6 us
  transfers between devices with their start and end apart: 67, of which 25 were waited for; matrix products, arithmetic and copies ran while one was open for 5% of the time, Pallas kernels for 31%

profile of v6, /device:TPU:0, one launch (start us, length us, event | category | flops | bytes accessed | tf_op | source)
XLA Modules:
  0.0 771.1 jit_solution(1401072262210958873)
XLA Ops:
  11.2 85.8 %start.1 = (f32[512,1024]{1,0:T(8,128)S(1)}, bf16[512,1024]{1,0:T(8,128)(2,1)S(1)}, bf16[512,1024]{1,0:T(8,128)(2,1)S(1)}, bf16[4,2,128,1024]{3,2,1,0:T(8,128)(2...) custom-call(bf16[512,1024]{1,0:T(8,128)(2,1)S(1)} %copy-done.5, ...), custom_call_target="tpu_custom_call" | custom-call | flops 30000001024 | bytes 1 | tf_op jit(solution)/shard_map/start/pallas_call | solution.py:1467
  115.1 17.7 %attend.4 = (bf16[512,256]{1,0:T(8,128)(2,1)S(1)}, bf16[512,256]{1,0:T(8,128)(2,1)S(1)}, f32[256,1024]{1,0:T(8,128)S(1)}, f32[2,8,1024]{2,1,0:T(8,128)S(1)}) custom-call(f32[4]{0:T(128)S(1)} %multiply_exponential_fusion.slope_ref, s32[2]{0:T(128)S(1)} %fusion.9.start_ref, s32[1]{0:T(128)} %bitcast.3.me_ref, bf16[512,768]{1,0:T(8,128)(2,1)S(1)} %copy-done.111, ...), custom_call_target="tpu_custom_call" | custom-call | flops 8499999744 | bytes 1 | tf_op jit(solution)/shard_map/attend/pallas_call | solution.py:614
  132.8 22.8 %collective-permute-start.1 = (bf16[512,256]{1,0:T(8,128)(2,1)S(1)}, bf16[512,256]{1,0:T(8,128)(2,1)S(1)}, u32[]{:S(2)}, u32[]{:S(2)}) collective-permute-start(bf16[512,256]{1,0:T(8,128)(2,1)S(1)} %get-tuple-element.221), channel_id=1, source_target_pairs={{0,4},{1,5},{2,6},{3,7},{4,0},{5,1},{6,2},{7,3},{8,12},{9,13},{10,... | collective-permute-start | bytes 786440 | tf_op jit(solution)/shard_map/ppermute | solution.py:426
  160.3 13.1 %attend.5 = (bf16[512,256]{1,0:T(8,128)(2,1)S(1)}, bf16[512,256]{1,0:T(8,128)(2,1)S(1)}, f32[256,1024]{1,0:T(8,128)S(1)}, f32[2,8,1024]{2,1,0:T(8,128)S(1)}) custom-call(f32[4]{0:T(128)S(1)} %multiply_exponential_fusion.slope_ref, s32[2]{0:T(128)S(1)} %fusion.9.start_ref, s32[1]{0:T(128)} %bitcast.3.me_ref, bf16[512,768]{1,0:T(8,128)(2,1)S(1)} %copy-done.111, ...), custom_call_target="tpu_custom_call" | custom-call | flops 8499999744 | bytes 1 | tf_op jit(solution)/shard_map/attend/pallas_call | solution.py:614
  175.5 3.5 collective-permute-start.5
  179.0 4.9 collective-permute-done.7.rest_5_
  194.1 14.5 %collective-permute-done.12 = bf16[128,1024]{1,0:T(8,128)(2,1)} collective-permute-done((bf16[128,1024]{1,0:T(8,128)(2,1)S(1)}, bf16[128,1024]{1,0:T(8,128)(2,1)}, u32[]{:S(2)}, u32[]{:S(2)}) %collective-permute-start.12) | collective-permute-done | bytes 262176 | tf_op jit(solution)/shard_map/ppermute | solution.py:426
  210.8 3.4 collective-permute-done.9.rest_3_
  214.3 15.4 %mlp_forward.2 = (bf16[1024,2048]{1,0:T(8,128)(2,1)S(1)}, bf16[1024,2048]{1,0:T(8,128)(2,1)S(1)}, f32[512,1024]{1,0:T(8,128)S(1)}, bf16[512,1024]{1,0:T(8,128)(2,1)}) custom-call(s32[1]{0:T(128)} %constant.8.clone.1.rest_2_.turn_ref.rest_6_.rest_10_, bf16[512,1024]{1,0:T(8,128)(2,1)S(1)} %copy-done.76, bf16[512,1024]{1,0:T(8,128)(2,1)} %collective-permute-done.13.other_ref, ...), custom_call_target="tpu_custom_call" | custom-call | flops 8999999488 | bytes 1 | tf_op jit(solution)/shard_map/mlp_forward/pallas_call | solution.py:1047
  235.0 5.1 collective-permute-start.14
  242.3 12.1 %collective-permute-done.15 = bf16[2,128,1024]{2,1,0:T(8,128)(2,1)S(1)} collective-permute-done((bf16[2,128,1024]{2,1,0:T(8,128)(2,1)S(1)}, bf16[2,128,1024]{2,1,0:T(8,128)(2,1)S(1)}, u32[]{:S(2)}, u32[]{:S(2)}) %collective-permute-start.15) | collective-permute-done | bytes 524320 | tf_op jit(solution)/shard_map/ppermute | solution.py:426
  262.1 6.9 collective-permute-done.18
  276.5 19.6 %collective-permute-done.20.rows_ref.far_ref = bf16[512,1024]{1,0:T(8,128)(2,1)S(1)} collective-permute-done((bf16[512,1024]{1,0:T(8,128)(2,1)S(1)}, bf16[512,1024]{1,0:T(8,128)(2,1)S(1)}, u32[]{:S(2)}, u32[]{:S(2)}) %collective-permute-start.20) | collective-permute-done | bytes 1048608 | tf_op jit(solution)/shard_map/ppermute | solution.py:426
  301.5 17.8 %attend.6 = (bf16[512,256]{1,0:T(8,128)(2,1)S(1)}, bf16[512,256]{1,0:T(8,128)(2,1)S(1)}, f32[256,1024]{1,0:T(8,128)S(1)}, f32[2,8,1024]{2,1,0:T(8,128)S(1)}) custom-call(f32[4]{0:T(128)S(1)} %multiply_exponential_fusion.slope_ref, s32[2]{0:T(128)S(1)} %fusion.9.start_ref, s32[1]{0:T(128)} %bitcast.3.me_ref, ...), custom_call_target="tpu_custom_call" | custom-call | flops 8499999744 | bytes 1 | tf_op jit(solution)/shard_map/attend/pallas_call | solution.py:614
  319.2 4.4 collective-permute-start.25
  330.4 13.1 %attend.7 = (bf16[512,256]{1,0:T(8,128)(2,1)S(1)}, bf16[512,256]{1,0:T(8,128)(2,1)S(1)}, f32[256,1024]{1,0:T(8,128)S(1)}, f32[2,8,1024]{2,1,0:T(8,128)S(1)}) custom-call(f32[4]{0:T(128)S(1)} %multiply_exponential_fusion.slope_ref, s32[2]{0:T(128)S(1)} %fusion.9.start_ref, s32[1]{0:T(128)} %bitcast.3.me_ref, ...), custom_call_target="tpu_custom_call" | custom-call | flops 8499999744 | bytes 1 | tf_op jit(solution)/shard_map/attend/pallas_call | solution.py:614
  343.5 3.0 collective-permute-start.29
  346.5 7.0 collective-permute-done.31.rest_3_
  359.5 12.7 %mlp_forward.3 = (bf16[1024,2048]{1,0:T(8,128)(2,1)S(1)}, bf16[1024,2048]{1,0:T(8,128)(2,1)S(1)}, f32[512,1024]{1,0:T(8,128)S(1)}, bf16[512,1024]{1,0:T(8,128)(2,1)S(1)}) custom-call(s32[1]{0:T(128)} %constant.8.clone.1.rest_2_.turn_ref.rest_6_.rest_10_, bf16[512,1024]{1,0:T(8,128)(2,1)S(1)} %get-tuple-element.293.normed_ref.left_ref, ...), custom_call_target="tpu_custom_call" | custom-call | flops 8999999488 | bytes 1 | tf_op jit(solution)/shard_map/mlp_forward/pallas_call | solution.py:1047
  381.3 16.1 %mlp_backward.2 = (bf16[1024,2048]{1,0:T(8,128)(2,1)S(1)}, f32[1,2048]{1,0:T(1,128)S(1)}, f32[512,1024]{1,0:T(8,128)S(1)}, bf16[512,1024]{1,0:T(8,128)(2,1)S(1)}) custom-call(s32[1]{0:T(128)} %constant.8.clone.1.rest_2_.turn_ref.rest_6_.rest_10_, f32[512,1024]{1,0:T(8,128)S(1)} %get-tuple-element.299.grad_ref.left_ref, ...), custom_call_target="tpu_custom_call" | custom-call | flops 11000000512 | bytes 1 | tf_op jit(solution)/shard_map/mlp_backward/pallas_call | solution.py:1125
  405.9 6.5 unit_grads.4
  414.6 6.6 unit_grads.5
  421.2 8.2 %collective-permute-done.38.grad_ref.grad_far_ref = bf16[512,1024]{1,0:T(8,128)(2,1)S(1)} collective-permute-done((bf16[512,1024]{1,0:T(8,128)(2,1)S(1)}, bf16[512,1024]{1,0:T(8,128)(2,1)S(1)}, u32[]{:S(2)}, u32[]{:S(2)}) %collective-permute-start.38) | collective-permute-done | bytes 1048608 | tf_op jit(solution)/shard_map/ppermute | solution.py:426
  431.8 18.5 %attend_pull.4 = (bf16[3,1024,128]{2,1,0:T(8,128)(2,1)S(1)}, bf16[3,1024,128]{2,1,0:T(8,128)(2,1)S(1)}) custom-call(f32[4]{0:T(128)S(1)} %multiply_exponential_fusion.slope_ref, s32[2]{0:T(128)S(1)} %fusion.9.start_ref, s32[1]{0:T(128)} %bitcast.3.me_ref, bf16[512,768]{1,0:T(8,128)(2,1)S(1)} %copy-done.81, bf16[512,768]{1,0:T(8,128)(2,1)S(1)} %copy-done.81, ...), custom_call_target="tpu_custom_call" | custom-call | flops 11000000512 | bytes 1 | tf_op jit(solution)/shard_map/attend_pull/pallas_call | solution.py:747
  450.3 9.5 %collective-permute-done.41 = bf16[2,2,2,128,1024]{4,3,2,1,0:T(8,128)(2,1)S(1)} collective-permute-done((bf16[2,2,2,128,1024]{4,3,2,1,0:T(8,128)(2,1)S(1)}, bf16[2,2,2,128,1024]{4,3,2,1,0:T(8,128)(2,1)S(1)}, u32[]{:S(2)}, u32[]{:S(2)}) %collective-permute-start.41) | collective-permute-done | bytes 2097184 | tf_op jit(solution)/shard_map/ppermute | solution.py:426
  461.2 18.7 %attend_pull.5 = (bf16[3,1024,128]{2,1,0:T(8,128)(2,1)S(1)}, bf16[3,1024,128]{2,1,0:T(8,128)(2,1)S(1)}) custom-call(f32[4]{0:T(128)S(1)} %multiply_exponential_fusion.slope_ref, s32[2]{0:T(128)S(1)} %fusion.9.start_ref, s32[1]{0:T(128)} %bitcast.3.me_ref, bf16[512,768]{1,0:T(8,128)(2,1)S(1)} %copy-done.81, bf16[512,768]{1,0:T(8,128)(2,1)S(1)} %copy-done.81, ...), custom_call_target="tpu_custom_call" | custom-call | flops 11000000512 | bytes 1 | tf_op jit(solution)/shard_map/attend_pull/pallas_call | solution.py:747
  482.7 3.1 collective-permute-start.46
  490.6 4.9 head_grads.2
  498.2 3.9 copy.55
  502.1 7.4 collective-permute-done.46
  512.2 5.1 fusion.4
  519.3 4.1 unproject_near.2
  524.7 4.0 copy.54
  529.0 3.9 slice_add_fusion
  535.8 17.4 %mlp_backward.3 = (bf16[1024,2048]{1,0:T(8,128)(2,1)S(1)}, f32[1,2048]{1,0:T(1,128)S(1)}, f32[512,1024]{1,0:T(8,128)S(1)}, bf16[512,1024]{1,0:T(8,128)(2,1)S(1)}) custom-call(s32[1]{0:T(128)} %constant.8.clone.1.rest_2_.turn_ref.rest_6_.rest_10_, f32[512,1024]{1,0:T(8,128)S(1)} %copy-done.59, bf16[512,1024]{1,0:T(8,128)(2,1)S(1)} %collective-permute-done.49.other_ref, ...), custom_call_target="tpu_custom_call" | custom-call | flops 11000000512 | bytes 1 | tf_op jit(solution)/shard_map/mlp_backward/pallas_call | solution.py:1125
  569.7 6.5 unit_grads.6
  578.7 7.8 %unit_grads.7 = (bf16[2,2,128,1024]{3,2,1,0:T(8,128)(2,1)S(1)}, bf16[2,2,2,128,1024]{4,3,2,1,0:T(8,128)(2,1)S(1)}, bf16[2,2,128,1024]{3,2,1,0:T(8,128)(2,1)S(1)}) custom-call(bf16[512,1024]{1,0:T(8,128)(2,1)S(1)} %copy-done.77, bf16[512,1024]{1,0:T(8,128)(2,1)} %collective-permute-done.13.other_ref, bf16[1024,2048]{1,0:T(8,128)(2,1)S(1)} %copy-done.89), custom_call_target="tpu_custom_call" | custom-call | flops 5000000000 | bytes 1 | tf_op jit(solution)/shard_map/unit_grads/pallas_call | solution.py:1187
  587.3 5.9 collective-permute-done.53.grad_ref.grad_far_ref
  601.0 19.4 %attend_pull.6 = (bf16[3,1024,128]{2,1,0:T(8,128)(2,1)S(1)}, bf16[3,1024,128]{2,1,0:T(8,128)(2,1)}) custom-call(f32[4]{0:T(128)S(1)} %multiply_exponential_fusion.slope_ref, s32[2]{0:T(128)S(1)} %fusion.9.start_ref, s32[1]{0:T(128)} %bitcast.3.me_ref, bf16[512,768]{1,0:T(8,128)(2,1)S(1)} %copy-done.112, bf16[512,768]{1,0:T(8,128)(2,1)S(1)} %copy-done.112, ...), custom_call_target="tpu_custom_call" | custom-call | flops 11000000512 | bytes 1 | tf_op jit(solution)/shard_map/attend_pull/pallas_call | solution.py:747
  621.2 3.8 collective-permute-done.57
  626.2 19.6 %attend_pull.7 = (bf16[3,1024,128]{2,1,0:T(8,128)(2,1)S(1)}, bf16[3,1024,128]{2,1,0:T(8,128)(2,1)}) custom-call(f32[4]{0:T(128)S(1)} %multiply_exponential_fusion.slope_ref, s32[2]{0:T(128)S(1)} %fusion.9.start_ref, s32[1]{0:T(128)} %bitcast.3.me_ref, bf16[512,768]{1,0:T(8,128)(2,1)S(1)} %copy-done.112, bf16[512,768]{1,0:T(8,128)(2,1)S(1)} %copy-done.112, ...), custom_call_target="tpu_custom_call" | custom-call | flops 11000000512 | bytes 1 | tf_op jit(solution)/shard_map/attend_pull/pallas_call | solution.py:747
  645.9 3.3 collective-permute-start.65
  662.3 3.4 unproject_far.3
  666.1 6.4 head_grads.3
  673.2 3.1 collective-permute-done.66
  680.0 10.8 %collective-permute-done.64.rest_4_ = bf16[512,1024]{1,0:T(8,128)(2,1)S(1)} collective-permute-done((bf16[512,1024]{1,0:T(8,128)(2,1)S(1)}, bf16[512,1024]{1,0:T(8,128)(2,1)S(1)}, u32[]{:S(2)}, u32[]{:S(2)}) %collective-permute-start.64) | collective-permute-done | bytes 1048608 | tf_op jit(solution)/shard_map/ppermute | solution.py:426
  690.8 5.7 unproject_near.3
  696.4 64.0 %finish.1 = (bf16[512,1024]{1,0:T(8,128)(2,1)S(1)}, f32[3,128,256]{2,1,0:T(8,128)S(1)}, f32[256,128]{1,0:T(8,128)S(1)}, f32[1024,128]{1,0:T(8,128)S(1)}, f32[128,1024]{1,0:T(8,128)S(1)}, /*index=5*/f32[24,128]{1,0:T(8,128)S(1)}) custom-call(bf16[512,1024]{1,0:T(8,128)(2,1)S(1)} %get-tuple-element.403.grad_ref, ...), custom_call_target="tpu_custom_call" | custom-call | flops 24999999488 | bytes 1 | tf_op jit(solution)/shard_map/finish/pallas_call | solution.py:1664
  (449 shorter events, 189.0 us)
Async XLA Ops:
  106.6 51.0 %collective-permute-start.2 = (bf16[2,128,2048]{2,1,0:T(8,128)(2,1)S(1)}, bf16[2,128,2048]{2,1,0:T(8,128)(2,1)}, u32[]{:S(2)}, u32[]{:S(2)}) collective-permute-start(bf16[2,128,2048]{2,1,0:T(8,128)(2,1)S(1)} %get-tuple-element.225.rest_0_), channel_id=1, source_target_pairs={{0,8},{1,9},{2,10},{3,11},{4,12},{5,13},{6,14},{7,15},{8,0},{9,1},... | collective-permute-start | bytes 3145736 | tf_op jit(solution)/shard_map/ppermute | solution.py:426
  108.1 49.5 %collective-permute-start.3 = (bf16[2,128,2048]{2,1,0:T(8,128)(2,1)S(1)}, bf16[2,128,2048]{2,1,0:T(8,128)(2,1)}, u32[]{:S(2)}, u32[]{:S(2)}) collective-permute-start(bf16[2,128,2048]{2,1,0:T(8,128)(2,1)S(1)} %get-tuple-element.225.rest_0_), channel_id=1, source_target_pairs={{0,16},{1,17},{2,18},{3,19},{4,20},{5,21},{6,22},{7,23},{8,24},{9,... | collective-permute-start | bytes 3145736 | tf_op jit(solution)/shard_map/ppermute | solution.py:426
  109.6 48.0 %collective-permute-start.4 = (bf16[2,128,2048]{2,1,0:T(8,128)(2,1)S(1)}, bf16[2,128,2048]{2,1,0:T(8,128)(2,1)}, u32[]{:S(2)}, u32[]{:S(2)}) collective-permute-start(bf16[2,128,2048]{2,1,0:T(8,128)(2,1)S(1)} %get-tuple-element.225.rest_0_), channel_id=1, source_target_pairs={{0,1},{1,0},{2,3},{3,2},{4,5},{5,4},{6,7},{7,6},{8,9},{9,8},{10,11... | collective-permute-start | bytes 3145736 | tf_op jit(solution)/shard_map/ppermute | solution.py:426
  132.8 23.9 %collective-permute-start.1 = (bf16[512,256]{1,0:T(8,128)(2,1)S(1)}, bf16[512,256]{1,0:T(8,128)(2,1)S(1)}, u32[]{:S(2)}, u32[]{:S(2)}) collective-permute-start(bf16[512,256]{1,0:T(8,128)(2,1)S(1)} %get-tuple-element.221), channel_id=1, source_target_pairs={{0,4},{1,5},{2,6},{3,7},{4,0},{5,1},{6,2},{7,3},{8,12},{9,13},{10,... | collective-permute-start | bytes 786440 | tf_op jit(solution)/shard_map/ppermute | solution.py:426
  157.6 31.8 %collective-permute-start.6 = (bf16[512,1024]{1,0:T(8,128)(2,1)S(1)}, bf16[512,1024]{1,0:T(8,128)(2,1)S(1)}, u32[]{:S(2)}, u32[]{:S(2)}) collective-permute-start(bf16[512,1024]{1,0:T(8,128)(2,1)S(1)} %mix_far.2), channel_id=1, source_target_pairs={{0,1},{1,0},{2,3},{3,2},{4,5},{5,4},{6,7},{7,6},{8,9},{9,8},{10,11... | collective-permute-start | bytes 3145736 | tf_op jit(solution)/shard_map/ppermute | solution.py:426
  157.7 26.2 %collective-permute-start.7 = (bf16[2,128,2048]{2,1,0:T(8,128)(2,1)}, bf16[2,128,2048]{2,1,0:T(8,128)(2,1)S(1)}, u32[]{:S(2)}, u32[]{:S(2)}) collective-permute-start(bf16[2,128,2048]{2,1,0:T(8,128)(2,1)} %collective-permute-done.4.rest_4_), channel_id=1, source_target_pairs={{0,8},{1,9},{2,10},{3,11},{4,12},{5,13},{6,14},{7,15},{8,0},{9,1},... | collective-permute-start | bytes 3145736 | tf_op jit(solution)/shard_map/ppermute | solution.py:426
  160.2 26.5 %collective-permute-start.8 = (bf16[2,128,2048]{2,1,0:T(8,128)(2,1)}, bf16[2,128,2048]{2,1,0:T(8,128)(2,1)}, u32[]{:S(2)}, u32[]{:S(2)}) collective-permute-start(bf16[2,128,2048]{2,1,0:T(8,128)(2,1)} %collective-permute-done.4.rest_4_), channel_id=1, source_target_pairs={{0,16},{1,17},{2,18},{3,19},{4,20},{5,21},{6,22},{7,23},{8,24},{9,... | collective-permute-start | bytes 3145736 | tf_op jit(solution)/shard_map/ppermute | solution.py:426
  173.4 20.7 %collective-permute-start.11 = (bf16[2,128,2048]{2,1,0:T(8,128)(2,1)S(1)}, bf16[2,128,2048]{2,1,0:T(8,128)(2,1)}, u32[]{:S(2)}, u32[]{:S(2)}) collective-permute-start(bf16[2,128,2048]{2,1,0:T(8,128)(2,1)S(1)} %bitcast.114), channel_id=1, source_target_pairs={{4,6},{5,7},{6,4},{7,5},{12,14},{13,15},{14,12},{15,13},{20,22},{2... | collective-permute-start | bytes 3145736 | tf_op jit(solution)/shard_map/ppermute | solution.py:431
  175.5 13.8 %collective-permute-start.5 = (bf16[512,256]{1,0:T(8,128)(2,1)S(1)}, bf16[512,256]{1,0:T(8,128)(2,1)S(1)}, u32[]{:S(2)}, u32[]{:S(2)}) collective-permute-start(bf16[512,256]{1,0:T(8,128)(2,1)S(1)} %get-tuple-element.234), channel_id=1, source_target_pairs={{0,4},{1,5},{2,6},{3,7},{4,0},{5,1},{6,2},{7,3},{8,12},{9,13},{10,... | collective-permute-start | bytes 786440 | tf_op jit(solution)/shard_map/ppermute | solution.py:426
  183.9 24.7 %collective-permute-start.12 = (bf16[128,1024]{1,0:T(8,128)(2,1)S(1)}, bf16[128,1024]{1,0:T(8,128)(2,1)}, u32[]{:S(2)}, u32[]{:S(2)}) collective-permute-start(bf16[128,1024]{1,0:T(8,128)(2,1)S(1)} %bitcast.117), channel_id=1, source_target_pairs={{0,2},{1,3},{2,0},{3,1},{4,6},{5,7},{6,4},{7,5},{8,10},{9,11},{10,... | collective-permute-start | bytes 786440 | tf_op jit(solution)/shard_map/ppermute | solution.py:426
  186.7 27.5 %collective-permute-start.10 = (bf16[2,128,2048]{2,1,0:T(8,128)(2,1)}, bf16[2,128,2048]{2,1,0:T(8,128)(2,1)}, u32[]{:S(2)}, u32[]{:S(2)}) collective-permute-start(bf16[2,128,2048]{2,1,0:T(8,128)(2,1)} %collective-permute-done.8.rest_6_), channel_id=1, source_target_pairs={{0,8},{1,9},{2,10},{3,11},{4,12},{5,13},{6,14},{7,15},{8,0},{9,1},... | collective-permute-start | bytes 3145736 | tf_op jit(solution)/shard_map/ppermute | solution.py:426
  189.3 24.9 %collective-permute-start.9 = (bf16[2,128,2048]{2,1,0:T(8,128)(2,1)}, bf16[2,128,2048]{2,1,0:T(8,128)(2,1)}, u32[]{:S(2)}, u32[]{:S(2)}) collective-permute-start(bf16[2,128,2048]{2,1,0:T(8,128)(2,1)} %collective-permute-done.2.rest_1_), channel_id=1, source_target_pairs={{0,16},{1,17},{2,18},{3,19},{4,20},{5,21},{6,22},{7,23},{8,24},{9,... | collective-permute-start | bytes 3145736 | tf_op jit(solution)/shard_map/ppermute | solution.py:426
  194.1 20.2 %collective-permute-start.13 = (bf16[512,1024]{1,0:T(8,128)(2,1)}, bf16[512,1024]{1,0:T(8,128)(2,1)}, u32[]{:S(2)}, u32[]{:S(2)}) collective-permute-start(bf16[512,1024]{1,0:T(8,128)(2,1)} %get-tuple-element.252), channel_id=1, source_target_pairs={{0,4},{1,5},{2,6},{3,7},{4,0},{5,1},{6,2},{7,3},{8,12},{9,13},{10,... | collective-permute-start | bytes 3145736 | tf_op jit(solution)/shard_map/ppermute | solution.py:426
  208.7 48.3 %collective-permute-start.17 = (bf16[2,128,2048]{2,1,0:T(8,128)(2,1)S(1)}, bf16[2,128,2048]{2,1,0:T(8,128)(2,1)S(1)}, u32[]{:S(2)}, u32[]{:S(2)}) collective-permute-start(bf16[2,128,2048]{2,1,0:T(8,128)(2,1)S(1)} %broadcast_select_fusion.rest_0_), channel_id=1, source_target_pairs={{0,1},{1,0},{2,3},{3,2},{4,5},{5,4},{6,7},{7,6},{8,9},{9,8},{10,11... | collective-permute-start | bytes 3145736 | tf_op jit(solution)/shard_map/ppermute | solution.py:426
  235.0 22.1 %collective-permute-start.14 = (bf16[512,1024]{1,0:T(8,128)(2,1)}, bf16[512,1024]{1,0:T(8,128)(2,1)S(1)}, u32[]{:S(2)}, u32[]{:S(2)}) collective-permute-start(bf16[512,1024]{1,0:T(8,128)(2,1)} %get-tuple-element.255), channel_id=1, source_target_pairs={{0,4},{1,5},{2,6},{3,7},{4,0},{5,1},{6,2},{7,3},{8,12},{9,13},{10,... | collective-permute-start | bytes 3145736 | tf_op jit(solution)/shard_map/ppermute | solution.py:426
  240.0 14.4 %collective-permute-start.15 = (bf16[2,128,1024]{2,1,0:T(8,128)(2,1)S(1)}, bf16[2,128,1024]{2,1,0:T(8,128)(2,1)S(1)}, u32[]{:S(2)}, u32[]{:S(2)}) collective-permute-start(bf16[2,128,1024]{2,1,0:T(8,128)(2,1)S(1)} %get-tuple-element.463), channel_id=1, source_target_pairs={{0,8},{1,9},{2,10},{3,11},{4,12},{5,13},{6,14},{7,15},{8,0},{9,1},... | collective-permute-start | bytes 1572872 | tf_op jit(solution)/shard_map/ppermute | solution.py:426
  270.5 25.6 %collective-permute-start.20 = (bf16[512,1024]{1,0:T(8,128)(2,1)S(1)}, bf16[512,1024]{1,0:T(8,128)(2,1)S(1)}, u32[]{:S(2)}, u32[]{:S(2)}) collective-permute-start(bf16[512,1024]{1,0:T(8,128)(2,1)S(1)} %get-tuple-element.260.rows_ref.near_ref), channel_id=1, source_target_pairs={{0,1},{1,0},{2,3},{3,2},{4,5},{5,4},{6,7},{7,6},{8,9},{9,8},{10,11... | collective-permute-start | bytes 3145736 | tf_op jit(solution)/shard_map/ppermute | solution.py:426
  271.8 28.1 %collective-permute-start.23 = (bf16[2,128,2048]{2,1,0:T(8,128)(2,1)S(1)}, bf16[2,128,2048]{2,1,0:T(8,128)(2,1)S(1)}, u32[]{:S(2)}, u32[]{:S(2)}) collective-permute-start(bf16[2,128,2048]{2,1,0:T(8,128)(2,1)S(1)} %broadcast_select_fusion.rest_0_), channel_id=1, source_target_pairs={{0,8},{1,9},{2,10},{3,11},{4,12},{5,13},{6,14},{7,15},{8,0},{9,1},... | collective-permute-start | bytes 3145736 | tf_op jit(solution)/shard_map/ppermute | solution.py:426
  273.2 27.4 %collective-permute-start.24 = (bf16[2,128,2048]{2,1,0:T(8,128)(2,1)S(1)}, bf16[2,128,2048]{2,1,0:T(8,128)(2,1)S(1)}, u32[]{:S(2)}, u32[]{:S(2)}) collective-permute-start(bf16[2,128,2048]{2,1,0:T(8,128)(2,1)S(1)} %broadcast_select_fusion.rest_0_), channel_id=1, source_target_pairs={{0,16},{1,17},{2,18},{3,19},{4,20},{5,21},{6,22},{7,23},{8,24},{9,... | collective-permute-start | bytes 3145736 | tf_op jit(solution)/shard_map/ppermute | solution.py:426
  298.5 27.2 %collective-permute-start.26 = (bf16[2,128,2048]{2,1,0:T(8,128)(2,1)S(1)}, bf16[2,128,2048]{2,1,0:T(8,128)(2,1)S(1)}, u32[]{:S(2)}, u32[]{:S(2)}) collective-permute-start(bf16[2,128,2048]{2,1,0:T(8,128)(2,1)S(1)} %copy-done.14), channel_id=1, source_target_pairs={{0,8},{1,9},{2,10},{3,11},{4,12},{5,13},{6,14},{7,15},{8,0},{9,1},... | collective-permute-start | bytes 3145736 | tf_op jit(solution)/shard_map/ppermute | solution.py:426
  299.9 25.8 %collective-permute-start.27 = (bf16[2,128,2048]{2,1,0:T(8,128)(2,1)S(1)}, bf16[2,128,2048]{2,1,0:T(8,128)(2,1)S(1)}, u32[]{:S(2)}, u32[]{:S(2)}) collective-permute-start(bf16[2,128,2048]{2,1,0:T(8,128)(2,1)S(1)} %copy-done.14), channel_id=1, source_target_pairs={{0,16},{1,17},{2,18},{3,19},{4,20},{5,21},{6,22},{7,23},{8,24},{9,... | collective-permute-start | bytes 3145736 | tf_op jit(solution)/shard_map/ppermute | solution.py:426
  300.5 25.2 %collective-permute-start.28 = (bf16[512,1024]{1,0:T(8,128)(2,1)S(1)}, bf16[512,1024]{1,0:T(8,128)(2,1)S(1)}, u32[]{:S(2)}, u32[]{:S(2)}) collective-permute-start(bf16[512,1024]{1,0:T(8,128)(2,1)S(1)} %copy-done.6), channel_id=1, source_target_pairs={{2,4},{3,5},{4,2},{5,3},{10,12},{11,13},{12,10},{13,11},{18,20},{1... | collective-permute-start | bytes 3145736 | tf_op jit(solution)/shard_map/ppermute | solution.py:439
  325.6 27.9 %collective-permute-start.30 = (bf16[512,1024]{1,0:T(8,128)(2,1)S(1)}, bf16[512,1024]{1,0:T(8,128)(2,1)S(1)}, u32[]{:S(2)}, u32[]{:S(2)}) collective-permute-start(bf16[512,1024]{1,0:T(8,128)(2,1)S(1)} %mix_far.3), channel_id=1, source_target_pairs={{0,1},{1,0},{2,3},{3,2},{4,5},{5,4},{6,7},{7,6},{8,9},{9,8},{10,11... | collective-permute-start | bytes 3145736 | tf_op jit(solution)/shard_map/ppermute | solution.py:426
  325.7 27.8 %collective-permute-start.32 = (bf16[2,128,2048]{2,1,0:T(8,128)(2,1)S(1)}, bf16[2,128,2048]{2,1,0:T(8,128)(2,1)S(1)}, u32[]{:S(2)}, u32[]{:S(2)}) collective-permute-start(bf16[2,128,2048]{2,1,0:T(8,128)(2,1)S(1)} %collective-permute-done.27.rest_6_), channel_id=1, source_target_pairs={{0,8},{1,9},{2,10},{3,11},{4,12},{5,13},{6,14},{7,15},{8,0},{9,1},... | collective-permute-start | bytes 3145736 | tf_op jit(solution)/shard_map/ppermute | solution.py:426
  329.8 23.7 %collective-permute-start.31 = (bf16[2,128,2048]{2,1,0:T(8,128)(2,1)S(1)}, bf16[2,128,2048]{2,1,0:T(8,128)(2,1)S(1)}, u32[]{:S(2)}, u32[]{:S(2)}) collective-permute-start(bf16[2,128,2048]{2,1,0:T(8,128)(2,1)S(1)} %collective-permute-done.23.rest_1_), channel_id=1, source_target_pairs={{0,16},{1,17},{2,18},{3,19},{4,20},{5,21},{6,22},{7,23},{8,24},{9,... | collective-permute-start | bytes 3145736 | tf_op jit(solution)/shard_map/ppermute | solution.py:426
  403.3 26.0 %collective-permute-start.38 = (bf16[512,1024]{1,0:T(8,128)(2,1)S(1)}, bf16[512,1024]{1,0:T(8,128)(2,1)S(1)}, u32[]{:S(2)}, u32[]{:S(2)}) collective-permute-start(bf16[512,1024]{1,0:T(8,128)(2,1)S(1)} %get-tuple-element.308.grad_ref.grad_near_ref), channel_id=1, source_target_pairs={{0,1},{1,0},{2,3},{3,2},{4,5},{5,4},{6,7},{7,6},{8,9},{9,8},{10,11... | collective-permute-start | bytes 3145736 | tf_op jit(solution)/shard_map/ppermute | solution.py:426
  412.4 47.4 %collective-permute-start.41 = (bf16[2,2,2,128,1024]{4,3,2,1,0:T(8,128)(2,1)S(1)}, bf16[2,2,2,128,1024]{4,3,2,1,0:T(8,128)(2,1)S(1)}, u32[]{:S(2)}, u32[]{:S(2)}) collective-permute-start(bf16[2,2,2,128,1024]{4,3,2,1,0:T(8,128)(2,1)S(1)} %get-tuple-element.323), channel_id=1, source_target_pairs={{0,16},{1,17},{2,18},{3,19},{4,20},{5,21},{6,22},{7,23},{8,24},{9,... | collective-permute-start | bytes 6291464 | tf_op jit(solution)/shard_map/ppermute | solution.py:426
  413.8 17.9 %collective-permute-start.39 = (bf16[512,256]{1,0:T(8,128)(2,1)S(1)}, bf16[512,256]{1,0:T(8,128)(2,1)S(1)}, u32[]{:S(2)}, u32[]{:S(2)}) collective-permute-start(bf16[512,256]{1,0:T(8,128)(2,1)S(1)} %get-tuple-element.315), channel_id=1, source_target_pairs={{0,4},{1,5},{2,6},{3,7},{4,0},{5,1},{6,2},{7,3},{8,12},{9,13},{10,... | collective-permute-start | bytes 786440 | tf_op jit(solution)/shard_map/ppermute | solution.py:426
  430.2 50.4 %collective-permute-start.35 = (bf16[512,1024]{1,0:T(8,128)(2,1)S(1)}, bf16[512,1024]{1,0:T(8,128)(2,1)S(1)}, u32[]{:S(2)}, u32[]{:S(2)}) collective-permute-start(bf16[512,1024]{1,0:T(8,128)(2,1)S(1)} %get-tuple-element.298), channel_id=1, source_target_pairs={{2,4},{3,5},{4,2},{5,3},{10,12},{11,13},{12,10},{13,11},{18,20},{1... | collective-permute-start | bytes 3145736 | tf_op jit(solution)/shard_map/ppermute | solution.py:439
  431.1 51.6 %collective-permute-start.44 = (bf16[2,2,2,128,1024]{4,3,2,1,0:T(8,128)(2,1)S(1)}, bf16[2,2,2,128,1024]{4,3,2,1,0:T(8,128)(2,1)S(1)}, u32[]{:S(2)}, u32[]{:S(2)}) collective-permute-start(bf16[2,2,2,128,1024]{4,3,2,1,0:T(8,128)(2,1)S(1)} %get-tuple-element.333), channel_id=1, source_target_pairs={{0,8},{1,9},{2,10},{3,11},{4,12},{5,13},{6,14},{7,15},{8,0},{9,1},... | collective-permute-start | bytes 6291464 | tf_op jit(solution)/shard_map/ppermute | solution.py:426
  482.7 26.8 %collective-permute-start.46 = (bf16[2,2,128,1024]{3,2,0,1:T(8,128)(2,1)}, bf16[2,2,128,1024]{3,2,0,1:T(8,128)(2,1)}, u32[]{:S(2)}, u32[]{:S(2)}) collective-permute-start(bf16[2,2,128,1024]{3,2,0,1:T(8,128)(2,1)} %copy.48), channel_id=1, source_target_pairs={{0,8},{1,9},{2,10},{3,11},{4,12},{5,13},{6,14},{7,15},{8,0},{9,1},... | collective-permute-start | bytes 3145736 | tf_op jit(solution)/shard_map/ppermute | solution.py:426
  487.0 25.2 %collective-permute-start.47 = (bf16[2,2,128,1024]{3,2,0,1:T(8,128)(2,1)}, bf16[2,2,128,1024]{3,2,0,1:T(8,128)(2,1)}, u32[]{:S(2)}, u32[]{:S(2)}) collective-permute-start(bf16[2,2,128,1024]{3,2,0,1:T(8,128)(2,1)} %copy.49), channel_id=1, source_target_pairs={{0,16},{1,17},{2,18},{3,19},{4,20},{5,21},{6,22},{7,23},{8,24},{9,... | collective-permute-start | bytes 3145736 | tf_op jit(solution)/shard_map/ppermute | solution.py:426
  490.3 28.1 %collective-permute-start.45 = (bf16[512,1024]{1,0:T(8,128)(2,1)}, bf16[512,1024]{1,0:T(8,128)(2,1)}, u32[]{:S(2)}, u32[]{:S(2)}) collective-permute-start(bf16[512,1024]{1,0:T(8,128)(2,1)} %unproject_far.2), channel_id=1, source_target_pairs={{0,1},{1,0},{2,3},{3,2},{4,5},{5,4},{6,7},{7,6},{8,9},{9,8},{10,11... | collective-permute-start | bytes 3145736 | tf_op jit(solution)/shard_map/ppermute | solution.py:426
  502.1 26.9 %collective-permute-start.48 = (bf16[4,2,128,1024]{2,3,1,0:T(8,128)(2,1)}, bf16[4,2,128,1024]{2,3,1,0:T(8,128)(2,1)}, u32[]{:S(2)}, u32[]{:S(2)}) collective-permute-start(bf16[4,2,128,1024]{2,3,1,0:T(8,128)(2,1)} %copy.55), channel_id=1, source_target_pairs={{0,4},{1,5},{2,6},{3,7},{4,0},{5,1},{6,2},{7,3},{8,12},{9,13},{10,... | collective-permute-start | bytes 6291464 | tf_op jit(solution)/shard_map/ppermute | solution.py:426
  528.7 27.9 %collective-permute-start.51 = (bf16[2,2,128,1024]{3,2,0,1:T(8,128)(2,1)}, bf16[2,2,128,1024]{3,2,0,1:T(8,128)(2,1)}, u32[]{:S(2)}, u32[]{:S(2)}) collective-permute-start(bf16[2,2,128,1024]{3,2,0,1:T(8,128)(2,1)} %pad_maximum_fusion.2), channel_id=1, source_target_pairs={{0,1},{1,0},{2,3},{3,2},{4,5},{5,4},{6,7},{7,6},{8,9},{9,8},{10,11... | collective-permute-start | bytes 3145736 | tf_op jit(solution)/shard_map/ppermute | solution.py:426
  532.9 25.6 %collective-permute-start.52 = (bf16[2,2,128,1024]{2,3,1,0:T(8,128)(2,1)}, bf16[2,2,128,1024]{2,3,1,0:T(8,128)(2,1)}, u32[]{:S(2)}, u32[]{:S(2)}) collective-permute-start(bf16[2,2,128,1024]{2,3,1,0:T(8,128)(2,1)} %get-tuple-element.450), channel_id=1, source_target_pairs={{0,16},{1,17},{2,18},{3,19},{4,20},{5,21},{6,22},{7,23},{8,24},{9,... | collective-permute-start | bytes 3145736 | tf_op jit(solution)/shard_map/ppermute | solution.py:426
  559.7 34.5 %collective-permute-start.56 = (bf16[2,128,1024]{1,2,0:T(8,128)(2,1)S(1)}, bf16[2,128,1024]{1,2,0:T(8,128)(2,1)S(1)}, u32[]{:S(2)}, u32[]{:S(2)}) collective-permute-start(bf16[2,128,1024]{1,2,0:T(8,128)(2,1)S(1)} %fusion.2), channel_id=1, source_target_pairs={{0,8},{1,9},{2,10},{3,11},{4,12},{5,13},{6,14},{7,15},{8,0},{9,1},... | collective-permute-start | bytes 1572872 | tf_op jit(solution)/shard_map/ppermute | solution.py:426
  567.9 25.3 %collective-permute-start.53 = (bf16[512,1024]{1,0:T(8,128)(2,1)S(1)}, bf16[512,1024]{1,0:T(8,128)(2,1)S(1)}, u32[]{:S(2)}, u32[]{:S(2)}) collective-permute-start(bf16[512,1024]{1,0:T(8,128)(2,1)S(1)} %get-tuple-element.358.grad_ref.grad_near_ref), channel_id=1, source_target_pairs={{0,1},{1,0},{2,3},{3,2},{4,5},{5,4},{6,7},{7,6},{8,9},{9,8},{10,11... | collective-permute-start | bytes 3145736 | tf_op jit(solution)/shard_map/ppermute | solution.py:426
  576.9 20.2 %collective-permute-start.54 = (bf16[512,256]{1,0:T(8,128)(2,1)S(1)}, bf16[512,256]{1,0:T(8,128)(2,1)S(1)}, u32[]{:S(2)}, u32[]{:S(2)}) collective-permute-start(bf16[512,256]{1,0:T(8,128)(2,1)S(1)} %get-tuple-element.365), channel_id=1, source_target_pairs={{0,4},{1,5},{2,6},{3,7},{4,0},{5,1},{6,2},{7,3},{8,12},{9,13},{10,... | collective-permute-start | bytes 786440 | tf_op jit(solution)/shard_map/ppermute | solution.py:426
  577.0 48.0 %collective-permute-start.57 = (bf16[2,2,2,128,1024]{4,3,2,1,0:T(8,128)(2,1)S(1)}, bf16[2,2,2,128,1024]{4,3,2,1,0:T(8,128)(2,1)S(1)}, u32[]{:S(2)}, u32[]{:S(2)}) collective-permute-start(bf16[2,2,2,128,1024]{4,3,2,1,0:T(8,128)(2,1)S(1)} %get-tuple-element.379), channel_id=1, source_target_pairs={{0,16},{1,17},{2,18},{3,19},{4,20},{5,21},{6,22},{7,23},{8,24},{9,... | collective-permute-start | bytes 6291464 | tf_op jit(solution)/shard_map/ppermute | solution.py:426
  586.5 59.4 %collective-permute-start.60 = (bf16[2,2,2,128,1024]{4,3,2,1,0:T(8,128)(2,1)S(1)}, bf16[2,2,2,128,1024]{4,3,2,1,0:T(8,128)(2,1)S(1)}, u32[]{:S(2)}, u32[]{:S(2)}) collective-permute-start(bf16[2,2,2,128,1024]{4,3,2,1,0:T(8,128)(2,1)S(1)} %get-tuple-element.389), channel_id=1, source_target_pairs={{0,8},{1,9},{2,10},{3,11},{4,12},{5,13},{6,14},{7,15},{8,0},{9,1},... | collective-permute-start | bytes 6291464 | tf_op jit(solution)/shard_map/ppermute | solution.py:426
  596.2 54.3 %collective-permute-start.61 = (bf16[2,128,1024]{2,1,0:T(8,128)(2,1)S(1)}, bf16[2,128,1024]{2,1,0:T(8,128)(2,1)S(1)}, u32[]{:S(2)}, u32[]{:S(2)}) collective-permute-start(bf16[2,128,1024]{2,1,0:T(8,128)(2,1)S(1)} %get-tuple-element.459), channel_id=1, source_target_pairs={{4,6},{5,7},{6,4},{7,5},{12,14},{13,15},{14,12},{15,13},{20,22},{2... | collective-permute-start | bytes 1572872 | tf_op jit(solution)/shard_map/ppermute | solution.py:431
  597.1 54.1 %collective-permute-start.62 = (bf16[2,128,1024]{2,1,0:T(8,128)(2,1)S(1)}, bf16[2,128,1024]{2,1,0:T(8,128)(2,1)S(1)}, u32[]{:S(2)}, u32[]{:S(2)}) collective-permute-start(bf16[2,128,1024]{2,1,0:T(8,128)(2,1)S(1)} %get-tuple-element.458), channel_id=1, source_target_pairs={{0,4},{1,5},{2,6},{3,7},{4,2},{5,3},{6,0},{7,1},{8,12},{9,13},{10,... | collective-permute-start | bytes 1572872 | tf_op jit(solution)/shard_map/ppermute | solution.py:431
  598.3 50.9 %collective-permute-start.63 = (bf16[128,1024]{0,1:T(8,128)(2,1)S(1)}, bf16[128,1024]{0,1:T(8,128)(2,1)S(1)}, u32[]{:S(2)}, u32[]{:S(2)}) collective-permute-start(bf16[128,1024]{0,1:T(8,128)(2,1)S(1)} %get-tuple-element.460), channel_id=1, source_target_pairs={{0,2},{1,3},{2,0},{3,1},{4,6},{5,7},{6,4},{7,5},{8,10},{9,11},{10,... | collective-permute-start | bytes 786440 | tf_op jit(solution)/shard_map/ppermute | solution.py:426
  625.0 33.2 %collective-permute-start.58 = (bf16[3,1024,128]{2,1,0:T(8,128)(2,1)}, bf16[3,1024,128]{2,1,0:T(8,128)(2,1)}, u32[]{:S(2)}, u32[]{:S(2)}) collective-permute-start(bf16[3,1024,128]{2,1,0:T(8,128)(2,1)} %get-tuple-element.386), channel_id=1, source_target_pairs={{0,4},{1,5},{2,6},{3,7},{4,0},{5,1},{6,2},{7,3},{8,12},{9,13},{10,... | collective-permute-start | bytes 2359304 | tf_op jit(solution)/shard_map/ppermute | solution.py:426
  645.9 27.4 %collective-permute-start.65 = (bf16[2,2,128,1024]{3,2,1,0:T(8,128)(2,1)}, bf16[2,2,128,1024]{3,2,1,0:T(8,128)(2,1)}, u32[]{:S(2)}, u32[]{:S(2)}) collective-permute-start(bf16[2,2,128,1024]{3,2,1,0:T(8,128)(2,1)} %bitcast_add_fusion.1), channel_id=1, source_target_pairs={{0,8},{1,9},{2,10},{3,11},{4,12},{5,13},{6,14},{7,15},{8,0},{9,1},... | collective-permute-start | bytes 3145736 | tf_op jit(solution)/shard_map/ppermute | solution.py:426
  650.5 25.8 %collective-permute-start.66 = (bf16[2,2,128,1024]{3,2,1,0:T(8,128)(2,1)}, bf16[2,2,128,1024]{3,2,1,0:T(8,128)(2,1)}, u32[]{:S(2)}, u32[]{:S(2)}) collective-permute-start(bf16[2,2,128,1024]{3,2,1,0:T(8,128)(2,1)} %bitcast_add_fusion), channel_id=1, source_target_pairs={{0,16},{1,17},{2,18},{3,19},{4,20},{5,21},{6,22},{7,23},{8,24},{9,... | collective-permute-start | bytes 3145736 | tf_op jit(solution)/shard_map/ppermute | solution.py:426
  665.7 25.1 %collective-permute-start.64 = (bf16[512,1024]{1,0:T(8,128)(2,1)S(1)}, bf16[512,1024]{1,0:T(8,128)(2,1)S(1)}, u32[]{:S(2)}, u32[]{:S(2)}) collective-permute-start(bf16[512,1024]{1,0:T(8,128)(2,1)S(1)} %unproject_far.3), channel_id=1, source_target_pairs={{0,1},{1,0},{2,3},{3,2},{4,5},{5,4},{6,7},{7,6},{8,9},{9,8},{10,11... | collective-permute-start | bytes 3145736 | tf_op jit(solution)/shard_map/ppermute | solution.py:426
  (155 other events, 1320.0 us)

commit v7 on v6

--- a/solution.py
+++ b/solution.py
@@ -1271,16 +1271,27 @@
 SMALL_ROWS = 11
 
 
-def start_kernel(
-    layers, x_ref, project_ref, output_ref, expand_ref, reduce_ref,
-    *rest,
-):
-    six_refs, bias_ref, unit_row_ref, rest = rest[:6], rest[6], rest[7], rest[8:]
+def start_kernel(layers, x_ref, *rest):
+    sources, rest = rest[:13], rest[13:]
+    targets, (vector_ref, head_bias_ref, unit_bias_ref, starts_ref), rest = rest[:12], rest[12:16], rest[16:]
+    loaded, made, rest = rest[:13], rest[13:25], rest[25:]
+    project_ref, output_ref, expand_ref, reduce_ref, *six_refs, bias_ref, unit_row_ref, places_ref = loaded
     (
-    resid_ref, normed_ref, far_ref, even_ref, odd_ref, first_ref, heads_ref, pairs_ref, vector_ref, head_bias_ref, unit_bias_ref,
-    near_mine_ref, far_mine_ref, got_near_ref, got_far_ref,
-    came_ref, piece_ref, every_ref, near_other_ref, far_other_ref, local_sem, send_sem, recv_sem,
+        resid_ref, normed_ref, far_ref, even_ref, odd_ref, first_ref, heads_ref, pairs_ref,
+        near_mine_ref, far_mine_ref, got_near_ref, got_far_ref,
+    ) = made
+    (
+        came_ref, piece_ref, every_ref, near_other_ref, far_other_ref, local_sem, load_sem, store_sem, send_sem, recv_sem,
     ) = rest
+    loads = [pltpu.make_async_copy(s, t, load_sem.at[i]) for i, (s, t) in enumerate(zip(sources, loaded))]
+    for one in loads:
+        one.start()
+    stores = {id(s): pltpu.make_async_copy(s, t, store_sem.at[i]) for i, (s, t) in enumerate(zip(made, targets))}
+
+    def store(*refs):
+        for ref in refs:
+            stores[id(ref)].start()
+
     own, place = lax.axis_index("dp"), lax.axis_index("tensor")
     core = own % 2
     keep = core == place // 2
@@ -1305,6 +1316,9 @@
     @pl.when(jnp.logical_not(keep))
     def _():
         tokens.start()
+
+    for one in loads:
+        one.wait()
 
     def pack_heads_into(target, layer):
         for part in range(3):
@@ -1330,6 +1344,7 @@
             ours = jnp.where(lane // 32 == own % 4, bias_ref[layer, part:part + 1, :].astype(F32), 0.0)
             every_ref[0, 0, pl.ds(base + 6 + 2 * part + own // 4, 1), :] = ours
         every_ref[0, 0, base + 10:base + 11, :] = unit_row_ref[layer:layer + 1, :].astype(F32)
+    every_ref[0, 0, layers * SMALL_ROWS:layers * SMALL_ROWS + 1, :] = places_ref[...]
     smalls = [
         (copy(every_ref.at[0, pl.ds(0, width)], every_ref.at[0, pl.ds(width, width)], peer(mask)))
         for width, mask in ((1, CORE), (2, XBIT), (4, YBIT))
@@ -1359,6 +1374,8 @@
     cores = [copy(even_ref.at[chip], odd_ref.at[chip], peer(CORE)) for chip in range(4)]
     cores[0].start()
     smalls[4].wait()
+    half = place // 2
+    starts_ref[...] = every_ref[0, core + half - 2 * core * half, layers * SMALL_ROWS:layers * SMALL_ROWS + 1, :]
     for layer in range(layers):
         base = layer * SMALL_ROWS
         later = min(layer + 1, layers - 1) * SMALL_ROWS
@@ -1392,6 +1409,7 @@
         resid_ref[:, block * 128:(block + 1) * 128] = came_ref[:, here].astype(F32)
     normed = (normalize(resid_ref[...])[0] * vector_ref[0, 0:1] + vector_ref[0, 1:2]).astype(BF)
     normed_ref[...] = normed
+    store(resid_ref, normed_ref)
     beside = copy(normed_ref, far_ref, peer(Z0))
     beside.start()
     cross.start()
@@ -1417,36 +1435,46 @@
     cores[3].start()
     for one in cores:
         one.wait()
+    store(even_ref, odd_ref)
     weights = (even_ref, odd_ref)
     project_rows(normed_ref[...], weights, head_bias_ref, 0, (near_mine_ref, near_other_ref))
     back_near = copy(near_other_ref, got_near_ref, peer(CORE))
     back_near.start()
+    store(near_mine_ref)
     beside.wait()
     project_rows(far_ref[...], weights, head_bias_ref, 0, (far_mine_ref, far_other_ref))
     back_far = copy(far_other_ref, got_far_ref, peer(CORE))
     back_far.start()
-    back_near.wait()
-    back_far.wait()
-    cross.wait()
-
-    @pl.when(core == 1)
-    def _():
-        same.wait()
-
+    store(far_ref, far_mine_ref)
     for one in ahead:
         one.wait()
-
-
-def start(x, project_weight, output_weight, expand_weight, reduce_weight, six, project_bias, expand_bias):
+    store(heads_ref, pairs_ref)
+    back_near.wait()
+    store(got_near_ref)
+    cross.wait()
+
+    @pl.when(core == 1)
+    def _():
+        same.wait()
+
+    store(first_ref)
+    back_far.wait()
+    store(got_far_ref)
+    for one in stores.values():
+        one.wait()
+
+
+def start(x, project_weight, output_weight, expand_weight, reduce_weight, six, project_bias, expand_bias, places):
     rows, features = x.shape
     layers = expand_bias.shape[0]
-    small = 8 * (-(-SMALL_ROWS * layers // 8))
+    small = 8 * (-(-(SMALL_ROWS * layers + 1) // 8))
     project_bias = jnp.tile(project_bias, (1, 1, 4))
-    vmem = pl.BlockSpec(memory_space=pltpu.VMEM)
-
+    places = jnp.pad(places.astype(F32), ((0, 0), (0, 128 - places.shape[1])))
+    args = [project_weight, output_weight, expand_weight, reduce_weight, *six, project_bias, expand_bias, places]
+    vmem, hbm = pl.BlockSpec(memory_space=pltpu.VMEM), pl.BlockSpec(memory_space=pltpu.HBM)
     triple = jax.ShapeDtypeStruct((rows, 768), BF)
     heads = jax.ShapeDtypeStruct((4, 2, 128, 1024), BF)
-    outs = [
+    made = [
         jax.ShapeDtypeStruct((rows, features), F32),
         jax.ShapeDtypeStruct((rows, features), BF),
         jax.ShapeDtypeStruct((rows, features), BF),
@@ -1455,34 +1483,40 @@
         jax.ShapeDtypeStruct((2, 128, 2048), BF),
         jax.ShapeDtypeStruct((layers - 1, 128, 1024), BF),
         jax.ShapeDtypeStruct((layers - 1, 2, 128, 2048), BF),
-        jax.ShapeDtypeStruct((layers, 8, features), F32),
-        jax.ShapeDtypeStruct((layers, 2, 768), F32),
-        jax.ShapeDtypeStruct((layers, 1, 2048), F32),
         triple,
         triple,
         triple,
         triple,
     ]
+    spread = [
+        jax.ShapeDtypeStruct((layers, 8, features), F32),
+        jax.ShapeDtypeStruct((layers, 2, 768), F32),
+        jax.ShapeDtypeStruct((layers, 1, 2048), F32),
+        jax.ShapeDtypeStruct((1, 128), F32),
+    ]
     copies = 19 + layers - 1
     return pl.pallas_call(
         functools.partial(start_kernel, layers),
-        in_specs=[vmem] * 13,
-        out_specs=[vmem] * len(outs),
-        out_shape=outs,
+        in_specs=[hbm] * (1 + len(args)),
+        out_specs=[hbm] * len(made) + [vmem] * len(spread),
+        out_shape=made + spread,
         scratch_shapes=[
+            *[pltpu.VMEM(a.shape, a.dtype) for a in args + made],
             pltpu.VMEM((rows, features), BF),
             pltpu.VMEM((128, 2048), BF),
             pltpu.VMEM((4, 8, small, 128), F32),
             pltpu.VMEM((rows, 768), BF),
             pltpu.VMEM((rows, 768), BF),
             pltpu.SemaphoreType.DMA,
+            pltpu.SemaphoreType.DMA((len(args),)),
+            pltpu.SemaphoreType.DMA((len(made),)),
             pltpu.SemaphoreType.DMA((copies,)),
             pltpu.SemaphoreType.DMA((copies,)),
         ],
-        compiler_params=pltpu.CompilerParams(vmem_limit_bytes=VMEM_LIMIT, collective_id=0, has_side_effects=True),
+        compiler_params=pltpu.CompilerParams(vmem_limit_bytes=60 * 1024 * 1024, collective_id=0, has_side_effects=True),
         cost_estimate=took(60),
         name="start",
-    )(x, project_weight, output_weight, expand_weight, reduce_weight, *six, project_bias, expand_bias)
+    )(x, *args)
 
 
 def finish_kernel(
@@ -1837,13 +1871,16 @@
     slopes = head_slopes((place ^ (2 * core)) * 4, 4)
 
     turn = jnp.zeros((1,), jnp.int32)
-    resid, normed, far, even, odd, first_pieces, own_heads, own_units, vectors_of, head_bias_of, unit_bias_of, *blocks = start(
+    (
+        resid, normed, far, even, odd, first_pieces, own_heads, own_units, near_mine, far_mine, got_near, got_far,
+        vectors_of, head_bias_of, unit_bias_of, places,
+    ) = start(
         layer_input, project_weight, output_weight, expand_weight, reduce_weight,
         (first_gain, first_shift, output_bias, second_gain, second_shift, reduce_bias), project_bias, expand_bias,
+        picture_start,
     )
-    near_mine, far_mine, got_near, got_far = blocks
     small = [(vectors_of[i], head_bias_of[i], unit_bias_of[i]) for i in range(LAYERS)]
-    starts = jnp.where(keep, picture_start, redeal(picture_start))[0]
+    starts = places[0, :picture_start.shape[1]].astype(jnp.int32)
     heads, units = [[] for i in range(LAYERS)], [([], []) for i in range(LAYERS)]
     heads[0] += [even, odd, turn]
     head_tasks, unit_tasks = [None], [task(fetch_units_near(first_pieces, *units[0]))]

time: 784 us -> 745 us (0.950)
  starting transfers between devices: 90.7 us -> 65.3 us
  local copies, waits for them, and re-layouts: 87.3 us -> 72.2 us
  waiting for transfers between devices: 134 us -> 121 us
  Pallas kernels: 426 us -> 437 us
    ppermute x61, starting transfers between devices: 84 us -> 61 us  [swap(): return lax.ppermute(values, AXES, [(i, i ^ mask) for i in range(32)])]
    unnamed x274 -> x260, local copies, waits for them, and re-layouts: 68.6 us -> 52.3 us
    ppermute x61, waiting for transfers between devices: 134 us -> 121 us  [swap(): return lax.ppermute(values, AXES, [(i, i ^ mask) for i in range(32)])]
  transfers between devices with their start and end apart: 67 -> 66, of which waited for: 25 -> 24; matrix products, arithmetic and copies ran while one was open for 5% -> 6% of each run, Pallas kernels for 31% -> 34%
where the time goes in v7:
time: 745 us; the launch traced here: 733 us
  Pallas kernels  437 us (59%)
  waiting for transfers between devices  121 us (16%)
  local copies, waits for them, and re-layouts  72.2 us (10%)
  starting transfers between devices  65.3 us (9%)
  other arithmetic  34.2 us (5%)
    ppermute x61, waiting for transfers between devices, swap(): return lax.ppermute(values, AXES, [(i, i ^ mask) for i in range(32)])  121 us
    pallas_call x1, Pallas kernels, start(): pl.pallas_call(functools.partial(start_kernel, layers), in_specs=[hbm] *...  87.6 us
    pallas_call x4, Pallas kernels, attend_pull(): pl.pallas_call(functools.partial(pull_kernel, block, pair), grid=(4,), in...  81.1 us
    pallas_call x4, Pallas kernels, attend(): pl.pallas_call(functools.partial(attend_kernel, block, rest_bit), grid=(p...  65.7 us
    pallas_call x1, Pallas kernels, finish(): pl.pallas_call(functools.partial(finish_kernel, layers), in_specs=[vmem]...  63.9 us
    ppermute x61, starting transfers between devices, swap(): return lax.ppermute(values, AXES, [(i, i ^ mask) for i in range(32)])  61 us
    unnamed x260, local copies, waits for them, and re-layouts  52.3 us
    pallas_call x20, Pallas kernels, call_once(): pl.pallas_call(kernel, in_specs=placed(args), out_specs=placed(outs), out...  46.5 us
  transfers between devices with their start and end apart: 66, of which 24 were waited for; matrix products, arithmetic and copies ran while one was open for 6% of the time, Pallas kernels for 34%

profile of v7, /device:TPU:0, one launch (start us, length us, event | category | flops | bytes accessed | tf_op | source)
XLA Modules:
  0.0 732.7 jit_solution(8931850211814150385)
XLA Ops:
  3.2 87.6 %start.1 = (f32[512,1024]{1,0:T(8,128)}, bf16[512,1024]{1,0:T(8,128)(2,1)}, bf16[512,1024]{1,0:T(8,128)(2,1)}, bf16[4,2,128,1024]{3,2,1,0:T(8,128)(2,1)}, bf16[4...) custom-call(bf16[512,1024]{1,0:T(8,128)(2,1)} %x_ref.1, ...), custom_call_target="tpu_custom_call" | custom-call | flops 30000001024 | bytes 1 | tf_op jit(solution)/shard_map/start/pallas_call | solution.py:1498
  99.0 17.9 %attend.4 = (bf16[512,256]{1,0:T(8,128)(2,1)S(1)}, bf16[512,256]{1,0:T(8,128)(2,1)S(1)}, f32[256,1024]{1,0:T(8,128)S(1)}, f32[2,8,1024]{2,1,0:T(8,128)S(1)}) custom-call(f32[4]{0:T(128)S(1)} %multiply_exponential_fusion.slope_ref, s32[2]{0:T(128)S(1)} %convert_bitcast_fusion.start_ref, s32[1]{0:T(128)} %bitcast.3.me_ref, bf16[512,768]{1,0:T(8,128)(2,1)S(1)} %copy-done.95, ...), custom_call_target="tpu_custom_call" | custom-call | flops 8499999744 | bytes 1 | tf_op jit(solution)/shard_map/attend/pallas_call | solution.py:614
  121.6 14.9 %attend.5 = (bf16[512,256]{1,0:T(8,128)(2,1)S(1)}, bf16[512,256]{1,0:T(8,128)(2,1)S(1)}, f32[256,1024]{1,0:T(8,128)S(1)}, f32[2,8,1024]{2,1,0:T(8,128)S(1)}) custom-call(f32[4]{0:T(128)S(1)} %multiply_exponential_fusion.slope_ref, s32[2]{0:T(128)S(1)} %convert_bitcast_fusion.start_ref, s32[1]{0:T(128)} %bitcast.3.me_ref, bf16[512,768]{1,0:T(8,128)(2,1)S(1)} %copy-done.95, ...), custom_call_target="tpu_custom_call" | custom-call | flops 8499999744 | bytes 1 | tf_op jit(solution)/shard_map/attend/pallas_call | solution.py:614
  138.2 3.4 collective-permute-start.4
  141.6 4.5 collective-permute-done.6.rest_5_
  147.2 2.6 collective-permute-start.11
  157.3 13.3 %collective-permute-done.11 = bf16[128,1024]{1,0:T(8,128)(2,1)} collective-permute-done((bf16[128,1024]{1,0:T(8,128)(2,1)S(1)}, bf16[128,1024]{1,0:T(8,128)(2,1)}, u32[]{:S(2)}, u32[]{:S(2)}) %collective-permute-start.11) | collective-permute-done | bytes 262176 | tf_op jit(solution)/shard_map/ppermute | solution.py:426
  175.6 15.5 %mlp_forward.2 = (bf16[1024,2048]{1,0:T(8,128)(2,1)S(1)}, bf16[1024,2048]{1,0:T(8,128)(2,1)S(1)}, f32[512,1024]{1,0:T(8,128)S(1)}, bf16[512,1024]{1,0:T(8,128)(2,1)}) custom-call(s32[1]{0:T(128)} %constant.10.clone.1.rest_2_.turn_ref.rest_6_.rest_10_, bf16[512,1024]{1,0:T(8,128)(2,1)S(1)} %copy-done.63, bf16[512,1024]{1,0:T(8,128)(2,1)} %collective-permute-done.12.other_ref, ...), custom_call_target="tpu_custom_call" | custom-call | flops 8999999488 | bytes 1 | tf_op jit(solution)/shard_map/mlp_forward/pallas_call | solution.py:1047
  196.4 6.8 collective-permute-start.13
  204.8 12.3 %collective-permute-done.14 = bf16[2,128,1024]{2,1,0:T(8,128)(2,1)S(1)} collective-permute-done((bf16[2,128,1024]{2,1,0:T(8,128)(2,1)S(1)}, bf16[2,128,1024]{2,1,0:T(8,128)(2,1)S(1)}, u32[]{:S(2)}, u32[]{:S(2)}) %collective-permute-start.14) | collective-permute-done | bytes 524320 | tf_op jit(solution)/shard_map/ppermute | solution.py:426
  223.6 6.7 collective-permute-done.17
  237.9 19.6 %collective-permute-done.19.rows_ref.far_ref = bf16[512,1024]{1,0:T(8,128)(2,1)S(1)} collective-permute-done((bf16[512,1024]{1,0:T(8,128)(2,1)S(1)}, bf16[512,1024]{1,0:T(8,128)(2,1)S(1)}, u32[]{:S(2)}, u32[]{:S(2)}) %collective-permute-start.19) | collective-permute-done | bytes 1048608 | tf_op jit(solution)/shard_map/ppermute | solution.py:426
  262.6 18.0 %attend.6 = (bf16[512,256]{1,0:T(8,128)(2,1)S(1)}, bf16[512,256]{1,0:T(8,128)(2,1)S(1)}, f32[256,1024]{1,0:T(8,128)S(1)}, f32[2,8,1024]{2,1,0:T(8,128)S(1)}) custom-call(f32[4]{0:T(128)S(1)} %multiply_exponential_fusion.slope_ref, s32[2]{0:T(128)S(1)} %convert_bitcast_fusion.start_ref, s32[1]{0:T(128)} %bitcast.3.me_ref, ...), custom_call_target="tpu_custom_call" | custom-call | flops 8499999744 | bytes 1 | tf_op jit(solution)/shard_map/attend/pallas_call | solution.py:614
  280.6 4.6 collective-permute-start.24
  288.3 2.6 enter.1
  292.1 14.9 %attend.7 = (bf16[512,256]{1,0:T(8,128)(2,1)S(1)}, bf16[512,256]{1,0:T(8,128)(2,1)S(1)}, f32[256,1024]{1,0:T(8,128)S(1)}, f32[2,8,1024]{2,1,0:T(8,128)S(1)}) custom-call(f32[4]{0:T(128)S(1)} %multiply_exponential_fusion.slope_ref, s32[2]{0:T(128)S(1)} %convert_bitcast_fusion.start_ref, s32[1]{0:T(128)} %bitcast.3.me_ref, ...), custom_call_target="tpu_custom_call" | custom-call | flops 8499999744 | bytes 1 | tf_op jit(solution)/shard_map/attend/pallas_call | solution.py:614
  307.0 3.0 collective-permute-start.28
  310.0 4.7 collective-permute-done.30.rest_3_
  320.7 13.4 %mlp_forward.3 = (bf16[1024,2048]{1,0:T(8,128)(2,1)S(1)}, bf16[1024,2048]{1,0:T(8,128)(2,1)S(1)}, f32[512,1024]{1,0:T(8,128)S(1)}, bf16[512,1024]{1,0:T(8,128)(2,1)S(1)}) custom-call(s32[1]{0:T(128)} %constant.10.clone.1.rest_2_.turn_ref.rest_6_.rest_10_, bf16[512,1024]{1,0:T(8,128)(2,1)S(1)} %get-tuple-element.295.normed_ref.left_ref, ...), custom_call_target="tpu_custom_call" | custom-call | flops 8999999488 | bytes 1 | tf_op jit(solution)/shard_map/mlp_forward/pallas_call | solution.py:1047
  343.3 16.7 %mlp_backward.2 = (bf16[1024,2048]{1,0:T(8,128)(2,1)S(1)}, f32[1,2048]{1,0:T(1,128)S(1)}, f32[512,1024]{1,0:T(8,128)S(1)}, bf16[512,1024]{1,0:T(8,128)(2,1)S(1)}) custom-call(s32[1]{0:T(128)} %constant.10.clone.1.rest_2_.turn_ref.rest_6_.rest_10_, f32[512,1024]{1,0:T(8,128)S(1)} %get-tuple-element.301.grad_ref.left_ref, ...), custom_call_target="tpu_custom_call" | custom-call | flops 11000000512 | bytes 1 | tf_op jit(solution)/shard_map/mlp_backward/pallas_call | solution.py:1125
  368.3 6.4 unit_grads.4
  377.0 6.6 unit_grads.5
  383.6 8.2 %collective-permute-done.37.grad_ref.grad_far_ref = bf16[512,1024]{1,0:T(8,128)(2,1)S(1)} collective-permute-done((bf16[512,1024]{1,0:T(8,128)(2,1)S(1)}, bf16[512,1024]{1,0:T(8,128)(2,1)S(1)}, u32[]{:S(2)}, u32[]{:S(2)}) %collective-permute-start.37) | collective-permute-done | bytes 1048608 | tf_op jit(solution)/shard_map/ppermute | solution.py:426
  394.7 19.8 %attend_pull.4 = (bf16[3,1024,128]{2,1,0:T(8,128)(2,1)S(1)}, bf16[3,1024,128]{2,1,0:T(8,128)(2,1)S(1)}) custom-call(f32[4]{0:T(128)S(1)} %multiply_exponential_fusion.slope_ref, s32[2]{0:T(128)S(1)} %convert_bitcast_fusion.start_ref, s32[1]{0:T(128)} %bitcast.3.me_ref, bf16[512,768]{1,0:T(8,128)(2,1)S(1)} %copy-done.68, bf16[512,768]{1,0:T(8,128)(2,1)S(1)} %copy-done.68, ...), custom_call_target="tpu_custom_call" | custom-call | flops 11000000512 | bytes 1 | tf_op jit(solution)/shard_map/attend_pull/pallas_call | solution.py:747
  414.4 7.8 %collective-permute-done.40 = bf16[2,2,2,128,1024]{4,3,2,1,0:T(8,128)(2,1)S(1)} collective-permute-done((bf16[2,2,2,128,1024]{4,3,2,1,0:T(8,128)(2,1)S(1)}, bf16[2,2,2,128,1024]{4,3,2,1,0:T(8,128)(2,1)S(1)}, u32[]{:S(2)}, u32[]{:S(2)}) %collective-permute-start.40) | collective-permute-done | bytes 2097184 | tf_op jit(solution)/shard_map/ppermute | solution.py:426
  423.8 20.0 %attend_pull.5 = (bf16[3,1024,128]{2,1,0:T(8,128)(2,1)S(1)}, bf16[3,1024,128]{2,1,0:T(8,128)(2,1)S(1)}) custom-call(f32[4]{0:T(128)S(1)} %multiply_exponential_fusion.slope_ref, s32[2]{0:T(128)S(1)} %convert_bitcast_fusion.start_ref, s32[1]{0:T(128)} %bitcast.3.me_ref, bf16[512,768]{1,0:T(8,128)(2,1)S(1)} %copy-done.68, bf16[512,768]{1,0:T(8,128)(2,1)S(1)} %copy-done.68, ...), custom_call_target="tpu_custom_call" | custom-call | flops 11000000512 | bytes 1 | tf_op jit(solution)/shard_map/attend_pull/pallas_call | solution.py:747
  450.2 2.8 unproject_far.2
  453.3 4.9 head_grads.2
  460.8 3.9 copy.55
  464.7 7.2 collective-permute-done.45
  473.6 5.1 fusion.4
  480.7 4.1 unproject_near.2
  486.3 4.0 copy.54
  490.5 3.9 slice_add_fusion
  498.4 17.1 %mlp_backward.3 = (bf16[1024,2048]{1,0:T(8,128)(2,1)S(1)}, f32[1,2048]{1,0:T(1,128)S(1)}, f32[512,1024]{1,0:T(8,128)S(1)}, bf16[512,1024]{1,0:T(8,128)(2,1)S(1)}) custom-call(s32[1]{0:T(128)} %constant.10.clone.1.rest_2_.turn_ref.rest_6_.rest_10_, f32[512,1024]{1,0:T(8,128)S(1)} %copy-done.47, bf16[512,1024]{1,0:T(8,128)(2,1)S(1)} %collective-permute-done.48.other_ref, ...), custom_call_target="tpu_custom_call" | custom-call | flops 11000000512 | bytes 1 | tf_op jit(solution)/shard_map/mlp_backward/pallas_call | solution.py:1125
  531.4 6.4 unit_grads.6
  540.4 7.8 %unit_grads.7 = (bf16[2,2,128,1024]{3,2,1,0:T(8,128)(2,1)S(1)}, bf16[2,2,2,128,1024]{4,3,2,1,0:T(8,128)(2,1)S(1)}, bf16[2,2,128,1024]{3,2,1,0:T(8,128)(2,1)S(1)}) custom-call(bf16[512,1024]{1,0:T(8,128)(2,1)S(1)} %copy-done.64, bf16[512,1024]{1,0:T(8,128)(2,1)} %collective-permute-done.12.other_ref, bf16[1024,2048]{1,0:T(8,128)(2,1)S(1)} %copy-done.76), custom_call_target="tpu_custom_call" | custom-call | flops 5000000000 | bytes 1 | tf_op jit(solution)/shard_map/unit_grads/pallas_call | solution.py:1187
  549.5 5.4 collective-permute-done.52.grad_ref.grad_far_ref
  560.0 2.6 collective-permute-start.62
  562.7 20.6 %attend_pull.6 = (bf16[3,1024,128]{2,1,0:T(8,128)(2,1)S(1)}, bf16[3,1024,128]{2,1,0:T(8,128)(2,1)}) custom-call(f32[4]{0:T(128)S(1)} %multiply_exponential_fusion.slope_ref, s32[2]{0:T(128)S(1)} %convert_bitcast_fusion.start_ref, s32[1]{0:T(128)} %bitcast.3.me_ref, bf16[512,768]{1,0:T(8,128)(2,1)S(1)} %copy-done.96, bf16[512,768]{1,0:T(8,128)(2,1)S(1)} %copy-done.96, ...), custom_call_target="tpu_custom_call" | custom-call | flops 11000000512 | bytes 1 | tf_op jit(solution)/shard_map/attend_pull/pallas_call | solution.py:747
  584.2 2.5 collective-permute-done.56
  588.0 20.8 %attend_pull.7 = (bf16[3,1024,128]{2,1,0:T(8,128)(2,1)S(1)}, bf16[3,1024,128]{2,1,0:T(8,128)(2,1)}) custom-call(f32[4]{0:T(128)S(1)} %multiply_exponential_fusion.slope_ref, s32[2]{0:T(128)S(1)} %convert_bitcast_fusion.start_ref, s32[1]{0:T(128)} %bitcast.3.me_ref, bf16[512,768]{1,0:T(8,128)(2,1)S(1)} %copy-done.96, bf16[512,768]{1,0:T(8,128)(2,1)S(1)} %copy-done.96, ...), custom_call_target="tpu_custom_call" | custom-call | flops 11000000512 | bytes 1 | tf_op jit(solution)/shard_map/attend_pull/pallas_call | solution.py:747
  623.7 3.4 unproject_far.3
  627.5 6.4 head_grads.3
  640.4 12.0 %collective-permute-done.63.rest_4_ = bf16[512,1024]{1,0:T(8,128)(2,1)S(1)} collective-permute-done((bf16[512,1024]{1,0:T(8,128)(2,1)S(1)}, bf16[512,1024]{1,0:T(8,128)(2,1)S(1)}, u32[]{:S(2)}, u32[]{:S(2)}) %collective-permute-start.63) | collective-permute-done | bytes 1048608 | tf_op jit(solution)/shard_map/ppermute | solution.py:426
  652.4 5.7 unproject_near.3
  658.1 63.9 %finish.1 = (bf16[512,1024]{1,0:T(8,128)(2,1)S(1)}, f32[3,128,256]{2,1,0:T(8,128)S(1)}, f32[256,128]{1,0:T(8,128)S(1)}, f32[1024,128]{1,0:T(8,128)S(1)}, f32[128,1024]{1,0:T(8,128)S(1)}, /*index=5*/f32[24,128]{1,0:T(8,128)S(1)}) custom-call(bf16[512,1024]{1,0:T(8,128)(2,1)S(1)} %get-tuple-element.405.grad_ref, ...), custom_call_target="tpu_custom_call" | custom-call | flops 24999999488 | bytes 1 | tf_op jit(solution)/shard_map/finish/pallas_call | solution.py:1698
  725.6 2.6 copy.60
  (435 shorter events, 165.5 us)
Async XLA Ops:
  90.7 29.7 %collective-permute-start.1 = (bf16[2,128,2048]{2,1,0:T(8,128)(2,1)}, bf16[2,128,2048]{2,1,0:T(8,128)(2,1)S(1)}, u32[]{:S(2)}, u32[]{:S(2)}) collective-permute-start(bf16[2,128,2048]{2,1,0:T(8,128)(2,1)} %get-tuple-element.227.rest_0_), channel_id=1, source_target_pairs={{0,8},{1,9},{2,10},{3,11},{4,12},{5,13},{6,14},{7,15},{8,0},{9,1},... | collective-permute-start | bytes 3145736 | tf_op jit(solution)/shard_map/ppermute | solution.py:426
  92.3 28.1 %collective-permute-start.2 = (bf16[2,128,2048]{2,1,0:T(8,128)(2,1)}, bf16[2,128,2048]{2,1,0:T(8,128)(2,1)S(1)}, u32[]{:S(2)}, u32[]{:S(2)}) collective-permute-start(bf16[2,128,2048]{2,1,0:T(8,128)(2,1)} %get-tuple-element.227.rest_0_), channel_id=1, source_target_pairs={{0,16},{1,17},{2,18},{3,19},{4,20},{5,21},{6,22},{7,23},{8,24},{9,... | collective-permute-start | bytes 3145736 | tf_op jit(solution)/shard_map/ppermute | solution.py:426
  93.8 26.6 %collective-permute-start.3 = (bf16[2,128,2048]{2,1,0:T(8,128)(2,1)}, bf16[2,128,2048]{2,1,0:T(8,128)(2,1)}, u32[]{:S(2)}, u32[]{:S(2)}) collective-permute-start(bf16[2,128,2048]{2,1,0:T(8,128)(2,1)} %get-tuple-element.227.rest_0_), channel_id=1, source_target_pairs={{0,1},{1,0},{2,3},{3,2},{4,5},{5,4},{6,7},{7,6},{8,9},{9,8},{10,11... | collective-permute-start | bytes 3145736 | tf_op jit(solution)/shard_map/ppermute | solution.py:426
  120.3 30.5 %collective-permute-start.5 = (bf16[512,1024]{1,0:T(8,128)(2,1)S(1)}, bf16[512,1024]{1,0:T(8,128)(2,1)S(1)}, u32[]{:S(2)}, u32[]{:S(2)}) collective-permute-start(bf16[512,1024]{1,0:T(8,128)(2,1)S(1)} %mix_far.2), channel_id=1, source_target_pairs={{0,1},{1,0},{2,3},{3,2},{4,5},{5,4},{6,7},{7,6},{8,9},{9,8},{10,11... | collective-permute-start | bytes 3145736 | tf_op jit(solution)/shard_map/ppermute | solution.py:426
  120.4 25.7 %collective-permute-start.6 = (bf16[2,128,2048]{2,1,0:T(8,128)(2,1)}, bf16[2,128,2048]{2,1,0:T(8,128)(2,1)S(1)}, u32[]{:S(2)}, u32[]{:S(2)}) collective-permute-start(bf16[2,128,2048]{2,1,0:T(8,128)(2,1)} %collective-permute-done.3.rest_4_), channel_id=1, source_target_pairs={{0,8},{1,9},{2,10},{3,11},{4,12},{5,13},{6,14},{7,15},{8,0},{9,1},... | collective-permute-start | bytes 3145736 | tf_op jit(solution)/shard_map/ppermute | solution.py:426
  121.1 28.7 %collective-permute-start.7 = (bf16[2,128,2048]{2,1,0:T(8,128)(2,1)}, bf16[2,128,2048]{2,1,0:T(8,128)(2,1)}, u32[]{:S(2)}, u32[]{:S(2)}) collective-permute-start(bf16[2,128,2048]{2,1,0:T(8,128)(2,1)} %collective-permute-done.3.rest_4_), channel_id=1, source_target_pairs={{0,16},{1,17},{2,18},{3,19},{4,20},{5,21},{6,22},{7,23},{8,24},{9,... | collective-permute-start | bytes 3145736 | tf_op jit(solution)/shard_map/ppermute | solution.py:426
  137.5 18.9 %collective-permute-start.10 = (bf16[2,128,2048]{2,1,0:T(8,128)(2,1)}, bf16[2,128,2048]{2,1,0:T(8,128)(2,1)S(1)}, u32[]{:S(2)}, u32[]{:S(2)}) collective-permute-start(bf16[2,128,2048]{2,1,0:T(8,128)(2,1)} %bitcast.5), channel_id=1, source_target_pairs={{4,6},{5,7},{6,4},{7,5},{12,14},{13,15},{14,12},{15,13},{20,22},{2... | collective-permute-start | bytes 3145736 | tf_op jit(solution)/shard_map/ppermute | solution.py:431
  147.2 23.4 %collective-permute-start.11 = (bf16[128,1024]{1,0:T(8,128)(2,1)S(1)}, bf16[128,1024]{1,0:T(8,128)(2,1)}, u32[]{:S(2)}, u32[]{:S(2)}) collective-permute-start(bf16[128,1024]{1,0:T(8,128)(2,1)S(1)} %bitcast.122), channel_id=1, source_target_pairs={{0,2},{1,3},{2,0},{3,1},{4,6},{5,7},{6,4},{7,5},{8,10},{9,11},{10,... | collective-permute-start | bytes 786440 | tf_op jit(solution)/shard_map/ppermute | solution.py:426
  149.8 25.8 %collective-permute-start.9 = (bf16[2,128,2048]{2,1,0:T(8,128)(2,1)}, bf16[2,128,2048]{2,1,0:T(8,128)(2,1)}, u32[]{:S(2)}, u32[]{:S(2)}) collective-permute-start(bf16[2,128,2048]{2,1,0:T(8,128)(2,1)} %collective-permute-done.7.rest_6_), channel_id=1, source_target_pairs={{0,8},{1,9},{2,10},{3,11},{4,12},{5,13},{6,14},{7,15},{8,0},{9,1},... | collective-permute-start | bytes 3145736 | tf_op jit(solution)/shard_map/ppermute | solution.py:426
  150.9 24.7 %collective-permute-start.8 = (bf16[2,128,2048]{2,1,0:T(8,128)(2,1)S(1)}, bf16[2,128,2048]{2,1,0:T(8,128)(2,1)}, u32[]{:S(2)}, u32[]{:S(2)}) collective-permute-start(bf16[2,128,2048]{2,1,0:T(8,128)(2,1)S(1)} %collective-permute-done.1.rest_1_), channel_id=1, source_target_pairs={{0,16},{1,17},{2,18},{3,19},{4,20},{5,21},{6,22},{7,23},{8,24},{9,... | collective-permute-start | bytes 3145736 | tf_op jit(solution)/shard_map/ppermute | solution.py:426
  156.3 19.3 %collective-permute-start.12 = (bf16[512,1024]{1,0:T(8,128)(2,1)}, bf16[512,1024]{1,0:T(8,128)(2,1)}, u32[]{:S(2)}, u32[]{:S(2)}) collective-permute-start(bf16[512,1024]{1,0:T(8,128)(2,1)} %get-tuple-element.254), channel_id=1, source_target_pairs={{0,4},{1,5},{2,6},{3,7},{4,0},{5,1},{6,2},{7,3},{8,12},{9,13},{10,... | collective-permute-start | bytes 3145736 | tf_op jit(solution)/shard_map/ppermute | solution.py:426
  172.1 46.8 %collective-permute-start.16 = (bf16[2,128,2048]{2,1,0:T(8,128)(2,1)S(1)}, bf16[2,128,2048]{2,1,0:T(8,128)(2,1)}, u32[]{:S(2)}, u32[]{:S(2)}) collective-permute-start(bf16[2,128,2048]{2,1,0:T(8,128)(2,1)S(1)} %broadcast_select_fusion.rest_0_), channel_id=1, source_target_pairs={{0,1},{1,0},{2,3},{3,2},{4,5},{5,4},{6,7},{7,6},{8,9},{9,8},{10,11... | collective-permute-start | bytes 3145736 | tf_op jit(solution)/shard_map/ppermute | solution.py:426
  196.4 22.5 %collective-permute-start.13 = (bf16[512,1024]{1,0:T(8,128)(2,1)}, bf16[512,1024]{1,0:T(8,128)(2,1)S(1)}, u32[]{:S(2)}, u32[]{:S(2)}) collective-permute-start(bf16[512,1024]{1,0:T(8,128)(2,1)} %get-tuple-element.257), channel_id=1, source_target_pairs={{0,4},{1,5},{2,6},{3,7},{4,0},{5,1},{6,2},{7,3},{8,12},{9,13},{10,... | collective-permute-start | bytes 3145736 | tf_op jit(solution)/shard_map/ppermute | solution.py:426
  203.3 13.8 %collective-permute-start.14 = (bf16[2,128,1024]{2,1,0:T(8,128)(2,1)S(1)}, bf16[2,128,1024]{2,1,0:T(8,128)(2,1)S(1)}, u32[]{:S(2)}, u32[]{:S(2)}) collective-permute-start(bf16[2,128,1024]{2,1,0:T(8,128)(2,1)S(1)} %get-tuple-element.465), channel_id=1, source_target_pairs={{0,8},{1,9},{2,10},{3,11},{4,12},{5,13},{6,14},{7,15},{8,0},{9,1},... | collective-permute-start | bytes 1572872 | tf_op jit(solution)/shard_map/ppermute | solution.py:426
  203.8 13.6 %collective-permute-start.15 = (bf16[2,128,1024]{2,1,0:T(8,128)(2,1)S(1)}, bf16[2,128,1024]{2,1,0:T(8,128)(2,1)S(1)}, u32[]{:S(2)}, u32[]{:S(2)}) collective-permute-start(bf16[2,128,1024]{2,1,0:T(8,128)(2,1)S(1)} %get-tuple-element.465), channel_id=1, source_target_pairs={{0,16},{1,17},{2,18},{3,19},{4,20},{5,21},{6,22},{7,23},{8,24},{9,... | collective-permute-start | bytes 1572872 | tf_op jit(solution)/shard_map/ppermute | solution.py:426
  217.4 12.9 %collective-permute-start.17 = (bf16[2,128,1024]{2,1,0:T(8,128)(2,1)S(1)}, bf16[2,128,1024]{2,1,0:T(8,128)(2,1)}, u32[]{:S(2)}, u32[]{:S(2)}) collective-permute-start(bf16[2,128,1024]{2,1,0:T(8,128)(2,1)S(1)} %collective-permute-done.15), channel_id=1, source_target_pairs={{0,8},{1,9},{2,10},{3,11},{4,12},{5,13},{6,14},{7,15},{8,0},{9,1},... | collective-permute-start | bytes 1572872 | tf_op jit(solution)/shard_map/ppermute | solution.py:426
  232.0 25.6 %collective-permute-start.19 = (bf16[512,1024]{1,0:T(8,128)(2,1)S(1)}, bf16[512,1024]{1,0:T(8,128)(2,1)S(1)}, u32[]{:S(2)}, u32[]{:S(2)}) collective-permute-start(bf16[512,1024]{1,0:T(8,128)(2,1)S(1)} %get-tuple-element.262.rows_ref.near_ref), channel_id=1, source_target_pairs={{0,1},{1,0},{2,3},{3,2},{4,5},{5,4},{6,7},{7,6},{8,9},{9,8},{10,11... | collective-permute-start | bytes 3145736 | tf_op jit(solution)/shard_map/ppermute | solution.py:426
  232.5 28.8 %collective-permute-start.22 = (bf16[2,128,2048]{2,1,0:T(8,128)(2,1)S(1)}, bf16[2,128,2048]{2,1,0:T(8,128)(2,1)S(1)}, u32[]{:S(2)}, u32[]{:S(2)}) collective-permute-start(bf16[2,128,2048]{2,1,0:T(8,128)(2,1)S(1)} %broadcast_select_fusion.rest_0_), channel_id=1, source_target_pairs={{0,8},{1,9},{2,10},{3,11},{4,12},{5,13},{6,14},{7,15},{8,0},{9,1},... | collective-permute-start | bytes 3145736 | tf_op jit(solution)/shard_map/ppermute | solution.py:426
  233.8 28.0 %collective-permute-start.23 = (bf16[2,128,2048]{2,1,0:T(8,128)(2,1)S(1)}, bf16[2,128,2048]{2,1,0:T(8,128)(2,1)S(1)}, u32[]{:S(2)}, u32[]{:S(2)}) collective-permute-start(bf16[2,128,2048]{2,1,0:T(8,128)(2,1)S(1)} %broadcast_select_fusion.rest_0_), channel_id=1, source_target_pairs={{0,16},{1,17},{2,18},{3,19},{4,20},{5,21},{6,22},{7,23},{8,24},{9,... | collective-permute-start | bytes 3145736 | tf_op jit(solution)/shard_map/ppermute | solution.py:426
  259.9 27.3 %collective-permute-start.25 = (bf16[2,128,2048]{2,1,0:T(8,128)(2,1)}, bf16[2,128,2048]{2,1,0:T(8,128)(2,1)S(1)}, u32[]{:S(2)}, u32[]{:S(2)}) collective-permute-start(bf16[2,128,2048]{2,1,0:T(8,128)(2,1)} %collective-permute-done.16.rest_4_), channel_id=1, source_target_pairs={{0,8},{1,9},{2,10},{3,11},{4,12},{5,13},{6,14},{7,15},{8,0},{9,1},... | collective-permute-start | bytes 3145736 | tf_op jit(solution)/shard_map/ppermute | solution.py:426
  261.3 25.9 %collective-permute-start.26 = (bf16[2,128,2048]{2,1,0:T(8,128)(2,1)}, bf16[2,128,2048]{2,1,0:T(8,128)(2,1)S(1)}, u32[]{:S(2)}, u32[]{:S(2)}) collective-permute-start(bf16[2,128,2048]{2,1,0:T(8,128)(2,1)} %collective-permute-done.16.rest_4_), channel_id=1, source_target_pairs={{0,16},{1,17},{2,18},{3,19},{4,20},{5,21},{6,22},{7,23},{8,24},{9,... | collective-permute-start | bytes 3145736 | tf_op jit(solution)/shard_map/ppermute | solution.py:426
  261.8 25.4 %collective-permute-start.27 = (bf16[512,1024]{1,0:T(8,128)(2,1)S(1)}, bf16[512,1024]{1,0:T(8,128)(2,1)S(1)}, u32[]{:S(2)}, u32[]{:S(2)}) collective-permute-start(bf16[512,1024]{1,0:T(8,128)(2,1)S(1)} %copy-done.5), channel_id=1, source_target_pairs={{2,4},{3,5},{4,2},{5,3},{10,12},{11,13},{12,10},{13,11},{18,20},{1... | collective-permute-start | bytes 3145736 | tf_op jit(solution)/shard_map/ppermute | solution.py:439
  287.1 27.6 %collective-permute-start.29 = (bf16[512,1024]{1,0:T(8,128)(2,1)S(1)}, bf16[512,1024]{1,0:T(8,128)(2,1)S(1)}, u32[]{:S(2)}, u32[]{:S(2)}) collective-permute-start(bf16[512,1024]{1,0:T(8,128)(2,1)S(1)} %mix_far.3), channel_id=1, source_target_pairs={{0,1},{1,0},{2,3},{3,2},{4,5},{5,4},{6,7},{7,6},{8,9},{9,8},{10,11... | collective-permute-start | bytes 3145736 | tf_op jit(solution)/shard_map/ppermute | solution.py:426
  287.2 27.4 %collective-permute-start.31 = (bf16[2,128,2048]{2,1,0:T(8,128)(2,1)S(1)}, bf16[2,128,2048]{2,1,0:T(8,128)(2,1)S(1)}, u32[]{:S(2)}, u32[]{:S(2)}) collective-permute-start(bf16[2,128,2048]{2,1,0:T(8,128)(2,1)S(1)} %collective-permute-done.26.rest_6_), channel_id=1, source_target_pairs={{0,8},{1,9},{2,10},{3,11},{4,12},{5,13},{6,14},{7,15},{8,0},{9,1},... | collective-permute-start | bytes 3145736 | tf_op jit(solution)/shard_map/ppermute | solution.py:426
  290.9 23.8 %collective-permute-start.30 = (bf16[2,128,2048]{2,1,0:T(8,128)(2,1)S(1)}, bf16[2,128,2048]{2,1,0:T(8,128)(2,1)S(1)}, u32[]{:S(2)}, u32[]{:S(2)}) collective-permute-start(bf16[2,128,2048]{2,1,0:T(8,128)(2,1)S(1)} %collective-permute-done.22.rest_1_), channel_id=1, source_target_pairs={{0,16},{1,17},{2,18},{3,19},{4,20},{5,21},{6,22},{7,23},{8,24},{9,... | collective-permute-start | bytes 3145736 | tf_op jit(solution)/shard_map/ppermute | solution.py:426
  365.8 26.0 %collective-permute-start.37 = (bf16[512,1024]{1,0:T(8,128)(2,1)S(1)}, bf16[512,1024]{1,0:T(8,128)(2,1)S(1)}, u32[]{:S(2)}, u32[]{:S(2)}) collective-permute-start(bf16[512,1024]{1,0:T(8,128)(2,1)S(1)} %get-tuple-element.310.grad_ref.grad_near_ref), channel_id=1, source_target_pairs={{0,1},{1,0},{2,3},{3,2},{4,5},{5,4},{6,7},{7,6},{8,9},{9,8},{10,11... | collective-permute-start | bytes 3145736 | tf_op jit(solution)/shard_map/ppermute | solution.py:426
  374.8 47.5 %collective-permute-start.40 = (bf16[2,2,2,128,1024]{4,3,2,1,0:T(8,128)(2,1)S(1)}, bf16[2,2,2,128,1024]{4,3,2,1,0:T(8,128)(2,1)S(1)}, u32[]{:S(2)}, u32[]{:S(2)}) collective-permute-start(bf16[2,2,2,128,1024]{4,3,2,1,0:T(8,128)(2,1)S(1)} %get-tuple-element.325), channel_id=1, source_target_pairs={{0,16},{1,17},{2,18},{3,19},{4,20},{5,21},{6,22},{7,23},{8,24},{9,... | collective-permute-start | bytes 6291464 | tf_op jit(solution)/shard_map/ppermute | solution.py:426
  376.7 17.9 %collective-permute-start.38 = (bf16[512,256]{1,0:T(8,128)(2,1)S(1)}, bf16[512,256]{1,0:T(8,128)(2,1)S(1)}, u32[]{:S(2)}, u32[]{:S(2)}) collective-permute-start(bf16[512,256]{1,0:T(8,128)(2,1)S(1)} %get-tuple-element.317), channel_id=1, source_target_pairs={{0,4},{1,5},{2,6},{3,7},{4,0},{5,1},{6,2},{7,3},{8,12},{9,13},{10,... | collective-permute-start | bytes 786440 | tf_op jit(solution)/shard_map/ppermute | solution.py:426
  392.7 51.7 %collective-permute-start.34 = (bf16[512,1024]{1,0:T(8,128)(2,1)S(1)}, bf16[512,1024]{1,0:T(8,128)(2,1)S(1)}, u32[]{:S(2)}, u32[]{:S(2)}) collective-permute-start(bf16[512,1024]{1,0:T(8,128)(2,1)S(1)} %get-tuple-element.300), channel_id=1, source_target_pairs={{2,4},{3,5},{4,2},{5,3},{10,12},{11,13},{12,10},{13,11},{18,20},{1... | collective-permute-start | bytes 3145736 | tf_op jit(solution)/shard_map/ppermute | solution.py:439
  393.5 52.9 %collective-permute-start.43 = (bf16[2,2,2,128,1024]{4,3,2,1,0:T(8,128)(2,1)S(1)}, bf16[2,2,2,128,1024]{4,3,2,1,0:T(8,128)(2,1)S(1)}, u32[]{:S(2)}, u32[]{:S(2)}) collective-permute-start(bf16[2,2,2,128,1024]{4,3,2,1,0:T(8,128)(2,1)S(1)} %get-tuple-element.335), channel_id=1, source_target_pairs={{0,8},{1,9},{2,10},{3,11},{4,12},{5,13},{6,14},{7,15},{8,0},{9,1},... | collective-permute-start | bytes 6291464 | tf_op jit(solution)/shard_map/ppermute | solution.py:426
  446.5 25.5 %collective-permute-start.45 = (bf16[2,2,128,1024]{3,2,0,1:T(8,128)(2,1)}, bf16[2,2,128,1024]{3,2,0,1:T(8,128)(2,1)}, u32[]{:S(2)}, u32[]{:S(2)}) collective-permute-start(bf16[2,2,128,1024]{3,2,0,1:T(8,128)(2,1)} %copy.48), channel_id=1, source_target_pairs={{0,8},{1,9},{2,10},{3,11},{4,12},{5,13},{6,14},{7,15},{8,0},{9,1},... | collective-permute-start | bytes 3145736 | tf_op jit(solution)/shard_map/ppermute | solution.py:426
  448.1 25.5 %collective-permute-start.46 = (bf16[2,2,128,1024]{3,2,0,1:T(8,128)(2,1)}, bf16[2,2,128,1024]{3,2,0,1:T(8,128)(2,1)}, u32[]{:S(2)}, u32[]{:S(2)}) collective-permute-start(bf16[2,2,128,1024]{3,2,0,1:T(8,128)(2,1)} %copy.49), channel_id=1, source_target_pairs={{0,16},{1,17},{2,18},{3,19},{4,20},{5,21},{6,22},{7,23},{8,24},{9,... | collective-permute-start | bytes 3145736 | tf_op jit(solution)/shard_map/ppermute | solution.py:426
  453.0 26.8 %collective-permute-start.44 = (bf16[512,1024]{1,0:T(8,128)(2,1)}, bf16[512,1024]{1,0:T(8,128)(2,1)}, u32[]{:S(2)}, u32[]{:S(2)}) collective-permute-start(bf16[512,1024]{1,0:T(8,128)(2,1)} %unproject_far.2), channel_id=1, source_target_pairs={{0,1},{1,0},{2,3},{3,2},{4,5},{5,4},{6,7},{7,6},{8,9},{9,8},{10,11... | collective-permute-start | bytes 3145736 | tf_op jit(solution)/shard_map/ppermute | solution.py:426
  464.7 25.7 %collective-permute-start.47 = (bf16[4,2,128,1024]{2,3,1,0:T(8,128)(2,1)}, bf16[4,2,128,1024]{2,3,1,0:T(8,128)(2,1)}, u32[]{:S(2)}, u32[]{:S(2)}) collective-permute-start(bf16[4,2,128,1024]{2,3,1,0:T(8,128)(2,1)} %copy.55), channel_id=1, source_target_pairs={{0,4},{1,5},{2,6},{3,7},{4,0},{5,1},{6,2},{7,3},{8,12},{9,13},{10,... | collective-permute-start | bytes 6291464 | tf_op jit(solution)/shard_map/ppermute | solution.py:426
  490.2 28.5 %collective-permute-start.50 = (bf16[2,2,128,1024]{3,2,0,1:T(8,128)(2,1)}, bf16[2,2,128,1024]{3,2,0,1:T(8,128)(2,1)}, u32[]{:S(2)}, u32[]{:S(2)}) collective-permute-start(bf16[2,2,128,1024]{3,2,0,1:T(8,128)(2,1)} %pad_maximum_fusion.2), channel_id=1, source_target_pairs={{0,1},{1,0},{2,3},{3,2},{4,5},{5,4},{6,7},{7,6},{8,9},{9,8},{10,11... | collective-permute-start | bytes 3145736 | tf_op jit(solution)/shard_map/ppermute | solution.py:426
  494.4 26.2 %collective-permute-start.51 = (bf16[2,2,128,1024]{2,3,1,0:T(8,128)(2,1)}, bf16[2,2,128,1024]{2,3,1,0:T(8,128)(2,1)}, u32[]{:S(2)}, u32[]{:S(2)}) collective-permute-start(bf16[2,2,128,1024]{2,3,1,0:T(8,128)(2,1)} %get-tuple-element.452), channel_id=1, source_target_pairs={{0,16},{1,17},{2,18},{3,19},{4,20},{5,21},{6,22},{7,23},{8,24},{9,... | collective-permute-start | bytes 3145736 | tf_op jit(solution)/shard_map/ppermute | solution.py:426
  521.9 34.0 %collective-permute-start.55 = (bf16[2,128,1024]{1,2,0:T(8,128)(2,1)S(1)}, bf16[2,128,1024]{1,2,0:T(8,128)(2,1)S(1)}, u32[]{:S(2)}, u32[]{:S(2)}) collective-permute-start(bf16[2,128,1024]{1,2,0:T(8,128)(2,1)S(1)} %fusion.2), channel_id=1, source_target_pairs={{0,8},{1,9},{2,10},{3,11},{4,12},{5,13},{6,14},{7,15},{8,0},{9,1},... | collective-permute-start | bytes 1572872 | tf_op jit(solution)/shard_map/ppermute | solution.py:426
  529.6 25.3 %collective-permute-start.52 = (bf16[512,1024]{1,0:T(8,128)(2,1)S(1)}, bf16[512,1024]{1,0:T(8,128)(2,1)S(1)}, u32[]{:S(2)}, u32[]{:S(2)}) collective-permute-start(bf16[512,1024]{1,0:T(8,128)(2,1)S(1)} %get-tuple-element.360.grad_ref.grad_near_ref), channel_id=1, source_target_pairs={{0,1},{1,0},{2,3},{3,2},{4,5},{5,4},{6,7},{7,6},{8,9},{9,8},{10,11... | collective-permute-start | bytes 3145736 | tf_op jit(solution)/shard_map/ppermute | solution.py:426
  538.6 20.2 %collective-permute-start.53 = (bf16[512,256]{1,0:T(8,128)(2,1)S(1)}, bf16[512,256]{1,0:T(8,128)(2,1)S(1)}, u32[]{:S(2)}, u32[]{:S(2)}) collective-permute-start(bf16[512,256]{1,0:T(8,128)(2,1)S(1)} %get-tuple-element.367), channel_id=1, source_target_pairs={{0,4},{1,5},{2,6},{3,7},{4,0},{5,1},{6,2},{7,3},{8,12},{9,13},{10,... | collective-permute-start | bytes 786440 | tf_op jit(solution)/shard_map/ppermute | solution.py:426
  538.7 48.0 %collective-permute-start.56 = (bf16[2,2,2,128,1024]{4,3,2,1,0:T(8,128)(2,1)S(1)}, bf16[2,2,2,128,1024]{4,3,2,1,0:T(8,128)(2,1)S(1)}, u32[]{:S(2)}, u32[]{:S(2)}) collective-permute-start(bf16[2,2,2,128,1024]{4,3,2,1,0:T(8,128)(2,1)S(1)} %get-tuple-element.381), channel_id=1, source_target_pairs={{0,16},{1,17},{2,18},{3,19},{4,20},{5,21},{6,22},{7,23},{8,24},{9,... | collective-permute-start | bytes 6291464 | tf_op jit(solution)/shard_map/ppermute | solution.py:426
  548.2 60.6 %collective-permute-start.59 = (bf16[2,2,2,128,1024]{4,3,2,1,0:T(8,128)(2,1)S(1)}, bf16[2,2,2,128,1024]{4,3,2,1,0:T(8,128)(2,1)S(1)}, u32[]{:S(2)}, u32[]{:S(2)}) collective-permute-start(bf16[2,2,2,128,1024]{4,3,2,1,0:T(8,128)(2,1)S(1)} %get-tuple-element.391), channel_id=1, source_target_pairs={{0,8},{1,9},{2,10},{3,11},{4,12},{5,13},{6,14},{7,15},{8,0},{9,1},... | collective-permute-start | bytes 6291464 | tf_op jit(solution)/shard_map/ppermute | solution.py:426
  557.9 52.8 %collective-permute-start.60 = (bf16[2,128,1024]{2,1,0:T(8,128)(2,1)S(1)}, bf16[2,128,1024]{2,1,0:T(8,128)(2,1)S(1)}, u32[]{:S(2)}, u32[]{:S(2)}) collective-permute-start(bf16[2,128,1024]{2,1,0:T(8,128)(2,1)S(1)} %get-tuple-element.461), channel_id=1, source_target_pairs={{4,6},{5,7},{6,4},{7,5},{12,14},{13,15},{14,12},{15,13},{20,22},{2... | collective-permute-start | bytes 1572872 | tf_op jit(solution)/shard_map/ppermute | solution.py:431
  558.8 53.8 %collective-permute-start.61 = (bf16[2,128,1024]{2,1,0:T(8,128)(2,1)S(1)}, bf16[2,128,1024]{2,1,0:T(8,128)(2,1)S(1)}, u32[]{:S(2)}, u32[]{:S(2)}) collective-permute-start(bf16[2,128,1024]{2,1,0:T(8,128)(2,1)S(1)} %get-tuple-element.460), channel_id=1, source_target_pairs={{0,4},{1,5},{2,6},{3,7},{4,2},{5,3},{6,0},{7,1},{8,12},{9,13},{10,... | collective-permute-start | bytes 1572872 | tf_op jit(solution)/shard_map/ppermute | solution.py:431
  560.0 48.9 %collective-permute-start.62 = (bf16[128,1024]{0,1:T(8,128)(2,1)S(1)}, bf16[128,1024]{0,1:T(8,128)(2,1)S(1)}, u32[]{:S(2)}, u32[]{:S(2)}) collective-permute-start(bf16[128,1024]{0,1:T(8,128)(2,1)S(1)} %get-tuple-element.462), channel_id=1, source_target_pairs={{0,2},{1,3},{2,0},{3,1},{4,6},{5,7},{6,4},{7,5},{8,10},{9,11},{10,... | collective-permute-start | bytes 786440 | tf_op jit(solution)/shard_map/ppermute | solution.py:426
  586.8 33.0 %collective-permute-start.57 = (bf16[3,1024,128]{2,1,0:T(8,128)(2,1)}, bf16[3,1024,128]{2,1,0:T(8,128)(2,1)}, u32[]{:S(2)}, u32[]{:S(2)}) collective-permute-start(bf16[3,1024,128]{2,1,0:T(8,128)(2,1)} %get-tuple-element.388), channel_id=1, source_target_pairs={{0,4},{1,5},{2,6},{3,7},{4,0},{5,1},{6,2},{7,3},{8,12},{9,13},{10,... | collective-permute-start | bytes 2359304 | tf_op jit(solution)/shard_map/ppermute | solution.py:426
  608.8 25.8 %collective-permute-start.64 = (bf16[2,2,128,1024]{3,2,1,0:T(8,128)(2,1)}, bf16[2,2,128,1024]{3,2,1,0:T(8,128)(2,1)}, u32[]{:S(2)}, u32[]{:S(2)}) collective-permute-start(bf16[2,2,128,1024]{3,2,1,0:T(8,128)(2,1)} %bitcast_add_fusion.1), channel_id=1, source_target_pairs={{0,8},{1,9},{2,10},{3,11},{4,12},{5,13},{6,14},{7,15},{8,0},{9,1},... | collective-permute-start | bytes 3145736 | tf_op jit(solution)/shard_map/ppermute | solution.py:426
  610.8 25.9 %collective-permute-start.65 = (bf16[2,2,128,1024]{3,2,1,0:T(8,128)(2,1)}, bf16[2,2,128,1024]{3,2,1,0:T(8,128)(2,1)}, u32[]{:S(2)}, u32[]{:S(2)}) collective-permute-start(bf16[2,2,128,1024]{3,2,1,0:T(8,128)(2,1)} %bitcast_add_fusion), channel_id=1, source_target_pairs={{0,16},{1,17},{2,18},{3,19},{4,20},{5,21},{6,22},{7,23},{8,24},{9,... | collective-permute-start | bytes 3145736 | tf_op jit(solution)/shard_map/ppermute | solution.py:426
  627.1 25.3 %collective-permute-start.63 = (bf16[512,1024]{1,0:T(8,128)(2,1)S(1)}, bf16[512,1024]{1,0:T(8,128)(2,1)S(1)}, u32[]{:S(2)}, u32[]{:S(2)}) collective-permute-start(bf16[512,1024]{1,0:T(8,128)(2,1)S(1)} %unproject_far.3), channel_id=1, source_target_pairs={{0,1},{1,0},{2,3},{3,2},{4,5},{5,4},{6,7},{7,6},{8,9},{9,8},{10,11... | collective-permute-start | bytes 3145736 | tf_op jit(solution)/shard_map/ppermute | solution.py:426
  (147 other events, 1219.3 us)

commit v8 on v7

--- a/solution.py
+++ b/solution.py
@@ -550,21 +550,26 @@
         acc_ref[head] = acc_ref[head] * jnp.exp(old - new) + dot_nn(vt, weights)
         max_ref[head] = new
 
+    def absorb_both(both, place, rows):
+        olds = [max_ref[head] for head in range(2)]
+        news = [jnp.maximum(olds[head], jnp.max(both[head], axis=0, keepdims=True)) for head in range(2)]
+        weights = [jnp.exp(both[head] - news[head]).astype(BF) for head in range(2)]
+        terms = [dot_nn(vt_ref[head, :, pl.ds(place, rows)], weights[head]) for head in range(2)]
+        for head in range(2):
+            acc_ref[head] = acc_ref[head] * jnp.exp(olds[head] - news[head]) + terms[head]
+            max_ref[head] = news[head]
+
     def full(index, carry):
         place = at(index)
         keys = k_ref[pl.ds(place, block), :]
         slant = ramp(block, index * block, first)
-        for head in range(2):
-            absorb(head, dot_nt(keys, heads[head]) + slopes[head] * slant, vt_ref[head, :, pl.ds(place, block)])
+        both = [dot_nt(keys, heads[head]) + slopes[head] * slant for head in range(2)]
+        absorb_both(both, place, block)
         return carry
 
     place = at(step)
-    for head in range(2):
-        absorb(
-            head,
-            dot_nt(k_ref[pl.ds(place, block), :], heads[head]) + slopes[head] * bias_ref[...],
-            vt_ref[head, :, pl.ds(place, block)],
-        )
+    keys = k_ref[pl.ds(place, block), :]
+    absorb_both([dot_nt(keys, heads[head]) + slopes[head] * bias_ref[...] for head in range(2)], place, block)
     lax.fori_loop(0, step, full, 0)
     edge = first + block
 
@@ -691,14 +696,18 @@
         values = v_ref[pl.ds(place, rows), :]
         dk = dk_acc[pl.ds(place, rows), :]
         dv = dv_acc[pl.ds(place, rows), :]
+        scores = [dot_nt(keys, q_heads[head]) + slopes[head] * bias_of for head in range(2)]
+        grad_p = [dot_nt(values, g_heads[head]) for head in range(2)]
+        weights = [jnp.exp(scores[head] - log_total[head:head + 1, :]) for head in range(2)]
+        grad_s = [(weights[head] * (grad_p[head] - deltas[head])).astype(BF) for head in range(2)]
+        dv = dv + dot_nn(
+            jnp.concatenate([weights[head].astype(BF) for head in range(2)], axis=1), jnp.concatenate(g_heads, axis=0)
+        )
+        dk = dk + dot_nn(jnp.concatenate(grad_s, axis=1), jnp.concatenate(q_heads, axis=0))
         for head in range(2):
-            scores = dot_nt(keys, q_heads[head]) + slopes[head] * bias_of
-            weights = jnp.exp(scores - log_total[head:head + 1, :])
-            dv = dv + dot_nn(weights.astype(BF), g_heads[head])
-            grad_p = dot_nt(values, g_heads[head])
-            grad_s = (weights * (grad_p - deltas[head])).astype(BF)
-            dk = dk + dot_nn(grad_s, q_heads[head])
-            dqt_ref[head * HD:(head + 1) * HD, :] += dot_nn(kt_ref[head * HD:(head + 1) * HD, pl.ds(place, rows)], grad_s)
+            dqt_ref[head * HD:(head + 1) * HD, :] += dot_nn(
+                kt_ref[head * HD:(head + 1) * HD, pl.ds(place, rows)], grad_s[head]
+            )
         dk_acc[pl.ds(place, rows), :] = dk
         dv_acc[pl.ds(place, rows), :] = dv
 

time: 745 us -> 741 us (level)
  Pallas kernels: 437 us -> 422 us
  waiting for transfers between devices: 121 us -> 131 us
    ppermute x61, waiting for transfers between devices: 121 us -> 131 us  [swap(): return lax.ppermute(values, AXES, [(i, i ^ mask) for i in range(32)])]
    pallas_call x4, Pallas kernels: 65.7 us -> 57 us  [attend(): pl.pallas_call(functools.partial(attend_kernel, block, rest_bit), grid=(p...]
  transfers between devices with their start and end apart: 66 -> 66, of which waited for: 24 -> 27; matrix products, arithmetic and copies ran while one was open for 6% -> 6% of each run, Pallas kernels for 34% -> 32%
where the time goes in v8:
time: 741 us; the launch traced here: 729 us
  Pallas kernels  422 us (57%)
  waiting for transfers between devices  131 us (18%)
  local copies, waits for them, and re-layouts  72.6 us (10%)
  starting transfers between devices  67 us (9%)
  other arithmetic  33.9 us (5%)
    ppermute x61, waiting for transfers between devices, swap(): return lax.ppermute(values, AXES, [(i, i ^ mask) for i in range(32)])  131 us
    pallas_call x1, Pallas kernels, start(): pl.pallas_call(functools.partial(start_kernel, layers), in_specs=[hbm] *...  87.6 us
    pallas_call x4, Pallas kernels, attend_pull(): pl.pallas_call(functools.partial(pull_kernel, block, pair), grid=(4,), in...  74.8 us
    pallas_call x1, Pallas kernels, finish(): pl.pallas_call(functools.partial(finish_kernel, layers), in_specs=[vmem]...  64.2 us
    ppermute x61, starting transfers between devices, swap(): return lax.ppermute(values, AXES, [(i, i ^ mask) for i in range(32)])  62.7 us
    pallas_call x4, Pallas kernels, attend(): pl.pallas_call(functools.partial(attend_kernel, block, rest_bit), grid=(p...  57 us
    unnamed x260, local copies, waits for them, and re-layouts  52.8 us
    pallas_call x20, Pallas kernels, call_once(): pl.pallas_call(kernel, in_specs=placed(args), out_specs=placed(outs), out...  46.4 us
  transfers between devices with their start and end apart: 66, of which 27 were waited for; matrix products, arithmetic and copies ran while one was open for 6% of the time, Pallas kernels for 32%

profile of v8, /device:TPU:0, one launch (start us, length us, event | category | flops | bytes accessed | tf_op | source)
XLA Modules:
  0.0 729.1 jit_solution(16184226747128762082)
XLA Ops:
  3.2 87.6 %start.1 = (f32[512,1024]{1,0:T(8,128)}, bf16[512,1024]{1,0:T(8,128)(2,1)}, bf16[512,1024]{1,0:T(8,128)(2,1)}, bf16[4,2,128,1024]{3,2,1,0:T(8,128)(2,1)}, bf16[4...) custom-call(bf16[512,1024]{1,0:T(8,128)(2,1)} %x_ref.1, ...), custom_call_target="tpu_custom_call" | custom-call | flops 30000001024 | bytes 1 | tf_op jit(solution)/shard_map/start/pallas_call | solution.py:1507
  99.0 16.4 %attend.4 = (bf16[512,256]{1,0:T(8,128)(2,1)S(1)}, bf16[512,256]{1,0:T(8,128)(2,1)S(1)}, f32[256,1024]{1,0:T(8,128)S(1)}, f32[2,8,1024]{2,1,0:T(8,128)S(1)}) custom-call(f32[4]{0:T(128)S(1)} %multiply_exponential_fusion.slope_ref, s32[2]{0:T(128)S(1)} %convert_bitcast_fusion.start_ref, s32[1]{0:T(128)} %bitcast.3.me_ref, bf16[512,768]{1,0:T(8,128)(2,1)S(1)} %copy-done.95, ...), custom_call_target="tpu_custom_call" | custom-call | flops 8499999744 | bytes 1 | tf_op jit(solution)/shard_map/attend/pallas_call | solution.py:619
  120.1 12.1 %attend.5 = (bf16[512,256]{1,0:T(8,128)(2,1)S(1)}, bf16[512,256]{1,0:T(8,128)(2,1)S(1)}, f32[256,1024]{1,0:T(8,128)S(1)}, f32[2,8,1024]{2,1,0:T(8,128)S(1)}) custom-call(f32[4]{0:T(128)S(1)} %multiply_exponential_fusion.slope_ref, s32[2]{0:T(128)S(1)} %convert_bitcast_fusion.start_ref, s32[1]{0:T(128)} %bitcast.3.me_ref, bf16[512,768]{1,0:T(8,128)(2,1)S(1)} %copy-done.95, ...), custom_call_target="tpu_custom_call" | custom-call | flops 8499999744 | bytes 1 | tf_op jit(solution)/shard_map/attend/pallas_call | solution.py:619
  134.0 5.1 collective-permute-start.4
  139.1 5.6 collective-permute-done.6.rest_5_
  157.9 11.1 %collective-permute-done.11 = bf16[128,1024]{1,0:T(8,128)(2,1)} collective-permute-done((bf16[128,1024]{1,0:T(8,128)(2,1)S(1)}, bf16[128,1024]{1,0:T(8,128)(2,1)}, u32[]{:S(2)}, u32[]{:S(2)}) %collective-permute-start.11) | collective-permute-done | bytes 262176 | tf_op jit(solution)/shard_map/ppermute | solution.py:426
  175.1 15.5 %mlp_forward.2 = (bf16[1024,2048]{1,0:T(8,128)(2,1)S(1)}, bf16[1024,2048]{1,0:T(8,128)(2,1)S(1)}, f32[512,1024]{1,0:T(8,128)S(1)}, bf16[512,1024]{1,0:T(8,128)(2,1)}) custom-call(s32[1]{0:T(128)} %constant.10.clone.1.rest_2_.turn_ref.rest_6_.rest_10_, bf16[512,1024]{1,0:T(8,128)(2,1)S(1)} %copy-done.63, bf16[512,1024]{1,0:T(8,128)(2,1)} %collective-permute-done.12.other_ref, ...), custom_call_target="tpu_custom_call" | custom-call | flops 8999999488 | bytes 1 | tf_op jit(solution)/shard_map/mlp_forward/pallas_call | solution.py:1056
  195.9 5.6 collective-permute-start.13
  202.8 12.6 %collective-permute-done.14 = bf16[2,128,1024]{2,1,0:T(8,128)(2,1)S(1)} collective-permute-done((bf16[2,128,1024]{2,1,0:T(8,128)(2,1)S(1)}, bf16[2,128,1024]{2,1,0:T(8,128)(2,1)S(1)}, u32[]{:S(2)}, u32[]{:S(2)}) %collective-permute-start.14) | collective-permute-done | bytes 524320 | tf_op jit(solution)/shard_map/ppermute | solution.py:426
  221.9 7.0 collective-permute-done.17
  236.6 19.6 %collective-permute-done.19.rows_ref.far_ref = bf16[512,1024]{1,0:T(8,128)(2,1)S(1)} collective-permute-done((bf16[512,1024]{1,0:T(8,128)(2,1)S(1)}, bf16[512,1024]{1,0:T(8,128)(2,1)S(1)}, u32[]{:S(2)}, u32[]{:S(2)}) %collective-permute-start.19) | collective-permute-done | bytes 1048608 | tf_op jit(solution)/shard_map/ppermute | solution.py:426
  261.0 16.4 %attend.6 = (bf16[512,256]{1,0:T(8,128)(2,1)S(1)}, bf16[512,256]{1,0:T(8,128)(2,1)S(1)}, f32[256,1024]{1,0:T(8,128)S(1)}, f32[2,8,1024]{2,1,0:T(8,128)S(1)}) custom-call(f32[4]{0:T(128)S(1)} %multiply_exponential_fusion.slope_ref, s32[2]{0:T(128)S(1)} %convert_bitcast_fusion.start_ref, s32[1]{0:T(128)} %bitcast.3.me_ref, ...), custom_call_target="tpu_custom_call" | custom-call | flops 8499999744 | bytes 1 | tf_op jit(solution)/shard_map/attend/pallas_call | solution.py:619
  277.5 4.6 collective-permute-start.24
  289.0 12.1 %attend.7 = (bf16[512,256]{1,0:T(8,128)(2,1)S(1)}, bf16[512,256]{1,0:T(8,128)(2,1)S(1)}, f32[256,1024]{1,0:T(8,128)S(1)}, f32[2,8,1024]{2,1,0:T(8,128)S(1)}) custom-call(f32[4]{0:T(128)S(1)} %multiply_exponential_fusion.slope_ref, s32[2]{0:T(128)S(1)} %convert_bitcast_fusion.start_ref, s32[1]{0:T(128)} %bitcast.3.me_ref, ...), custom_call_target="tpu_custom_call" | custom-call | flops 8499999744 | bytes 1 | tf_op jit(solution)/shard_map/attend/pallas_call | solution.py:619
  301.2 4.5 collective-permute-start.28
  305.7 5.6 collective-permute-done.30.rest_3_
  318.0 13.4 %mlp_forward.3 = (bf16[1024,2048]{1,0:T(8,128)(2,1)S(1)}, bf16[1024,2048]{1,0:T(8,128)(2,1)S(1)}, f32[512,1024]{1,0:T(8,128)S(1)}, bf16[512,1024]{1,0:T(8,128)(2,1)S(1)}) custom-call(s32[1]{0:T(128)} %constant.10.clone.1.rest_2_.turn_ref.rest_6_.rest_10_, bf16[512,1024]{1,0:T(8,128)(2,1)S(1)} %get-tuple-element.295.normed_ref.left_ref, ...), custom_call_target="tpu_custom_call" | custom-call | flops 8999999488 | bytes 1 | tf_op jit(solution)/shard_map/mlp_forward/pallas_call | solution.py:1056
  340.6 16.7 %mlp_backward.2 = (bf16[1024,2048]{1,0:T(8,128)(2,1)S(1)}, f32[1,2048]{1,0:T(1,128)S(1)}, f32[512,1024]{1,0:T(8,128)S(1)}, bf16[512,1024]{1,0:T(8,128)(2,1)S(1)}) custom-call(s32[1]{0:T(128)} %constant.10.clone.1.rest_2_.turn_ref.rest_6_.rest_10_, f32[512,1024]{1,0:T(8,128)S(1)} %get-tuple-element.301.grad_ref.left_ref, ...), custom_call_target="tpu_custom_call" | custom-call | flops 11000000512 | bytes 1 | tf_op jit(solution)/shard_map/mlp_backward/pallas_call | solution.py:1134
  364.4 6.4 unit_grads.4
  373.3 6.6 unit_grads.5
  379.9 8.7 %collective-permute-done.37.grad_ref.grad_far_ref = bf16[512,1024]{1,0:T(8,128)(2,1)S(1)} collective-permute-done((bf16[512,1024]{1,0:T(8,128)(2,1)S(1)}, bf16[512,1024]{1,0:T(8,128)(2,1)S(1)}, u32[]{:S(2)}, u32[]{:S(2)}) %collective-permute-start.37) | collective-permute-done | bytes 1048608 | tf_op jit(solution)/shard_map/ppermute | solution.py:426
  391.5 18.1 %attend_pull.4 = (bf16[3,1024,128]{2,1,0:T(8,128)(2,1)S(1)}, bf16[3,1024,128]{2,1,0:T(8,128)(2,1)S(1)}) custom-call(f32[4]{0:T(128)S(1)} %multiply_exponential_fusion.slope_ref, s32[2]{0:T(128)S(1)} %convert_bitcast_fusion.start_ref, s32[1]{0:T(128)} %bitcast.3.me_ref, bf16[512,768]{1,0:T(8,128)(2,1)S(1)} %copy-done.68, bf16[512,768]{1,0:T(8,128)(2,1)S(1)} %copy-done.68, ...), custom_call_target="tpu_custom_call" | custom-call | flops 11000000512 | bytes 1 | tf_op jit(solution)/shard_map/attend_pull/pallas_call | solution.py:756
  409.7 8.9 %collective-permute-done.40 = bf16[2,2,2,128,1024]{4,3,2,1,0:T(8,128)(2,1)S(1)} collective-permute-done((bf16[2,2,2,128,1024]{4,3,2,1,0:T(8,128)(2,1)S(1)}, bf16[2,2,2,128,1024]{4,3,2,1,0:T(8,128)(2,1)S(1)}, u32[]{:S(2)}, u32[]{:S(2)}) %collective-permute-start.40) | collective-permute-done | bytes 2097184 | tf_op jit(solution)/shard_map/ppermute | solution.py:426
  420.0 18.4 %attend_pull.5 = (bf16[3,1024,128]{2,1,0:T(8,128)(2,1)S(1)}, bf16[3,1024,128]{2,1,0:T(8,128)(2,1)S(1)}) custom-call(f32[4]{0:T(128)S(1)} %multiply_exponential_fusion.slope_ref, s32[2]{0:T(128)S(1)} %convert_bitcast_fusion.start_ref, s32[1]{0:T(128)} %bitcast.3.me_ref, bf16[512,768]{1,0:T(8,128)(2,1)S(1)} %copy-done.68, bf16[512,768]{1,0:T(8,128)(2,1)S(1)} %copy-done.68, ...), custom_call_target="tpu_custom_call" | custom-call | flops 11000000512 | bytes 1 | tf_op jit(solution)/shard_map/attend_pull/pallas_call | solution.py:756
  441.1 3.4 collective-permute-start.45
  445.7 2.8 unproject_far.2
  449.1 4.9 head_grads.2
  456.6 3.9 copy.55
  460.5 7.7 %collective-permute-done.45 = bf16[2,2,128,1024]{3,2,0,1:T(8,128)(2,1)} collective-permute-done((bf16[2,2,128,1024]{3,2,0,1:T(8,128)(2,1)}, bf16[2,2,128,1024]{3,2,0,1:T(8,128)(2,1)}, u32[]{:S(2)}, u32[]{:S(2)}) %collective-permute-start.45) | collective-permute-done | bytes 1048608 | tf_op jit(solution)/shard_map/ppermute | solution.py:426
  468.2 2.7 collective-permute-done.46
  470.9 5.1 fusion.4
  478.0 4.1 unproject_near.2
  483.5 4.0 copy.54
  488.0 3.9 slice_add_fusion
  495.1 17.1 %mlp_backward.3 = (bf16[1024,2048]{1,0:T(8,128)(2,1)S(1)}, f32[1,2048]{1,0:T(1,128)S(1)}, f32[512,1024]{1,0:T(8,128)S(1)}, bf16[512,1024]{1,0:T(8,128)(2,1)S(1)}) custom-call(s32[1]{0:T(128)} %constant.10.clone.1.rest_2_.turn_ref.rest_6_.rest_10_, f32[512,1024]{1,0:T(8,128)S(1)} %copy-done.47, bf16[512,1024]{1,0:T(8,128)(2,1)S(1)} %collective-permute-done.48.other_ref, ...), custom_call_target="tpu_custom_call" | custom-call | flops 11000000512 | bytes 1 | tf_op jit(solution)/shard_map/mlp_backward/pallas_call | solution.py:1134
  528.1 6.4 unit_grads.6
  537.1 7.8 %unit_grads.7 = (bf16[2,2,128,1024]{3,2,1,0:T(8,128)(2,1)S(1)}, bf16[2,2,2,128,1024]{4,3,2,1,0:T(8,128)(2,1)S(1)}, bf16[2,2,128,1024]{3,2,1,0:T(8,128)(2,1)S(1)}) custom-call(bf16[512,1024]{1,0:T(8,128)(2,1)S(1)} %copy-done.64, bf16[512,1024]{1,0:T(8,128)(2,1)} %collective-permute-done.12.other_ref, bf16[1024,2048]{1,0:T(8,128)(2,1)S(1)} %copy-done.76), custom_call_target="tpu_custom_call" | custom-call | flops 5000000000 | bytes 1 | tf_op jit(solution)/shard_map/unit_grads/pallas_call | solution.py:1196
  546.2 5.5 collective-permute-done.52.grad_ref.grad_far_ref
  559.4 19.0 %attend_pull.6 = (bf16[3,1024,128]{2,1,0:T(8,128)(2,1)S(1)}, bf16[3,1024,128]{2,1,0:T(8,128)(2,1)}) custom-call(f32[4]{0:T(128)S(1)} %multiply_exponential_fusion.slope_ref, s32[2]{0:T(128)S(1)} %convert_bitcast_fusion.start_ref, s32[1]{0:T(128)} %bitcast.3.me_ref, bf16[512,768]{1,0:T(8,128)(2,1)S(1)} %copy-done.96, bf16[512,768]{1,0:T(8,128)(2,1)S(1)} %copy-done.96, ...), custom_call_target="tpu_custom_call" | custom-call | flops 11000000512 | bytes 1 | tf_op jit(solution)/shard_map/attend_pull/pallas_call | solution.py:756
  579.3 4.1 collective-permute-done.56
  584.6 19.2 %attend_pull.7 = (bf16[3,1024,128]{2,1,0:T(8,128)(2,1)S(1)}, bf16[3,1024,128]{2,1,0:T(8,128)(2,1)}) custom-call(f32[4]{0:T(128)S(1)} %multiply_exponential_fusion.slope_ref, s32[2]{0:T(128)S(1)} %convert_bitcast_fusion.start_ref, s32[1]{0:T(128)} %bitcast.3.me_ref, bf16[512,768]{1,0:T(8,128)(2,1)S(1)} %copy-done.96, bf16[512,768]{1,0:T(8,128)(2,1)S(1)} %copy-done.96, ...), custom_call_target="tpu_custom_call" | custom-call | flops 11000000512 | bytes 1 | tf_op jit(solution)/shard_map/attend_pull/pallas_call | solution.py:756
  603.9 3.3 collective-permute-start.64
  619.7 3.4 unproject_far.3
  623.8 6.4 head_grads.3
  631.3 3.1 collective-permute-done.65
  638.1 10.5 %collective-permute-done.63.rest_4_ = bf16[512,1024]{1,0:T(8,128)(2,1)S(1)} collective-permute-done((bf16[512,1024]{1,0:T(8,128)(2,1)S(1)}, bf16[512,1024]{1,0:T(8,128)(2,1)S(1)}, u32[]{:S(2)}, u32[]{:S(2)}) %collective-permute-start.63) | collective-permute-done | bytes 1048608 | tf_op jit(solution)/shard_map/ppermute | solution.py:426
  648.6 5.7 unproject_near.3
  654.3 64.2 %finish.1 = (bf16[512,1024]{1,0:T(8,128)(2,1)S(1)}, f32[3,128,256]{2,1,0:T(8,128)S(1)}, f32[256,128]{1,0:T(8,128)S(1)}, f32[1024,128]{1,0:T(8,128)S(1)}, f32[128,1024]{1,0:T(8,128)S(1)}, /*index=5*/f32[24,128]{1,0:T(8,128)S(1)}) custom-call(bf16[512,1024]{1,0:T(8,128)(2,1)S(1)} %get-tuple-element.405.grad_ref, ...), custom_call_target="tpu_custom_call" | custom-call | flops 24999999488 | bytes 1 | tf_op jit(solution)/shard_map/finish/pallas_call | solution.py:1707
  (435 shorter events, 170.1 us)
Async XLA Ops:
  90.7 28.1 %collective-permute-start.1 = (bf16[2,128,2048]{2,1,0:T(8,128)(2,1)}, bf16[2,128,2048]{2,1,0:T(8,128)(2,1)S(1)}, u32[]{:S(2)}, u32[]{:S(2)}) collective-permute-start(bf16[2,128,2048]{2,1,0:T(8,128)(2,1)} %get-tuple-element.227.rest_0_), channel_id=1, source_target_pairs={{0,8},{1,9},{2,10},{3,11},{4,12},{5,13},{6,14},{7,15},{8,0},{9,1},... | collective-permute-start | bytes 3145736 | tf_op jit(solution)/shard_map/ppermute | solution.py:426
  92.3 26.6 %collective-permute-start.2 = (bf16[2,128,2048]{2,1,0:T(8,128)(2,1)}, bf16[2,128,2048]{2,1,0:T(8,128)(2,1)S(1)}, u32[]{:S(2)}, u32[]{:S(2)}) collective-permute-start(bf16[2,128,2048]{2,1,0:T(8,128)(2,1)} %get-tuple-element.227.rest_0_), channel_id=1, source_target_pairs={{0,16},{1,17},{2,18},{3,19},{4,20},{5,21},{6,22},{7,23},{8,24},{9,... | collective-permute-start | bytes 3145736 | tf_op jit(solution)/shard_map/ppermute | solution.py:426
  93.8 25.3 %collective-permute-start.3 = (bf16[2,128,2048]{2,1,0:T(8,128)(2,1)}, bf16[2,128,2048]{2,1,0:T(8,128)(2,1)}, u32[]{:S(2)}, u32[]{:S(2)}) collective-permute-start(bf16[2,128,2048]{2,1,0:T(8,128)(2,1)} %get-tuple-element.227.rest_0_), channel_id=1, source_target_pairs={{0,1},{1,0},{2,3},{3,2},{4,5},{5,4},{6,7},{7,6},{8,9},{9,8},{10,11... | collective-permute-start | bytes 3145736 | tf_op jit(solution)/shard_map/ppermute | solution.py:426
  118.8 31.6 %collective-permute-start.5 = (bf16[512,1024]{1,0:T(8,128)(2,1)S(1)}, bf16[512,1024]{1,0:T(8,128)(2,1)S(1)}, u32[]{:S(2)}, u32[]{:S(2)}) collective-permute-start(bf16[512,1024]{1,0:T(8,128)(2,1)S(1)} %mix_far.2), channel_id=1, source_target_pairs={{0,1},{1,0},{2,3},{3,2},{4,5},{5,4},{6,7},{7,6},{8,9},{9,8},{10,11... | collective-permute-start | bytes 3145736 | tf_op jit(solution)/shard_map/ppermute | solution.py:426
  119.1 25.5 %collective-permute-start.6 = (bf16[2,128,2048]{2,1,0:T(8,128)(2,1)}, bf16[2,128,2048]{2,1,0:T(8,128)(2,1)S(1)}, u32[]{:S(2)}, u32[]{:S(2)}) collective-permute-start(bf16[2,128,2048]{2,1,0:T(8,128)(2,1)} %collective-permute-done.3.rest_4_), channel_id=1, source_target_pairs={{0,8},{1,9},{2,10},{3,11},{4,12},{5,13},{6,14},{7,15},{8,0},{9,1},... | collective-permute-start | bytes 3145736 | tf_op jit(solution)/shard_map/ppermute | solution.py:426
  120.1 28.1 %collective-permute-start.7 = (bf16[2,128,2048]{2,1,0:T(8,128)(2,1)}, bf16[2,128,2048]{2,1,0:T(8,128)(2,1)}, u32[]{:S(2)}, u32[]{:S(2)}) collective-permute-start(bf16[2,128,2048]{2,1,0:T(8,128)(2,1)} %collective-permute-done.3.rest_4_), channel_id=1, source_target_pairs={{0,16},{1,17},{2,18},{3,19},{4,20},{5,21},{6,22},{7,23},{8,24},{9,... | collective-permute-start | bytes 3145736 | tf_op jit(solution)/shard_map/ppermute | solution.py:426
  133.2 23.7 %collective-permute-start.10 = (bf16[2,128,2048]{2,1,0:T(8,128)(2,1)}, bf16[2,128,2048]{2,1,0:T(8,128)(2,1)S(1)}, u32[]{:S(2)}, u32[]{:S(2)}) collective-permute-start(bf16[2,128,2048]{2,1,0:T(8,128)(2,1)} %bitcast.5), channel_id=1, source_target_pairs={{4,6},{5,7},{6,4},{7,5},{12,14},{13,15},{14,12},{15,13},{20,22},{2... | collective-permute-start | bytes 3145736 | tf_op jit(solution)/shard_map/ppermute | solution.py:431
  134.0 17.5 %collective-permute-start.4 = (bf16[512,256]{1,0:T(8,128)(2,1)S(1)}, bf16[512,256]{1,0:T(8,128)(2,1)S(1)}, u32[]{:S(2)}, u32[]{:S(2)}) collective-permute-start(bf16[512,256]{1,0:T(8,128)(2,1)S(1)} %get-tuple-element.236), channel_id=1, source_target_pairs={{0,4},{1,5},{2,6},{3,7},{4,0},{5,1},{6,2},{7,3},{8,12},{9,13},{10,... | collective-permute-start | bytes 786440 | tf_op jit(solution)/shard_map/ppermute | solution.py:426
  145.6 23.4 %collective-permute-start.11 = (bf16[128,1024]{1,0:T(8,128)(2,1)S(1)}, bf16[128,1024]{1,0:T(8,128)(2,1)}, u32[]{:S(2)}, u32[]{:S(2)}) collective-permute-start(bf16[128,1024]{1,0:T(8,128)(2,1)S(1)} %bitcast.122), channel_id=1, source_target_pairs={{0,2},{1,3},{2,0},{3,1},{4,6},{5,7},{6,4},{7,5},{8,10},{9,11},{10,... | collective-permute-start | bytes 786440 | tf_op jit(solution)/shard_map/ppermute | solution.py:426
  148.3 26.8 %collective-permute-start.9 = (bf16[2,128,2048]{2,1,0:T(8,128)(2,1)}, bf16[2,128,2048]{2,1,0:T(8,128)(2,1)}, u32[]{:S(2)}, u32[]{:S(2)}) collective-permute-start(bf16[2,128,2048]{2,1,0:T(8,128)(2,1)} %collective-permute-done.7.rest_6_), channel_id=1, source_target_pairs={{0,8},{1,9},{2,10},{3,11},{4,12},{5,13},{6,14},{7,15},{8,0},{9,1},... | collective-permute-start | bytes 3145736 | tf_op jit(solution)/shard_map/ppermute | solution.py:426
  150.3 24.7 %collective-permute-start.8 = (bf16[2,128,2048]{2,1,0:T(8,128)(2,1)S(1)}, bf16[2,128,2048]{2,1,0:T(8,128)(2,1)}, u32[]{:S(2)}, u32[]{:S(2)}) collective-permute-start(bf16[2,128,2048]{2,1,0:T(8,128)(2,1)S(1)} %collective-permute-done.1.rest_1_), channel_id=1, source_target_pairs={{0,16},{1,17},{2,18},{3,19},{4,20},{5,21},{6,22},{7,23},{8,24},{9,... | collective-permute-start | bytes 3145736 | tf_op jit(solution)/shard_map/ppermute | solution.py:426
  156.9 18.1 %collective-permute-start.12 = (bf16[512,1024]{1,0:T(8,128)(2,1)}, bf16[512,1024]{1,0:T(8,128)(2,1)}, u32[]{:S(2)}, u32[]{:S(2)}) collective-permute-start(bf16[512,1024]{1,0:T(8,128)(2,1)} %get-tuple-element.254), channel_id=1, source_target_pairs={{0,4},{1,5},{2,6},{3,7},{4,0},{5,1},{6,2},{7,3},{8,12},{9,13},{10,... | collective-permute-start | bytes 3145736 | tf_op jit(solution)/shard_map/ppermute | solution.py:426
  170.6 46.6 %collective-permute-start.16 = (bf16[2,128,2048]{2,1,0:T(8,128)(2,1)S(1)}, bf16[2,128,2048]{2,1,0:T(8,128)(2,1)}, u32[]{:S(2)}, u32[]{:S(2)}) collective-permute-start(bf16[2,128,2048]{2,1,0:T(8,128)(2,1)S(1)} %broadcast_select_fusion.rest_0_), channel_id=1, source_target_pairs={{0,1},{1,0},{2,3},{3,2},{4,5},{5,4},{6,7},{7,6},{8,9},{9,8},{10,11... | collective-permute-start | bytes 3145736 | tf_op jit(solution)/shard_map/ppermute | solution.py:426
  195.9 21.3 %collective-permute-start.13 = (bf16[512,1024]{1,0:T(8,128)(2,1)}, bf16[512,1024]{1,0:T(8,128)(2,1)S(1)}, u32[]{:S(2)}, u32[]{:S(2)}) collective-permute-start(bf16[512,1024]{1,0:T(8,128)(2,1)} %get-tuple-element.257), channel_id=1, source_target_pairs={{0,4},{1,5},{2,6},{3,7},{4,0},{5,1},{6,2},{7,3},{8,12},{9,13},{10,... | collective-permute-start | bytes 3145736 | tf_op jit(solution)/shard_map/ppermute | solution.py:426
  201.6 13.8 %collective-permute-start.14 = (bf16[2,128,1024]{2,1,0:T(8,128)(2,1)S(1)}, bf16[2,128,1024]{2,1,0:T(8,128)(2,1)S(1)}, u32[]{:S(2)}, u32[]{:S(2)}) collective-permute-start(bf16[2,128,1024]{2,1,0:T(8,128)(2,1)S(1)} %get-tuple-element.465), channel_id=1, source_target_pairs={{0,8},{1,9},{2,10},{3,11},{4,12},{5,13},{6,14},{7,15},{8,0},{9,1},... | collective-permute-start | bytes 1572872 | tf_op jit(solution)/shard_map/ppermute | solution.py:426
  202.6 13.6 %collective-permute-start.15 = (bf16[2,128,1024]{2,1,0:T(8,128)(2,1)S(1)}, bf16[2,128,1024]{2,1,0:T(8,128)(2,1)S(1)}, u32[]{:S(2)}, u32[]{:S(2)}) collective-permute-start(bf16[2,128,1024]{2,1,0:T(8,128)(2,1)S(1)} %get-tuple-element.465), channel_id=1, source_target_pairs={{0,16},{1,17},{2,18},{3,19},{4,20},{5,21},{6,22},{7,23},{8,24},{9,... | collective-permute-start | bytes 1572872 | tf_op jit(solution)/shard_map/ppermute | solution.py:426
  230.6 25.6 %collective-permute-start.19 = (bf16[512,1024]{1,0:T(8,128)(2,1)S(1)}, bf16[512,1024]{1,0:T(8,128)(2,1)S(1)}, u32[]{:S(2)}, u32[]{:S(2)}) collective-permute-start(bf16[512,1024]{1,0:T(8,128)(2,1)S(1)} %get-tuple-element.262.rows_ref.near_ref), channel_id=1, source_target_pairs={{0,1},{1,0},{2,3},{3,2},{4,5},{5,4},{6,7},{7,6},{8,9},{9,8},{10,11... | collective-permute-start | bytes 3145736 | tf_op jit(solution)/shard_map/ppermute | solution.py:426
  231.9 27.7 %collective-permute-start.22 = (bf16[2,128,2048]{2,1,0:T(8,128)(2,1)S(1)}, bf16[2,128,2048]{2,1,0:T(8,128)(2,1)S(1)}, u32[]{:S(2)}, u32[]{:S(2)}) collective-permute-start(bf16[2,128,2048]{2,1,0:T(8,128)(2,1)S(1)} %broadcast_select_fusion.rest_0_), channel_id=1, source_target_pairs={{0,8},{1,9},{2,10},{3,11},{4,12},{5,13},{6,14},{7,15},{8,0},{9,1},... | collective-permute-start | bytes 3145736 | tf_op jit(solution)/shard_map/ppermute | solution.py:426
  232.5 27.7 %collective-permute-start.23 = (bf16[2,128,2048]{2,1,0:T(8,128)(2,1)S(1)}, bf16[2,128,2048]{2,1,0:T(8,128)(2,1)S(1)}, u32[]{:S(2)}, u32[]{:S(2)}) collective-permute-start(bf16[2,128,2048]{2,1,0:T(8,128)(2,1)S(1)} %broadcast_select_fusion.rest_0_), channel_id=1, source_target_pairs={{0,16},{1,17},{2,18},{3,19},{4,20},{5,21},{6,22},{7,23},{8,24},{9,... | collective-permute-start | bytes 3145736 | tf_op jit(solution)/shard_map/ppermute | solution.py:426
  258.6 25.5 %collective-permute-start.25 = (bf16[2,128,2048]{2,1,0:T(8,128)(2,1)}, bf16[2,128,2048]{2,1,0:T(8,128)(2,1)S(1)}, u32[]{:S(2)}, u32[]{:S(2)}) collective-permute-start(bf16[2,128,2048]{2,1,0:T(8,128)(2,1)} %collective-permute-done.16.rest_4_), channel_id=1, source_target_pairs={{0,8},{1,9},{2,10},{3,11},{4,12},{5,13},{6,14},{7,15},{8,0},{9,1},... | collective-permute-start | bytes 3145736 | tf_op jit(solution)/shard_map/ppermute | solution.py:426
  259.6 25.1 %collective-permute-start.26 = (bf16[2,128,2048]{2,1,0:T(8,128)(2,1)}, bf16[2,128,2048]{2,1,0:T(8,128)(2,1)S(1)}, u32[]{:S(2)}, u32[]{:S(2)}) collective-permute-start(bf16[2,128,2048]{2,1,0:T(8,128)(2,1)} %collective-permute-done.16.rest_4_), channel_id=1, source_target_pairs={{0,16},{1,17},{2,18},{3,19},{4,20},{5,21},{6,22},{7,23},{8,24},{9,... | collective-permute-start | bytes 3145736 | tf_op jit(solution)/shard_map/ppermute | solution.py:426
  260.3 24.4 %collective-permute-start.27 = (bf16[512,1024]{1,0:T(8,128)(2,1)S(1)}, bf16[512,1024]{1,0:T(8,128)(2,1)S(1)}, u32[]{:S(2)}, u32[]{:S(2)}) collective-permute-start(bf16[512,1024]{1,0:T(8,128)(2,1)S(1)} %copy-done.5), channel_id=1, source_target_pairs={{2,4},{3,5},{4,2},{5,3},{10,12},{11,13},{12,10},{13,11},{18,20},{1... | collective-permute-start | bytes 3145736 | tf_op jit(solution)/shard_map/ppermute | solution.py:439
  284.0 27.8 %collective-permute-start.29 = (bf16[512,1024]{1,0:T(8,128)(2,1)S(1)}, bf16[512,1024]{1,0:T(8,128)(2,1)S(1)}, u32[]{:S(2)}, u32[]{:S(2)}) collective-permute-start(bf16[512,1024]{1,0:T(8,128)(2,1)S(1)} %mix_far.3), channel_id=1, source_target_pairs={{0,1},{1,0},{2,3},{3,2},{4,5},{5,4},{6,7},{7,6},{8,9},{9,8},{10,11... | collective-permute-start | bytes 3145736 | tf_op jit(solution)/shard_map/ppermute | solution.py:426
  284.7 26.6 %collective-permute-start.31 = (bf16[2,128,2048]{2,1,0:T(8,128)(2,1)S(1)}, bf16[2,128,2048]{2,1,0:T(8,128)(2,1)S(1)}, u32[]{:S(2)}, u32[]{:S(2)}) collective-permute-start(bf16[2,128,2048]{2,1,0:T(8,128)(2,1)S(1)} %collective-permute-done.26.rest_6_), channel_id=1, source_target_pairs={{0,8},{1,9},{2,10},{3,11},{4,12},{5,13},{6,14},{7,15},{8,0},{9,1},... | collective-permute-start | bytes 3145736 | tf_op jit(solution)/shard_map/ppermute | solution.py:426
  288.3 23.0 %collective-permute-start.30 = (bf16[2,128,2048]{2,1,0:T(8,128)(2,1)S(1)}, bf16[2,128,2048]{2,1,0:T(8,128)(2,1)S(1)}, u32[]{:S(2)}, u32[]{:S(2)}) collective-permute-start(bf16[2,128,2048]{2,1,0:T(8,128)(2,1)S(1)} %collective-permute-done.22.rest_1_), channel_id=1, source_target_pairs={{0,16},{1,17},{2,18},{3,19},{4,20},{5,21},{6,22},{7,23},{8,24},{9,... | collective-permute-start | bytes 3145736 | tf_op jit(solution)/shard_map/ppermute | solution.py:426
  363.2 25.4 %collective-permute-start.37 = (bf16[512,1024]{1,0:T(8,128)(2,1)S(1)}, bf16[512,1024]{1,0:T(8,128)(2,1)S(1)}, u32[]{:S(2)}, u32[]{:S(2)}) collective-permute-start(bf16[512,1024]{1,0:T(8,128)(2,1)S(1)} %get-tuple-element.310.grad_ref.grad_near_ref), channel_id=1, source_target_pairs={{0,1},{1,0},{2,3},{3,2},{4,5},{5,4},{6,7},{7,6},{8,9},{9,8},{10,11... | collective-permute-start | bytes 3145736 | tf_op jit(solution)/shard_map/ppermute | solution.py:426
  370.9 47.7 %collective-permute-start.40 = (bf16[2,2,2,128,1024]{4,3,2,1,0:T(8,128)(2,1)S(1)}, bf16[2,2,2,128,1024]{4,3,2,1,0:T(8,128)(2,1)S(1)}, u32[]{:S(2)}, u32[]{:S(2)}) collective-permute-start(bf16[2,2,2,128,1024]{4,3,2,1,0:T(8,128)(2,1)S(1)} %get-tuple-element.325), channel_id=1, source_target_pairs={{0,16},{1,17},{2,18},{3,19},{4,20},{5,21},{6,22},{7,23},{8,24},{9,... | collective-permute-start | bytes 6291464 | tf_op jit(solution)/shard_map/ppermute | solution.py:426
  373.2 18.3 %collective-permute-start.38 = (bf16[512,256]{1,0:T(8,128)(2,1)S(1)}, bf16[512,256]{1,0:T(8,128)(2,1)S(1)}, u32[]{:S(2)}, u32[]{:S(2)}) collective-permute-start(bf16[512,256]{1,0:T(8,128)(2,1)S(1)} %get-tuple-element.317), channel_id=1, source_target_pairs={{0,4},{1,5},{2,6},{3,7},{4,0},{5,1},{6,2},{7,3},{8,12},{9,13},{10,... | collective-permute-start | bytes 786440 | tf_op jit(solution)/shard_map/ppermute | solution.py:426
  389.5 49.5 %collective-permute-start.34 = (bf16[512,1024]{1,0:T(8,128)(2,1)S(1)}, bf16[512,1024]{1,0:T(8,128)(2,1)S(1)}, u32[]{:S(2)}, u32[]{:S(2)}) collective-permute-start(bf16[512,1024]{1,0:T(8,128)(2,1)S(1)} %get-tuple-element.300), channel_id=1, source_target_pairs={{2,4},{3,5},{4,2},{5,3},{10,12},{11,13},{12,10},{13,11},{18,20},{1... | collective-permute-start | bytes 3145736 | tf_op jit(solution)/shard_map/ppermute | solution.py:439
  390.3 50.8 %collective-permute-start.43 = (bf16[2,2,2,128,1024]{4,3,2,1,0:T(8,128)(2,1)S(1)}, bf16[2,2,2,128,1024]{4,3,2,1,0:T(8,128)(2,1)S(1)}, u32[]{:S(2)}, u32[]{:S(2)}) collective-permute-start(bf16[2,2,2,128,1024]{4,3,2,1,0:T(8,128)(2,1)S(1)} %get-tuple-element.335), channel_id=1, source_target_pairs={{0,8},{1,9},{2,10},{3,11},{4,12},{5,13},{6,14},{7,15},{8,0},{9,1},... | collective-permute-start | bytes 6291464 | tf_op jit(solution)/shard_map/ppermute | solution.py:426
  441.1 27.1 %collective-permute-start.45 = (bf16[2,2,128,1024]{3,2,0,1:T(8,128)(2,1)}, bf16[2,2,128,1024]{3,2,0,1:T(8,128)(2,1)}, u32[]{:S(2)}, u32[]{:S(2)}) collective-permute-start(bf16[2,2,128,1024]{3,2,0,1:T(8,128)(2,1)} %copy.48), channel_id=1, source_target_pairs={{0,8},{1,9},{2,10},{3,11},{4,12},{5,13},{6,14},{7,15},{8,0},{9,1},... | collective-permute-start | bytes 3145736 | tf_op jit(solution)/shard_map/ppermute | solution.py:426
  445.7 25.2 %collective-permute-start.46 = (bf16[2,2,128,1024]{3,2,0,1:T(8,128)(2,1)}, bf16[2,2,128,1024]{3,2,0,1:T(8,128)(2,1)}, u32[]{:S(2)}, u32[]{:S(2)}) collective-permute-start(bf16[2,2,128,1024]{3,2,0,1:T(8,128)(2,1)} %copy.49), channel_id=1, source_target_pairs={{0,16},{1,17},{2,18},{3,19},{4,20},{5,21},{6,22},{7,23},{8,24},{9,... | collective-permute-start | bytes 3145736 | tf_op jit(solution)/shard_map/ppermute | solution.py:426
  448.5 28.5 %collective-permute-start.44 = (bf16[512,1024]{1,0:T(8,128)(2,1)}, bf16[512,1024]{1,0:T(8,128)(2,1)}, u32[]{:S(2)}, u32[]{:S(2)}) collective-permute-start(bf16[512,1024]{1,0:T(8,128)(2,1)} %unproject_far.2), channel_id=1, source_target_pairs={{0,1},{1,0},{2,3},{3,2},{4,5},{5,4},{6,7},{7,6},{8,9},{9,8},{10,11... | collective-permute-start | bytes 3145736 | tf_op jit(solution)/shard_map/ppermute | solution.py:426
  460.5 27.4 %collective-permute-start.47 = (bf16[4,2,128,1024]{2,3,1,0:T(8,128)(2,1)}, bf16[4,2,128,1024]{2,3,1,0:T(8,128)(2,1)}, u32[]{:S(2)}, u32[]{:S(2)}) collective-permute-start(bf16[4,2,128,1024]{2,3,1,0:T(8,128)(2,1)} %copy.55), channel_id=1, source_target_pairs={{0,4},{1,5},{2,6},{3,7},{4,0},{5,1},{6,2},{7,3},{8,12},{9,13},{10,... | collective-permute-start | bytes 6291464 | tf_op jit(solution)/shard_map/ppermute | solution.py:426
  487.5 28.2 %collective-permute-start.50 = (bf16[2,2,128,1024]{3,2,0,1:T(8,128)(2,1)}, bf16[2,2,128,1024]{3,2,0,1:T(8,128)(2,1)}, u32[]{:S(2)}, u32[]{:S(2)}) collective-permute-start(bf16[2,2,128,1024]{3,2,0,1:T(8,128)(2,1)} %pad_maximum_fusion.2), channel_id=1, source_target_pairs={{0,1},{1,0},{2,3},{3,2},{4,5},{5,4},{6,7},{7,6},{8,9},{9,8},{10,11... | collective-permute-start | bytes 3145736 | tf_op jit(solution)/shard_map/ppermute | solution.py:426
  491.9 25.6 %collective-permute-start.51 = (bf16[2,2,128,1024]{2,3,1,0:T(8,128)(2,1)}, bf16[2,2,128,1024]{2,3,1,0:T(8,128)(2,1)}, u32[]{:S(2)}, u32[]{:S(2)}) collective-permute-start(bf16[2,2,128,1024]{2,3,1,0:T(8,128)(2,1)} %get-tuple-element.452), channel_id=1, source_target_pairs={{0,16},{1,17},{2,18},{3,19},{4,20},{5,21},{6,22},{7,23},{8,24},{9,... | collective-permute-start | bytes 3145736 | tf_op jit(solution)/shard_map/ppermute | solution.py:426
  518.8 33.8 %collective-permute-start.55 = (bf16[2,128,1024]{1,2,0:T(8,128)(2,1)S(1)}, bf16[2,128,1024]{1,2,0:T(8,128)(2,1)S(1)}, u32[]{:S(2)}, u32[]{:S(2)}) collective-permute-start(bf16[2,128,1024]{1,2,0:T(8,128)(2,1)S(1)} %fusion.2), channel_id=1, source_target_pairs={{0,8},{1,9},{2,10},{3,11},{4,12},{5,13},{6,14},{7,15},{8,0},{9,1},... | collective-permute-start | bytes 1572872 | tf_op jit(solution)/shard_map/ppermute | solution.py:426
  526.6 25.1 %collective-permute-start.52 = (bf16[512,1024]{1,0:T(8,128)(2,1)S(1)}, bf16[512,1024]{1,0:T(8,128)(2,1)S(1)}, u32[]{:S(2)}, u32[]{:S(2)}) collective-permute-start(bf16[512,1024]{1,0:T(8,128)(2,1)S(1)} %get-tuple-element.360.grad_ref.grad_near_ref), channel_id=1, source_target_pairs={{0,1},{1,0},{2,3},{3,2},{4,5},{5,4},{6,7},{7,6},{8,9},{9,8},{10,11... | collective-permute-start | bytes 3145736 | tf_op jit(solution)/shard_map/ppermute | solution.py:426
  535.3 20.2 %collective-permute-start.53 = (bf16[512,256]{1,0:T(8,128)(2,1)S(1)}, bf16[512,256]{1,0:T(8,128)(2,1)S(1)}, u32[]{:S(2)}, u32[]{:S(2)}) collective-permute-start(bf16[512,256]{1,0:T(8,128)(2,1)S(1)} %get-tuple-element.367), channel_id=1, source_target_pairs={{0,4},{1,5},{2,6},{3,7},{4,0},{5,1},{6,2},{7,3},{8,12},{9,13},{10,... | collective-permute-start | bytes 786440 | tf_op jit(solution)/shard_map/ppermute | solution.py:426
  535.4 48.0 %collective-permute-start.56 = (bf16[2,2,2,128,1024]{4,3,2,1,0:T(8,128)(2,1)S(1)}, bf16[2,2,2,128,1024]{4,3,2,1,0:T(8,128)(2,1)S(1)}, u32[]{:S(2)}, u32[]{:S(2)}) collective-permute-start(bf16[2,2,2,128,1024]{4,3,2,1,0:T(8,128)(2,1)S(1)} %get-tuple-element.381), channel_id=1, source_target_pairs={{0,16},{1,17},{2,18},{3,19},{4,20},{5,21},{6,22},{7,23},{8,24},{9,... | collective-permute-start | bytes 6291464 | tf_op jit(solution)/shard_map/ppermute | solution.py:426
  544.9 59.0 %collective-permute-start.59 = (bf16[2,2,2,128,1024]{4,3,2,1,0:T(8,128)(2,1)S(1)}, bf16[2,2,2,128,1024]{4,3,2,1,0:T(8,128)(2,1)S(1)}, u32[]{:S(2)}, u32[]{:S(2)}) collective-permute-start(bf16[2,2,2,128,1024]{4,3,2,1,0:T(8,128)(2,1)S(1)} %get-tuple-element.391), channel_id=1, source_target_pairs={{0,8},{1,9},{2,10},{3,11},{4,12},{5,13},{6,14},{7,15},{8,0},{9,1},... | collective-permute-start | bytes 6291464 | tf_op jit(solution)/shard_map/ppermute | solution.py:426
  554.6 53.9 %collective-permute-start.60 = (bf16[2,128,1024]{2,1,0:T(8,128)(2,1)S(1)}, bf16[2,128,1024]{2,1,0:T(8,128)(2,1)S(1)}, u32[]{:S(2)}, u32[]{:S(2)}) collective-permute-start(bf16[2,128,1024]{2,1,0:T(8,128)(2,1)S(1)} %get-tuple-element.461), channel_id=1, source_target_pairs={{4,6},{5,7},{6,4},{7,5},{12,14},{13,15},{14,12},{15,13},{20,22},{2... | collective-permute-start | bytes 1572872 | tf_op jit(solution)/shard_map/ppermute | solution.py:431
  555.5 53.1 %collective-permute-start.61 = (bf16[2,128,1024]{2,1,0:T(8,128)(2,1)S(1)}, bf16[2,128,1024]{2,1,0:T(8,128)(2,1)S(1)}, u32[]{:S(2)}, u32[]{:S(2)}) collective-permute-start(bf16[2,128,1024]{2,1,0:T(8,128)(2,1)S(1)} %get-tuple-element.460), channel_id=1, source_target_pairs={{0,4},{1,5},{2,6},{3,7},{4,2},{5,3},{6,0},{7,1},{8,12},{9,13},{10,... | collective-permute-start | bytes 1572872 | tf_op jit(solution)/shard_map/ppermute | solution.py:431
  556.7 50.5 %collective-permute-start.62 = (bf16[128,1024]{0,1:T(8,128)(2,1)S(1)}, bf16[128,1024]{0,1:T(8,128)(2,1)S(1)}, u32[]{:S(2)}, u32[]{:S(2)}) collective-permute-start(bf16[128,1024]{0,1:T(8,128)(2,1)S(1)} %get-tuple-element.462), channel_id=1, source_target_pairs={{0,2},{1,3},{2,0},{3,1},{4,6},{5,7},{6,4},{7,5},{8,10},{9,11},{10,... | collective-permute-start | bytes 786440 | tf_op jit(solution)/shard_map/ppermute | solution.py:426
  583.4 32.3 %collective-permute-start.57 = (bf16[3,1024,128]{2,1,0:T(8,128)(2,1)}, bf16[3,1024,128]{2,1,0:T(8,128)(2,1)}, u32[]{:S(2)}, u32[]{:S(2)}) collective-permute-start(bf16[3,1024,128]{2,1,0:T(8,128)(2,1)} %get-tuple-element.388), channel_id=1, source_target_pairs={{0,4},{1,5},{2,6},{3,7},{4,0},{5,1},{6,2},{7,3},{8,12},{9,13},{10,... | collective-permute-start | bytes 2359304 | tf_op jit(solution)/shard_map/ppermute | solution.py:426
  603.9 27.4 %collective-permute-start.64 = (bf16[2,2,128,1024]{3,2,1,0:T(8,128)(2,1)}, bf16[2,2,128,1024]{3,2,1,0:T(8,128)(2,1)}, u32[]{:S(2)}, u32[]{:S(2)}) collective-permute-start(bf16[2,2,128,1024]{3,2,1,0:T(8,128)(2,1)} %bitcast_add_fusion.1), channel_id=1, source_target_pairs={{0,8},{1,9},{2,10},{3,11},{4,12},{5,13},{6,14},{7,15},{8,0},{9,1},... | collective-permute-start | bytes 3145736 | tf_op jit(solution)/shard_map/ppermute | solution.py:426
  608.6 25.8 %collective-permute-start.65 = (bf16[2,2,128,1024]{3,2,1,0:T(8,128)(2,1)}, bf16[2,2,128,1024]{3,2,1,0:T(8,128)(2,1)}, u32[]{:S(2)}, u32[]{:S(2)}) collective-permute-start(bf16[2,2,128,1024]{3,2,1,0:T(8,128)(2,1)} %bitcast_add_fusion), channel_id=1, source_target_pairs={{0,16},{1,17},{2,18},{3,19},{4,20},{5,21},{6,22},{7,23},{8,24},{9,... | collective-permute-start | bytes 3145736 | tf_op jit(solution)/shard_map/ppermute | solution.py:426
  623.1 25.5 %collective-permute-start.63 = (bf16[512,1024]{1,0:T(8,128)(2,1)S(1)}, bf16[512,1024]{1,0:T(8,128)(2,1)S(1)}, u32[]{:S(2)}, u32[]{:S(2)}) collective-permute-start(bf16[512,1024]{1,0:T(8,128)(2,1)S(1)} %unproject_far.3), channel_id=1, source_target_pairs={{0,1},{1,0},{2,3},{3,2},{4,5},{5,4},{6,7},{7,6},{8,9},{9,8},{10,11... | collective-permute-start | bytes 3145736 | tf_op jit(solution)/shard_map/ppermute | solution.py:426
  (147 other events, 1224.8 us)
